TPU v7x, 32 devices: a whole 2x2x4 slice. The times are simulated.
32 devices in a mesh: seq: 4 (over y, x), batch: 8 (over z, core).
Axes of the slice: x: 2, y: 2, z: 4, core: 2. Of those that a mesh axis runs over, the one named last changes fastest.
Arguments:
- inputs: bfloat16 [8, 512, 2048], P('batch', 'seq'), may hold values from -6 to 6
- cotangent: bfloat16 [8, 512, 2048], P('batch', 'seq'), may hold values from -6 to 6
- doc_lengths: int32 [8, 4], P('batch'), may hold values from 1 to 509, as said below
- head_width: int32 [8], P('batch'), may hold values from 16 to 64, as said below
- pre_gain: float32 [2048], replicated, may hold values from 0.5 to 1.5
- in_weight: bfloat16 [2048, 8448], P(('seq', 'batch')), may hold values from -0.125 to 0.125
- step_weight: bfloat16 [2048, 64], P(('seq', 'batch')), may hold values from -0.125 to 0.125
- conv_weight: float32 [4, 4352], replicated, may hold values from -0.8 to 0.8
- conv_bias: float32 [4352], replicated, may hold values from -0.5 to 0.5
- step_bias: float32 [64], replicated, may hold values from -7 to -5
- decay_log: float32 [64], replicated, may hold values from -2.3 to 3
- skip_gain: float32 [64], replicated, may hold values from 0.5 to 1.5
- norm_gain: float32 [4096], replicated, may hold values from 0.5 to 1.5
- out_weight: bfloat16 [4096, 2048], P(('seq', 'batch')), may hold values from -0.09375 to 0.09375
Outputs:
- output: bfloat16 [8, 512, 2048], P('batch', 'seq')
- grad_inputs: float32 [8, 512, 2048], P('batch', 'seq')
- grad_pre_gain: float32 [2048], replicated
- grad_in_weight: float32 [2048, 8448], P(('seq', 'batch'))
- grad_step_weight: float32 [2048, 64], P(('seq', 'batch'))
- grad_conv_weight: float32 [4, 4352], replicated
- grad_conv_bias: float32 [4352], replicated
- grad_step_bias: float32 [64], replicated
- grad_decay_log: float32 [64], replicated
- grad_skip_gain: float32 [64], replicated
- grad_norm_gain: float32 [4096], replicated
- grad_out_weight: float32 [4096, 2048], P(('seq', 'batch'))
Inputs may be any that keep to these rules, and one draw needn't show every extreme that they name: `doc_lengths`: each row holds the lengths of the 4 documents of one packed sequence in order; they sum to 512. Some sequence has a document of the most length. `head_width`: heads used by each sequence's nested model, a multiple of a quarter of 64; some sequence uses all 64.
All inputs are finite; a program needn't handle non-finite values.
Results may differ from a plain program's by a relative error of at most 0.0095.
Values may be sent and summed in bfloat16 or wider, within the bound.
A program may use at most 448 MiB of HBM per device.

v0:
```python
from functools import partial

import jax
import jax.numpy as jnp
from jax import lax
from jax.sharding import PartitionSpec as P

H = 64
P_SIZE = 64
N = 128
CONV = 4
E = 4096


epsilon = 1e-05
block_precision = lax.Precision.HIGH


def shifted(shard, axis, by):
    peers = lax.axis_size(axis)
    pairs = [(i, i + by) for i in range(peers) if 0 <= i + by < peers]
    return lax.ppermute(shard, axis, pairs)


def prefix(shard, axis, combine, identity):
    peers, mine = (lax.axis_size(axis), lax.axis_index(axis))
    everything = jax.tree.map(
        lambda part, kind: lax.all_gather(part.astype(kind), axis),
        shard,
        (jnp.bfloat16, jnp.bfloat16),
    )
    start = jax.tree.map(
        lambda part, zero: jnp.broadcast_to(jnp.asarray(zero, part.dtype), part.shape),
        shard,
        identity,
    )

    def step(k, before):
        reached = k < mine
        new = combine(
            before, jax.tree.map(lambda part, own: part[k].astype(own.dtype), everything, shard)
        )
        return jax.tree.map(lambda a, b: jnp.where(reached, a, b), new, before)

    return lax.fori_loop(0, peers, step, start)


def entering(shard, axis, join, neutral):
    count = lax.axis_size(axis)
    place = lax.axis_index(axis)
    ahead = count - 1 - place
    gathered = jax.tree.map(
        lambda a, kind: lax.all_gather(a.astype(kind), axis),
        shard,
        jax.tree.map(lambda a: jnp.bfloat16 if a.dtype == jnp.float32 else a.dtype, shard),
    )
    state = jax.tree.map(lambda a, e: jnp.zeros_like(a) + jnp.asarray(e, a.dtype), shard, neutral)

    def one(step, state):
        source = count - 1 - step
        return join(
            state,
            jax.tree.map(
                lambda a, own: lax.dynamic_index_in_dim(a, source, 0, False).astype(own.dtype),
                gathered,
                shard,
            ),
        )

    return lax.fori_loop(0, ahead, one, state)


def doc_index(places, doc_ends):
    return jnp.sum((places[:, None] >= doc_ends[None, :-1]).astype(jnp.int32), axis=1)


def within_group(scores, same_doc, grouped):
    values, step_sizes, cum_decay = grouped
    spread = cum_decay[:, :, None] - cum_decay[:, None, :]
    decay_rows = jnp.where(same_doc[None], jnp.exp(jnp.minimum(spread, 0.0)), 0.0)
    weights = decay_rows * scores[None] * step_sizes[:, None, :]
    return jnp.einsum("gts,gsp->gtp", weights, values, precision=block_precision)


def combine_carry(previous, current):
    return (previous[0] * current[0], current[1] + current[0][:, None, None] * previous[1])


def mixer_inputs(activated, step_raw, step_bias, decay_log):
    step_sizes = jax.nn.softplus(step_raw + step_bias[None, :])
    values = activated[:, :E].reshape(activated.shape[0], H, P_SIZE)
    log_decay = -step_sizes * jnp.exp(decay_log)[None, :]
    return (values, activated[:, E : E + N], activated[:, E + N :], step_sizes, log_decay)


def block_summary(doc_ids, inflow, activated, step_raw, step_bias, decay_log):
    values, write_keys, read_keys, step_sizes, log_decay = mixer_inputs(
        activated, step_raw, step_bias, decay_log
    )
    cum_decay = jnp.cumsum(log_decay, axis=0)
    final_weight = (
        jnp.where(
            (doc_ids == doc_ids[-1])[:, None], jnp.exp(cum_decay[-1][None, :] - cum_decay), 0.0
        )
        * step_sizes
    )
    block_add = jnp.einsum(
        "thp,tn->hpn", values * final_weight[:, :, None], write_keys, precision=block_precision
    )
    block_gain = inflow[-1] * jnp.exp(cum_decay[-1])
    return (block_gain, block_add)


def block_output(doc_ids, inflow, activated, step_raw, step_bias, decay_log, skip_gain, state_in):
    values, write_keys, read_keys, step_sizes, log_decay = mixer_inputs(
        activated, step_raw, step_bias, decay_log
    )
    length_block = values.shape[0]
    cum_decay = jnp.cumsum(log_decay, axis=0)
    row_ids = jnp.arange(length_block)
    same_doc = (doc_ids[:, None] == doc_ids[None, :]) & (row_ids[:, None] >= row_ids[None, :])
    scores = jnp.dot(
        read_keys, write_keys.T, precision=block_precision, preferred_element_type=jnp.float32
    )
    group_size = H // 4
    grouped = (
        values.transpose(1, 0, 2).reshape(4, group_size, length_block, P_SIZE),
        step_sizes.T.reshape(4, group_size, length_block),
        cum_decay.T.reshape(4, group_size, length_block),
    )
    within = lax.map(jax.checkpoint(partial(within_group, scores, same_doc)), grouped)
    within = within.reshape(H, length_block, P_SIZE).transpose(1, 0, 2)
    carry_weight = inflow[:, None] * jnp.exp(cum_decay)
    carried = (
        jnp.einsum("tn,hpn->thp", read_keys, state_in, precision=block_precision)
        * carry_weight[:, :, None]
    )
    return within + carried + skip_gain[None, :, None] * values


def gated_norm(head_mask, head_total, mixer_rows, gate_rows, norm_gain):
    masked = (mixer_rows * head_mask[None, :, None]).reshape(mixer_rows.shape[0], E)
    gated_rows = masked * jax.nn.silu(gate_rows)
    mean_square = jnp.sum(gated_rows * gated_rows, axis=1, keepdims=True) / head_total
    return gated_rows * lax.rsqrt(mean_square + epsilon) * norm_gain[None, :]


def pre_norm(rows_in, gain_in):
    inv_rms = lax.rsqrt(jnp.mean(rows_in * rows_in, axis=1, keepdims=True) + epsilon)
    return rows_in * inv_rms * gain_in[None, :]


def body(
    inputs,
    cotangent,
    doc_lengths,
    head_width,
    pre_gain,
    in_weight,
    step_weight,
    conv_weight,
    conv_bias,
    step_bias,
    decay_log,
    skip_gain,
    norm_gain,
    out_weight,
):
    tokens = inputs.shape[1]
    seq_rows = inputs[0].astype(jnp.float32)
    cot_rows = cotangent[0]
    full_in, full_step, full_out = (
        lax.all_gather(in_weight, ("seq", "batch"), axis=0, tiled=True),
        lax.all_gather(step_weight, ("seq", "batch"), axis=0, tiled=True),
        lax.all_gather(out_weight, ("seq", "batch"), axis=0, tiled=True),
    )
    first_pos = lax.axis_index("seq") * tokens
    places = first_pos + jnp.arange(tokens, dtype=jnp.int32)
    doc_ends = jnp.cumsum(doc_lengths[0])
    doc_ids = doc_index(places, doc_ends)
    inflow = (doc_ids == doc_index(jnp.reshape(first_pos - 1, (1,)), doc_ends)).astype(jnp.float32)
    head_count = head_width[0]
    head_mask = (jnp.arange(H) < head_count).astype(jnp.float32)
    head_total = (head_count * P_SIZE).astype(jnp.float32)
    tap_masks = []
    for tap_index in range(CONV):
        source = places - (CONV - 1 - tap_index)
        tap_masks.append(
            ((source >= 0) & (doc_index(source, doc_ends) == doc_ids)).astype(jnp.float32)
        )
    normed_f32, pre_back = jax.vjp(pre_norm, seq_rows, pre_gain)
    normed = normed_f32.astype(jnp.bfloat16)
    projected = jnp.dot(normed, full_in, preferred_element_type=jnp.float32)
    step_raw = jnp.dot(normed, full_step, preferred_element_type=jnp.float32)
    gate_rows = projected[:, :E]
    conv_in = projected[:, E:].astype(jnp.bfloat16)
    edge_rows = shifted(conv_in[tokens - (CONV - 1) :], "seq", 1)
    extended = jnp.concatenate([edge_rows, conv_in], axis=0).astype(jnp.float32)

    def convolve(rows_in, tap_weight, tap_bias):
        conv_total = tap_bias[None, :] + jnp.zeros((tokens, rows_in.shape[1]), jnp.float32)
        for tap_index in range(CONV):
            conv_total = (
                conv_total
                + tap_weight[tap_index][None, :]
                * rows_in[tap_index : tap_index + tokens]
                * tap_masks[tap_index][:, None]
            )
        return jax.nn.silu(conv_total)

    activated_f32, conv_back = jax.vjp(convolve, extended, conv_weight, conv_bias)
    activated = activated_f32.astype(jnp.bfloat16).astype(jnp.float32)
    summary = partial(block_summary, doc_ids, inflow)
    (chain_gain, chain_add), summary_back = jax.vjp(
        summary, activated, step_raw, step_bias, decay_log
    )
    identity = (jnp.ones((H,), jnp.float32), jnp.zeros((H, P_SIZE, N), jnp.float32))
    state_in = prefix((chain_gain, chain_add), "seq", combine_carry, identity)[1]
    output_fn = partial(block_output, doc_ids, inflow)
    mixer_rows, output_back = jax.vjp(
        output_fn, activated, step_raw, step_bias, decay_log, skip_gain, state_in
    )
    norm_fn = partial(gated_norm, head_mask, head_total)
    normed_out, gate_back = jax.vjp(norm_fn, mixer_rows, gate_rows, norm_gain)
    mixed_rows = normed_out.astype(jnp.bfloat16)
    branch = jnp.dot(mixed_rows, full_out, preferred_element_type=jnp.float32)
    output = (seq_rows + branch).astype(jnp.bfloat16)[None]
    contract_cols = (((1,), (1,)), ((), ()))
    contract_rows = (((0,), (0,)), ((), ()))
    grad_mixed = lax.dot_general(
        cot_rows, full_out, contract_cols, preferred_element_type=jnp.float32
    )
    out_term = lax.dot_general(
        mixed_rows, cot_rows, contract_rows, preferred_element_type=jnp.float32
    )
    grad_out_weight = lax.psum_scatter(out_term, ("seq", "batch"), scatter_dimension=0, tiled=True)
    grad_mixer, grad_gate, grad_norm_gain = gate_back(grad_mixed)
    grad_act_out, grad_raw_out, grad_bias_out, grad_log_out, grad_skip, state_grad = output_back(
        grad_mixer
    )
    later_grad = entering((chain_gain, state_grad), "seq", combine_carry, identity)[1]
    grad_gain = jnp.sum(later_grad * state_in, axis=(1, 2))
    grad_act_sum, grad_raw_sum, grad_bias_sum, grad_log_sum = summary_back((grad_gain, later_grad))
    grad_ext, grad_conv_weight, grad_conv_bias = conv_back(grad_act_out + grad_act_sum)
    back_rows = shifted(grad_ext[: CONV - 1].astype(jnp.bfloat16), "seq", -1).astype(jnp.float32)
    grad_conv_in = jnp.concatenate(
        [grad_ext[CONV - 1 : tokens], grad_ext[tokens:] + back_rows], axis=0
    )
    grad_projected = jnp.concatenate([grad_gate, grad_conv_in], axis=1).astype(jnp.bfloat16)
    grad_step_raw = (grad_raw_out + grad_raw_sum).astype(jnp.bfloat16)
    grad_normed = lax.dot_general(
        grad_projected, full_in, contract_cols, preferred_element_type=jnp.float32
    )
    grad_normed = grad_normed + lax.dot_general(
        grad_step_raw, full_step, contract_cols, preferred_element_type=jnp.float32
    )
    grad_seq, grad_pre_gain = pre_back(grad_normed)
    grad_inputs = (grad_seq + cot_rows.astype(jnp.float32))[None]
    grad_cols = jnp.concatenate([grad_projected, grad_step_raw], axis=1)
    in_term = lax.dot_general(normed, grad_cols, contract_rows, preferred_element_type=jnp.float32)
    grad_in_all = lax.psum_scatter(in_term, ("seq", "batch"), scatter_dimension=0, tiled=True)
    in_cols = in_weight.shape[1]
    small_sums = lax.psum(
        (
            grad_pre_gain,
            grad_conv_weight,
            grad_conv_bias,
            grad_bias_out + grad_bias_sum,
            grad_log_out + grad_log_sum,
            grad_skip,
            grad_norm_gain,
        ),
        ("seq", "batch"),
    )
    return (
        output,
        grad_inputs,
        small_sums[0],
        grad_in_all[:, :in_cols],
        grad_in_all[:, in_cols:],
        small_sums[1],
        small_sums[2],
        small_sums[3],
        small_sums[4],
        small_sums[5],
        small_sums[6],
        grad_out_weight,
    )


def solution(mesh):
    in_specs = (
        P("batch", "seq", None),
        P("batch", "seq", None),
        P("batch", None),
        P("batch"),
        P(),
        P(("seq", "batch"), None),
        P(("seq", "batch"), None),
        P(),
        P(),
        P(),
        P(),
        P(),
        P(),
        P(("seq", "batch"), None),
    )
    out_specs = (
        P("batch", "seq", None),
        P("batch", "seq", None),
        P(),
        P(("seq", "batch"), None),
        P(("seq", "batch"), None),
        P(),
        P(),
        P(),
        P(),
        P(),
        P(),
        P(("seq", "batch"), None),
    )
    return jax.shard_map(body, mesh=mesh, in_specs=in_specs, out_specs=out_specs, check_vma=False)
```

profile of v0, /device:TPU:0, one launch (start us, length us, event | category | flops | bytes accessed | tf_op | source)
XLA Modules:
  0.0 1815.9 jit_solution(18403645164661642623)
XLA Ops:
  14.5 48.3 %all_gather.27 = bf16[2048,64]{1,0:T(8,128)(2,1)S(1)} all-gather(bf16[64,64]{1,0:T(8,128)(2,1)} %param.29), channel_id=1, replica_groups=mesh['seq'=4,'batch'=8] {'seq','batch'}, dimensions={0}, use_global_device_ids=true | all-gather | bytes 270336 | tf_op jit(solution)/shard_map/all_gather | solution.py:174
  65.7 152.2 %all-gather.8.cloned.1.call-done = bf16[2048,8448]{1,0:T(8,128)(2,1)} async-done(((bf16[64,8448]{1,0:T(8,128)(2,1)}), bf16[2048,8448]{1,0:T(8,128)(2,1)}) %all-gather.8.cloned.1.call-update) | async-done | bytes 34603024 | tf_op jit(solution)/shard_map/all_gather | solution.py:173
  217.9 17.8 fusion.145
  235.8 3.3 collective-permute-start
  241.0 2.8 multiply_convert_fusion
  246.4 2.9 copy.143
  249.3 3.3 fusion.76
  254.3 10.1 all-gather.2
  268.5 12.3 while.62
  268.5 3.1 fusion.175
  271.6 3.1 fusion.175
  274.7 3.1 fusion.175
  277.8 3.1 fusion.175
  280.8 24.6 %all-gather.12.cloned.1.call-done = bf16[256,64,128]{2,1,0:T(8,128)(2,1)} async-done(((bf16[64,64,128]{2,1,0:T(8,128)(2,1)}), bf16[256,64,128]{2,1,0:T(8,128)(2,1)}) %all-gather.12.cloned.1.call-update) | async-done | bytes 4194320 | tf_op jit(solution)/shard_map/all_gather | solution.py:28
  305.4 13.9 while.63
  305.5 2.9 fusion.176
  308.4 3.6 fusion.176
  312.0 3.6 fusion.176
  315.5 3.8 fusion.176
  319.3 5.7 fusion.66
  325.1 2.9 copy.146
  328.0 4.3 multiply_reduce_fusion.10
  332.8 90.6 %all-gather.10.cloned.1.call-done = bf16[4096,2048]{1,0:T(8,128)(2,1)} async-done(((bf16[128,2048]{1,0:T(8,128)(2,1)}), bf16[4096,2048]{1,0:T(8,128)(2,1)}) %all-gather.10.cloned.1.call-update) | async-done | bytes 16777232 | tf_op jit(solution)/shard_map/all_gather | solution.py:175
  423.4 14.1 multiply_reduce_fusion.4
  438.2 6.3 multiply_reduce_fusion.5
  444.5 2.9 copy.148
  447.4 3.2 multiply_reduce_fusion.8
  457.3 43.2 %while.64 = (s32[]{:T(128)}, f32[128,128]{1,0:T(8,128)S(1)}, f32[4,16,128,64]{2,3,1,0:T(8,128)}, f32[4,16,128]{2,1,0:T(8,128)}, f32[4,16,128]{2,1,0:T(8,128)}, /...) while((s32[]{:T(128)}, f32[128,128]{1,0:T(8,128)S(1)}, ...), condition=%wide.region_19.21_spmd.clone, body=%wide.region_14.20_spmd.clone.sunk | while | flops 207681536 | bytes 5268347 | solution.py:131
  475.0 2.5 fusion.183
  500.5 3.8 bitcast_add_fusion
  504.2 2.9 copy.149
  508.5 4.0 fusion.87
  515.0 10.5 while.61
  515.0 3.5 convert_add_fusion.3
  518.5 3.4 convert_add_fusion.3
  522.0 3.4 convert_add_fusion.3
  525.6 4.5 multiply_reduce_fusion.7
  532.5 2.9 copy.150
  535.5 5.2 multiply_reduce_fusion.3
  552.4 25.5 %fusion.48 = f32[2048,8512]{1,0:T(8,128)} fusion(bf16[128,64]{1,0:T(8,128)(2,1)S(1)} %add_convert_fusion, bf16[3,4352]{1,0:T(4,128)(2,1)S(1)} %fusion.106, bf16[125,4352]{1,0:T(8,128)(2,1)S(1)} %slice.120, bf16[128,4096]{1,0:T(8,128)(2,1)} %get-tuple-element.716, bf16[1,128,2048]{2,1,0:T(8,128)(2,1)S(1)} %copy-done.5, f32[2048]{0:T(1024)S(1)} %copy-done.15, ...), kind=kOutput, calls=%fused_computation.77 | convolution fusion | flops 4472504320 | bytes 72442368 | tf_op jit(solution)/shard_map/dot_general | solution.py:260
  579.6 13.5 fusion.101
  594.1 9.3 fusion.45
  603.5 17.8 fusion.56
  623.1 42.1 %all-reduce.15 = (f32[2048]{0:T(1024)}, f32[4352]{0:T(1024)}, f32[64]{0:T(128)}, f32[64]{0:T(128)}, f32[64]{0:T(128)}, /*index=5*/f32[4096]{0:T(1024)}) all-reduce(f32[2048]{0:T(1024)S(1)} %get-tuple-element.617, f32[4352]{0:T(1024)S(1)} %copy-done.43, f32[64]{0:T(128)S(1)} %add.289, ...), channel_id=1, replica_groups=mesh['seq'=4,'batch'=8] {'seq','batch'}, use_global_device_ids=true, to_apply=%region_30.32 | all-reduce | flops 10688 | bytes 85504 | tf_op jit(solution)/shard_map/psum | solution.py:263
  666.6 653.0 %reduce-scatter.3.cloned.1.call-done = f32[64,8512]{1,0:T(8,128)} async-done(((f32[2048,8512]{1,0:T(8,128)}), f32[64,8512]{1,0:T(8,128)}) %reduce-scatter.3.cloned.1.call-update) | async-done | bytes 2179088 | tf_op jit(solution)/shard_map/reduce_scatter | solution.py:261
  1319.6 3.1 slice.123
  1324.1 116.9 %all-reduce.18.cloned.1.call-done = f32[4,4352]{1,0:T(4,128)} async-done(((f32[4,4352]{1,0:T(4,128)}), f32[4,4352]{1,0:T(4,128)}) %all-reduce.18.cloned.1.call-update) | async-done | bytes 69648 | tf_op jit(solution)/shard_map/psum | solution.py:263
  1441.0 366.3 %reduce-scatter.5.cloned.1.call-done = f32[128,2048]{1,0:T(8,128)} async-done(((f32[4096,2048]{1,0:T(8,128)}), f32[128,2048]{1,0:T(8,128)}) %reduce-scatter.5.cloned.1.call-update) | async-done | bytes 1048592 | tf_op jit(solution)/shard_map/reduce_scatter | solution.py:236
  (347 shorter events, 94.4 us)
Async XLA Ops:
  7.2 57.0 %copy-start.5 = (bf16[1,128,2048]{2,1,0:T(8,128)(2,1)S(1)}, bf16[1,128,2048]{2,1,0:T(8,128)(2,1)}, u32[]{:S(2)}) copy-start(bf16[1,128,2048]{2,1,0:T(8,128)(2,1)} %param.23) | copy-start | bytes 1572868
  7.2 57.0 %copy-start.84 = (f32[64]{0:T(128)S(1)}, f32[64]{0:T(128)}, u32[]{:S(2)}) copy-start(f32[64]{0:T(128)} %param.32) | copy-start | bytes 772
  7.2 57.0 %copy-start.15 = (f32[2048]{0:T(1024)S(1)}, f32[2048]{0:T(1024)}, u32[]{:S(2)}) copy-start(f32[2048]{0:T(1024)} %param.27) | copy-start | bytes 24580
  7.2 57.6 %copy-start.46 = (f32[4,4352]{1,0:T(4,128)S(1)}, f32[4,4352]{1,0:T(4,128)}, u32[]{:S(2)}) copy-start(f32[4,4352]{1,0:T(4,128)} %param.30) | copy-start | bytes 208900
  7.2 210.7 %all-gather.8.cloned.1.call-start = ((), (), s32[]{:S(2)}) async-start(), calls=%async_computation.2 | async-start | bytes 35684352 | tf_op jit(solution)/shard_map/all_gather | solution.py:173
  8.0 297.5 %all-gather.12.cloned.1.call-start = ((), (), s32[]{:S(2)}) async-start(), calls=%async_computation.7 | async-start | bytes 5242880 | tf_op jit(solution)/shard_map/all_gather | solution.py:28
  8.7 56.0 %copy-start.79 = (f32[64]{0:T(128)}, f32[64]{0:T(128)S(1)}, u32[]{:S(2)}) copy-start(f32[64]{0:T(128)S(1)} %exp.47) | copy-start | bytes 772
  13.9 221.8 %copy-start.56 = (pred[128]{0:T(512)(128)(4,1)}, pred[128]{0:T(512)(128)(4,1)S(1)}, u32[]{:S(2)}) copy-start(pred[128]{0:T(512)(128)(4,1)S(1)} %get-tuple-element.734) | copy-start | bytes 388
  13.9 221.8 %copy-start.70 = (f32[128]{0:T(128)}, f32[128]{0:T(128)S(1)}, u32[]{:S(2)}) copy-start(f32[128]{0:T(128)S(1)} %get-tuple-element.733) | copy-start | bytes 1540
  13.9 227.0 %copy-start.58 = (f32[128]{0:T(128)}, f32[128]{0:T(128)S(1)}, u32[]{:S(2)}) copy-start(f32[128]{0:T(128)S(1)} %get-tuple-element.735) | copy-start | bytes 1540
  13.9 227.0 %copy-start.60 = (f32[128]{0:T(128)}, f32[128]{0:T(128)S(1)}, u32[]{:S(2)}) copy-start(f32[128]{0:T(128)S(1)} %get-tuple-element.736) | copy-start | bytes 1540
  14.0 227.0 %copy-start.62 = (f32[128]{0:T(128)}, f32[128]{0:T(128)S(1)}, u32[]{:S(2)}) copy-start(f32[128]{0:T(128)S(1)} %get-tuple-element.737) | copy-start | bytes 1540
  64.2 171.5 %copy-start.77 = (f32[128]{0:T(128)}, f32[128]{0:T(128)S(1)}, u32[]{:S(2)}) copy-start(f32[128]{0:T(128)S(1)} %fusion.94) | copy-start | bytes 1540
  64.2 171.5 %copy-start.51 = (f32[128]{0:T(128)}, f32[128]{0:T(128)S(1)}, u32[]{:S(2)}) copy-start(f32[128]{0:T(128)S(1)} %fusion.128) | copy-start | bytes 1540
  64.6 171.1 %copy-start.17 = (f32[128,64]{1,0:T(8,128)}, f32[128,64]{1,0:T(8,128)S(1)}, u32[]{:S(2)}) copy-start(f32[128,64]{1,0:T(8,128)S(1)} %get-tuple-element.741) | copy-start | bytes 98308
  65.0 176.0 %copy-start.32 = (f32[4352]{0:T(1024)}, f32[4352]{0:T(1024)S(1)}, u32[]{:S(2)}) copy-start(f32[4352]{0:T(1024)S(1)} %get-tuple-element.619) | copy-start | bytes 52228
  65.0 176.0 %copy-start.34 = (f32[4352]{0:T(1024)}, f32[4352]{0:T(1024)S(1)}, u32[]{:S(2)}) copy-start(f32[4352]{0:T(1024)S(1)} %get-tuple-element.620) | copy-start | bytes 52228
  65.0 176.0 %copy-start.36 = (f32[4352]{0:T(1024)}, f32[4352]{0:T(1024)S(1)}, u32[]{:S(2)}) copy-start(f32[4352]{0:T(1024)S(1)} %get-tuple-element.621) | copy-start | bytes 52228
  65.1 176.0 %copy-start.38 = (f32[4352]{0:T(1024)}, f32[4352]{0:T(1024)S(1)}, u32[]{:S(2)}) copy-start(f32[4352]{0:T(1024)S(1)} %get-tuple-element.622) | copy-start | bytes 52228
  65.6 170.1 %copy-start.64 = (f32[64]{0:T(128)}, f32[64]{0:T(128)S(1)}, u32[]{:S(2)}) copy-start(f32[64]{0:T(128)S(1)} %get-tuple-element.732) | copy-start | bytes 772
  235.8 4.9 collective-permute-start
  239.2 10.1 copy-start.19
  252.6 170.8 %all-gather.10.cloned.1.call-start = ((), (), s32[]{:S(2)}) async-start(), calls=%async_computation.3 | async-start | bytes 17301504 | tf_op jit(solution)/shard_map/all_gather | solution.py:175
  253.3 260.1 %all-gather.14.cloned.1.call-start = ((), (), s32[]{:S(2)}) async-start(), calls=%async_computation.8 | async-start | bytes 5242880 | tf_op jit(solution)/shard_map/all_gather | solution.py:53
  254.3 65.1 %copy-start.21 = (f32[128,64]{0,1:T(8,128)}, f32[128,64]{0,1:T(8,128)S(1)}, u32[]{:S(2)}) copy-start(f32[128,64]{0,1:T(8,128)S(1)} %copy.145) | copy-start | bytes 98308
  264.4 54.9 %copy-start.68 = (f32[64]{0:T(128)}, f32[64]{0:T(128)S(1)}, u32[]{:S(2)}) copy-start(f32[64]{0:T(128)S(1)} %compare_convert_fusion) | copy-start | bytes 772
  280.8 24.6 %copy-start.25 = (f32[4,16,128]{2,1,0:T(8,128)}, f32[4,16,128]{2,1,0:T(8,128)S(1)}, u32[]{:S(2)}) copy-start(f32[4,16,128]{2,1,0:T(8,128)S(1)} %get-tuple-element.1108) | copy-start | bytes 98308
  280.8 24.6 %copy-start.26 = (f32[4,16,128]{2,1,0:T(8,128)}, f32[4,16,128]{2,1,0:T(8,128)S(1)}, u32[]{:S(2)}) copy-start(f32[4,16,128]{2,1,0:T(8,128)S(1)} %get-tuple-element.1109) | copy-start | bytes 98308
  280.8 24.6 %copy-start.48 = (f32[1,128,128]{2,1,0:T(8,128)}, f32[1,128,128]{2,1,0:T(8,128)S(1)}, u32[]{:S(2)}) copy-start(f32[1,128,128]{2,1,0:T(8,128)S(1)} %get-tuple-element.1113) | copy-start | bytes 196612
  305.4 13.9 copy-start.72
  328.0 95.4 %copy-start.7 = (bf16[1,128,2048]{2,1,0:T(8,128)(2,1)S(1)}, bf16[1,128,2048]{2,1,0:T(8,128)(2,1)}, u32[]{:S(2)}) copy-start(bf16[1,128,2048]{2,1,0:T(8,128)(2,1)} %param.24) | copy-start | bytes 1572868
  454.4 865.2 %reduce-scatter.3.cloned.1.call-start = ((), (), s32[]{:S(2)}) async-start(), calls=%async_computation.4 | async-start | bytes 72450048 | tf_op jit(solution)/shard_map/reduce_scatter | solution.py:261
  515.0 10.5 copy-start.20
  541.5 8.3 copy-start.80
  543.6 8.7 copy-start.52
  545.3 6.2 collective-permute-start.1
  550.7 27.2 %copy-start.11 = (bf16[125,4352]{1,0:T(8,128)(2,1)}, bf16[125,4352]{1,0:T(8,128)(2,1)S(1)}, u32[]{:S(2)}) copy-start(bf16[125,4352]{1,0:T(8,128)(2,1)S(1)} %slice.120) | copy-start | bytes 3264004
  578.0 863.0 %all-reduce.18.cloned.1.call-start = ((), (), s32[]{:S(2)}) async-start(), calls=%async_computation.5 | async-start | bytes 139264 | tf_op jit(solution)/shard_map/psum | solution.py:263
  579.4 1227.9 %reduce-scatter.5.cloned.1.call-start = ((), (), s32[]{:S(2)}) async-start(), calls=%async_computation.6 | async-start | bytes 34603008 | tf_op jit(solution)/shard_map/reduce_scatter | solution.py:236
  594.0 9.3 copy-start.81
  594.1 9.3 copy-start.82
  594.1 9.3 copy-start.73
  594.1 9.3 copy-start.74
  594.1 9.3 copy-start.83
  594.1 9.3 copy-start.12
  603.5 17.8 copy-start.14
  603.5 17.8 copy-start.53
  621.3 43.9 %copy-start.78 = (f32[128]{0:T(128)S(1)}, f32[128]{0:T(128)}, u32[]{:S(2)}) copy-start(f32[128]{0:T(128)} %copy-done.77) | copy-start | bytes 1540
  (67 other events, 207.6 us)
Sparse Core Ops, SparseCore 0:
  11.1 206.7 all-gather.7
  252.7 52.6 all-gather.11
  308.4 114.8 all-gather.9
  454.5 50.9 all-gather.13
  578.1 741.4 reduce-scatter.2
  1326.5 114.4 all-reduce.17
  1444.0 363.3 reduce-scatter.4
where the time goes:
time: 1830 us; the launch traced here: 1820 us
  waiting for transfers between devices  1410 us (77%)
  matrix products  157 us (9%)
  blocking collectives  100 us (5%)
  other arithmetic  81.7 us (4%)
  local copies, waits for them, and re-layouts  47.5 us (3%)
    reduce_scatter x1, waiting for transfers between devices, body(): lax.psum_scatter(in_term, ('seq', 'batch'), scatter_dimension=0, tiled=True)  653 us
    reduce_scatter x1, waiting for transfers between devices, body(): lax.psum_scatter(out_term, ('seq', 'batch'), scatter_dimension=0, tiled=T...  366 us
    all_gather x1, waiting for transfers between devices, body(): lax.all_gather(in_weight, ('seq', 'batch'), axis=0, tiled=True)  152 us
    psum x1, waiting for transfers between devices, body(): lax.psum((grad_pre_gain, grad_conv_weight, grad_conv_bias, grad_bias_out...  117 us
    all_gather x1, waiting for transfers between devices, body(): lax.all_gather(out_weight, ('seq', 'batch'), axis=0, tiled=True)  90.6 us
    all_gather x1, blocking collectives, body(): lax.all_gather(step_weight, ('seq', 'batch'), axis=0, tiled=True)  48.3 us
    psum x1, blocking collectives, body(): lax.psum((grad_pre_gain, grad_conv_weight, grad_conv_bias, grad_bias_out...  42.1 us
  transfers between devices with their start and end apart: 9, of which 8 were waited for; matrix products, arithmetic and copies ran while one was open for 9% of the time, Pallas kernels for 0%

commit v1 on v0

v1 whole, which is shorter than its diff:
```python
from functools import partial

import jax
import jax.numpy as jnp
from jax import lax
from jax.experimental import pallas as pl
from jax.experimental.pallas import tpu as pltpu
from jax.sharding import PartitionSpec as P

H = 64
P_SIZE = 64
N = 128
CONV = 4
E = 4096
KEYS = 2 * N
STEP_PAD = 128
CHUNK = 128
epsilon = 1e-05
f32 = jnp.float32
bf16 = jnp.bfloat16


def mm(a, b, dims):
    return lax.dot_general(a, b, (dims, ((), ())), preferred_element_type=f32)


NN = ((1,), (0,))
NT = ((1,), (1,))
TN = ((0,), (0,))


def pair_cols(low, col, first):
    return jnp.where(low, col[:, first : first + 1], col[:, first + 1 : first + 2])


def scan_forward_kernel(
    act_ref, cum_ref, cum_t_ref, dt_ref, dt_t_ref, doc_ref, doc_t_ref, flow_ref, skip_ref, y_ref, state_ref, state
):
    heads = cum_ref.shape[1]
    inner = heads * P_SIZE

    @pl.when(pl.program_id(0) == 0)
    def _():
        state[...] = jnp.zeros_like(state)

    state_ref[0] = state[...].astype(bf16)
    cum = cum_ref[...]
    last = cum[CHUNK - 1 :, :]
    doc = doc_ref[...]
    doc_t = doc_t_ref[...]
    flow = flow_ref[...]
    rows = lax.broadcasted_iota(jnp.int32, (CHUNK, CHUNK), 0)
    cols = lax.broadcasted_iota(jnp.int32, (CHUNK, CHUNK), 1)
    bias = jnp.where((doc == doc_t) & (rows >= cols), 0.0, -1e30)
    carry_w = flow * jnp.exp(cum)
    final_w = jnp.where(doc == doc[CHUNK - 1 :, :], jnp.exp(last - cum), 0.0) * dt_ref[...]
    gain = carry_w[CHUNK - 1 :, :]
    low = cols < P_SIZE
    low_row = low[:1]
    write = act_ref[:, inner : inner + N]
    read = act_ref[:, inner + N :]
    write_t = write.astype(f32).T.astype(bf16)
    scores = mm(read, write, NT)
    for pair in range(heads // 2):
        first = 2 * pair
        lanes = slice(pair * 128, pair * 128 + 128)
        x = act_ref[:, lanes]
        xf = x.astype(f32)
        weights = []
        for h in (first, first + 1):
            decay = jnp.exp(cum[:, h : h + 1] - cum_t_ref[h : h + 1, :] + bias)
            weights.append((decay * scores * dt_t_ref[h : h + 1, :]).astype(bf16))
        stacked = jnp.concatenate(
            [jnp.where(low, xf, 0.0).astype(bf16), jnp.where(low, 0.0, xf).astype(bf16)], axis=0
        )
        old = state[:, lanes]
        y = mm(jnp.concatenate(weights, axis=1), stacked, NN)
        y = y + pair_cols(low, carry_w, first) * mm(read, old.astype(bf16), NN)
        y_ref[:, lanes] = y + skip_ref[:, lanes] * xf
        state[:, lanes] = pair_cols(low_row, gain, first) * old + mm(
            write_t, (pair_cols(low, final_w, first) * xf).astype(bf16), NN
        )


def scan_backward_kernel(
    act_ref, cum_ref, cum_t_ref, dt_ref, doc_ref, doc_t_ref, flow_ref, skip_ref, state_ref, dy_ref,
    dact_ref, dcum_ref, dcum_t_ref, ddt_ref, dskip_ref, dstate,
):
    heads = cum_ref.shape[1]
    inner = heads * P_SIZE

    @pl.when(pl.program_id(0) == 0)
    def _():
        dstate[...] = jnp.zeros_like(dstate)
        dskip_ref[...] = jnp.zeros_like(dskip_ref)

    cum = cum_ref[...]
    dt = dt_ref[...]
    last = cum[CHUNK - 1 :, :]
    doc = doc_ref[...]
    doc_t = doc_t_ref[...]
    flow = flow_ref[...]
    rows = lax.broadcasted_iota(jnp.int32, (CHUNK, CHUNK), 0)
    cols = lax.broadcasted_iota(jnp.int32, (CHUNK, CHUNK), 1)
    bias = jnp.where((doc == doc_t) & (cols >= rows), 0.0, -1e30)
    carry_w = flow * jnp.exp(cum)
    final_d = jnp.where(doc == doc[CHUNK - 1 :, :], jnp.exp(last - cum), 0.0)
    final_w = final_d * dt
    gain = carry_w[CHUNK - 1 :, :]
    low = cols < P_SIZE
    low_row = low[:1]
    write = act_ref[:, inner : inner + N]
    read = act_ref[:, inner + N :]
    read_t = read.astype(f32).T.astype(bf16)
    scores_t = mm(write, read, NT)
    dscores_t = jnp.zeros((CHUNK, CHUNK), f32)
    dwrite = jnp.zeros((CHUNK, N), f32)
    dread = jnp.zeros((CHUNK, N), f32)
    end_row = lax.broadcasted_iota(jnp.int32, (CHUNK, 1), 0) == CHUNK - 1
    dcum_cols = []
    dcum_rows = []
    ddt_cols = []
    for pair in range(heads // 2):
        first = 2 * pair
        lanes = slice(pair * 128, pair * 128 + 128)
        x = act_ref[:, lanes]
        xf = x.astype(f32)
        dy = dy_ref[:, lanes]
        dyb = dy.astype(bf16)
        x_stack = jnp.concatenate(
            [jnp.where(low, xf, 0.0).astype(bf16), jnp.where(low, 0.0, xf).astype(bf16)], axis=0
        )
        dy_stack = jnp.concatenate(
            [jnp.where(low, dy, 0.0).astype(bf16), jnp.where(low, 0.0, dy).astype(bf16)], axis=0
        )
        dweights = mm(x_stack, dyb, NT)
        old = state_ref[0, :, lanes]
        grad = dstate[:, lanes]
        gradb = grad.astype(bf16)
        carried = mm(read, old, NN)
        pushed = mm(write, gradb, NN)
        carry_p = pair_cols(low, carry_w, first)
        final_p = pair_cols(low, final_w, first)
        carry_prod = dy * carried
        final_prod = xf * pushed
        gain_prod = jnp.sum(grad * old.astype(f32), axis=0, keepdims=True)
        weights = []
        for which, h in enumerate((first, first + 1)):
            col = dt[:, h : h + 1]
            decay = jnp.exp(cum_t_ref[h : h + 1, :] - cum[:, h : h + 1] + bias)
            weighted = decay * col
            weights.append((weighted * scores_t).astype(bf16))
            dw = dweights[which * CHUNK : (which + 1) * CHUNK]
            dscores_t = dscores_t + dw * weighted
            direct = dw * decay * scores_t
            ddt_in = jnp.sum(direct, axis=1, keepdims=True)
            dcum_rows.append(jnp.sum(direct * col, axis=0, keepdims=True))
            half = low if which == 0 else ~low
            half_row = low_row if which == 0 else ~low_row
            carry_sum = jnp.sum(jnp.where(half, carry_prod, 0.0), axis=1, keepdims=True)
            final_sum = jnp.sum(jnp.where(half, final_prod, 0.0), axis=1, keepdims=True)
            push = final_w[:, h : h + 1] * final_sum
            at_end = jnp.sum(push, axis=0, keepdims=True) + gain[:, h : h + 1] * jnp.sum(
                jnp.where(half_row, gain_prod, 0.0), axis=1, keepdims=True
            )
            ddt_cols.append(ddt_in + final_d[:, h : h + 1] * final_sum)
            dcum_cols.append(
                carry_w[:, h : h + 1] * carry_sum - push - col * ddt_in + jnp.where(end_row, at_end, 0.0)
            )
        dx = mm(jnp.concatenate(weights, axis=1), dy_stack, NN)
        dact_ref[:, lanes] = dx + final_p * pushed + skip_ref[:, lanes] * dy
        dskip_ref[:, lanes] += jnp.sum(dy * xf, axis=0, keepdims=True)
        dwrite = dwrite + mm((final_p * xf).astype(bf16), gradb, NT)
        carry_dy = (carry_p * dy).astype(bf16)
        dread = dread + mm(carry_dy, old, NT)
        dstate[:, lanes] = pair_cols(low_row, gain, first) * grad + mm(read_t, carry_dy, NN)
    dsb = dscores_t.astype(bf16)
    dact_ref[:, inner : inner + N] = dwrite + mm(dsb, read, NN)
    dact_ref[:, inner + N :] = dread + mm(dsb, write, TN)
    dcum_ref[...] = jnp.concatenate(dcum_cols, axis=1)
    dcum_t_ref[...] = jnp.concatenate(dcum_rows, axis=0)
    ddt_ref[...] = jnp.concatenate(ddt_cols, axis=1)


def scan_forward(act, cum, cum_t, dt, dt_t, doc, doc_t, flow, skip):
    length, channels = act.shape
    heads = cum.shape[1]
    inner = heads * P_SIZE
    steps = length // CHUNK
    row = lambda width: pl.BlockSpec((CHUNK, width), lambda i: (i, 0))
    lane = lambda height: pl.BlockSpec((height, CHUNK), lambda i: (0, i))
    return pl.pallas_call(
        scan_forward_kernel,
        grid=(steps,),
        in_specs=[
            row(channels), row(heads), lane(heads), row(heads), lane(heads), row(1), lane(1), row(1),
            pl.BlockSpec((1, inner), lambda i: (0, 0)),
        ],
        out_specs=[row(inner), pl.BlockSpec((1, N, inner), lambda i: (i, 0, 0))],
        out_shape=[
            jax.ShapeDtypeStruct((length, inner), f32),
            jax.ShapeDtypeStruct((steps, N, inner), bf16),
        ],
        scratch_shapes=[pltpu.VMEM((N, inner), f32)],
        compiler_params=pltpu.CompilerParams(vmem_limit_bytes=40 * 2**20),
        cost_estimate=pl.CostEstimate(
            flops=length * inner * 1024, bytes_accessed=length * inner * 10, transcendentals=length * heads * CHUNK
        ),
    )(act, cum, cum_t, dt, dt_t, doc, doc_t, flow, skip)


def scan_backward(act, cum, cum_t, dt, doc, doc_t, flow, skip, states, dy):
    length, channels = act.shape
    heads = cum.shape[1]
    inner = heads * P_SIZE
    steps = length // CHUNK
    row = lambda width: pl.BlockSpec((CHUNK, width), lambda i: (steps - 1 - i, 0))
    lane = lambda height: pl.BlockSpec((height, CHUNK), lambda i: (0, steps - 1 - i))
    whole = pl.BlockSpec((1, inner), lambda i: (0, 0))
    return pl.pallas_call(
        scan_backward_kernel,
        grid=(steps,),
        in_specs=[
            row(channels), row(heads), lane(heads), row(heads), row(1), lane(1), row(1), whole,
            pl.BlockSpec((1, N, inner), lambda i: (steps - 1 - i, 0, 0)), row(inner),
        ],
        out_specs=[row(channels), row(heads), lane(heads), row(heads), whole],
        out_shape=[
            jax.ShapeDtypeStruct((length, channels), f32),
            jax.ShapeDtypeStruct((length, heads), f32),
            jax.ShapeDtypeStruct((heads, length), f32),
            jax.ShapeDtypeStruct((length, heads), f32),
            jax.ShapeDtypeStruct((1, inner), f32),
        ],
        scratch_shapes=[pltpu.VMEM((N, inner), f32)],
        compiler_params=pltpu.CompilerParams(vmem_limit_bytes=40 * 2**20),
        cost_estimate=pl.CostEstimate(
            flops=length * inner * 3072, bytes_accessed=length * inner * 14, transcendentals=length * heads * CHUNK
        ),
    )(act, cum, cum_t, dt, doc, doc_t, flow, skip, states, dy)


def doc_index(places, doc_ends):
    return jnp.sum((places[:, None] >= doc_ends[None, :-1]).astype(jnp.int32), axis=1)


def convolve(conv_in, weight, bias, masks):
    length = conv_in.shape[0]
    padded = jnp.concatenate([jnp.zeros((CONV - 1, conv_in.shape[1]), conv_in.dtype), conv_in], axis=0)
    total = jnp.broadcast_to(bias[None, :], conv_in.shape)
    for k in range(CONV):
        total = total + weight[k][None, :] * padded[k : k + length].astype(f32) * masks[k][:, None]
    return total


def body(
    inputs, cotangent, doc_lengths, head_width, pre_gain, in_weight, step_weight, conv_weight, conv_bias,
    step_bias, decay_log, skip_gain, norm_gain, out_weight,
):
    peers = lax.axis_size("seq")
    groups = lax.axis_size("batch")
    mine = lax.axis_index("seq")
    tokens = inputs.shape[1]
    width = inputs.shape[2]
    length = tokens * peers
    heads = H // peers
    inner = heads * P_SIZE
    rows = in_weight.shape[0]
    channels = inner + KEYS
    seq_rows = inputs[0].astype(f32)
    cot_rows = cotangent[0]

    def per_peer(part):
        return part.reshape(rows, peers, -1).transpose(1, 0, 2)

    keys_part = jnp.broadcast_to(in_weight[None, :, 2 * E :], (peers, rows, KEYS))
    step_part = jnp.pad(per_peer(step_weight), ((0, 0), (0, 0), (0, STEP_PAD - heads)))
    value_send = jnp.concatenate([per_peer(in_weight[:, E : 2 * E]), keys_part, step_part], axis=2)
    gate_send = per_peer(in_weight[:, :E])
    value_w = lax.all_to_all(value_send, "seq", 0, 0)
    gate_w = lax.all_to_all(gate_send, "seq", 0, 0)
    value_w = lax.all_gather(value_w.reshape(peers * rows, -1), "batch", axis=0, tiled=True)
    gate_w = lax.all_gather(gate_w.reshape(peers * rows, -1), "batch", axis=0, tiled=True)
    out_w = lax.all_gather(out_weight, "batch", axis=0, tiled=True)

    inv_rms = lax.rsqrt(jnp.mean(seq_rows * seq_rows, axis=1, keepdims=True) + epsilon)
    normed = (seq_rows * inv_rms * pre_gain[None, :]).astype(bf16)
    normed = normed.reshape(tokens, peers, groups, rows).transpose(0, 2, 1, 3).reshape(tokens, width)
    normed = lax.all_gather(normed, "seq", axis=0, tiled=True)
    cot_all = lax.all_gather(cot_rows, "seq", axis=0, tiled=True)

    places = jnp.arange(length, dtype=jnp.int32)
    doc_ends = jnp.cumsum(doc_lengths[0])
    doc_ids = doc_index(places, doc_ends)
    flow = (doc_ids == doc_index(places // CHUNK * CHUNK - 1, doc_ends)).astype(f32)[:, None]
    doc = doc_ids[:, None]
    doc_t = doc_ids[None, :]
    head_count = head_width[0]
    head_total = (head_count * P_SIZE).astype(f32)
    my_heads = mine * heads + jnp.arange(heads)
    head_mask = jnp.repeat((my_heads < head_count).astype(f32), P_SIZE)[None, :]
    masks = []
    for k in range(CONV):
        source = places - (CONV - 1 - k)
        masks.append(((source >= 0) & (doc_index(source, doc_ends) == doc_ids)).astype(f32))

    def own(vector, size):
        return lax.dynamic_slice_in_dim(vector, mine * size, size, axis=-1)

    conv_w = jnp.concatenate([own(conv_weight[:, :E], inner), conv_weight[:, E:]], axis=1)
    conv_b = jnp.concatenate([own(conv_bias[:E], inner), conv_bias[E:]])
    step_b = own(step_bias, heads)
    rate = jnp.exp(own(decay_log, heads))
    skip = jnp.repeat(own(skip_gain, heads), P_SIZE)[None, :]
    gain = own(norm_gain, inner)[None, :]

    value_out = mm(normed, value_w, NN)
    conv_in = value_out[:, :channels].astype(bf16)
    step_raw = value_out[:, channels : channels + heads] + step_b[None, :]
    gate = mm(normed, gate_w, NN)
    conv_sum = convolve(conv_in, conv_w, conv_b, masks)
    act = jax.nn.silu(conv_sum).astype(bf16)
    dt = jax.nn.softplus(step_raw)
    log_decay = -dt * rate[None, :]
    cum = jnp.cumsum(log_decay.reshape(-1, CHUNK, heads), axis=1).reshape(length, heads)
    y, states = scan_forward(act, cum, cum.T, dt, dt.T, doc, doc_t, flow, skip)
    grad_mixed = mm(cot_all, out_w, NT)
    sig_gate = jax.nn.sigmoid(gate)
    silu_gate = gate * sig_gate
    masked = y * head_mask
    gated = masked * silu_gate
    scaled = grad_mixed * gain
    partial_sums = jnp.stack([jnp.sum(gated * gated, axis=1), jnp.sum(scaled * gated, axis=1)])
    sums = jnp.sum(lax.all_gather(partial_sums, "seq", axis=0), axis=0)
    inv = lax.rsqrt(sums[0] / head_total + epsilon)[:, None]
    pull = inv * inv * inv * sums[1][:, None] / head_total
    mixed = (gated * inv * gain).astype(bf16)
    branch = mm(mixed, out_w, NN).astype(bf16)
    branch = lax.all_to_all(branch.reshape(peers, tokens, width), "seq", 0, 0)
    output = (seq_rows + jnp.sum(branch.astype(f32), axis=0)).astype(bf16)[None]

    out_term = mm(mixed, cot_all, TN).astype(bf16)
    grad_out_weight = lax.psum_scatter(out_term, "batch", scatter_dimension=0, tiled=True).astype(f32)
    grad_norm_gain = jnp.sum(grad_mixed * gated * inv, axis=0)
    grad_gated = inv * scaled - pull * gated
    dy = grad_gated * silu_gate * head_mask
    grad_gate = (grad_gated * masked * (sig_gate * (1.0 + gate * (1.0 - sig_gate)))).astype(bf16)
    gate_term = mm(normed, grad_gate, TN).astype(bf16)
    gate_term = lax.psum_scatter(gate_term, "batch", scatter_dimension=0, tiled=True)
    dact, dcum, dcum_t, ddt, dskip = scan_backward(
        act, cum, cum.T, dt, doc, doc_t, flow, skip, states, dy
    )
    dcum = (dcum + dcum_t.T).reshape(-1, CHUNK, heads)
    dlog = lax.cumsum(dcum, axis=1, reverse=True).reshape(length, heads)
    grad_dt = ddt - rate[None, :] * dlog
    grad_decay_log = -jnp.sum(dt * rate[None, :] * dlog, axis=0)
    grad_step_f32 = grad_dt * jax.nn.sigmoid(step_raw)
    grad_step_bias = jnp.sum(grad_step_f32, axis=0)
    grad_skip = jnp.sum(dskip.reshape(heads, P_SIZE), axis=1)
    sig = jax.nn.sigmoid(conv_sum)
    dconv = dact * (sig * (1.0 + conv_sum * (1.0 - sig)))
    padded = jnp.concatenate([jnp.zeros((CONV - 1, channels), bf16), conv_in], axis=0)
    grad_conv_bias = jnp.sum(dconv, axis=0)
    conv_rows = []
    grad_conv_in = jnp.zeros_like(dconv)
    for k in range(CONV):
        taken = dconv * masks[k][:, None]
        conv_rows.append(jnp.sum(taken * padded[k : k + length].astype(f32), axis=0))
        lead = CONV - 1 - k
        moved = jnp.concatenate([taken[lead:], jnp.zeros((lead, channels), f32)], axis=0)
        grad_conv_in = grad_conv_in + conv_w[k][None, :] * moved
    grad_conv_weight = jnp.stack(conv_rows)
    grad_step_raw = jnp.pad(grad_step_f32.astype(bf16), ((0, 0), (0, STEP_PAD - heads)))
    grad_value = jnp.concatenate([grad_conv_in.astype(bf16), grad_step_raw], axis=1)
    value_term = mm(normed, grad_value, TN).astype(bf16)
    value_term = lax.psum_scatter(value_term, "batch", scatter_dimension=0, tiled=True)
    grad_normed = mm(grad_gate, gate_w, NT) + mm(grad_value, value_w, NT)
    grad_normed = grad_normed.astype(bf16).reshape(peers, tokens, width)
    grad_normed = jnp.sum(lax.all_to_all(grad_normed, "seq", 0, 0).astype(f32), axis=0)
    grad_normed = grad_normed.reshape(tokens, groups, peers, rows).transpose(0, 2, 1, 3).reshape(tokens, width)

    scaled_in = grad_normed * pre_gain[None, :]
    dot = jnp.mean(scaled_in * seq_rows, axis=1, keepdims=True)
    grad_seq = inv_rms * scaled_in - seq_rows * (inv_rms * inv_rms * inv_rms * dot)
    grad_pre_gain = jnp.sum(grad_normed * seq_rows * inv_rms, axis=0)
    grad_inputs = (grad_seq + cot_rows.astype(f32))[None]

    gate_back = lax.all_to_all(gate_term.reshape(peers, rows, inner), "seq", 0, 0)
    value_back = lax.all_to_all(value_term.reshape(peers, rows, -1), "seq", 0, 0)

    def join(part):
        return part.astype(f32).transpose(1, 0, 2).reshape(rows, -1)

    grad_in_weight = jnp.concatenate(
        [
            join(gate_back),
            join(value_back[:, :, :inner]),
            jnp.sum(value_back[:, :, inner:channels].astype(f32), axis=0),
        ],
        axis=1,
    )
    grad_step_weight = join(value_back[:, :, channels : channels + heads])

    def spread(part, total):
        full = jnp.zeros(part.shape[:-1] + (total,), f32)
        return lax.dynamic_update_slice_in_dim(full, part, mine * part.shape[-1], axis=-1)

    conv_all = jnp.concatenate([grad_conv_weight, grad_conv_bias[None]], axis=0)
    small = lax.psum(
        (
            grad_pre_gain,
            jnp.concatenate([spread(conv_all[:, :inner], E), conv_all[:, inner:]], axis=1),
            spread(grad_step_bias, H),
            spread(grad_decay_log, H),
            spread(grad_skip, H),
            spread(grad_norm_gain, E),
        ),
        ("seq", "batch"),
    )
    return (
        output, grad_inputs, small[0], grad_in_weight, grad_step_weight, small[1][:CONV], small[1][CONV],
        small[2], small[3], small[4], small[5], grad_out_weight,
    )


def solution(mesh):
    both = P(("seq", "batch"), None)
    tok = P("batch", "seq", None)
    in_specs = (
        tok, tok, P("batch", None), P("batch"), P(), both, both, P(), P(), P(), P(), P(), P(), both,
    )
    out_specs = (tok, tok, P(), both, both, P(), P(), P(), P(), P(), P(), both)
    return jax.shard_map(body, mesh=mesh, in_specs=in_specs, out_specs=out_specs, check_vma=False)
```

time: 1830 us -> 602 us (0.33)
  waiting for transfers between devices: 1410 us -> 343 us
  matrix products: 157 us -> 56.6 us
  other arithmetic: 81.7 us -> 43.1 us
  blocking collectives: 100 us -> 75.9 us
  local copies, waits for them, and re-layouts: 47.5 us -> 27.9 us
  Pallas kernels: 0 us -> 19.2 us
    reduce_scatter x2 -> x3, waiting for transfers between devices: 1020 us -> 108 us  [the longest x1 55.1 us: body(): lax.psum_scatter(value_term, 'batch', scatter_dimension=0, tiled=True)]
    dot_general x29 -> x9, matrix products: 157 us -> 56.6 us  [mm(): return lax.dot_general(a, b, (dims, ((), ())), preferred_element_type=f32)]
    all_gather x4 -> x5, waiting for transfers between devices: 267 us -> 171 us  [the longest x1 54.3 us: body(): lax.all_gather(value_w.reshape(peers * rows, -1), 'batch', axis=0, tiled=...]
    psum x1, waiting for transfers between devices: 117 us -> 40.8 us  [body(): lax.psum((grad_pre_gain, jnp.concatenate([spread(conv_all[:, :inner], E),...]
    all_gather x2 -> x1, blocking collectives: 58.4 us -> 8.3 us  [body(): sums = jnp.sum(lax.all_gather(partial_sums, 'seq', axis=0), axis=0)]
    all_to_all x0 -> x2, blocking collectives: none -> 26.5 us  [the longest x1 14.2 us: body(): gate_w = lax.all_to_all(gate_send, 'seq', 0, 0)]
    all_to_all x0 -> x4, waiting for transfers between devices: none -> 21.4 us  [the longest x1 17 us: body(): lax.all_to_all(grad_normed, 'seq', 0, 0).astype(f32)]
    pallas_call x0 -> x2, Pallas kernels: none -> 19.2 us  [the longest x1 14 us: scan_backward(): pl.pallas_call(scan_backward_kernel, grid=(steps,), in_specs=[row(channel...]
  transfers between devices with their start and end apart: 9 -> 13, of which waited for: 8 -> 11; matrix products, arithmetic and copies ran while one was open for 9% -> 16% of each run, Pallas kernels for 0% -> 1%
where the time goes in v1:
time: 602 us; the launch traced here: 598 us
  waiting for transfers between devices  343 us (57%)
  blocking collectives  75.9 us (13%)
  matrix products  56.6 us (9%)
  other arithmetic  43.1 us (7%)
  local copies, waits for them, and re-layouts  27.9 us (5%)
  Pallas kernels  19.2 us (3%)
  starting transfers between devices  16.7 us (3%)
  between operations  15.5 us (3%)
    dot_general x9, matrix products, mm(): return lax.dot_general(a, b, (dims, ((), ())), preferred_element_type=f32)  56.6 us
    reduce_scatter x1, waiting for transfers between devices, body(): lax.psum_scatter(value_term, 'batch', scatter_dimension=0, tiled=True)  55.1 us
    all_gather x1, waiting for transfers between devices, body(): lax.all_gather(value_w.reshape(peers * rows, -1), 'batch', axis=0, tiled=...  54.3 us
    all_gather x1, waiting for transfers between devices, body(): lax.all_gather(gate_w.reshape(peers * rows, -1), 'batch', axis=0, tiled=T...  49 us
    reduce_scatter x1, waiting for transfers between devices, body(): lax.psum_scatter(gate_term, 'batch', scatter_dimension=0, tiled=True)  48.8 us
    all_gather x1, waiting for transfers between devices, body(): out_w = lax.all_gather(out_weight, 'batch', axis=0, tiled=True)  48.6 us
    psum x1, blocking collectives, body(): lax.psum((grad_pre_gain, jnp.concatenate([spread(conv_all[:, :inner], E),...  41.1 us
    psum x1, waiting for transfers between devices, body(): lax.psum((grad_pre_gain, jnp.concatenate([spread(conv_all[:, :inner], E),...  40.8 us
  transfers between devices with their start and end apart: 13, of which 11 were waited for; matrix products, arithmetic and copies ran while one was open for 16% of the time, Pallas kernels for 1%

profile of v1, /device:TPU:0, one launch (start us, length us, event | category | flops | bytes accessed | tf_op | source)
XLA Modules:
  0.0 597.9 jit_solution(7635313210345807142)
XLA Ops:
  8.5 1.6 multiply_reduce_fusion.3
  12.8 14.2 %all_to_all.30 = bf16[4,64,1024]{2,1,0:T(8,128)(2,1)} all-to-all(bf16[4,64,1024]{2,1,0:T(8,128)(2,1)S(1)} %copy.165), channel_id=1, replica_groups=mesh['seq'=4,'batch'=8] {'seq'}, dimensions={0} | all-to-all | bytes 1048576 | tf_op jit(solution)/shard_map/all_to_all | solution.py:281
  28.3 12.3 %all_to_all.31 = bf16[4,64,1408]{2,1,0:T(8,128)(2,1)} all-to-all(bf16[4,64,1408]{2,1,0:T(8,128)(2,1)S(1)} %copy.159), channel_id=1, replica_groups=mesh['seq'=4,'batch'=8] {'seq'}, dimensions={0} | all-to-all | bytes 1441792 | tf_op jit(solution)/shard_map/all_to_all | solution.py:280
  45.1 6.1 %all-gather.9.cloned.1.call-done = bf16[512,2048]{0,1:T(8,128)(2,1)} async-done(((bf16[128,2048]{0,1:T(8,128)(2,1)}), bf16[512,2048]{0,1:T(8,128)(2,1)}) %all-gather.9.cloned.1.call-update) | async-done | bytes 2097168 | tf_op jit(solution)/shard_map/all_gather | solution.py:289
  51.3 49.0 %all-gather.13.cloned.1.call-done = bf16[2048,1024]{1,0:T(8,128)(2,1)} async-done(((bf16[256,1024]{1,0:T(8,128)(2,1)}), bf16[2048,1024]{1,0:T(8,128)(2,1)}) %all-gather.13.cloned.1.call-update) | async-done | bytes 4194320 | tf_op jit(solution)/shard_map/all_gather | solution.py:283
  100.2 6.5 %fusion.60 = f32[512,1024]{1,0:T(8,128)} fusion(bf16[512,2048]{0,1:T(8,128)(2,1)} %all-gather.9.cloned.1.call-done, bf16[2048,1024]{1,0:T(8,128)(2,1)} %all-gather.13.cloned.1.call-done), kind=kOutput, calls=%fused_computation.145 | convolution fusion | flops 2147483648 | bytes 8388608 | tf_op jit(solution)/shard_map/dot_general | solution.py:24
  106.7 54.3 %all-gather.11.cloned.1.call-done = bf16[2048,1408]{1,0:T(8,128)(2,1)} async-done(((bf16[256,1408]{1,0:T(8,128)(2,1)}), bf16[2048,1408]{1,0:T(8,128)(2,1)}) %all-gather.11.cloned.1.call-update) | async-done | bytes 5767184 | tf_op jit(solution)/shard_map/all_gather | solution.py:282
  161.0 5.6 fusion.59
  166.7 1.3 slice.208
  169.1 6.8 %multiply_convert_fusion = (bf16[512,1280]{1,0:T(8,128)(2,1)S(1)}, f32[512,1280]{1,0:T(8,128)}) fusion(bf16[512,1280]{1,0:T(8,128)(2,1)} %slice.208, f32[1280]{0:T(1024)S(1)} %get-tuple-element.109, f32[512]{0:T(512)S(1)} %get-tuple-element.143, f32[1280]{0:T(1024)S(1)} %get-tuple-element.110, f32[512]{0:T(512)S(1)} %get-tuple-element.144, ...), kind=kLoop, calls=%fused_computation.31 | loop fusion | flops 13107200 | bytes 5274624 | tf_op jit(solution)/shard_map/convert_element_type | solution.py:322
  175.9 5.2 shard_map.229
  181.1 1.3 copy-done
  183.4 13.4 %all-gather.17.cloned.1.call-done = bf16[1,512,2048]{2,1,0:T(8,128)(2,1)} async-done(((bf16[1,128,2048]{2,1,0:T(8,128)(2,1)}), bf16[1,512,2048]{2,1,0:T(8,128)(2,1)}) %all-gather.17.cloned.1.call-update) | async-done | bytes 2097168 | tf_op jit(solution)/shard_map/all_gather | solution.py:290
  196.8 48.6 %all-gather.15.cloned.1.call-done = bf16[1024,2048]{1,0:T(8,128)(2,1)} async-done(((bf16[128,2048]{1,0:T(8,128)(2,1)}), bf16[1024,2048]{1,0:T(8,128)(2,1)}) %all-gather.15.cloned.1.call-update) | async-done | bytes 4194320 | tf_op jit(solution)/shard_map/all_gather | solution.py:284
  245.4 8.7 %multiply_reduce_fusion.2 = (f32[512]{0:T(512)S(1)}, f32[512]{0:T(512)S(1)}, f32[512,1024]{1,0:T(8,128)}, f32[512,1024]{1,0:T(8,128)}) fusion(f32[1024]{0:T(1024)S(1)} %dynamic_slice.23, f32[512,1024]{1,0:T(8,128)} %fusion.60, f32[512,1024]{1,0:T(8,128)} %copy-done, f32[1024]{0:T(1024)S(1)} %mul.442, bf16[1024,2048]{1,0:T(8,128)(2,1)} %all-gather.15.cloned.1.call-done, ...), kind=kOutput, calls=%fused_computation.43 | convolution fusion | flops 2153249792 | bytes 14692352 | tf_op jit(solution)/shard_map/dot_general | solution.py:24
  254.1 8.3 %all-gather.2 = f32[4,2,512]{2,1,0:T(2,128)S(1)} all-gather(f32[1,2,512]{2,1,0:T(2,128)S(1)} %maximum_bitcast_fusion), channel_id=3, replica_groups=mesh['seq'=4,'batch'=8] {'seq'}, dimensions={0}, use_global_device_ids=true | all-gather | bytes 20480 | tf_op jit(solution)/shard_map/all_gather | solution.py:334
  262.5 5.2 multiply_multiply_fusion.1
  267.7 14.0 %shard_map.230 = (f32[512,1280]{1,0:T(8,128)S(1)}, f32[512,16]{1,0:T(8,128)S(1)}, f32[16,512]{1,0:T(8,128)S(1)}, f32[512,16]{1,0:T(8,128)S(1)}, f32[1,1024]{1,0:T(1,128)S(1)}) custom-call(bf16[512,1280]{1,0:T(8,128)(2,1)S(1)} %get-tuple-element.130.act_ref, f32[512,16]{1,0:T(8,128)S(1)} %bitcast.97, f32[16,512]{1,0:T(8,128)S(1)} %bitcast.99, ...), custom_call_target="tpu_custom_call" | custom-call | flops 1610612736 | bytes 7340032 | tf_op jit(solution)/shard_map/pallas_call | solution.py:220
  281.7 5.2 fusion.53
  287.9 6.0 convolution_convert_fusion.2
  294.4 3.6 slice.142
  298.0 1.7 slice.141
  300.7 1.6 slice.140
  302.3 4.4 reduce_window_sum.29
  307.9 5.0 add_convert_fusion.1
  313.9 5.2 convolution_convert_fusion
  320.7 6.1 %convolution_convert_fusion.1 = bf16[1024,2048]{1,0:T(8,128)(2,1)} fusion(bf16[1,512,2048]{2,1,0:T(8,128)(2,1)} %all-gather.17.cloned.1.call-done, f32[512,1024]{1,0:T(8,128)S(1)} %copy-done.12, f32[512]{0:T(512)S(1)} %bitcast.127, f32[1024]{0:T(1024)S(1)} %dynamic_slice.23), kind=kOutput, calls=%fused_computation.4 | convolution fusion | flops 2151153664 | bytes 8394752 | tf_op jit(solution)/shard_map/dot_general | solution.py:24
  326.8 4.7 fusion.61
  331.6 7.3 %add_convert_fusion = bf16[512,2048]{1,0:T(8,128)(2,1)} fusion(f32[512,2048]{1,0:T(8,128)S(1)} %fusion.61, bf16[2048,1408]{1,0:T(8,128)(2,1)} %all-gather.11.cloned.1.call-done, bf16[512,16]{1,0:T(8,128)(2,1)S(1)} %copy-done.19, bf16[512,1280]{1,0:T(8,128)(2,1)S(1)} %copy-done.14), kind=kOutput, calls=%fused_computation.2 | convolution fusion | flops 2959212544 | bytes 13385728 | tf_op jit(solution)/shard_map/dot_general | solution.py:24
  338.8 3.6 all-to-all-start.3
  342.5 6.6 %convolution_convert_fusion.3 = bf16[512,2048]{1,0:T(8,128)(2,1)} fusion(bf16[1024,2048]{1,0:T(8,128)(2,1)} %all-gather.15.cloned.1.call-done, f32[512,1024]{1,0:T(8,128)} %get-tuple-element.127, f32[512]{0:T(512)S(1)} %bitcast.128, f32[1024]{0:T(1024)S(1)} %dynamic_slice.23), kind=kOutput, calls=%fused_computation.14 | convolution fusion | flops 2150105088 | bytes 8394752 | tf_op jit(solution)/shard_map/dot_general | solution.py:24
  349.0 17.0 %all-to-all-done.3 = bf16[4,128,2048]{2,1,0:T(8,128)(2,1)S(1)} async-done(((bf16[4,128,2048]{2,1,0:T(8,128)(2,1)}), bf16[4,128,2048]{2,1,0:T(8,128)(2,1)S(1)}, u32[]{:S(2)}, u32[]{:S(2)}) %all-to-all-start.3) | async-done | bytes 2097184 | tf_op jit(solution)/shard_map/all_to_all | solution.py:379
  366.1 4.4 all-to-all-start.2
  372.7 40.8 %all-reduce.9.cloned.1.call-done = f32[5,4352]{1,0:T(8,128)} async-done(((f32[5,4352]{1,0:T(8,128)}), f32[5,4352]{1,0:T(8,128)}) %all-reduce.9.cloned.1.call-update) | async-done | bytes 87056 | tf_op jit(solution)/shard_map/psum | solution.py:409
  413.5 1.5 slice.148
  415.0 1.6 slice_reduce_fusion
  417.4 1.3 copy.172
  419.4 48.8 %reduce-scatter.4.cloned.1.call-done = bf16[256,1024]{1,0:T(8,128)(2,1)} async-done(((bf16[2048,1024]{1,0:T(8,128)(2,1)}), bf16[256,1024]{1,0:T(8,128)(2,1)}) %reduce-scatter.4.cloned.1.call-update) | async-done | bytes 524304 | tf_op jit(solution)/shard_map/reduce_scatter | solution.py:349
  468.2 3.6 all-to-all-start.4
  471.8 2.2 convert_reduce_fusion.1
  474.0 4.4 all-to-all-done.4
  478.4 55.1 %reduce-scatter.6.cloned.1.call-done = bf16[256,1408]{1,0:T(8,128)(2,1)} async-done(((bf16[2048,1408]{1,0:T(8,128)(2,1)}), bf16[256,1408]{1,0:T(8,128)(2,1)}) %reduce-scatter.6.cloned.1.call-update) | async-done | bytes 720912 | tf_op jit(solution)/shard_map/reduce_scatter | solution.py:376
  533.5 3.6 all-to-all-start.5
  537.2 2.6 convert_add_fusion
  539.8 41.1 %all-reduce.6 = (f32[2048]{0:T(1024)}, f32[64]{0:T(128)}, f32[64]{0:T(128)}, f32[64]{0:T(128)}, f32[4096]{0:T(1024)}) all-reduce(f32[2048]{0:T(1024)S(1)} %reduce_sum.235, f32[64]{0:T(128)S(1)} %dynamic_update_slice.16, f32[64]{0:T(128)S(1)} %negate_dynamic-update-slice_fusion, ...), channel_id=1, replica_groups=mesh['seq'=4,'batch'=8] {'seq','batch'}, use_global_device_ids=true, to_apply=%region_16.17 | all-reduce | flops 6336 | bytes 50688 | tf_op jit(solution)/shard_map/psum | solution.py:409
  580.9 4.4 reduce-scatter.8.cloned.1.call-done
  585.2 2.1 convert_element_type.182
  589.6 1.5 pad_maximum_fusion
  (171 shorter events, 23.0 us)
Async XLA Ops:
  7.2 44.1 %all-gather.9.cloned.1.call-start = ((), (), s32[]{:S(2)}) async-start(), calls=%async_computation.9 | async-start | bytes 2621440 | tf_op jit(solution)/shard_map/all_gather | solution.py:289
  8.5 3.8 copy-start.7
  8.5 3.7 copy-start.16
  12.1 88.1 %all-gather.13.cloned.1.call-start = ((), (), s32[]{:S(2)}) async-start(), calls=%async_computation.11 | async-start | bytes 4718592 | tf_op jit(solution)/shard_map/all_gather | solution.py:283
  12.3 14.8 %copy-start.21 = (bf16[64,64]{1,0:T(8,128)(2,1)S(1)}, bf16[64,64]{1,0:T(8,128)(2,1)}, u32[]{:S(2)}) copy-start(bf16[64,64]{1,0:T(8,128)(2,1)} %param.20) | copy-start | bytes 24580
  12.7 15.1 %slice-start = ((bf16[64,8448]{1,0:T(8,128)(2,1)}), bf16[64,256]{1,0:T(8,128)(2,1)S(1)}, s32[]{:S(2)}) async-start(bf16[64,8448]{1,0:T(8,128)(2,1)} %param.19), calls=%async_computation.18 | async-start | bytes 65536 | tf_op jit(solution)/shard_map/slice | solution.py:276
  27.1 134.0 %all-gather.11.cloned.1.call-start = ((), (), s32[]{:S(2)}) async-start(), calls=%async_computation.10 | async-start | bytes 6488064 | tf_op jit(solution)/shard_map/all_gather | solution.py:282
  28.1 14.3 %copy-start.24 = (s32[1,4]{1,0:T(1,128)S(1)}, s32[1,4]{1,0:T(1,128)}, u32[]{:S(2)}) copy-start(s32[1,4]{1,0:T(1,128)} %param.16) | copy-start | bytes 52
  28.1 15.2 %slice-start.4 = ((f32[4352]{0:T(1024)}), f32[4096]{0:T(1024)S(1)}, s32[]{:S(2)}) async-start(f32[4352]{0:T(1024)} %param.22), calls=%async_computation.22 | async-start | bytes 32768 | tf_op jit(solution)/shard_map/slice | solution.py:311
  28.2 15.6 %copy-start.25 = (f32[64]{0:T(128)S(1)}, f32[64]{0:T(128)}, u32[]{:S(2)}) copy-start(f32[64]{0:T(128)} %param.23) | copy-start | bytes 772
  28.2 15.7 %copy-start.26 = (f32[64]{0:T(128)S(1)}, f32[64]{0:T(128)}, u32[]{:S(2)}) copy-start(f32[64]{0:T(128)} %param.25) | copy-start | bytes 772
  28.3 16.7 %slice-start.2 = ((f32[4,4352]{1,0:T(4,128)}), f32[4,4096]{1,0:T(4,128)S(1)}, s32[]{:S(2)}) async-start(f32[4,4352]{1,0:T(4,128)} %param.21), calls=%async_computation.20 | async-start | bytes 131072 | tf_op jit(solution)/shard_map/slice | solution.py:310
  28.3 16.7 %slice-start.1 = ((f32[4,4352]{1,0:T(4,128)}), f32[4,256]{1,0:T(4,128)S(1)}, s32[]{:S(2)}) async-start(f32[4,4352]{1,0:T(4,128)} %param.21), calls=%async_computation.19 | async-start | bytes 8192 | tf_op jit(solution)/shard_map/slice | solution.py:310
  28.3 16.8 %copy-start.27 = (f32[64]{0:T(128)S(1)}, f32[64]{0:T(128)}, u32[]{:S(2)}) copy-start(f32[64]{0:T(128)} %param.24) | copy-start | bytes 772
  28.3 16.8 %slice-start.3 = ((f32[4352]{0:T(1024)}), f32[256]{0:T(256)S(1)}, s32[]{:S(2)}) async-start(f32[4352]{0:T(1024)} %param.22), calls=%async_computation.21 | async-start | bytes 2048 | tf_op jit(solution)/shard_map/slice | solution.py:311
  40.7 156.1 %all-gather.17.cloned.1.call-start = ((), (), s32[]{:S(2)}) async-start(), calls=%async_computation.17 | async-start | bytes 2621440 | tf_op jit(solution)/shard_map/all_gather | solution.py:290
  41.2 204.1 %all-gather.15.cloned.1.call-start = ((), (), s32[]{:S(2)}) async-start(), calls=%async_computation.12 | async-start | bytes 4718592 | tf_op jit(solution)/shard_map/all_gather | solution.py:284
  41.8 371.6 %all-reduce.9.cloned.1.call-start = ((), (), s32[]{:S(2)}) async-start(), calls=%async_computation.15 | async-start | bytes 278528 | tf_op jit(solution)/shard_map/psum | solution.py:409
  51.3 109.8 %copy-start.22 = (bf16[512,2048]{0,1:T(8,128)(2,1)S(1)}, bf16[512,2048]{0,1:T(8,128)(2,1)}, u32[]{:S(2)}) copy-start(bf16[512,2048]{0,1:T(8,128)(2,1)} %all-gather.9.cloned.1.call-done) | copy-start | bytes 6291460
  166.7 2.0 copy-start.15
  181.1 1.4 copy-start
  182.4 1.0 copy-start.1
  262.5 5.2 copy-start.2
  267.7 14.0 %copy-start.3 = (bf16[512,1280]{1,0:T(8,128)(2,1)S(1)}, bf16[512,1280]{1,0:T(8,128)(2,1)}, u32[]{:S(2)}) copy-start(bf16[512,1280]{1,0:T(8,128)(2,1)} %slice.208) | copy-start | bytes 3932164
  267.7 14.0 %copy-start.6 = (f32[512,1280]{1,0:T(8,128)S(1)}, f32[512,1280]{1,0:T(8,128)}, u32[]{:S(2)}) copy-start(f32[512,1280]{1,0:T(8,128)} %get-tuple-element.131) | copy-start | bytes 7864324
  281.7 6.2 %copy-start.17 = (bf16[512,1024]{1,0:T(8,128)(2,1)S(1)}, bf16[512,1024]{1,0:T(8,128)(2,1)}, u32[]{:S(2)}) copy-start(bf16[512,1024]{1,0:T(8,128)(2,1)} %get-tuple-element.133) | copy-start | bytes 3145732
  287.8 180.3 %reduce-scatter.4.cloned.1.call-start = ((), (), s32[]{:S(2)}) async-start(), calls=%async_computation.13 | async-start | bytes 4718592 | tf_op jit(solution)/shard_map/reduce_scatter | solution.py:349
  293.9 239.6 %reduce-scatter.6.cloned.1.call-start = ((), (), s32[]{:S(2)}) async-start(), calls=%async_computation.14 | async-start | bytes 6488064 | tf_op jit(solution)/shard_map/reduce_scatter | solution.py:376
  294.4 3.6 copy-start.5
  298.0 2.7 copy-start.4
  307.9 5.0 copy-start.18
  307.9 6.0 %copy-start.23 = (bf16[512,2048]{0,1:T(8,128)(2,1)S(1)}, bf16[512,2048]{0,1:T(8,128)(2,1)}, u32[]{:S(2)}) copy-start(bf16[512,2048]{0,1:T(8,128)(2,1)} %all-gather.9.cloned.1.call-done) | copy-start | bytes 6291460
  312.9 1.1 copy-start.13
  319.1 1.6 copy-start.12
  319.1 266.1 %reduce-scatter.8.cloned.1.call-start = ((), (), s32[]{:S(2)}) async-start(), calls=%async_computation.16 | async-start | bytes 4718592 | tf_op jit(solution)/shard_map/reduce_scatter | solution.py:343
  326.8 4.8 copy-start.14
  326.8 4.7 copy-start.19
  338.8 27.2 %all-to-all-start.3 = ((bf16[4,128,2048]{2,1,0:T(8,128)(2,1)}), bf16[4,128,2048]{2,1,0:T(8,128)(2,1)S(1)}, u32[]{:S(2)}, u32[]{:S(2)}) async-start(bf16[4,128,2048]{2,1,0:T(8,128)(2,1)} %bitcast.113), calls=%async_computation.3 | async-start | bytes 4194304 | tf_op jit(solution)/shard_map/all_to_all | solution.py:379
  366.1 53.3 %all-to-all-start.2 = ((bf16[4,128,2048]{2,1,0:T(8,128)(2,1)}), bf16[4,128,2048]{2,1,0:T(8,128)(2,1)}, u32[]{:S(2)}, u32[]{:S(2)}) async-start(bf16[4,128,2048]{2,1,0:T(8,128)(2,1)} %bitcast.112), calls=%async_computation.2 | async-start | bytes 4194304 | tf_op jit(solution)/shard_map/all_to_all | solution.py:339
  417.3 1.4 copy-start.8
  468.2 10.2 %all-to-all-start.4 = ((bf16[4,64,1024]{2,1,0:T(8,128)(2,1)}), bf16[4,64,1024]{2,1,0:T(8,128)(2,1)S(1)}, u32[]{:S(2)}, u32[]{:S(2)}) async-start(bf16[4,64,1024]{2,1,0:T(8,128)(2,1)} %bitcast.121), calls=%async_computation.5 | async-start | bytes 1048576 | tf_op jit(solution)/shard_map/all_to_all | solution.py:388
  471.8 65.3 %copy-start.9 = (bf16[1,128,2048]{2,1,0:T(8,128)(2,1)S(1)}, bf16[1,128,2048]{2,1,0:T(8,128)(2,1)}, u32[]{:S(2)}) copy-start(bf16[1,128,2048]{2,1,0:T(8,128)(2,1)} %param.14) | copy-start | bytes 1572868
  471.8 65.3 %copy-start.10 = (f32[1,128,2048]{2,1,0:T(8,128)S(1)}, f32[1,128,2048]{2,1,0:T(8,128)}, u32[]{:S(2)}) copy-start(f32[1,128,2048]{2,1,0:T(8,128)} %copy.172) | copy-start | bytes 3145732
  471.8 65.3 %copy-start.20 = (f32[2048]{0:T(1024)S(1)}, f32[2048]{0:T(1024)}, u32[]{:S(2)}) copy-start(f32[2048]{0:T(1024)} %param.18) | copy-start | bytes 24580
  478.4 55.1 %copy-start.11 = (bf16[4,64,1024]{2,1,0:T(8,128)(2,1)}, bf16[4,64,1024]{2,1,0:T(8,128)(2,1)S(1)}, u32[]{:S(2)}) copy-start(bf16[4,64,1024]{2,1,0:T(8,128)(2,1)S(1)} %all-to-all-done.4) | copy-start | bytes 1572868
  533.5 55.1 %all-to-all-start.5 = ((bf16[4,64,1408]{2,1,0:T(8,128)(2,1)}), bf16[4,64,1408]{2,1,0:T(8,128)(2,1)S(1)}, u32[]{:S(2)}, u32[]{:S(2)}) async-start(bf16[4,64,1408]{2,1,0:T(8,128)(2,1)} %bitcast.120), calls=%async_computation.7 | async-start | bytes 1441792 | tf_op jit(solution)/shard_map/all_to_all | solution.py:389
Sparse Core Ops, SparseCore 0:
  12.2 38.9 all-gather.8
  52.8 47.3 all-gather.12
  101.9 59.1 all-gather.10
  162.7 33.9 all-gather.16
  198.2 47.1 all-gather.14
  287.9 125.4 all-reduce.8
  415.8 52.3 reduce-scatter.3
  470.5 62.9 reduce-scatter.5
  535.8 49.3 reduce-scatter.7

commit v2 on v1

v2 whole, which is shorter than its diff:
```python
from functools import partial

import jax
import jax.numpy as jnp
from jax import lax
from jax.experimental import pallas as pl
from jax.experimental.pallas import tpu as pltpu
from jax.sharding import PartitionSpec as P

H = 64
P_SIZE = 64
N = 128
CONV = 4
DOCS = 4
E = 4096
KEYS = 2 * N
STEP_PAD = 128
CHUNK = 128
epsilon = 1e-05
f32 = jnp.float32
bf16 = jnp.bfloat16


def mm(a, b, dims):
    return lax.dot_general(a, b, (dims, ((), ())), preferred_element_type=f32)


NN = ((1,), (0,))
NT = ((1,), (1,))
TN = ((0,), (0,))


def pair_cols(low, col, first):
    return jnp.where(low, col[:, first : first + 1], col[:, first + 1 : first + 2])


def scan_forward_kernel(
    val_ref, key_ref, cum_ref, cum_t_ref, dt_ref, dt_t_ref, doc_ref, doc_t_ref, flow_ref, skip_ref, y_ref, state_ref, state
):
    heads = cum_ref.shape[1]

    @pl.when(pl.program_id(0) == 0)
    def _():
        state[...] = jnp.zeros_like(state)

    state_ref[0] = state[...].astype(bf16)
    cum = cum_ref[...]
    last = cum[CHUNK - 1 :, :]
    doc = doc_ref[...]
    doc_t = doc_t_ref[...]
    flow = flow_ref[...]
    rows = lax.broadcasted_iota(jnp.int32, (CHUNK, CHUNK), 0)
    cols = lax.broadcasted_iota(jnp.int32, (CHUNK, CHUNK), 1)
    bias = jnp.where((doc == doc_t) & (rows >= cols), 0.0, -1e30)
    carry_w = flow * jnp.exp(cum)
    final_w = jnp.where(doc == doc[CHUNK - 1 :, :], jnp.exp(last - cum), 0.0) * dt_ref[...]
    gain = carry_w[CHUNK - 1 :, :]
    low = cols < P_SIZE
    low_row = low[:1]
    write = key_ref[:, :N]
    read = key_ref[:, N:]
    write_t = write.astype(f32).T.astype(bf16)
    scores = mm(read, write, NT)
    for pair in range(heads // 2):
        first = 2 * pair
        lanes = slice(pair * 128, pair * 128 + 128)
        x = val_ref[:, lanes]
        xf = x.astype(f32)
        weights = []
        for h in (first, first + 1):
            decay = jnp.exp(cum[:, h : h + 1] - cum_t_ref[h : h + 1, :] + bias)
            weights.append((decay * scores * dt_t_ref[h : h + 1, :]).astype(bf16))
        stacked = jnp.concatenate(
            [jnp.where(low, xf, 0.0).astype(bf16), jnp.where(low, 0.0, xf).astype(bf16)], axis=0
        )
        old = state[:, lanes]
        y = mm(jnp.concatenate(weights, axis=1), stacked, NN)
        y = y + pair_cols(low, carry_w, first) * mm(read, old.astype(bf16), NN)
        y_ref[:, lanes] = y + skip_ref[:, lanes] * xf
        state[:, lanes] = pair_cols(low_row, gain, first) * old + mm(
            write_t, (pair_cols(low, final_w, first) * xf).astype(bf16), NN
        )


def scan_backward_kernel(
    val_ref, key_ref, cum_ref, cum_t_ref, dt_ref, doc_ref, doc_t_ref, flow_ref, skip_ref, state_ref, dy_ref,
    dval_ref, dkey_ref, dcum_ref, dcum_t_ref, ddt_ref, dskip_ref, dstate,
):
    heads = cum_ref.shape[1]

    @pl.when(pl.program_id(0) == 0)
    def _():
        dstate[...] = jnp.zeros_like(dstate)
        dskip_ref[...] = jnp.zeros_like(dskip_ref)

    cum = cum_ref[...]
    dt = dt_ref[...]
    last = cum[CHUNK - 1 :, :]
    doc = doc_ref[...]
    doc_t = doc_t_ref[...]
    flow = flow_ref[...]
    rows = lax.broadcasted_iota(jnp.int32, (CHUNK, CHUNK), 0)
    cols = lax.broadcasted_iota(jnp.int32, (CHUNK, CHUNK), 1)
    bias = jnp.where((doc == doc_t) & (cols >= rows), 0.0, -1e30)
    carry_w = flow * jnp.exp(cum)
    final_d = jnp.where(doc == doc[CHUNK - 1 :, :], jnp.exp(last - cum), 0.0)
    final_w = final_d * dt
    gain = carry_w[CHUNK - 1 :, :]
    low = cols < P_SIZE
    low_row = low[:1]
    write = key_ref[:, :N]
    read = key_ref[:, N:]
    read_t = read.astype(f32).T.astype(bf16)
    scores_t = mm(write, read, NT)
    dscores_t = jnp.zeros((CHUNK, CHUNK), f32)
    dwrite = jnp.zeros((CHUNK, N), f32)
    dread = jnp.zeros((CHUNK, N), f32)
    end_row = lax.broadcasted_iota(jnp.int32, (CHUNK, 1), 0) == CHUNK - 1
    dcum_cols = []
    dcum_rows = []
    ddt_cols = []
    for pair in range(heads // 2):
        first = 2 * pair
        lanes = slice(pair * 128, pair * 128 + 128)
        x = val_ref[:, lanes]
        xf = x.astype(f32)
        dy = dy_ref[:, lanes]
        dyb = dy.astype(bf16)
        x_stack = jnp.concatenate(
            [jnp.where(low, xf, 0.0).astype(bf16), jnp.where(low, 0.0, xf).astype(bf16)], axis=0
        )
        dy_stack = jnp.concatenate(
            [jnp.where(low, dy, 0.0).astype(bf16), jnp.where(low, 0.0, dy).astype(bf16)], axis=0
        )
        dweights = mm(x_stack, dyb, NT)
        old = state_ref[0, :, lanes]
        grad = dstate[:, lanes]
        gradb = grad.astype(bf16)
        carried = mm(read, old, NN)
        pushed = mm(write, gradb, NN)
        carry_p = pair_cols(low, carry_w, first)
        final_p = pair_cols(low, final_w, first)
        carry_prod = dy * carried
        final_prod = xf * pushed
        gain_prod = jnp.sum(grad * old.astype(f32), axis=0, keepdims=True)
        weights = []
        for which, h in enumerate((first, first + 1)):
            col = dt[:, h : h + 1]
            decay = jnp.exp(cum_t_ref[h : h + 1, :] - cum[:, h : h + 1] + bias)
            weighted = decay * col
            weights.append((weighted * scores_t).astype(bf16))
            dw = dweights[which * CHUNK : (which + 1) * CHUNK]
            dscores_t = dscores_t + dw * weighted
            direct = dw * decay * scores_t
            ddt_in = jnp.sum(direct, axis=1, keepdims=True)
            dcum_rows.append(jnp.sum(direct * col, axis=0, keepdims=True))
            half = low if which == 0 else ~low
            half_row = low_row if which == 0 else ~low_row
            carry_sum = jnp.sum(jnp.where(half, carry_prod, 0.0), axis=1, keepdims=True)
            final_sum = jnp.sum(jnp.where(half, final_prod, 0.0), axis=1, keepdims=True)
            push = final_w[:, h : h + 1] * final_sum
            at_end = jnp.sum(push, axis=0, keepdims=True) + gain[:, h : h + 1] * jnp.sum(
                jnp.where(half_row, gain_prod, 0.0), axis=1, keepdims=True
            )
            ddt_cols.append(ddt_in + final_d[:, h : h + 1] * final_sum)
            dcum_cols.append(
                carry_w[:, h : h + 1] * carry_sum - push - col * ddt_in + jnp.where(end_row, at_end, 0.0)
            )
        dx = mm(jnp.concatenate(weights, axis=1), dy_stack, NN)
        dval_ref[:, lanes] = dx + final_p * pushed + skip_ref[:, lanes] * dy
        dskip_ref[:, lanes] += jnp.sum(dy * xf, axis=0, keepdims=True)
        dwrite = dwrite + mm((final_p * xf).astype(bf16), gradb, NT)
        carry_dy = (carry_p * dy).astype(bf16)
        dread = dread + mm(carry_dy, old, NT)
        dstate[:, lanes] = pair_cols(low_row, gain, first) * grad + mm(read_t, carry_dy, NN)
    dsb = dscores_t.astype(bf16)
    dkey_ref[:, :N] = dwrite + mm(dsb, read, NN)
    dkey_ref[:, N:] = dread + mm(dsb, write, TN)
    dcum_ref[...] = jnp.concatenate(dcum_cols, axis=1)
    dcum_t_ref[...] = jnp.concatenate(dcum_rows, axis=0)
    ddt_ref[...] = jnp.concatenate(ddt_cols, axis=1)


def scan_forward(val, keys, cum, cum_t, dt, dt_t, doc, doc_t, flow, skip):
    length = val.shape[0]
    heads = cum.shape[1]
    inner = heads * P_SIZE
    steps = length // CHUNK
    row = lambda width: pl.BlockSpec((CHUNK, width), lambda i: (i, 0))
    lane = lambda height: pl.BlockSpec((height, CHUNK), lambda i: (0, i))
    return pl.pallas_call(
        scan_forward_kernel,
        grid=(steps,),
        in_specs=[
            row(inner), row(KEYS), row(heads), lane(heads), row(heads), lane(heads), row(1), lane(1), row(1),
            pl.BlockSpec((1, inner), lambda i: (0, 0)),
        ],
        out_specs=[row(inner), pl.BlockSpec((1, N, inner), lambda i: (i, 0, 0))],
        out_shape=[
            jax.ShapeDtypeStruct((length, inner), f32),
            jax.ShapeDtypeStruct((steps, N, inner), bf16),
        ],
        scratch_shapes=[pltpu.VMEM((N, inner), f32)],
        compiler_params=pltpu.CompilerParams(vmem_limit_bytes=40 * 2**20),
        cost_estimate=pl.CostEstimate(
            flops=length * inner * 1024, bytes_accessed=length * inner * 10, transcendentals=length * heads * CHUNK
        ),
    )(val, keys, cum, cum_t, dt, dt_t, doc, doc_t, flow, skip)


def scan_backward(val, keys, cum, cum_t, dt, doc, doc_t, flow, skip, states, dy):
    length = val.shape[0]
    heads = cum.shape[1]
    inner = heads * P_SIZE
    steps = length // CHUNK
    row = lambda width: pl.BlockSpec((CHUNK, width), lambda i: (steps - 1 - i, 0))
    lane = lambda height: pl.BlockSpec((height, CHUNK), lambda i: (0, steps - 1 - i))
    whole = pl.BlockSpec((1, inner), lambda i: (0, 0))
    return pl.pallas_call(
        scan_backward_kernel,
        grid=(steps,),
        in_specs=[
            row(inner), row(KEYS), row(heads), lane(heads), row(heads), row(1), lane(1), row(1), whole,
            pl.BlockSpec((1, N, inner), lambda i: (steps - 1 - i, 0, 0)), row(inner),
        ],
        out_specs=[row(inner), row(KEYS), row(heads), lane(heads), row(heads), whole],
        out_shape=[
            jax.ShapeDtypeStruct((length, inner), f32),
            jax.ShapeDtypeStruct((length, KEYS), f32),
            jax.ShapeDtypeStruct((length, heads), f32),
            jax.ShapeDtypeStruct((heads, length), f32),
            jax.ShapeDtypeStruct((length, heads), f32),
            jax.ShapeDtypeStruct((1, inner), f32),
        ],
        scratch_shapes=[pltpu.VMEM((N, inner), f32)],
        compiler_params=pltpu.CompilerParams(vmem_limit_bytes=40 * 2**20),
        cost_estimate=pl.CostEstimate(
            flops=length * inner * 3072, bytes_accessed=length * inner * 14, transcendentals=length * heads * CHUNK
        ),
    )(val, keys, cum, cum_t, dt, doc, doc_t, flow, skip, states, dy)


MESH = pl.DeviceIdType.MESH
HBM = pl.BlockSpec(memory_space=pl.ANY)
VMEM = pl.BlockSpec(memory_space=pltpu.VMEM)


def z_pair(peers, groups):
    planes = groups // 2
    return 2 if planes % 2 == 0 and (E // (peers * planes)) % (2 * P_SIZE) == 0 else 1


def flip(value, bits):
    bit = 1
    while bit <= bits:
        if bits & bit:
            value = value + bit - 2 * bit * (value // bit % 2)
        bit *= 2
    return value


class Place:
    def __init__(self):
        self.peers = lax.axis_size("seq")
        groups = lax.axis_size("batch")
        self.near = z_pair(self.peers, groups)
        self.far = groups // 2 // self.near
        self.s = lax.axis_index("seq")
        b = lax.axis_index("batch")
        self.c = b % 2
        self.zl = b // 2 % self.near
        self.zh = b // 2 // self.near

    def at(self, s=0, zl=0, zh=0, c=0):
        return (flip(self.s, s), (flip(self.zh, zh) * self.near + flip(self.zl, zl)) * 2 + flip(self.c, c))

    def partners(self):
        cube = [self.at(s=o // self.near, zl=o % self.near) for o in range(1, self.peers * self.near)]
        return cube, [self.at(zh=o) for o in range(1, self.far)], [self.at(c=1)]


def greet(devices):
    barrier = pltpu.get_barrier_semaphore()
    for device in devices:
        pl.semaphore_signal(barrier, inc=1, device_id=device, device_id_type=MESH)
    pl.semaphore_wait(barrier, len(devices))


class Mover:
    def __init__(self, send, recv, local):
        self.send, self.recv, self.local = send, recv, local
        self.sent, self.kept = 0, 0
        self.open = []

    def put(self, src, dst, device):
        copy = pltpu.make_async_remote_copy(
            src_ref=src, dst_ref=dst, send_sem=self.send.at[self.sent], recv_sem=self.recv.at[self.sent],
            device_id=device, device_id_type=MESH,
        )
        copy.start()
        self.sent += 1
        self.open.append(copy)
        return copy

    def keep(self, src, dst):
        copy = pltpu.make_async_copy(src, dst, self.local.at[self.kept])
        copy.start()
        self.kept += 1
        return copy

    def close(self):
        for copy in self.open:
            copy.wait_send()


def run_paths(paths):
    paths = list(paths)
    while paths:
        alive = []
        for path in paths:
            try:
                next(path)
                alive.append(path)
            except StopIteration:
                pass
        paths = alive


def bits_of(peers):
    return [1 << i for i in range(peers.bit_length() - 1)]


def combos(bits):
    out = [0]
    for bit in reversed(bits):
        out = [bit | o for o in out] + out
    return out


def gather_kernel(
    send_ref, key_ref, out_ref, rows_ref, cot_ref, meta_ref,
    w_ref, k_ref, o_ref, x_ref, ct_ref, m_ref, send, recv, local,
):
    me = Place()
    s, zl, zh, c = me.s, me.zl, me.zh, me.c
    cube, far, sibling = me.partners()
    greet(cube + far + sibling)
    mover = Mover(send, recv, local)
    bits = bits_of(me.peers)

    def rows_path(src, dst, order):
        own = mover.keep(src, dst.at[zl, s])
        near = [mover.put(src, dst.at[zl, s], me.at(zl=o)) for o in range(1, me.near)]
        yield
        own.wait()
        for copy in near:
            copy.wait_recv()
        held = [0]
        for bit in order:
            copies = [mover.put(dst.at[:, flip(s, h)], dst.at[:, flip(s, h)], me.at(s=bit)) for h in held]
            held = held + [h ^ bit for h in held]
            yield
            for copy in copies:
                copy.wait_recv()

    def meta_path():
        own = mover.keep(meta_ref, m_ref.at[zl])
        near = [mover.put(meta_ref, m_ref.at[zl], me.at(zl=o)) for o in range(1, me.near)]
        yield
        own.wait()
        for copy in near:
            copy.wait_recv()

    def key_path():
        own = mover.keep(key_ref, k_ref.at[zh, c, s, zl])
        copies = [mover.put(key_ref, k_ref.at[zh, c, s, zl], me.at(zh=o)) for o in range(1, me.far)]
        yield
        own.wait()
        for copy in copies:
            copy.wait_recv()
        block = k_ref.at[:, c, s, zl]
        copies = [mover.put(block, block, me.at(zl=o)) for o in range(1, me.near)]
        yield
        for copy in copies:
            copy.wait_recv()
        held = [0]
        for bit in bits:
            copies = [mover.put(k_ref.at[:, c, flip(s, h)], k_ref.at[:, c, flip(s, h)], me.at(s=bit)) for h in held]
            held = held + [h ^ bit for h in held]
            yield
            for copy in copies:
                copy.wait_recv()
        copy = mover.put(k_ref.at[:, c], k_ref.at[:, c], me.at(c=1))
        yield
        copy.wait_recv()

    def spread_path(copies, view):
        last = []
        for o, copy in copies:
            yield
            copy.wait_recv()
            last.append(mover.put(view(flip(zh, o)), view(flip(zh, o)), me.at(c=1)))
        return last

    def out_path():
        own = mover.keep(out_ref, o_ref.at[zh, c])
        copies = [(o, mover.put(out_ref, o_ref.at[zh, c], me.at(zh=o))) for o in range(1, me.far)]
        first = mover.put(out_ref, o_ref.at[zh, c], me.at(c=1))
        last = yield from spread_path(copies, lambda h: o_ref.at[h, c])
        yield
        own.wait()
        for copy in last + [first]:
            copy.wait_recv()

    weights = {}

    def weight_path():
        for step in range(me.peers):
            for o in range(me.near):
                if step or o:
                    weights[step, o] = mover.put(
                        send_ref.at[flip(s, step), flip(zl, o)], w_ref.at[zh, c, s, zl], me.at(s=step, zl=o)
                    )
                else:
                    weights[step, o] = mover.keep(send_ref.at[s, zl], w_ref.at[zh, c, s, zl])
        pieces = []
        for step in range(me.peers):
            yield
            for o in range(me.near):
                if step or o:
                    weights[step, o].wait_recv()
                else:
                    weights[step, o].wait()
            block = w_ref.at[zh, c, flip(s, step)]
            copies = [(o, mover.put(block, block, me.at(zh=o))) for o in range(1, me.far)]
            pieces.append((step, copies, mover.put(block, block, me.at(c=1))))
        last = []
        for step, copies, first in pieces:
            last.append(first)
            last += yield from spread_path(copies, lambda h, step=step: w_ref.at[h, c, flip(s, step)])
        yield
        for copy in last:
            copy.wait_recv()

    run_paths(
        [
            rows_path(rows_ref, x_ref, bits), rows_path(cot_ref, ct_ref, bits[::-1]), meta_path(), key_path(),
            weight_path(), out_path(),
        ]
    )
    mover.close()


def remote_params(identity):
    return pltpu.CompilerParams(collective_id=identity, has_side_effects=True, vmem_limit_bytes=58 * 2**20)


def sems(copies, kept):
    return [pltpu.SemaphoreType.DMA((copies,)), pltpu.SemaphoreType.DMA((copies,)), pltpu.SemaphoreType.DMA((kept,))]


def gather(send, keys, out_w, rows, cot, meta):
    me = Place()
    peers, near, far = me.peers, me.near, me.far
    shape = lambda lead, part: jax.ShapeDtypeStruct(lead + part, bf16)
    copies = (peers * near - 1) + (peers + 1) * (2 * far - 1) + 3 * (near + peers - 2) + near - 1 + far
    return pl.pallas_call(
        gather_kernel,
        out_shape=[
            shape((far, 2, peers, near), send.shape[2:]),
            shape((far, 2, peers, near), keys.shape),
            shape((far, 2), out_w.shape),
            shape((near, peers), rows.shape),
            shape((near, peers), cot.shape),
            jax.ShapeDtypeStruct((near,) + meta.shape, meta.dtype),
        ],
        in_specs=[HBM] * 6,
        out_specs=[HBM] * 6,
        scratch_shapes=sems(copies, 8),
        compiler_params=remote_params(0),
        name="gather_all",
    )(send, keys, out_w, rows, cot, meta)


def total_kernel(part_ref, sum_ref, box, send, recv, local):
    me = Place()
    cube = me.partners()[0]
    greet(cube)
    mover = Mover(send, recv, local)
    copies = [mover.put(part_ref, box.at[i], device) for i, device in enumerate(cube)]
    total = part_ref[...]
    for i, copy in enumerate(copies):
        copy.wait_recv()
        total = total + box[i]
    sum_ref[...] = total
    mover.close()


def cube_total(part):
    me = Place()
    count = me.peers * me.near - 1
    return pl.pallas_call(
        total_kernel,
        out_shape=jax.ShapeDtypeStruct(part.shape, f32),
        in_specs=[VMEM],
        out_specs=VMEM,
        scratch_shapes=[pltpu.VMEM((count,) + part.shape, f32)] + sems(count, 1),
        compiler_params=remote_params(1),
        name="cube_total",
    )(part)


def add_rows(out, parts):
    shape = out.shape
    tile = min(16, shape[-2])
    lead = [()]
    for size in shape[:-2]:
        lead = [l + (i,) for l in lead for i in range(size)]
    for l in lead:

        def step(i, carry, l=l):
            at = l + (pl.ds(pl.multiple_of(i * tile, tile), tile), slice(None))
            total = parts[0][at].astype(f32)
            for part in parts[1:]:
                total = total + part[at].astype(f32)
            out[at] = total.astype(out.dtype)
            return carry

        lax.fori_loop(0, shape[-2] // tile, step, 0)


def scatter_kernel(
    bp_ref, gn_ref, gw_ref, go_ref, gk_ref, v_ref,
    ob_ref, og_ref, ow_ref, oo_ref, ok_ref, ov_ref,
    b_own, b_box, b_near, n_own, n_box, n_near, w_own, w_box, w_far, o_own, o_box, o_far,
    k_own, k_box, k_near, k_far, k_bits, v_box, send, recv, local,
):
    me = Place()
    s, zl, zh, c = me.s, me.zl, me.zh, me.c
    cube, far, sibling = me.partners()
    greet(cube + far + sibling)
    mover = Mover(send, recv, local)
    bits = bits_of(me.peers)

    def halve(own, box, order, first_src):
        base = 0
        todo = combos(order[1:])
        copies = [mover.put(first_src(flip(s, order[0] ^ o)), box.at[base + j], me.at(s=order[0])) for j, o in enumerate(todo)]
        for i, bit in enumerate(order):
            rest = order[i + 1 :]
            count = 1 << len(rest)
            offset = (1 << (len(order) - 1)) - count
            coming = []
            for j in range(count):
                yield
                copies[j].wait_recv()
                add_rows(own.at[offset + j], [own.at[offset + j], box.at[base + j]])
                if rest and j < count // 2:
                    coming.append(mover.put(own.at[offset + j], box.at[base + count + j], me.at(s=rest[0])))
            base += count
            copies = coming

    def rows_path(src, own, box, near_box, out, order):
        loads = [mover.keep(src.at[:, flip(s, o)], own.at[j]) for j, o in enumerate(combos(order[1:]))]

        def first_src(at):
            return src.at[:, at]

        path = halve(own, box, order, first_src)
        next(path)
        for load in loads:
            load.wait()
        yield
        yield from path
        last = own.shape[0] - 1
        copies = [mover.put(own.at[last, flip(zl, o)], near_box.at[o - 1], me.at(zl=o)) for o in range(1, me.near)]
        yield
        for copy in copies:
            copy.wait_recv()
        add_rows(out, [own.at[last, zl]] + [near_box.at[o - 1] for o in range(1, me.near)])

    def weight_path():
        order = [(o, k) for o in range(1, me.far) for k in range(me.peers)] + [(0, k) for k in range(me.peers)]
        loads, copies = {}, {}
        for o, k in order:
            copies[o, k] = mover.put(gw_ref.at[flip(zh, o), 1 - c, flip(s, k)], w_box.at[o, k], me.at(c=1))
            loads[o, k] = mover.keep(gw_ref.at[flip(zh, o), c, flip(s, k)], w_own.at[o, k])
        far_copies = {}
        for o, k in order:
            yield
            loads[o, k].wait()
            copies[o, k].wait_recv()
            if o:
                add_rows(w_own.at[o, k], [w_own.at[o, k], w_box.at[o, k]])
                far_copies[o, k] = mover.put(w_own.at[o, k], w_far.at[o - 1, k], me.at(zh=o))
        ends = []
        for k in range(me.peers):
            yield
            for o in range(1, me.far):
                far_copies[o, k].wait_recv()
            parts = [w_own.at[0, k], w_box.at[0, k]] + [w_far.at[o - 1, k] for o in range(1, me.far)]
            add_rows(w_own.at[0, k], parts)
            for o in range(me.near):
                if k or o:
                    ends.append(mover.put(w_own.at[0, k, flip(zl, o)], ow_ref.at[s, zl], me.at(s=k, zl=o)))
                else:
                    own = mover.keep(w_own.at[0, 0, zl], ow_ref.at[s, zl])
        yield
        own.wait()
        for copy in ends:
            copy.wait_recv()

    def out_path():
        order = list(range(1, me.far)) + [0]
        copies, loads = {}, {}
        for o in order:
            copies[o] = mover.put(go_ref.at[flip(zh, o), 1 - c], o_box.at[o], me.at(c=1))
            loads[o] = mover.keep(go_ref.at[flip(zh, o), c], o_own.at[o])
        for _ in range(me.far * me.peers):
            yield
        far_copies = {}
        for o in order:
            loads[o].wait()
            copies[o].wait_recv()
            if o:
                add_rows(o_own.at[o], [o_own.at[o], o_box.at[o]])
                far_copies[o] = mover.put(o_own.at[o], o_far.at[o - 1], me.at(zh=o))
        for _ in range(me.peers):
            yield
        for o in range(1, me.far):
            far_copies[o].wait_recv()
        add_rows(oo_ref, [o_own.at[0], o_box.at[0]] + [o_far.at[o - 1] for o in range(1, me.far)])

    def key_path():
        blocks = combos(bits)
        copies, loads = [], []
        for j, o in enumerate(blocks):
            copies.append(mover.put(gk_ref.at[:, 1 - c, flip(s, o)], k_box.at[j], me.at(c=1)))
            loads.append(mover.keep(gk_ref.at[:, c, flip(s, o)], k_own.at[j]))
        half = me.peers // 2
        sent = []
        for j in range(me.peers):
            yield
            loads[j].wait()
            copies[j].wait_recv()
            add_rows(k_own.at[j], [k_own.at[j], k_box.at[j]])
            if j < half:
                sent.append(mover.put(k_own.at[j], k_bits.at[j], me.at(s=bits[0])))
        base = 0
        for i, bit in enumerate(bits):
            count = me.peers >> (i + 1)
            offset = me.peers - count
            coming = []
            for j in range(count):
                yield
                sent[j].wait_recv()
                add_rows(k_own.at[offset + j], [k_own.at[offset + j], k_bits.at[base + j]])
                if i + 1 < len(bits) and j < count // 2:
                    coming.append(mover.put(k_own.at[offset + j], k_bits.at[base + count + j], me.at(s=bits[i + 1])))
            base += count
            sent = coming
        end = k_own.at[me.peers - 1]
        copies = [mover.put(end.at[:, flip(zl, o)], k_near.at[o - 1], me.at(zl=o)) for o in range(1, me.near)]
        yield
        for copy in copies:
            copy.wait_recv()
        add_rows(end.at[:, zl], [end.at[:, zl]] + [k_near.at[o - 1] for o in range(1, me.near)])
        copies = [mover.put(end.at[flip(zh, o), zl], k_far.at[o - 1], me.at(zh=o)) for o in range(1, me.far)]
        yield
        for copy in copies:
            copy.wait_recv()
        add_rows(ok_ref, [end.at[zh, zl]] + [k_far.at[o - 1] for o in range(1, me.far)])

    def small_path():
        turns = [me.at(c=1)] + [me.at(zl=o) for o in bits_of(me.near)]
        turns += [me.at(s=o) for o in bits] + [me.at(zh=o) for o in bits_of(me.far)]
        rows = v_ref.shape[0]
        v_box[0] = v_ref[...]
        for i, device in enumerate(turns):
            copy = mover.put(v_box.at[2 * i], v_box.at[2 * i + 1], device)
            yield
            copy.wait_recv()
            v_box[2 * i + 2] = v_box[2 * i] + v_box[2 * i + 1]
        ov_ref[...] = v_box[2 * len(turns)]

    run_paths(
        [
            weight_path(),
            rows_path(gn_ref, n_own, n_box, n_near, og_ref, bits[::-1]),
            rows_path(bp_ref, b_own, b_box, b_near, ob_ref, bits),
            key_path(),
            small_path(),
            out_path(),
        ]
    )
    mover.close()


def scatter(branch, grads, gw, go, gk, small):
    me = Place()
    peers, near, far = me.peers, me.near, me.far
    tokens, width = branch.shape[2:]
    stages = len(bits_of(peers)) + len(bits_of(near)) + len(bits_of(far)) + 1
    vm = lambda *shape: pltpu.VMEM(shape, bf16)
    rows_scratch = [vm(peers // 2, near, tokens, width), vm(peers - 1, near, tokens, width), vm(max(near - 1, 1), tokens, width)]
    block = gw.shape[3:]
    kblock = gk.shape[3:]
    oblock = go.shape[2:]
    copies = 2 * (peers + near - 2) + 2 * far * peers + peers * (near - 1) + peers - 1 + 3 * far + 2 * peers + near - 4 + stages
    kept = peers + far * peers + 1 + far + peers + 4
    return pl.pallas_call(
        scatter_kernel,
        out_shape=[
            jax.ShapeDtypeStruct((tokens, width), f32),
            jax.ShapeDtypeStruct((tokens, width), f32),
            jax.ShapeDtypeStruct((peers,) + block, bf16),
            jax.ShapeDtypeStruct(oblock, f32),
            jax.ShapeDtypeStruct(kblock[1:], f32),
            jax.ShapeDtypeStruct(small.shape, f32),
        ],
        in_specs=[HBM] * 5 + [VMEM],
        out_specs=[VMEM, VMEM, HBM, VMEM, VMEM, VMEM],
        scratch_shapes=rows_scratch
        + rows_scratch
        + [vm(far, peers, *block), vm(far, peers, *block), vm(max(far - 1, 1), peers, *block)]
        + [vm(far, *oblock), vm(far, *oblock), vm(max(far - 1, 1), *oblock)]
        + [
            vm(peers, far, *kblock), vm(peers, far, *kblock), vm(max(near - 1, 1), far, *kblock[1:]),
            vm(max(far - 1, 1), *kblock[1:]), vm(peers - 1, far, *kblock),
            pltpu.VMEM((2 * stages + 1,) + small.shape, f32),
        ]
        + sems(copies, kept),
        compiler_params=remote_params(2),
        name="scatter_all",
    )(branch, grads, gw, go, gk, small)


def doc_index(places, doc_ends):
    return jnp.sum((places[:, None] >= doc_ends[None, :-1]).astype(jnp.int32), axis=1)


def moved_down(rows, by):
    return jnp.concatenate([jnp.zeros((by,) + rows.shape[1:], rows.dtype), rows[: rows.shape[0] - by]], axis=0)


def moved_up(rows, by):
    return jnp.concatenate([rows[by:], jnp.zeros((by,) + rows.shape[1:], rows.dtype)], axis=0)


def convolve(conv_in, weight, bias, masks):
    total = jnp.broadcast_to(bias[None, :], conv_in.shape)
    for k in range(CONV):
        total = total + weight[k][None, :] * moved_down(conv_in, CONV - 1 - k).astype(f32) * masks[k][:, None]
    return total


def convolve_back(dact, conv_in, conv_sum, weight, masks):
    sig = jax.nn.sigmoid(conv_sum)
    dconv = dact * (sig * (1.0 + conv_sum * (1.0 - sig)))
    sums = []
    grad_in = jnp.zeros_like(dconv)
    for k in range(CONV):
        taken = dconv * masks[k][:, None]
        sums.append(jnp.sum(taken * moved_down(conv_in, CONV - 1 - k).astype(f32), axis=0))
        grad_in = grad_in + weight[k][None, :] * moved_up(taken, CONV - 1 - k)
    sums.append(jnp.sum(dconv, axis=0))
    return grad_in.astype(bf16), jnp.stack(sums)


def body(
    inputs, cotangent, doc_lengths, head_width, pre_gain, in_weight, step_weight, conv_weight, conv_bias,
    step_bias, decay_log, skip_gain, norm_gain, out_weight,
):
    me = Place()
    peers, near, far = me.peers, me.near, me.far
    outer = far if near > 1 else 1
    tokens = inputs.shape[1]
    width = inputs.shape[2]
    span = tokens * peers
    length = span * near
    heads = H // (peers * near)
    inner = heads * P_SIZE
    rows = in_weight.shape[0]
    seq_rows = inputs[0].astype(f32)
    cot_rows = cotangent[0]

    def per_group(part):
        lead = part.shape[0]
        return part.reshape(lead, peers, outer, near, -1).transpose(1, 3, 0, 2, 4).reshape(peers, near, lead, -1)

    def whole_again(part):
        lead = part.shape[2]
        return part.reshape(peers, near, lead, outer, -1).transpose(2, 0, 3, 1, 4).reshape(lead, -1)

    def own(vector):
        part = vector.reshape(-1, peers, outer, near, vector.shape[-1] // (peers * outer * near))
        part = lax.dynamic_index_in_dim(part, me.s, 1, False)
        part = lax.dynamic_index_in_dim(part, me.zl, 2, False)
        return part.reshape(vector.shape[:-1] + (-1,))

    def spread(part):
        lead = part.shape[:-1]
        part = part.reshape(-1, 1, outer, 1, part.shape[-1] // outer)
        full = jnp.zeros((part.shape[0], peers, outer, near, part.shape[-1]), part.dtype)
        return lax.dynamic_update_slice(full, part, (0, me.s, 0, me.zl, 0)).reshape(lead + (-1,))

    def to_gathered(part):
        part = part.reshape(part.shape[0], peers, far, near, 2, rows)
        return part.transpose(0, 2, 4, 1, 3, 5).reshape(part.shape[0], width)

    def from_gathered(part):
        part = part.reshape(part.shape[0], far, 2, peers, near, rows)
        return part.transpose(0, 3, 1, 4, 2, 5).reshape(part.shape[0], width)

    send = jnp.concatenate([per_group(in_weight[:, :E]), per_group(in_weight[:, E : 2 * E])], axis=-1)
    key_send = jnp.concatenate(
        [in_weight[:, 2 * E :], step_weight, jnp.zeros((rows, STEP_PAD - H), bf16)], axis=1
    )
    inv_rms = lax.rsqrt(jnp.mean(seq_rows * seq_rows, axis=1, keepdims=True) + epsilon)
    normed = to_gathered((seq_rows * inv_rms * pre_gain[None, :]).astype(bf16))
    meta = jnp.zeros((8, 128), jnp.int32)
    meta = meta.at[0, :DOCS].set(doc_lengths[0]).at[1, 0].set(head_width[0])
    in_w, key_w, out_w, normed, cot_all, meta = gather(send, key_send, out_weight, normed, cot_rows, meta)
    in_w = in_w.reshape(width, 2 * inner)
    key_w = key_w.reshape(width, -1)
    out_w = out_w.reshape(inner, width)
    normed = normed.reshape(length, width)
    cot_all = cot_all.reshape(length, width)

    places = jnp.arange(span, dtype=jnp.int32)
    doc_ids = jnp.concatenate(
        [doc_index(places, jnp.cumsum(meta[i, 0, :DOCS])) + i * DOCS for i in range(near)]
    )
    before = jnp.concatenate([jnp.full((1,), -1, jnp.int32), doc_ids[CHUNK - 1 : -1 : CHUNK]])
    flow = (doc_ids == jnp.repeat(before, CHUNK)).astype(f32)[:, None]
    doc = doc_ids[:, None]
    doc_t = doc_ids[None, :]
    counts = meta[:, 1, 0]
    head_total = jnp.repeat((counts * P_SIZE).astype(f32), span)[:, None]
    my_heads = own(jnp.arange(H, dtype=jnp.int32))
    head_mask = jnp.repeat((my_heads[None, :] < counts[:, None]).astype(f32), P_SIZE, axis=1)
    head_mask = jnp.repeat(head_mask, span, axis=0)
    masks = []
    for k in range(CONV):
        lag = CONV - 1 - k
        masks.append((jnp.concatenate([jnp.full((lag,), -1, jnp.int32), doc_ids[: length - lag]]) == doc_ids).astype(f32))

    conv_all = jnp.concatenate([conv_weight, conv_bias[None]], axis=0)
    conv_v = own(conv_all[:, :E])
    conv_k = conv_all[:, E:]
    step_b = own(step_bias)
    rate = jnp.exp(own(decay_log))
    skip = jnp.repeat(own(skip_gain), P_SIZE)[None, :]
    gain = own(norm_gain)[None, :]

    projected = mm(normed, in_w, NN)
    gate = projected[:, :inner]
    value_in = projected[:, inner:].astype(bf16)
    key_out = mm(normed, key_w, NN)
    key_in = key_out[:, :KEYS].astype(bf16)
    step_raw = own(key_out[:, KEYS : KEYS + H]) + step_b[None, :]
    value_sum = convolve(value_in, conv_v[:CONV], conv_v[CONV], masks)
    values = jax.nn.silu(value_sum).astype(bf16)
    key_sum = convolve(key_in, conv_k[:CONV], conv_k[CONV], masks)
    keys = jax.nn.silu(key_sum).astype(bf16)
    dt = jax.nn.softplus(step_raw)
    log_decay = -dt * rate[None, :]
    cum = jnp.cumsum(log_decay.reshape(-1, CHUNK, heads), axis=1).reshape(length, heads)
    y, states = scan_forward(values, keys, cum, cum.T, dt, dt.T, doc, doc_t, flow, skip)
    grad_mixed = mm(cot_all, out_w, NT)
    sig_gate = jax.nn.sigmoid(gate)
    silu_gate = gate * sig_gate
    masked = y * head_mask
    gated = masked * silu_gate
    scaled = grad_mixed * gain
    part = jnp.stack([jnp.sum(gated * gated, axis=1), jnp.sum(scaled * gated, axis=1)])
    sums = cube_total(part.reshape(-1, 128)).reshape(2, length, 1)
    inv = lax.rsqrt(sums[0] / head_total + epsilon)
    pull = inv * inv * inv * sums[1] / head_total
    mixed = (gated * inv * gain).astype(bf16)
    branch = mm(mixed, out_w, NN).astype(bf16)

    grad_out = mm(mixed, cot_all, TN).astype(bf16)
    grad_norm_gain = jnp.sum(grad_mixed * gated * inv, axis=0)
    grad_gated = inv * scaled - pull * gated
    dy = grad_gated * silu_gate * head_mask
    grad_gate = (grad_gated * masked * (sig_gate * (1.0 + gate * (1.0 - sig_gate)))).astype(bf16)
    dvalues, dkeys, dcum, dcum_t, ddt, dskip = scan_backward(
        values, keys, cum, cum.T, dt, doc, doc_t, flow, skip, states, dy
    )
    dcum = (dcum + dcum_t.T).reshape(-1, CHUNK, heads)
    dlog = lax.cumsum(dcum, axis=1, reverse=True).reshape(length, heads)
    grad_dt = ddt - rate[None, :] * dlog
    grad_decay_log = -jnp.sum(dt * rate[None, :] * dlog, axis=0)
    grad_step = grad_dt * jax.nn.sigmoid(step_raw)
    grad_step_bias = jnp.sum(grad_step, axis=0)
    grad_skip = jnp.sum(dskip.reshape(heads, P_SIZE), axis=1)
    grad_value_in, sums_v = convolve_back(dvalues, value_in, value_sum, conv_v[:CONV], masks)
    grad_key_in, sums_k = convolve_back(dkeys, key_in, key_sum, conv_k[:CONV], masks)
    grad_cols = jnp.concatenate([grad_gate, grad_value_in], axis=1)
    step_cols = jnp.pad(spread(grad_step.astype(bf16)), ((0, 0), (0, STEP_PAD - H)))
    key_cols = jnp.concatenate([grad_key_in, step_cols], axis=1)
    grad_in = mm(normed, grad_cols, TN).astype(bf16)
    grad_keys = mm(normed, key_cols, TN).astype(bf16)
    grad_normed = mm(grad_cols, in_w, NT) + mm(key_cols, key_w, NT)
    grad_pre_gain = from_gathered(jnp.sum(grad_normed * normed.astype(f32), axis=0)[None])[0] / pre_gain

    small = jnp.concatenate(
        [
            grad_pre_gain,
            jnp.concatenate([spread(sums_v), sums_k], axis=1).reshape(-1),
            spread(grad_step_bias),
            spread(grad_decay_log),
            spread(grad_skip),
            spread(grad_norm_gain),
        ]
    )
    count = small.shape[0]
    padded = -count % 1024
    small = jnp.pad(small, (0, padded)).reshape(-1, 128)
    rows_of = lambda part: part.reshape(near, peers, tokens, width)
    blocks = (far, 2, peers, near, rows)
    branch, grad_normed, grad_in, grad_out_weight, grad_keys, small = scatter(
        rows_of(branch),
        rows_of(grad_normed.astype(bf16)),
        grad_in.reshape(blocks + (2 * inner,)),
        grad_out.reshape(far, 2, -1, width),
        grad_keys.reshape(blocks + (KEYS + STEP_PAD,)),
        small,
    )
    output = (seq_rows + branch).astype(bf16)[None]
    grad_normed = from_gathered(grad_normed)
    scaled_in = grad_normed * pre_gain[None, :]
    dot = jnp.mean(scaled_in * seq_rows, axis=1, keepdims=True)
    grad_seq = inv_rms * scaled_in - seq_rows * (inv_rms * inv_rms * inv_rms * dot)
    grad_inputs = (grad_seq + cot_rows.astype(f32))[None]
    grad_in = grad_in.astype(f32)
    grad_in_weight = jnp.concatenate(
        [whole_again(grad_in[..., :inner]), whole_again(grad_in[..., inner:]), grad_keys[:, :KEYS]], axis=1
    )
    grad_step_weight = grad_keys[:, KEYS : KEYS + H]
    small = small.reshape(-1)
    sizes = [width, (CONV + 1) * conv_weight.shape[1], H, H, H, E]
    parts = []
    for size in sizes:
        parts.append(small[:size])
        small = small[size:]
    conv_sums = parts[1].reshape(CONV + 1, -1)
    return (
        output, grad_inputs, parts[0], grad_in_weight, grad_step_weight, conv_sums[:CONV], conv_sums[CONV],
        parts[2], parts[3], parts[4], parts[5], grad_out_weight,
    )


def solution(mesh):
    both = P(("seq", "batch"), None)
    tok = P("batch", "seq", None)
    in_specs = (
        tok, tok, P("batch", None), P("batch"), P(), both, both, P(), P(), P(), P(), P(), P(), both,
    )
    out_specs = (tok, tok, P(), both, both, P(), P(), P(), P(), P(), P(), both)
    return jax.shard_map(body, mesh=mesh, in_specs=in_specs, out_specs=out_specs, check_vma=False)
```

time: 602 us -> 485 us (0.81)
  waiting for transfers between devices: 343 us -> 0 us
  Pallas kernels: 19.2 us -> 309 us
  blocking collectives: 75.9 us -> 0 us
  local copies, waits for them, and re-layouts: 27.9 us -> 55.4 us
  other arithmetic: 43.1 us -> 63.5 us
  starting transfers between devices: 16.7 us -> 0 us
  between operations: 15.5 us -> 2.73 us
  matrix products: 56.6 us -> 47.1 us
    pallas_call x2 -> x5, Pallas kernels: 19.2 us -> 309 us  [the longest x1 142 us: gather(): pl.pallas_call(gather_kernel, out_shape=[shape((far, 2, peers, near), sen...]
    all_gather x5 -> x0, waiting for transfers between devices: 171 us -> none  [the longest x1 54.3 us: body(): lax.all_gather(value_w.reshape(peers * rows, -1), 'batch', axis=0, tiled=...]
    reduce_scatter x3 -> x0, waiting for transfers between devices: 108 us -> none  [the longest x1 55.1 us: body(): lax.psum_scatter(value_term, 'batch', scatter_dimension=0, tiled=True)]
    psum x1 -> x0, blocking collectives: 41.1 us -> none  [body(): lax.psum((grad_pre_gain, jnp.concatenate([spread(conv_all[:, :inner], E),...]
    psum x1 -> x0, waiting for transfers between devices: 40.8 us -> none  [body(): lax.psum((grad_pre_gain, jnp.concatenate([spread(conv_all[:, :inner], E),...]
    all_to_all x2 -> x0, blocking collectives: 26.5 us -> none  [the longest x1 14.2 us: body(): gate_w = lax.all_to_all(gate_send, 'seq', 0, 0)]
    another operation x1, other arithmetic: 0.26 us -> 23.5 us  [body(): jnp.cumsum(log_decay.reshape(-1, CHUNK, heads), axis=1)]
    all_to_all x4 -> x0, waiting for transfers between devices: 21.4 us -> none  [the longest x1 17 us: body(): lax.all_to_all(grad_normed, 'seq', 0, 0).astype(f32)]
  transfers between devices with their start and end apart: 13 -> 0, of which waited for: 11 -> 0; matrix products, arithmetic and copies ran while one was open for 16% -> 0% of each run, Pallas kernels for 1% -> 0%
where the time goes in v2:
time: 485 us; the launch traced here: 478 us
  Pallas kernels  309 us (64%)
  other arithmetic  63.5 us (13%)
  local copies, waits for them, and re-layouts  55.4 us (11%)
  matrix products  47.1 us (10%)
    pallas_call x1, Pallas kernels, gather(): pl.pallas_call(gather_kernel, out_shape=[shape((far, 2, peers, near), sen...  142 us
    pallas_call x1, Pallas kernels, scatter(): pl.pallas_call(scatter_kernel, out_shape=[jax.ShapeDtypeStruct((tokens, w...  138 us
    dot_general x9, matrix products, mm(): return lax.dot_general(a, b, (dims, ((), ())), preferred_element_type=f32)  47.1 us
    another operation x1, other arithmetic, body(): jnp.cumsum(log_decay.reshape(-1, CHUNK, heads), axis=1)  23.5 us
    pallas_call x1, Pallas kernels, scan_backward(): pl.pallas_call(scan_backward_kernel, grid=(steps,), in_specs=[row(inner),...  14.9 us

profile of v2, /device:TPU:0, one launch (start us, length us, event | category | flops | bytes accessed | tf_op | source)
XLA Modules:
  0.0 477.8 jit_solution(13729850192254920288)
XLA Ops:
  1.3 1.2 fusion.28
  12.3 1.3 maximum_maximum_fusion.key_ref
  14.7 1.2 copy.191
  20.1 1.1 pad_maximum_fusion.4.send_ref
  21.2 141.6 %gather_all.1 = (bf16[2,2,4,2,64,1024]{5,4,3,2,1,0:T(8,128)(2,1)}, bf16[2,2,4,2,64,384]{5,4,3,2,1,0:T(8,128)(2,1)}, bf16[2,2,128,2048]{3,2,1,0:T(8,128)(2,1)}, b...) custom-call(bf16[4,2,64,1024]{3,2,1,0:T(8,128)(2,1)} %pad_maximum_fusion.4.send_ref, ...), custom_call_target="tpu_custom_call" | custom-call | tf_op jit(solution)/shard_map/gather_all/pallas_call | solution.py:467
  166.6 1.0 copy.203.doc_ref
  167.6 4.5 fusion.80
  173.3 23.5 %fusion.78 = f32[8,128,8]{2,0,1:T(8,128)S(1)} fusion(f32[8,128,8]{2,0,1:T(8,128)S(1)} %copy.196), kind=kOutput, calls=%fused_computation.184 | output fusion | flops 1040384 | bytes 65536 | tf_op jit(solution)/shard_map/jit(cumsum)/reduce_window_sum | solution.py:868
  197.0 1.0 copy.201.cum_ref
  198.0 1.1 compare_select_fusion.dt_ref
  199.3 1.2 fusion.95
  200.5 1.2 copy.202.dt_t_ref
  201.7 2.2 multiply_convert_fusion.3
  203.9 7.7 %fusion.77 = (bf16[1024,1024]{1,0:T(8,128)(2,1)S(1)}, f32[1024,1024]{1,0:T(8,128)S(1)}) fusion(bf16[1024,2048]{1,0:T(8,128)(2,1)} %bitcast.203, bf16[2048,1024]{1,0:T(8,128)(2,1)} %bitcast.265), kind=kOutput, calls=%fused_computation.183 | convolution fusion | flops 4296015872 | bytes 14680064 | tf_op jit(solution)/shard_map/dot_general | solution.py:25
  213.3 3.4 multiply_convert_fusion.2
  216.7 6.3 %shard_map.229 = (f32[1024,512]{1,0:T(8,128)S(1)}, bf16[8,128,512]{2,1,0:T(8,128)(2,1)S(1)}) custom-call(bf16[1024,512]{1,0:T(8,128)(2,1)S(1)} %get-tuple-element.105.val_ref, bf16[1024,256]{1,0:T(8,128)(2,1)S(1)} %get-tuple-element.103.key_ref, f32[1024,8]{1,0:T(8,128)S(1)} %copy-done.4, f32[8,1024]{1,0:T(8,128)S(1)} %bitcast.184, f32[1024,8]{1,0:T(8,128)S(1)} %copy-done.6, ...), custom_call_target="tpu_custom_call" | custom-call | flops 536870912 | bytes 5242880 | tf_op jit(solution)/shard_map/pallas_call | solution.py:191
  223.1 4.6 multiply_reduce_fusion.3
  228.3 8.3 %cube_total.1 = f32[16,128]{1,0:T(8,128)} custom-call(f32[16,128]{1,0:T(8,128)} %reshape.667.part_ref), custom_call_target="tpu_custom_call" | custom-call | tf_op jit(solution)/shard_map/cube_total/pallas_call | solution.py:502
  237.4 6.8 %convolution_convert_fusion.2 = bf16[512,2048]{1,0:T(8,128)(2,1)} fusion(bf16[1024,2048]{1,0:T(8,128)(2,1)} %bitcast.206, f32[1024,512]{1,0:T(8,128)} %get-tuple-element.98, f32[1024]{0:T(1024)S(1)} %get-tuple-element.137, f32[512]{0:T(512)S(1)} %bitcast.225), kind=kOutput, calls=%fused_computation.6 | convolution fusion | flops 2150105088 | bytes 8394752 | tf_op jit(solution)/shard_map/dot_general | solution.py:25
  244.2 3.0 multiply_convert_fusion
  247.3 4.4 convolution_convert_fusion
  251.7 14.9 %shard_map.230 = (f32[1024,512]{1,0:T(8,128)S(1)}, f32[1024,256]{1,0:T(8,128)S(1)}, f32[1024,8]{1,0:T(8,128)S(1)}, f32[8,1024]{1,0:T(8,128)S(1)}, f32[1024,8]{1,0:T(8,128)S(1)}, /*index=5*/f32[1,512]{1,0:T(1,128)S(1)}) custom-call(bf16[1024,512]{1,0:T(8,128)(2,1)S(1)} %get-tuple-element.105.val_ref, bf16[1024,256]{1,0:T(8,128)(2,1)S(1)} %copy-done.9, ...), custom_call_target="tpu_custom_call" | custom-call | flops 1610612736 | bytes 7340032 | tf_op jit(solution)/shard_map/pallas_call | solution.py:219
  267.2 1.0 copy-done.16
  268.2 2.3 fusion.63
  272.2 1.9 fusion.79
  274.0 1.2 copy.215
  275.3 1.2 copy.209
  276.5 1.4 fusion.65
  281.4 3.4 fusion.20
  284.8 1.4 slice.347
  286.9 1.8 copy-done.42
  288.7 3.6 convolution_convert_fusion.3
  292.3 3.6 fusion.5
  296.1 2.0 slice.344
  298.6 1.3 copy-done.25
  300.2 1.1 add_convert_fusion
  301.3 1.0 copy-done.43
  302.7 6.5 %convolution_convert_fusion.1 = bf16[2048,1024]{1,0:T(8,128)(2,1)} fusion(bf16[1024,2048]{1,0:T(8,128)(2,1)S(1)} %bitcast.205, bf16[1024,512]{1,0:T(8,128)(2,1)S(1)} %add_convert_fusion, bf16[1024,512]{1,0:T(8,128)(2,1)S(1)} %copy-done.53), kind=kOutput, calls=%fused_computation.3 | convolution fusion | flops 4301258752 | bytes 10485760 | tf_op jit(solution)/shard_map/dot_general | solution.py:25
  309.2 4.6 fusion.14
  313.8 4.5 multiply_reduce_fusion
  319.2 138.0 %scatter_all.1 = (f32[128,2048]{1,0:T(8,128)}, f32[128,2048]{1,0:T(8,128)}, bf16[4,2,64,1024]{3,2,1,0:T(8,128)(2,1)}, f32[128,2048]{1,0:T(8,128)}, f32[64,384]{1,0:T(8,128)}, /*index=5*/f32[224,128]{1,0:T(8,128)}) custom-call(bf16[2,4,128,2048]{3,2,1,0:T(8,128)(2,1)} %bitcast.197, bf16[2,4,128,2048]{3,2,1,0:T(8,128)(2,1)} %bitcast.192, ...), custom_call_target="tpu_custom_call" | custom-call | tf_op jit(solution)/shard_map/scatter_all/pallas_call | solution.py:711
  457.2 2.2 fusion.32
  463.2 1.5 copy.219
  465.2 1.0 copy.220
  466.2 1.6 copy.221
  467.8 1.3 convert_add_fusion
  470.9 1.8 reshape.691
  475.0 1.5 pad_maximum_fusion
  (279 shorter events, 40.7 us)
Async XLA Ops:
  3.9 12.4 %copy-start.59 = (s32[8,128]{1,0:T(8,128)}, s32[8,128]{1,0:T(8,128)S(1)}, u32[]{:S(2)}) copy-start(s32[8,128]{1,0:T(8,128)S(1)} %scatter.9.meta_ref) | copy-start | bytes 12292
  7.5 165.1 %copy-start.62 = (f32[8]{0:T(128)}, f32[8]{0:T(128)S(1)}, u32[]{:S(2)}) copy-start(f32[8]{0:T(128)S(1)} %exp.45) | copy-start | bytes 100
  11.5 4.8 %copy-start.57 = (f32[1,4352]{1,0:T(1,128)}, f32[1,4352]{1,0:T(1,128)S(1)}, u32[]{:S(2)}) copy-start(f32[1,4352]{1,0:T(1,128)S(1)} %broadcast_in_dim.34) | copy-start | bytes 52228
  172.5 29.2 %copy-start.13 = (bf16[1024,384]{1,0:T(8,128)(2,1)}, bf16[1024,384]{1,0:T(8,128)(2,1)S(1)}, u32[]{:S(2)}) copy-start(bf16[1024,384]{1,0:T(8,128)(2,1)S(1)} %copy.194) | copy-start | bytes 2359300
  172.6 26.5 %copy-start.54 = (f32[1024,4,2,2,4]{0,4,3,2,1:T(4,128)}, f32[1024,4,2,2,4]{0,4,3,2,1:T(4,128)S(1)}, u32[]{:S(2)}) copy-start(f32[1024,4,2,2,4]{0,4,3,2,1:T(4,128)S(1)} %reshape.644) | copy-start | bytes 786436
  173.0 26.3 %copy-start.29 = (f32[1024,8]{1,0:T(8,128)}, f32[1024,8]{1,0:T(8,128)S(1)}, u32[]{:S(2)}) copy-start(f32[1024,8]{1,0:T(8,128)S(1)} %copy.198) | copy-start | bytes 98308
  199.2 4.7 copy-start.33
  199.2 4.7 copy-start.35
  199.3 4.6 copy-start.37
  203.9 12.8 %copy-start.8 = (bf16[1024,256]{1,0:T(8,128)(2,1)}, bf16[1024,256]{1,0:T(8,128)(2,1)S(1)}, u32[]{:S(2)}) copy-start(bf16[1024,256]{1,0:T(8,128)(2,1)S(1)} %get-tuple-element.103.key_ref) | copy-start | bytes 1572868
  211.6 11.4 %copy-start.45 = (f32[1024,1024]{1,0:T(8,128)}, f32[1024,1024]{1,0:T(8,128)S(1)}, u32[]{:S(2)}) copy-start(f32[1024,1024]{1,0:T(8,128)S(1)} %get-tuple-element.144) | copy-start | bytes 12582916
  211.9 4.8 %copy-start.21 = (bf16[1022,512]{1,0:T(8,128)(2,1)}, bf16[1022,512]{1,0:T(8,128)(2,1)S(1)}, u32[]{:S(2)}) copy-start(bf16[1022,512]{1,0:T(8,128)(2,1)S(1)} %slice.334) | copy-start | bytes 3139588
  213.2 3.4 copy-start.23
  213.3 3.4 copy-start
  213.3 3.4 copy-start.2
  213.3 3.4 copy-start.4
  213.3 3.4 copy-start.6
  213.3 9.8 %copy-start.44 = (bf16[2,4,128,2048]{3,2,1,0:T(8,128)(2,1)S(1)}, bf16[2,4,128,2048]{3,2,1,0:T(8,128)(2,1)}, u32[]{:S(2)}) copy-start(bf16[2,4,128,2048]{3,2,1,0:T(8,128)(2,1)} %get-tuple-element.61) | copy-start | bytes 12582916
  216.7 6.4 %copy-start.47 = (bf16[2,2,128,2048]{3,2,1,0:T(8,128)(2,1)S(1)}, bf16[2,2,128,2048]{3,2,1,0:T(8,128)(2,1)}, u32[]{:S(2)}) copy-start(bf16[2,2,128,2048]{3,2,1,0:T(8,128)(2,1)} %get-tuple-element.62) | copy-start | bytes 6291460
  223.0 4.7 copy-start.10
  237.4 6.8 %copy-start.31 = (f32[1024,512]{1,0:T(8,128)S(1)}, f32[1024,512]{1,0:T(8,128)}, u32[]{:S(2)}) copy-start(f32[1024,512]{1,0:T(8,128)} %get-tuple-element.98) | copy-start | bytes 6291460
  237.4 6.8 %copy-start.32 = (f32[1024,512]{1,0:T(8,128)S(1)}, f32[1024,512]{1,0:T(8,128)}, u32[]{:S(2)}) copy-start(f32[1024,512]{1,0:T(8,128)} %get-tuple-element.145) | copy-start | bytes 6291460
  237.4 6.8 %copy-start.46 = (f32[1024,1024]{1,0:T(8,128)S(1)}, f32[1024,1024]{1,0:T(8,128)}, u32[]{:S(2)}) copy-start(f32[1024,1024]{1,0:T(8,128)} %copy-done.45) | copy-start | bytes 12582916
  244.2 3.0 copy-start.48
  247.2 4.4 copy-start.1
  247.2 4.4 copy-start.3
  247.2 4.4 copy-start.5
  247.3 4.4 copy-start.7
  247.3 4.4 copy-start.9
  247.3 4.4 copy-start.11
  251.7 15.0 %copy-start.14 = (bf16[1024,384]{1,0:T(8,128)(2,1)S(1)}, bf16[1024,384]{1,0:T(8,128)(2,1)}, u32[]{:S(2)}) copy-start(bf16[1024,384]{1,0:T(8,128)(2,1)} %copy-done.13) | copy-start | bytes 2359300
  251.7 15.0 %copy-start.39 = (f32[1024,256]{1,0:T(8,128)S(1)}, f32[1024,256]{1,0:T(8,128)}, u32[]{:S(2)}) copy-start(f32[1024,256]{1,0:T(8,128)} %get-tuple-element.104) | copy-start | bytes 3145732
  251.7 15.5 %copy-start.27 = (f32[1024,512]{1,0:T(8,128)S(1)}, f32[1024,512]{1,0:T(8,128)}, u32[]{:S(2)}) copy-start(f32[1024,512]{1,0:T(8,128)} %get-tuple-element.106) | copy-start | bytes 6291460
  270.6 6.0 %copy-start.30 = (f32[1024,8]{1,0:T(8,128)S(1)}, f32[1024,8]{1,0:T(8,128)}, u32[]{:S(2)}) copy-start(f32[1024,8]{1,0:T(8,128)} %copy-done.29) | copy-start | bytes 98308
  275.3 6.1 %copy-start.34 = (bf16[1023,256]{1,0:T(8,128)(2,1)S(1)}, bf16[1023,256]{1,0:T(8,128)(2,1)}, u32[]{:S(2)}) copy-start(bf16[1023,256]{1,0:T(8,128)(2,1)} %copy-done.33) | copy-start | bytes 1571332
  275.3 6.1 %copy-start.36 = (bf16[1022,256]{1,0:T(8,128)(2,1)S(1)}, bf16[1022,256]{1,0:T(8,128)(2,1)}, u32[]{:S(2)}) copy-start(bf16[1022,256]{1,0:T(8,128)(2,1)} %copy-done.35) | copy-start | bytes 1569796
  288.7 3.6 copy-start.12
  288.7 3.6 copy-start.20
  288.7 3.6 copy-start.22
  288.7 3.6 copy-start.24
  302.7 6.5 %copy-start.65 = (bf16[2,2,4,2,64,1024]{5,4,3,2,1,0:T(8,128)(2,1)S(1)}, bf16[2,2,4,2,64,1024]{5,4,3,2,1,0:T(8,128)(2,1)}, u32[]{:S(2)}) copy-start(bf16[2,2,4,2,64,1024]{5,4,3,2,1,0:T(8,128)(2,1)} %get-tuple-element.57) | copy-start | bytes 12582916
  309.2 4.6 copy-start.50
  313.8 4.7 copy-start.58
  313.8 4.7 copy-start.60
  313.8 4.7 copy-start.61
  319.2 138.0 %copy-start.28 = (bf16[1,128,2048]{2,1,0:T(8,128)(2,1)S(1)}, bf16[1,128,2048]{2,1,0:T(8,128)(2,1)}, u32[]{:S(2)}) copy-start(bf16[1,128,2048]{2,1,0:T(8,128)(2,1)} %param.18) | copy-start | bytes 1572868
  457.2 5.4 %copy-start.56 = (f32[64,384]{1,0:T(8,128)S(1)}, f32[64,384]{1,0:T(8,128)}, u32[]{:S(2)}) copy-start(f32[64,384]{1,0:T(8,128)} %get-tuple-element.74) | copy-start | bytes 294916
  457.2 7.6 %copy-start.18 = (f32[1,128,2048]{1,2,0:T(8,128)S(1)}, f32[1,128,2048]{1,2,0:T(8,128)}, u32[]{:S(2)}) copy-start(f32[1,128,2048]{1,2,0:T(8,128)} %copy-done.17) | copy-start | bytes 3145732
  (19 other events, 34.6 us)

commit v3 on v2

--- a/solution.py
+++ b/solution.py
@@ -274,6 +274,16 @@
     def at(self, s=0, zl=0, zh=0, c=0):
         return (flip(self.s, s), (flip(self.zh, zh) * self.near + flip(self.zl, zl)) * 2 + flip(self.c, c))
 
+    def column_runs(self, s, zl, width):
+        outer = self.far if self.near > 1 else 1
+        run = width // (2 * outer)
+        runs = []
+        for part in range(2):
+            for i in range(outer):
+                first = part * E + ((s * outer + i) * self.near + zl) * run
+                runs.append((pl.ds(pl.multiple_of(first, 128), run), pl.ds((part * outer + i) * run, run)))
+        return runs
+
     def partners(self):
         cube = [self.at(s=o // self.near, zl=o % self.near) for o in range(1, self.peers * self.near)]
         return cube, [self.at(zh=o) for o in range(1, self.far)], [self.at(c=1)]
@@ -326,6 +336,11 @@
         paths = alive
 
 
+def turn(paths):
+    for path in paths:
+        next(path, None)
+
+
 def bits_of(peers):
     return [1 << i for i in range(peers.bit_length() - 1)]
 
@@ -338,7 +353,7 @@
 
 
 def gather_kernel(
-    send_ref, key_ref, out_ref, rows_ref, cot_ref, meta_ref,
+    in_ref, key_ref, out_ref, rows_ref, cot_ref, meta_ref,
     w_ref, k_ref, o_ref, x_ref, ct_ref, m_ref, send, recv, local,
 ):
     me = Place()
@@ -348,20 +363,26 @@
     mover = Mover(send, recv, local)
     bits = bits_of(me.peers)
 
-    def rows_path(src, dst, order):
-        own = mover.keep(src, dst.at[zl, s])
-        near = [mover.put(src, dst.at[zl, s], me.at(zl=o)) for o in range(1, me.near)]
-        yield
-        own.wait()
-        for copy in near:
+    def plane_path(src, dst, order, near):
+        view = dst.at[flip(zl, near)]
+        if near:
+            copy = mover.put(src, dst.at[zl, s], me.at(zl=near))
+            yield
             copy.wait_recv()
+        else:
+            own = mover.keep(src, view.at[s])
         held = [0]
         for bit in order:
-            copies = [mover.put(dst.at[:, flip(s, h)], dst.at[:, flip(s, h)], me.at(s=bit)) for h in held]
+            copies = []
+            for h in held:
+                at = view.at[flip(s, h)]
+                copies.append(mover.put(at if near or h else src, at if near else dst.at[zl, flip(s, h)], me.at(s=bit)))
             held = held + [h ^ bit for h in held]
             yield
             for copy in copies:
                 copy.wait_recv()
+        if not near:
+            own.wait()
 
     def meta_path():
         own = mover.keep(meta_ref, m_ref.at[zl])
@@ -372,25 +393,30 @@
             copy.wait_recv()
 
     def key_path():
-        own = mover.keep(key_ref, k_ref.at[zh, c, s, zl])
-        copies = [mover.put(key_ref, k_ref.at[zh, c, s, zl], me.at(zh=o)) for o in range(1, me.far)]
+        block = k_ref.at[s, zh, zl, c]
+        own = mover.keep(key_ref, block)
+        copies = [mover.put(key_ref, block, me.at(zh=o)) for o in range(1, me.far)]
         yield
         own.wait()
         for copy in copies:
             copy.wait_recv()
-        block = k_ref.at[:, c, s, zl]
+        block = k_ref.at[s, :, zl, c]
         copies = [mover.put(block, block, me.at(zl=o)) for o in range(1, me.near)]
         yield
         for copy in copies:
             copy.wait_recv()
         held = [0]
         for bit in bits:
-            copies = [mover.put(k_ref.at[:, c, flip(s, h)], k_ref.at[:, c, flip(s, h)], me.at(s=bit)) for h in held]
+            copies = []
+            for h in held:
+                block = k_ref.at[flip(s, h), :, :, c]
+                copies.append(mover.put(block, block, me.at(s=bit)))
             held = held + [h ^ bit for h in held]
             yield
             for copy in copies:
                 copy.wait_recv()
-        copy = mover.put(k_ref.at[:, c], k_ref.at[:, c], me.at(c=1))
+        block = k_ref.at[:, :, :, c]
+        copy = mover.put(block, block, me.at(c=1))
         yield
         copy.wait_recv()
 
@@ -412,42 +438,49 @@
         for copy in last + [first]:
             copy.wait_recv()
 
-    weights = {}
-
     def weight_path():
+        moves = {}
         for step in range(me.peers):
             for o in range(me.near):
-                if step or o:
-                    weights[step, o] = mover.put(
-                        send_ref.at[flip(s, step), flip(zl, o)], w_ref.at[zh, c, s, zl], me.at(s=step, zl=o)
-                    )
-                else:
-                    weights[step, o] = mover.keep(send_ref.at[s, zl], w_ref.at[zh, c, s, zl])
+                to_s, to_zl = flip(s, step), flip(zl, o)
+                for src, dst in me.column_runs(to_s, to_zl, w_ref.shape[-1]):
+                    src = in_ref.at[:, src]
+                    dst = w_ref.at[s, zh, zl, c, :, dst]
+                    if step or o:
+                        copy = mover.put(src, dst, me.at(s=step, zl=o))
+                    else:
+                        copy = mover.keep(src, dst)
+                    moves.setdefault(step, []).append(copy)
         pieces = []
         for step in range(me.peers):
             yield
-            for o in range(me.near):
-                if step or o:
-                    weights[step, o].wait_recv()
+            for i, copy in enumerate(moves[step]):
+                if step == 0 and i < len(moves[0]) // me.near:
+                    copy.wait()
                 else:
-                    weights[step, o].wait()
-            block = w_ref.at[zh, c, flip(s, step)]
+                    copy.wait_recv()
+            block = w_ref.at[flip(s, step), zh, :, c]
             copies = [(o, mover.put(block, block, me.at(zh=o))) for o in range(1, me.far)]
             pieces.append((step, copies, mover.put(block, block, me.at(c=1))))
         last = []
         for step, copies, first in pieces:
             last.append(first)
-            last += yield from spread_path(copies, lambda h, step=step: w_ref.at[h, c, flip(s, step)])
+            last += yield from spread_path(copies, lambda h, step=step: w_ref.at[flip(s, step), h, :, c])
         yield
         for copy in last:
             copy.wait_recv()
 
-    run_paths(
-        [
-            rows_path(rows_ref, x_ref, bits), rows_path(cot_ref, ct_ref, bits[::-1]), meta_path(), key_path(),
-            weight_path(), out_path(),
-        ]
-    )
+    own_x = plane_path(rows_ref, x_ref, bits, 0)
+    own_c = plane_path(cot_ref, ct_ref, bits[::-1], 0)
+    near_x = [plane_path(rows_ref, x_ref, bits, o) for o in range(1, me.near)]
+    near_c = [plane_path(cot_ref, ct_ref, bits[::-1], o) for o in range(1, me.near)]
+    near = near_x + near_c
+    keys, weights, outs = key_path(), weight_path(), out_path()
+    turn([own_x, own_c, weights] + near + [keys, outs])
+    extra = meta_path()
+    turn([extra, own_x, own_c] + [weights] * me.peers + [keys] + near + [keys])
+    turn([own_x, own_c] + near + [keys, outs, weights, keys, weights])
+    run_paths([weights, extra, keys, outs, own_x, own_c] + near)
     mover.close()
 
 
@@ -459,16 +492,19 @@
     return [pltpu.SemaphoreType.DMA((copies,)), pltpu.SemaphoreType.DMA((copies,)), pltpu.SemaphoreType.DMA((kept,))]
 
 
-def gather(send, keys, out_w, rows, cot, meta):
+def gather(in_w, keys, out_w, rows, cot, meta):
     me = Place()
     peers, near, far = me.peers, me.near, me.far
     shape = lambda lead, part: jax.ShapeDtypeStruct(lead + part, bf16)
-    copies = (peers * near - 1) + (peers + 1) * (2 * far - 1) + 3 * (near + peers - 2) + near - 1 + far
+    columns = 2 * E // (peers * near)
+    runs = 2 * (far if near > 1 else 1)
+    copies = runs * (peers * near - 1) + (peers + 1) * (2 * far - 1) + 2 * (near * peers - 1)
+    copies += 2 * near + peers + far - 3
     return pl.pallas_call(
         gather_kernel,
         out_shape=[
-            shape((far, 2, peers, near), send.shape[2:]),
-            shape((far, 2, peers, near), keys.shape),
+            shape((peers, far, near, 2), (in_w.shape[0], columns)),
+            shape((peers, far, near, 2), keys.shape),
             shape((far, 2), out_w.shape),
             shape((near, peers), rows.shape),
             shape((near, peers), cot.shape),
@@ -476,10 +512,10 @@
         ],
         in_specs=[HBM] * 6,
         out_specs=[HBM] * 6,
-        scratch_shapes=sems(copies, 8),
+        scratch_shapes=sems(copies, runs + 5),
         compiler_params=remote_params(0),
         name="gather_all",
-    )(send, keys, out_w, rows, cot, meta)
+    )(in_w, keys, out_w, rows, cot, meta)
 
 
 def total_kernel(part_ref, sum_ref, box, send, recv, local):
@@ -530,10 +566,10 @@
 
 
 def scatter_kernel(
-    bp_ref, gn_ref, gw_ref, go_ref, gk_ref, v_ref,
-    ob_ref, og_ref, ow_ref, oo_ref, ok_ref, ov_ref,
+    bp_ref, gn_ref, gw_ref, go_ref, gk_ref, v_ref, u_ref,
+    ob_ref, og_ref, ow_ref, oo_ref, ok_ref, ov_ref, ou_ref,
     b_own, b_box, b_near, n_own, n_box, n_near, w_own, w_box, w_far, o_own, o_box, o_far,
-    k_own, k_box, k_near, k_far, k_bits, v_box, send, recv, local,
+    k_own, k_box, k_near, k_far, k_bits, v_box, u_box, send, recv, local,
 ):
     me = Place()
     s, zl, zh, c = me.s, me.zl, me.zh, me.c
@@ -542,10 +578,15 @@
     mover = Mover(send, recv, local)
     bits = bits_of(me.peers)
 
-    def halve(own, box, order, first_src):
+    def rows_path(src, own, box, near_box, out, order, near, arrivals):
+        own, box = own.at[near], box.at[near]
+        at_zl = src.at[flip(zl, near)]
+        todo = combos(order[1:])
+        copies, loads = [], []
+        for j, o in enumerate(todo):
+            copies.append(mover.put(at_zl.at[flip(s, order[0] ^ o)], box.at[j], me.at(s=order[0])))
+            loads.append(mover.keep(at_zl.at[flip(s, o)], own.at[j]))
         base = 0
-        todo = combos(order[1:])
-        copies = [mover.put(first_src(flip(s, order[0] ^ o)), box.at[base + j], me.at(s=order[0])) for j, o in enumerate(todo)]
         for i, bit in enumerate(order):
             rest = order[i + 1 :]
             count = 1 << len(rest)
@@ -554,37 +595,31 @@
             for j in range(count):
                 yield
                 copies[j].wait_recv()
-                add_rows(own.at[offset + j], [own.at[offset + j], box.at[base + j]])
+                if i == 0:
+                    loads[j].wait()
+                if rest or near:
+                    add_rows(own.at[offset + j], [own.at[offset + j], box.at[base + j]])
                 if rest and j < count // 2:
                     coming.append(mover.put(own.at[offset + j], box.at[base + count + j], me.at(s=rest[0])))
+            copies = coming
+            last = base
             base += count
-            copies = coming
-
-    def rows_path(src, own, box, near_box, out, order):
-        loads = [mover.keep(src.at[:, flip(s, o)], own.at[j]) for j, o in enumerate(combos(order[1:]))]
-
-        def first_src(at):
-            return src.at[:, at]
-
-        path = halve(own, box, order, first_src)
-        next(path)
-        for load in loads:
-            load.wait()
-        yield
-        yield from path
-        last = own.shape[0] - 1
-        copies = [mover.put(own.at[last, flip(zl, o)], near_box.at[o - 1], me.at(zl=o)) for o in range(1, me.near)]
-        yield
-        for copy in copies:
-            copy.wait_recv()
-        add_rows(out, [own.at[last, zl]] + [near_box.at[o - 1] for o in range(1, me.near)])
+        end = (1 << (len(order) - 1)) - 1
+        if near:
+            arrivals.append(mover.put(own.at[end], near_box.at[near - 1], me.at(zl=near)))
+            yield
+        else:
+            yield
+            for _ in range(me.near - 1):
+                arrivals.pop(0).wait_recv()
+            add_rows(out, [own.at[end], box.at[last]] + [near_box.at[o - 1] for o in range(1, me.near)])
 
     def weight_path():
         order = [(o, k) for o in range(1, me.far) for k in range(me.peers)] + [(0, k) for k in range(me.peers)]
         loads, copies = {}, {}
         for o, k in order:
-            copies[o, k] = mover.put(gw_ref.at[flip(zh, o), 1 - c, flip(s, k)], w_box.at[o, k], me.at(c=1))
-            loads[o, k] = mover.keep(gw_ref.at[flip(zh, o), c, flip(s, k)], w_own.at[o, k])
+            copies[o, k] = mover.put(gw_ref.at[flip(s, k), flip(zh, o), :, 1 - c], w_box.at[o, k], me.at(c=1))
+            loads[o, k] = mover.keep(gw_ref.at[flip(s, k), flip(zh, o), :, c], w_own.at[o, k])
         far_copies = {}
         for o, k in order:
             yield
@@ -593,7 +628,7 @@
             if o:
                 add_rows(w_own.at[o, k], [w_own.at[o, k], w_box.at[o, k]])
                 far_copies[o, k] = mover.put(w_own.at[o, k], w_far.at[o - 1, k], me.at(zh=o))
-        ends = []
+        ends, kept = [], []
         for k in range(me.peers):
             yield
             for o in range(1, me.far):
@@ -601,12 +636,15 @@
             parts = [w_own.at[0, k], w_box.at[0, k]] + [w_far.at[o - 1, k] for o in range(1, me.far)]
             add_rows(w_own.at[0, k], parts)
             for o in range(me.near):
-                if k or o:
-                    ends.append(mover.put(w_own.at[0, k, flip(zl, o)], ow_ref.at[s, zl], me.at(s=k, zl=o)))
-                else:
-                    own = mover.keep(w_own.at[0, 0, zl], ow_ref.at[s, zl])
+                for whole, mine in me.column_runs(s, zl, w_own.shape[-1]):
+                    src = w_own.at[0, k, flip(zl, o), :, mine]
+                    if k or o:
+                        ends.append(mover.put(src, ow_ref.at[:, whole], me.at(s=k, zl=o)))
+                    else:
+                        kept.append(mover.keep(src, ow_ref.at[:, whole]))
         yield
-        own.wait()
+        for copy in kept:
+            copy.wait()
         for copy in ends:
             copy.wait_recv()
 
@@ -616,8 +654,7 @@
         for o in order:
             copies[o] = mover.put(go_ref.at[flip(zh, o), 1 - c], o_box.at[o], me.at(c=1))
             loads[o] = mover.keep(go_ref.at[flip(zh, o), c], o_own.at[o])
-        for _ in range(me.far * me.peers):
-            yield
+        yield
         far_copies = {}
         for o in order:
             loads[o].wait()
@@ -625,7 +662,7 @@
             if o:
                 add_rows(o_own.at[o], [o_own.at[o], o_box.at[o]])
                 far_copies[o] = mover.put(o_own.at[o], o_far.at[o - 1], me.at(zh=o))
-        for _ in range(me.peers):
+        for _ in range(2 * me.peers + 4):
             yield
         for o in range(1, me.far):
             far_copies[o].wait_recv()
@@ -635,8 +672,8 @@
         blocks = combos(bits)
         copies, loads = [], []
         for j, o in enumerate(blocks):
-            copies.append(mover.put(gk_ref.at[:, 1 - c, flip(s, o)], k_box.at[j], me.at(c=1)))
-            loads.append(mover.keep(gk_ref.at[:, c, flip(s, o)], k_own.at[j]))
+            copies.append(mover.put(gk_ref.at[flip(s, o), :, :, 1 - c], k_box.at[j], me.at(c=1)))
+            loads.append(mover.keep(gk_ref.at[flip(s, o), :, :, c], k_own.at[j]))
         half = me.peers // 2
         sent = []
         for j in range(me.peers):
@@ -674,65 +711,76 @@
     def small_path():
         turns = [me.at(c=1)] + [me.at(zl=o) for o in bits_of(me.near)]
         turns += [me.at(s=o) for o in bits] + [me.at(zh=o) for o in bits_of(me.far)]
-        rows = v_ref.shape[0]
-        v_box[0] = v_ref[...]
+        pairs = [(v_ref, v_box, ov_ref), (u_ref, u_box, ou_ref)]
+        for src, box, _ in pairs:
+            box[0] = src[...]
         for i, device in enumerate(turns):
-            copy = mover.put(v_box.at[2 * i], v_box.at[2 * i + 1], device)
-            yield
-            copy.wait_recv()
-            v_box[2 * i + 2] = v_box[2 * i] + v_box[2 * i + 1]
-        ov_ref[...] = v_box[2 * len(turns)]
-
-    run_paths(
-        [
-            weight_path(),
-            rows_path(gn_ref, n_own, n_box, n_near, og_ref, bits[::-1]),
-            rows_path(bp_ref, b_own, b_box, b_near, ob_ref, bits),
-            key_path(),
-            small_path(),
-            out_path(),
-        ]
-    )
+            copies = [mover.put(box.at[2 * i], box.at[2 * i + 1], device) for _, box, _ in pairs]
+            yield
+            for copy, (_, box, _) in zip(copies, pairs):
+                copy.wait_recv()
+                box[2 * i + 2] = box[2 * i] + box[2 * i + 1]
+        for _, box, out in pairs:
+            out[...] = box[2 * len(turns)]
+
+    arrivals_n, arrivals_b = [], []
+    orders = (bits[::-1], bits)
+    grads = (gn_ref, n_own, n_box, n_near, og_ref, orders[0])
+    branch = (bp_ref, b_own, b_box, b_near, ob_ref, orders[1])
+    near_n = [rows_path(*grads, o, arrivals_n) for o in range(1, me.near)]
+    near_b = [rows_path(*branch, o, arrivals_b) for o in range(1, me.near)]
+    own_n, own_b = rows_path(*grads, 0, arrivals_n), rows_path(*branch, 0, arrivals_b)
+    near, own = near_n + near_b, [own_n, own_b]
+    weights, keys, small, outs = weight_path(), key_path(), small_path(), out_path()
+    turn([weights] + near + own + [keys, small, outs])
+    turn([weights] * (me.far * me.peers) + [outs, keys] * me.peers)
+    run_paths(near + [keys, small] + own + [weights, outs])
     mover.close()
 
 
-def scatter(branch, grads, gw, go, gk, small):
+def scatter(branch, grads, gw, go, gk, small, conv):
     me = Place()
     peers, near, far = me.peers, me.near, me.far
     tokens, width = branch.shape[2:]
     stages = len(bits_of(peers)) + len(bits_of(near)) + len(bits_of(far)) + 1
     vm = lambda *shape: pltpu.VMEM(shape, bf16)
-    rows_scratch = [vm(peers // 2, near, tokens, width), vm(peers - 1, near, tokens, width), vm(max(near - 1, 1), tokens, width)]
-    block = gw.shape[3:]
-    kblock = gk.shape[3:]
+    boxes = lambda part: pltpu.VMEM((2 * stages + 1,) + part.shape, f32)
+    rows_scratch = [
+        vm(near, peers // 2, tokens, width), vm(near, peers - 1, tokens, width), vm(max(near - 1, 1), tokens, width)
+    ]
+    block = gw.shape[2:3] + gw.shape[4:]
+    kblock = gk.shape[2:3] + gk.shape[4:]
     oblock = go.shape[2:]
-    copies = 2 * (peers + near - 2) + 2 * far * peers + peers * (near - 1) + peers - 1 + 3 * far + 2 * peers + near - 4 + stages
-    kept = peers + far * peers + 1 + far + peers + 4
+    runs = 2 * (far if near > 1 else 1)
+    copies = 2 * (peers * near - 1) + (2 * far - 1) * peers + runs * (peers * near - 1) + 2 * far - 1
+    copies += 2 * peers - 1 + near - 1 + far - 1 + 2 * stages
+    kept = peers * near + far * peers + runs + far + peers
+    same = lambda part: jax.ShapeDtypeStruct(part.shape, part.dtype)
     return pl.pallas_call(
         scatter_kernel,
         out_shape=[
             jax.ShapeDtypeStruct((tokens, width), f32),
             jax.ShapeDtypeStruct((tokens, width), f32),
-            jax.ShapeDtypeStruct((peers,) + block, bf16),
+            jax.ShapeDtypeStruct((block[1], 2 * E), bf16),
             jax.ShapeDtypeStruct(oblock, f32),
             jax.ShapeDtypeStruct(kblock[1:], f32),
-            jax.ShapeDtypeStruct(small.shape, f32),
+            same(small),
+            same(conv),
         ],
-        in_specs=[HBM] * 5 + [VMEM],
-        out_specs=[VMEM, VMEM, HBM, VMEM, VMEM, VMEM],
+        in_specs=[HBM] * 5 + [VMEM] * 2,
+        out_specs=[VMEM, VMEM, HBM, VMEM, VMEM, VMEM, VMEM],
         scratch_shapes=rows_scratch
         + rows_scratch
         + [vm(far, peers, *block), vm(far, peers, *block), vm(max(far - 1, 1), peers, *block)]
         + [vm(far, *oblock), vm(far, *oblock), vm(max(far - 1, 1), *oblock)]
         + [
             vm(peers, far, *kblock), vm(peers, far, *kblock), vm(max(near - 1, 1), far, *kblock[1:]),
-            vm(max(far - 1, 1), *kblock[1:]), vm(peers - 1, far, *kblock),
-            pltpu.VMEM((2 * stages + 1,) + small.shape, f32),
+            vm(max(far - 1, 1), *kblock[1:]), vm(peers - 1, far, *kblock), boxes(small), boxes(conv),
         ]
         + sems(copies, kept),
         compiler_params=remote_params(2),
         name="scatter_all",
-    )(branch, grads, gw, go, gk, small)
+    )(branch, grads, gw, go, gk, small, conv)
 
 
 def doc_index(places, doc_ends):
@@ -784,14 +832,6 @@
     seq_rows = inputs[0].astype(f32)
     cot_rows = cotangent[0]
 
-    def per_group(part):
-        lead = part.shape[0]
-        return part.reshape(lead, peers, outer, near, -1).transpose(1, 3, 0, 2, 4).reshape(peers, near, lead, -1)
-
-    def whole_again(part):
-        lead = part.shape[2]
-        return part.reshape(peers, near, lead, outer, -1).transpose(2, 0, 3, 1, 4).reshape(lead, -1)
-
     def own(vector):
         part = vector.reshape(-1, peers, outer, near, vector.shape[-1] // (peers * outer * near))
         part = lax.dynamic_index_in_dim(part, me.s, 1, False)
@@ -804,23 +844,14 @@
         full = jnp.zeros((part.shape[0], peers, outer, near, part.shape[-1]), part.dtype)
         return lax.dynamic_update_slice(full, part, (0, me.s, 0, me.zl, 0)).reshape(lead + (-1,))
 
-    def to_gathered(part):
-        part = part.reshape(part.shape[0], peers, far, near, 2, rows)
-        return part.transpose(0, 2, 4, 1, 3, 5).reshape(part.shape[0], width)
-
-    def from_gathered(part):
-        part = part.reshape(part.shape[0], far, 2, peers, near, rows)
-        return part.transpose(0, 3, 1, 4, 2, 5).reshape(part.shape[0], width)
-
-    send = jnp.concatenate([per_group(in_weight[:, :E]), per_group(in_weight[:, E : 2 * E])], axis=-1)
     key_send = jnp.concatenate(
         [in_weight[:, 2 * E :], step_weight, jnp.zeros((rows, STEP_PAD - H), bf16)], axis=1
     )
     inv_rms = lax.rsqrt(jnp.mean(seq_rows * seq_rows, axis=1, keepdims=True) + epsilon)
-    normed = to_gathered((seq_rows * inv_rms * pre_gain[None, :]).astype(bf16))
+    normed = (seq_rows * inv_rms * pre_gain[None, :]).astype(bf16)
     meta = jnp.zeros((8, 128), jnp.int32)
     meta = meta.at[0, :DOCS].set(doc_lengths[0]).at[1, 0].set(head_width[0])
-    in_w, key_w, out_w, normed, cot_all, meta = gather(send, key_send, out_weight, normed, cot_rows, meta)
+    in_w, key_w, out_w, normed, cot_all, meta = gather(in_weight, key_send, out_weight, normed, cot_rows, meta)
     in_w = in_w.reshape(width, 2 * inner)
     key_w = key_w.reshape(width, -1)
     out_w = out_w.reshape(inner, width)
@@ -903,52 +934,40 @@
     grad_in = mm(normed, grad_cols, TN).astype(bf16)
     grad_keys = mm(normed, key_cols, TN).astype(bf16)
     grad_normed = mm(grad_cols, in_w, NT) + mm(key_cols, key_w, NT)
-    grad_pre_gain = from_gathered(jnp.sum(grad_normed * normed.astype(f32), axis=0)[None])[0] / pre_gain
+    grad_pre_gain = jnp.sum(grad_normed * normed.astype(f32), axis=0) / pre_gain
 
     small = jnp.concatenate(
-        [
-            grad_pre_gain,
-            jnp.concatenate([spread(sums_v), sums_k], axis=1).reshape(-1),
-            spread(grad_step_bias),
-            spread(grad_decay_log),
-            spread(grad_skip),
-            spread(grad_norm_gain),
-        ]
+        [grad_pre_gain, spread(grad_norm_gain), spread(grad_step_bias), spread(grad_decay_log), spread(grad_skip)]
     )
-    count = small.shape[0]
-    padded = -count % 1024
-    small = jnp.pad(small, (0, padded)).reshape(-1, 128)
+    small = jnp.pad(small, (0, -small.shape[0] % 1024)).reshape(-1, 128)
+    conv_sums = jnp.concatenate([spread(sums_v), sums_k], axis=1)
+    conv_sums = jnp.pad(conv_sums, ((0, 8 - conv_sums.shape[0]), (0, 0)))
     rows_of = lambda part: part.reshape(near, peers, tokens, width)
-    blocks = (far, 2, peers, near, rows)
-    branch, grad_normed, grad_in, grad_out_weight, grad_keys, small = scatter(
+    blocks = (peers, far, near, 2, rows)
+    branch, grad_normed, grad_in, grad_out_weight, grad_keys, small, conv_sums = scatter(
         rows_of(branch),
         rows_of(grad_normed.astype(bf16)),
         grad_in.reshape(blocks + (2 * inner,)),
         grad_out.reshape(far, 2, -1, width),
         grad_keys.reshape(blocks + (KEYS + STEP_PAD,)),
         small,
+        conv_sums,
     )
     output = (seq_rows + branch).astype(bf16)[None]
-    grad_normed = from_gathered(grad_normed)
     scaled_in = grad_normed * pre_gain[None, :]
     dot = jnp.mean(scaled_in * seq_rows, axis=1, keepdims=True)
     grad_seq = inv_rms * scaled_in - seq_rows * (inv_rms * inv_rms * inv_rms * dot)
     grad_inputs = (grad_seq + cot_rows.astype(f32))[None]
-    grad_in = grad_in.astype(f32)
-    grad_in_weight = jnp.concatenate(
-        [whole_again(grad_in[..., :inner]), whole_again(grad_in[..., inner:]), grad_keys[:, :KEYS]], axis=1
-    )
+    grad_in_weight = jnp.concatenate([grad_in.astype(f32), grad_keys[:, :KEYS]], axis=1)
     grad_step_weight = grad_keys[:, KEYS : KEYS + H]
     small = small.reshape(-1)
-    sizes = [width, (CONV + 1) * conv_weight.shape[1], H, H, H, E]
     parts = []
-    for size in sizes:
+    for size in (width, E, H, H, H):
         parts.append(small[:size])
         small = small[size:]
-    conv_sums = parts[1].reshape(CONV + 1, -1)
     return (
         output, grad_inputs, parts[0], grad_in_weight, grad_step_weight, conv_sums[:CONV], conv_sums[CONV],
-        parts[2], parts[3], parts[4], parts[5], grad_out_weight,
+        parts[2], parts[3], parts[4], parts[1], grad_out_weight,
     )
 
 

time: 485 us -> 423 us (0.87)
  Pallas kernels: 309 us -> 267 us
  local copies, waits for them, and re-layouts: 55.4 us -> 37.2 us
    pallas_call x1, Pallas kernels: 142 us -> 102 us  [gather(): pl.pallas_call(gather_kernel, out_shape=[shape((peers, far, near, 2), (in...]
    pallas_call x1, Pallas kernels: 138 us -> 125 us  [scatter(): pl.pallas_call(scatter_kernel, out_shape=[jax.ShapeDtypeStruct((tokens, w...]
    pallas_call x1, Pallas kernels: 8.35 us -> 19.2 us  [cube_total(): pl.pallas_call(total_kernel, out_shape=jax.ShapeDtypeStruct(part.shape, f...]
    reshape x15 -> x1, local copies, waits for them, and re-layouts: 10.5 us -> 0.62 us  [body(): small = jnp.pad(small, (0, -small.shape[0] % 1024)).reshape(-1, 128)]
where the time goes in v3:
time: 423 us; the launch traced here: 418 us
  Pallas kernels  267 us (63%)
  other arithmetic  63.9 us (15%)
  matrix products  47.2 us (11%)
  local copies, waits for them, and re-layouts  37.2 us (9%)
    pallas_call x1, Pallas kernels, scatter(): pl.pallas_call(scatter_kernel, out_shape=[jax.ShapeDtypeStruct((tokens, w...  125 us
    pallas_call x1, Pallas kernels, gather(): pl.pallas_call(gather_kernel, out_shape=[shape((peers, far, near, 2), (in...  102 us
    dot_general x9, matrix products, mm(): return lax.dot_general(a, b, (dims, ((), ())), preferred_element_type=f32)  47.2 us
    another operation x1, other arithmetic, body(): jnp.cumsum(log_decay.reshape(-1, CHUNK, heads), axis=1)  23.5 us
    pallas_call x1, Pallas kernels, cube_total(): pl.pallas_call(total_kernel, out_shape=jax.ShapeDtypeStruct(part.shape, f...  19.2 us
    pallas_call x1, Pallas kernels, scan_backward(): pl.pallas_call(scan_backward_kernel, grid=(steps,), in_specs=[row(inner),...  14.9 us
    unnamed x127, local copies, waits for them, and re-layouts  8.6 us

profile of v3, /device:TPU:0, one launch (start us, length us, event | category | flops | bytes accessed | tf_op | source)
XLA Modules:
  0.0 417.9 jit_solution(2297526360977234766)
XLA Ops:
  1.3 1.2 fusion.26
  3.5 0.8 fusion.76
  11.1 1.3 maximum_maximum_fusion.key_ref
  12.4 0.9 pad_maximum_fusion.4
  13.4 2.0 fusion.28.rows_ref
  15.4 101.9 %gather_all.1 = (bf16[4,2,2,2,64,1024]{5,4,3,2,1,0:T(8,128)(2,1)}, bf16[4,2,2,2,64,384]{5,4,3,2,1,0:T(8,128)(2,1)}, bf16[2,2,128,2048]{3,2,1,0:T(8,128)(2,1)}, b...) custom-call(bf16[64,8448]{1,0:T(8,128)(2,1)} %in_ref.1, ...), custom_call_target="tpu_custom_call" | custom-call | tf_op jit(solution)/shard_map/gather_all/pallas_call | solution.py:503
  117.4 0.8 slice_reduce_fusion.1
  121.2 1.0 copy.123.doc_ref
  122.2 4.5 %fusion.81 = f32[1024,384]{0,1:T(8,128)S(1)} fusion(bf16[1024,2048]{1,0:T(8,128)(2,1)} %bitcast.168, bf16[2048,384]{1,0:T(8,128)(2,1)} %bitcast.178), kind=kOutput, calls=%fused_computation.185 | convolution fusion | flops 1610612736 | bytes 7340032 | tf_op jit(solution)/shard_map/dot_general | solution.py:25
  127.9 23.5 %fusion.79 = f32[8,128,8]{2,0,1:T(8,128)S(1)} fusion(f32[8,128,8]{2,0,1:T(8,128)S(1)} %copy.116), kind=kOutput, calls=%fused_computation.183 | output fusion | flops 1040384 | bytes 65536 | tf_op jit(solution)/shard_map/jit(cumsum)/reduce_window_sum | solution.py:899
  151.5 1.0 copy.121.cum_ref
  152.5 1.1 compare_select_fusion.dt_ref
  153.8 1.2 fusion.96
  155.0 1.2 copy.122.dt_t_ref
  156.2 2.2 multiply_convert_fusion.3
  158.4 7.7 %fusion.78 = (bf16[1024,1024]{1,0:T(8,128)(2,1)S(1)}, f32[1024,1024]{1,0:T(8,128)S(1)}) fusion(bf16[1024,2048]{1,0:T(8,128)(2,1)} %bitcast.169, bf16[2048,1024]{1,0:T(8,128)(2,1)} %bitcast.227), kind=kOutput, calls=%fused_computation.182 | convolution fusion | flops 4296015872 | bytes 14680064 | tf_op jit(solution)/shard_map/dot_general | solution.py:25
  166.5 1.0 copy-done.15
  167.8 3.4 multiply_convert_fusion.2
  171.3 6.3 %shard_map.229 = (f32[1024,512]{1,0:T(8,128)S(1)}, bf16[8,128,512]{2,1,0:T(8,128)(2,1)S(1)}) custom-call(bf16[1024,512]{1,0:T(8,128)(2,1)S(1)} %get-tuple-element.107.val_ref, bf16[1024,256]{1,0:T(8,128)(2,1)S(1)} %get-tuple-element.105.key_ref, f32[1024,8]{1,0:T(8,128)S(1)} %copy-done.4, f32[8,1024]{1,0:T(8,128)S(1)} %bitcast.157, f32[1024,8]{1,0:T(8,128)S(1)} %copy-done.6, ...), custom_call_target="tpu_custom_call" | custom-call | flops 536870912 | bytes 5242880 | tf_op jit(solution)/shard_map/pallas_call | solution.py:191
  177.6 4.6 %multiply_reduce_fusion.3 = (f32[1024]{0:T(1024)S(1)}, f32[1024]{0:T(1024)S(1)}, f32[1024,512]{1,0:T(8,128)}, f32[1024,512]{1,0:T(8,128)}) fusion(f32[512]{0:T(512)S(1)} %bitcast.186, f32[1024,1024]{1,0:T(8,128)S(1)} %get-tuple-element.144, f32[1024,512]{1,0:T(8,128)S(1)} %get-tuple-element.61, f32[2,512]{1,0:T(2,128)S(1)} %reshape.537, ...), kind=kOutput, calls=%fused_computation.41 | convolution fusion | flops 2153248768 | bytes 14694400 | tf_op jit(solution)/shard_map/dot_general | solution.py:25
  182.9 19.2 %cube_total.1 = f32[16,128]{1,0:T(8,128)} custom-call(f32[16,128]{1,0:T(8,128)} %reshape.542.part_ref), custom_call_target="tpu_custom_call" | custom-call | tf_op jit(solution)/shard_map/cube_total/pallas_call | solution.py:538
  202.8 6.8 %convolution_convert_fusion.2 = bf16[512,2048]{1,0:T(8,128)(2,1)} fusion(bf16[1024,2048]{1,0:T(8,128)(2,1)} %bitcast.172, f32[1024,512]{1,0:T(8,128)} %get-tuple-element.100, f32[1024]{0:T(1024)S(1)} %get-tuple-element.134, f32[512]{0:T(512)S(1)} %bitcast.187), kind=kOutput, calls=%fused_computation.6 | convolution fusion | flops 2150105088 | bytes 8394752 | tf_op jit(solution)/shard_map/dot_general | solution.py:25
  209.7 3.2 multiply_convert_fusion
  212.9 4.4 %convolution_convert_fusion = bf16[1024,2048]{1,0:T(8,128)(2,1)} fusion(bf16[512,2048]{1,0:T(8,128)(2,1)S(1)} %bitcast.176, f32[1024,512]{1,0:T(8,128)S(1)} %copy-done.28, f32[1024]{0:T(1024)S(1)} %get-tuple-element.134, f32[512]{0:T(512)S(1)} %bitcast.189), kind=kOutput, calls=%fused_computation.2 | convolution fusion | flops 2151153664 | bytes 8394752 | tf_op jit(solution)/shard_map/dot_general | solution.py:25
  217.4 14.9 %shard_map.230 = (f32[1024,512]{1,0:T(8,128)S(1)}, f32[1024,256]{1,0:T(8,128)S(1)}, f32[1024,8]{1,0:T(8,128)S(1)}, f32[8,1024]{1,0:T(8,128)S(1)}, f32[1024,8]{1,0:T(8,128)S(1)}, /*index=5*/f32[1,512]{1,0:T(1,128)S(1)}) custom-call(bf16[1024,512]{1,0:T(8,128)(2,1)S(1)} %get-tuple-element.107.val_ref, bf16[1024,256]{1,0:T(8,128)(2,1)S(1)} %copy-done.9, ...), custom_call_target="tpu_custom_call" | custom-call | flops 1610612736 | bytes 7340032 | tf_op jit(solution)/shard_map/pallas_call | solution.py:219
  232.8 1.0 copy-done.16
  233.9 2.3 fusion.66
  237.8 1.9 fusion.80
  239.7 1.2 copy.135
  240.9 1.2 copy.129
  242.4 1.0 fusion.44
  244.2 2.9 fusion.20
  247.1 1.4 slice.316
  249.2 1.8 copy-done.39
  251.0 3.6 convolution_convert_fusion.3
  254.6 3.6 fusion.5
  259.1 2.0 slice.313
  261.6 1.3 copy-done.23
  263.2 1.1 add_convert_fusion
  264.3 1.0 copy-done.40
  265.7 6.5 %convolution_convert_fusion.1 = bf16[2048,1024]{1,0:T(8,128)(2,1)} fusion(bf16[1024,2048]{1,0:T(8,128)(2,1)S(1)} %bitcast.171, bf16[1024,512]{1,0:T(8,128)(2,1)S(1)} %add_convert_fusion, bf16[1024,512]{1,0:T(8,128)(2,1)S(1)} %copy-done.50), kind=kOutput, calls=%fused_computation.3 | convolution fusion | flops 4301258752 | bytes 10485760 | tf_op jit(solution)/shard_map/dot_general | solution.py:25
  272.1 4.6 %fusion.14 = f32[1024,2048]{1,0:T(8,128)S(1)} fusion(bf16[2048,1024]{1,0:T(8,128)(2,1)S(1)} %bitcast.228, bf16[1024,512]{1,0:T(8,128)(2,1)S(1)} %add_convert_fusion, bf16[1024,512]{1,0:T(8,128)(2,1)S(1)} %copy-done.50), kind=kOutput, calls=%fused_computation.50 | convolution fusion | flops 4299161600 | bytes 14680064 | tf_op jit(solution)/shard_map/dot_general | solution.py:25
  276.7 4.4 %multiply_reduce_fusion = (f32[2048]{0:T(1024)S(1)}, bf16[1024,2048]{1,0:T(8,128)(2,1)}) fusion(bf16[2,4,128,2048]{3,2,1,0:T(8,128)(2,1)S(1)} %copy-done.40, f32[1024,2048]{1,0:T(8,128)S(1)} %fusion.14, bf16[2048,384]{1,0:T(8,128)(2,1)S(1)} %bitcast.179, bf16[1024,64]{1,0:T(8,128)(2,1)S(1)} %copy.132, bf16[1024,256]{1,0:T(8,128)(2,1)S(1)} %add_convert_fusion.1), kind=kOutput, calls=%fused_computation | convolution fusion | flops 1623455744 | bytes 19013632 | tf_op jit(solution)/shard_map/dot_general | solution.py:25
  281.9 124.9 %scatter_all.1 = (f32[128,2048]{1,0:T(8,128)}, f32[128,2048]{1,0:T(8,128)}, bf16[64,8192]{1,0:T(8,128)(2,1)}, f32[128,2048]{1,0:T(8,128)}, f32[64,384]{1,0:T(8,1...) custom-call(bf16[2,4,128,2048]{3,2,1,0:T(8,128)(2,1)} %bitcast.166, bf16[2,4,128,2048]{3,2,1,0:T(8,128)(2,1)} %bitcast.165, ...), custom_call_target="tpu_custom_call" | custom-call | tf_op jit(solution)/shard_map/scatter_all/pallas_call | solution.py:759
  406.8 1.5 fusion.30
  408.4 2.9 fusion.33
  415.1 1.5 pad_maximum_fusion
  416.7 1.0 copy.156
  (237 shorter events, 24.6 us)
Async XLA Ops:
  3.5 12.0 %copy-start.57 = (s32[8,128]{1,0:T(8,128)}, s32[8,128]{1,0:T(8,128)S(1)}, u32[]{:S(2)}) copy-start(s32[8,128]{1,0:T(8,128)S(1)} %scatter.9.meta_ref) | copy-start | bytes 12292
  10.3 107.0 %copy-start.54 = (f32[1,4352]{1,0:T(1,128)}, f32[1,4352]{1,0:T(1,128)S(1)}, u32[]{:S(2)}) copy-start(f32[1,4352]{1,0:T(1,128)S(1)} %broadcast_in_dim.36) | copy-start | bytes 52228
  127.1 29.1 %copy-start.13 = (bf16[1024,384]{1,0:T(8,128)(2,1)}, bf16[1024,384]{1,0:T(8,128)(2,1)S(1)}, u32[]{:S(2)}) copy-start(bf16[1024,384]{1,0:T(8,128)(2,1)S(1)} %copy.114) | copy-start | bytes 2359300
  127.2 26.4 %copy-start.51 = (f32[1024,4,2,2,4]{0,4,3,2,1:T(4,128)}, f32[1024,4,2,2,4]{0,4,3,2,1:T(4,128)S(1)}, u32[]{:S(2)}) copy-start(f32[1024,4,2,2,4]{0,4,3,2,1:T(4,128)S(1)} %reshape.519) | copy-start | bytes 786436
  127.6 26.2 %copy-start.26 = (f32[1024,8]{1,0:T(8,128)}, f32[1024,8]{1,0:T(8,128)S(1)}, u32[]{:S(2)}) copy-start(f32[1024,8]{1,0:T(8,128)S(1)} %copy.118) | copy-start | bytes 98308
  153.7 4.7 %copy-start.31 = (bf16[1023,256]{1,0:T(8,128)(2,1)}, bf16[1023,256]{1,0:T(8,128)(2,1)S(1)}, u32[]{:S(2)}) copy-start(bf16[1023,256]{1,0:T(8,128)(2,1)S(1)} %slice.309) | copy-start | bytes 1571332
  153.8 4.7 %copy-start.33 = (bf16[1022,256]{1,0:T(8,128)(2,1)}, bf16[1022,256]{1,0:T(8,128)(2,1)S(1)}, u32[]{:S(2)}) copy-start(bf16[1022,256]{1,0:T(8,128)(2,1)S(1)} %slice.308) | copy-start | bytes 1569796
  153.8 4.6 %copy-start.35 = (bf16[1021,256]{1,0:T(8,128)(2,1)}, bf16[1021,256]{1,0:T(8,128)(2,1)S(1)}, u32[]{:S(2)}) copy-start(bf16[1021,256]{1,0:T(8,128)(2,1)S(1)} %slice.307) | copy-start | bytes 1568260
  158.4 12.8 %copy-start.8 = (bf16[1024,256]{1,0:T(8,128)(2,1)}, bf16[1024,256]{1,0:T(8,128)(2,1)S(1)}, u32[]{:S(2)}) copy-start(bf16[1024,256]{1,0:T(8,128)(2,1)S(1)} %get-tuple-element.105.key_ref) | copy-start | bytes 1572868
  166.2 11.4 %copy-start.42 = (f32[1024,1024]{1,0:T(8,128)}, f32[1024,1024]{1,0:T(8,128)S(1)}, u32[]{:S(2)}) copy-start(f32[1024,1024]{1,0:T(8,128)S(1)} %get-tuple-element.144) | copy-start | bytes 12582916
  166.4 4.8 %copy-start.19 = (bf16[1022,512]{1,0:T(8,128)(2,1)}, bf16[1022,512]{1,0:T(8,128)(2,1)S(1)}, u32[]{:S(2)}) copy-start(bf16[1022,512]{1,0:T(8,128)(2,1)S(1)} %slice.303) | copy-start | bytes 3139588
  167.8 3.4 copy-start.21
  167.8 3.4 copy-start
  167.8 3.4 copy-start.2
  167.8 3.4 copy-start.4
  167.8 3.4 copy-start.6
  167.8 9.8 %copy-start.41 = (bf16[2,4,128,2048]{3,2,1,0:T(8,128)(2,1)S(1)}, bf16[2,4,128,2048]{3,2,1,0:T(8,128)(2,1)}, u32[]{:S(2)}) copy-start(bf16[2,4,128,2048]{3,2,1,0:T(8,128)(2,1)} %get-tuple-element.62) | copy-start | bytes 12582916
  171.2 6.4 %copy-start.44 = (bf16[2,2,128,2048]{3,2,1,0:T(8,128)(2,1)S(1)}, bf16[2,2,128,2048]{3,2,1,0:T(8,128)(2,1)}, u32[]{:S(2)}) copy-start(bf16[2,2,128,2048]{3,2,1,0:T(8,128)(2,1)} %get-tuple-element.63) | copy-start | bytes 6291460
  177.6 4.7 %copy-start.10 = (bf16[8,128,512]{2,1,0:T(8,128)(2,1)}, bf16[8,128,512]{2,1,0:T(8,128)(2,1)S(1)}, u32[]{:S(2)}) copy-start(bf16[8,128,512]{2,1,0:T(8,128)(2,1)S(1)} %get-tuple-element.64.state_ref) | copy-start | bytes 3145732
  202.8 6.9 %copy-start.28 = (f32[1024,512]{1,0:T(8,128)S(1)}, f32[1024,512]{1,0:T(8,128)}, u32[]{:S(2)}) copy-start(f32[1024,512]{1,0:T(8,128)} %get-tuple-element.100) | copy-start | bytes 6291460
  202.8 6.9 %copy-start.29 = (f32[1024,512]{1,0:T(8,128)S(1)}, f32[1024,512]{1,0:T(8,128)}, u32[]{:S(2)}) copy-start(f32[1024,512]{1,0:T(8,128)} %get-tuple-element.145) | copy-start | bytes 6291460
  202.8 6.8 %copy-start.43 = (f32[1024,1024]{1,0:T(8,128)S(1)}, f32[1024,1024]{1,0:T(8,128)}, u32[]{:S(2)}) copy-start(f32[1024,1024]{1,0:T(8,128)} %copy-done.42) | copy-start | bytes 12582916
  209.7 3.2 copy-start.45
  212.9 4.4 %copy-start.1 = (f32[1024,1]{1,0:T(8,128)S(1)}, f32[1024,1]{1,0:T(8,128)}, u32[]{:S(2)}) copy-start(f32[1024,1]{1,0:T(8,128)} %convert_element_type.150.flow_ref) | copy-start | bytes 12292
  212.9 4.4 %copy-start.3 = (s32[1024,1]{1,0:T(8,128)S(1)}, s32[1024,1]{1,0:T(8,128)}, u32[]{:S(2)}) copy-start(s32[1024,1]{1,0:T(8,128)} %copy.123.doc_ref) | copy-start | bytes 12292
  212.9 4.4 %copy-start.5 = (f32[1024,8]{1,0:T(8,128)S(1)}, f32[1024,8]{1,0:T(8,128)}, u32[]{:S(2)}) copy-start(f32[1024,8]{1,0:T(8,128)} %copy.121.cum_ref) | copy-start | bytes 98308
  212.9 4.4 %copy-start.7 = (f32[1024,8]{1,0:T(8,128)S(1)}, f32[1024,8]{1,0:T(8,128)}, u32[]{:S(2)}) copy-start(f32[1024,8]{1,0:T(8,128)} %compare_select_fusion.dt_ref) | copy-start | bytes 98308
  212.9 4.4 %copy-start.9 = (bf16[1024,256]{1,0:T(8,128)(2,1)S(1)}, bf16[1024,256]{1,0:T(8,128)(2,1)}, u32[]{:S(2)}) copy-start(bf16[1024,256]{1,0:T(8,128)(2,1)} %copy-done.8) | copy-start | bytes 1572868
  212.9 4.4 %copy-start.11 = (bf16[8,128,512]{2,1,0:T(8,128)(2,1)S(1)}, bf16[8,128,512]{2,1,0:T(8,128)(2,1)}, u32[]{:S(2)}) copy-start(bf16[8,128,512]{2,1,0:T(8,128)(2,1)} %copy-done.10) | copy-start | bytes 3145732
  217.3 15.0 %copy-start.14 = (bf16[1024,384]{1,0:T(8,128)(2,1)S(1)}, bf16[1024,384]{1,0:T(8,128)(2,1)}, u32[]{:S(2)}) copy-start(bf16[1024,384]{1,0:T(8,128)(2,1)} %copy-done.13) | copy-start | bytes 2359300
  217.3 15.0 %copy-start.37 = (f32[1024,256]{1,0:T(8,128)S(1)}, f32[1024,256]{1,0:T(8,128)}, u32[]{:S(2)}) copy-start(f32[1024,256]{1,0:T(8,128)} %get-tuple-element.106) | copy-start | bytes 3145732
  217.4 15.5 %copy-start.25 = (f32[1024,512]{1,0:T(8,128)S(1)}, f32[1024,512]{1,0:T(8,128)}, u32[]{:S(2)}) copy-start(f32[1024,512]{1,0:T(8,128)} %get-tuple-element.108) | copy-start | bytes 6291460
  236.2 6.0 %copy-start.27 = (f32[1024,8]{1,0:T(8,128)S(1)}, f32[1024,8]{1,0:T(8,128)}, u32[]{:S(2)}) copy-start(f32[1024,8]{1,0:T(8,128)} %copy-done.26) | copy-start | bytes 98308
  240.9 3.2 copy-start.32
  240.9 3.3 copy-start.34
  251.0 3.6 copy-start.12
  251.0 3.6 copy-start.18
  251.0 3.6 copy-start.20
  251.0 3.6 copy-start.22
  265.7 6.5 %copy-start.58 = (bf16[4,2,2,2,64,1024]{5,4,3,2,1,0:T(8,128)(2,1)S(1)}, bf16[4,2,2,2,64,1024]{5,4,3,2,1,0:T(8,128)(2,1)}, u32[]{:S(2)}) copy-start(bf16[4,2,2,2,64,1024]{5,4,3,2,1,0:T(8,128)(2,1)} %get-tuple-element.58) | copy-start | bytes 12582916
  272.1 4.6 %copy-start.47 = (bf16[4,2,2,2,64,384]{5,4,3,2,1,0:T(8,128)(2,1)S(1)}, bf16[4,2,2,2,64,384]{5,4,3,2,1,0:T(8,128)(2,1)}, u32[]{:S(2)}) copy-start(bf16[4,2,2,2,64,384]{5,4,3,2,1,0:T(8,128)(2,1)} %get-tuple-element.60) | copy-start | bytes 4718596
  276.7 4.5 %copy-start.52 = (f32[2048]{0:T(1024)S(1)}, f32[2048]{0:T(1024)}, u32[]{:S(2)}) copy-start(f32[2048]{0:T(1024)} %param.22) | copy-start | bytes 24580
  281.9 124.9 %copy-start.30 = (bf16[1,128,2048]{2,1,0:T(8,128)(2,1)S(1)}, bf16[1,128,2048]{2,1,0:T(8,128)(2,1)}, u32[]{:S(2)}) copy-start(bf16[1,128,2048]{2,1,0:T(8,128)(2,1)} %param.18) | copy-start | bytes 1572868
  281.9 126.4 %copy-start.46 = (bf16[1,128,2048]{2,1,0:T(8,128)(2,1)S(1)}, bf16[1,128,2048]{2,1,0:T(8,128)(2,1)}, u32[]{:S(2)}) copy-start(bf16[1,128,2048]{2,1,0:T(8,128)(2,1)} %param.19) | copy-start | bytes 1572868
  408.4 2.9 copy-start.56
  408.4 4.7 %copy-start.55 = (f32[8,4352]{1,0:T(8,128)S(1)}, f32[8,4352]{1,0:T(8,128)}, u32[]{:S(2)}) copy-start(f32[8,4352]{1,0:T(8,128)} %get-tuple-element.76) | copy-start | bytes 417796
  408.4 6.0 %copy-start.53 = (f32[64,384]{1,0:T(8,128)S(1)}, f32[64,384]{1,0:T(8,128)}, u32[]{:S(2)}) copy-start(f32[64,384]{1,0:T(8,128)} %get-tuple-element.75) | copy-start | bytes 294916
  408.4 6.6 %copy-start.48 = (bf16[64,8192]{1,0:T(8,128)(2,1)S(1)}, bf16[64,8192]{1,0:T(8,128)(2,1)}, u32[]{:S(2)}) copy-start(bf16[64,8192]{1,0:T(8,128)(2,1)} %get-tuple-element.74) | copy-start | bytes 3145732
  (12 other events, 22.4 us)

commit v4 on v3

--- a/solution.py
+++ b/solution.py
@@ -16,94 +16,211 @@
 KEYS = 2 * N
 STEP_PAD = 128
 CHUNK = 128
+LANES = 128
 epsilon = 1e-05
 f32 = jnp.float32
 bf16 = jnp.bfloat16
 
 
-def mm(a, b, dims):
-    return lax.dot_general(a, b, (dims, ((), ())), preferred_element_type=f32)
+def mm(a, b, dims, precision=None):
+    return lax.dot_general(a, b, (dims, ((), ())), precision=precision, preferred_element_type=f32)
 
 
 NN = ((1,), (0,))
 NT = ((1,), (1,))
 TN = ((0,), (0,))
+exact = lax.Precision.HIGHEST
 
 
 def pair_cols(low, col, first):
     return jnp.where(low, col[:, first : first + 1], col[:, first + 1 : first + 2])
 
 
-def scan_forward_kernel(
-    val_ref, key_ref, cum_ref, cum_t_ref, dt_ref, dt_t_ref, doc_ref, doc_t_ref, flow_ref, skip_ref, y_ref, state_ref, state
+def iota(shape, axis):
+    return lax.broadcasted_iota(jnp.int32, shape, axis)
+
+
+class Docs:
+    def __init__(self, meta_ref, chunk, span):
+        per = span // CHUNK
+        seq = chunk // per
+        self.start = (chunk - seq * per) * CHUNK
+        self.ends = []
+        total = 0
+        for i in range(DOCS - 1):
+            total = total + meta_ref[seq, i]
+            self.ends.append(total)
+        self.count = meta_ref[seq, DOCS]
+        self.pos = self.start + iota((CHUNK, 1), 0)
+        self.doc = self.index(self.pos)
+
+    def index(self, places):
+        found = (places >= self.ends[0]).astype(jnp.int32)
+        for end in self.ends[1:]:
+            found = found + (places >= end).astype(jnp.int32)
+        return found
+
+    def lag(self, by):
+        source = self.pos - by
+        return ((source >= 0) & (self.index(source) == self.doc)).astype(f32)
+
+    def flow(self):
+        return ((self.start > 0) & (self.index(self.start - 1) == self.doc)).astype(f32)
+
+    def row(self):
+        return self.index(self.start + iota((1, CHUNK), 1))
+
+    def tail(self):
+        return (self.doc == self.index(self.start + CHUNK - 1)).astype(f32)
+
+
+def shift_down(rows, before, by):
+    if by == 0:
+        return rows
+    moved = pltpu.roll(rows, by, 0)
+    top = jnp.where(iota((8, 1), 0) < by, pltpu.roll(before, by, 0), moved[:8])
+    return jnp.concatenate([top, moved[8:]], axis=0)
+
+
+def shift_up(rows, after, by):
+    if by == 0:
+        return rows
+    size = rows.shape[0]
+    moved = pltpu.roll(rows, size - by, 0)
+    end = jnp.where(iota((8, 1), 0) >= 8 - by, pltpu.roll(after, 8 - by, 0), moved[size - 8 :])
+    return jnp.concatenate([moved[: size - 8], end], axis=0)
+
+
+def silu_slope(v, sig):
+    return sig * (1.0 + v * (1.0 - sig))
+
+
+def forward_kernel(
+    meta_ref, proj_ref, key_ref, grad_ref, chan_ref, conv_k_ref, head_ref,
+    val_out, key_out, vsum_ref, ksum_ref, raw_ref, cum_ref, y_ref, state_ref, sums_ref,
+    state, last_v, last_k,
+    *, span, heads,
 ):
-    heads = cum_ref.shape[1]
-
-    @pl.when(pl.program_id(0) == 0)
+    i = pl.program_id(0)
+    chunks = pl.num_programs(0)
+    inner = heads * P_SIZE
+
+    @pl.when(i == 0)
     def _():
         state[...] = jnp.zeros_like(state)
+        last_v[...] = jnp.zeros_like(last_v)
+        last_k[...] = jnp.zeros_like(last_k)
+
+    docs = Docs(meta_ref, i, span)
+    lags = [docs.lag(by) for by in range(1, CONV)]
+
+    def convolve(rows, before, weight, bias):
+        total = bias + weight[CONV - 1 :] * rows
+        for by in range(1, CONV):
+            at = CONV - 1 - by
+            total = total + weight[at : at + 1] * (shift_down(rows, before, by) * lags[by - 1])
+        return total
+
+    rows_v = proj_ref[:, inner:].astype(bf16).astype(f32)
+    vsum = convolve(rows_v, last_v[...], chan_ref[:CONV, :], chan_ref[CONV : CONV + 1, :])
+    last_v[...] = rows_v[CHUNK - 8 :]
+    vsum_ref[...] = vsum
+    val_out[...] = (vsum * jax.nn.sigmoid(vsum)).astype(bf16)
+    rows_k = key_ref[:, :KEYS].astype(bf16).astype(f32)
+    ksum = convolve(rows_k, last_k[...], conv_k_ref[:CONV, :], conv_k_ref[CONV : CONV + 1, :])
+    last_k[...] = rows_k[CHUNK - 8 :]
+    ksum_ref[...] = ksum
+    keys = (ksum * jax.nn.sigmoid(ksum)).astype(bf16)
+    key_out[...] = keys
+
+    rows = iota((CHUNK, CHUNK), 0)
+    cols = iota((CHUNK, CHUNK), 1)
+    chosen = (rows == head_ref[2:3, :].astype(jnp.int32)).astype(f32)
+    raw = mm(key_ref[:, KEYS:], chosen, NN, exact) + head_ref[:1, :]
+    raw_ref[...] = raw
+    dt = jax.nn.softplus(raw)
+    cum = mm((rows >= cols).astype(f32), -dt * head_ref[1:2, :], NN, exact)
+    cum_ref[...] = cum
+    cum_t = cum.T
+    dt_t = dt.T
 
     state_ref[0] = state[...].astype(bf16)
-    cum = cum_ref[...]
-    last = cum[CHUNK - 1 :, :]
-    doc = doc_ref[...]
-    doc_t = doc_t_ref[...]
-    flow = flow_ref[...]
-    rows = lax.broadcasted_iota(jnp.int32, (CHUNK, CHUNK), 0)
-    cols = lax.broadcasted_iota(jnp.int32, (CHUNK, CHUNK), 1)
-    bias = jnp.where((doc == doc_t) & (rows >= cols), 0.0, -1e30)
-    carry_w = flow * jnp.exp(cum)
-    final_w = jnp.where(doc == doc[CHUNK - 1 :, :], jnp.exp(last - cum), 0.0) * dt_ref[...]
+    bias = jnp.where((docs.doc == docs.row()) & (rows >= cols), 0.0, -1e30)
+    carry_w = docs.flow() * jnp.exp(cum)
+    final_w = docs.tail() * jnp.exp(cum[CHUNK - 1 :, :] - cum) * dt
     gain = carry_w[CHUNK - 1 :, :]
     low = cols < P_SIZE
     low_row = low[:1]
-    write = key_ref[:, :N]
-    read = key_ref[:, N:]
+    write = keys[:, :N]
+    read = keys[:, N:]
     write_t = write.astype(f32).T.astype(bf16)
     scores = mm(read, write, NT)
+    square = jnp.zeros((CHUNK, LANES), f32)
+    cross = jnp.zeros((CHUNK, LANES), f32)
+    count = docs.count.astype(f32)
     for pair in range(heads // 2):
         first = 2 * pair
         lanes = slice(pair * 128, pair * 128 + 128)
-        x = val_ref[:, lanes]
-        xf = x.astype(f32)
+        xf = val_out[:, lanes].astype(f32)
         weights = []
         for h in (first, first + 1):
-            decay = jnp.exp(cum[:, h : h + 1] - cum_t_ref[h : h + 1, :] + bias)
-            weights.append((decay * scores * dt_t_ref[h : h + 1, :]).astype(bf16))
+            decay = jnp.exp(cum[:, h : h + 1] - cum_t[h : h + 1, :] + bias)
+            weights.append((decay * scores * dt_t[h : h + 1, :]).astype(bf16))
         stacked = jnp.concatenate(
             [jnp.where(low, xf, 0.0).astype(bf16), jnp.where(low, 0.0, xf).astype(bf16)], axis=0
         )
         old = state[:, lanes]
         y = mm(jnp.concatenate(weights, axis=1), stacked, NN)
         y = y + pair_cols(low, carry_w, first) * mm(read, old.astype(bf16), NN)
-        y_ref[:, lanes] = y + skip_ref[:, lanes] * xf
+        y = y + chan_ref[6:7, lanes] * xf
+        y = jnp.where(chan_ref[7:8, lanes] < count, y, 0.0)
+        y_ref[:, lanes] = y
         state[:, lanes] = pair_cols(low_row, gain, first) * old + mm(
             write_t, (pair_cols(low, final_w, first) * xf).astype(bf16), NN
         )
-
-
-def scan_backward_kernel(
-    val_ref, key_ref, cum_ref, cum_t_ref, dt_ref, doc_ref, doc_t_ref, flow_ref, skip_ref, state_ref, dy_ref,
-    dval_ref, dkey_ref, dcum_ref, dcum_t_ref, ddt_ref, dskip_ref, dstate,
+        gate = proj_ref[:, lanes]
+        gated = y * (gate * jax.nn.sigmoid(gate))
+        square = square + gated * gated
+        cross = cross + gated * (grad_ref[:, lanes] * chan_ref[5:6, lanes])
+    sums_ref[pl.ds(i, 1), :] = jnp.sum(square.T, axis=0, keepdims=True)
+    sums_ref[pl.ds(chunks + i, 1), :] = jnp.sum(cross.T, axis=0, keepdims=True)
+
+
+def backward_kernel(
+    meta_ref, proj_ref, key_in_ref, grad_ref, chan_ref, conv_k_ref, head_ref,
+    val_ref, key_ref, vsum_ref, ksum_ref, raw_ref, cum_ref, y_ref, state_ref, sums_ref,
+    mixed_ref, cols_ref, key_cols_ref, chan_sums, key_sums, head_sums,
+    dstate, dv, next_v, next_k, next_lags,
+    *, span, heads,
 ):
-    heads = cum_ref.shape[1]
+    chunks = pl.num_programs(0)
+    i = chunks - 1 - pl.program_id(0)
+    inner = heads * P_SIZE
 
     @pl.when(pl.program_id(0) == 0)
     def _():
-        dstate[...] = jnp.zeros_like(dstate)
-        dskip_ref[...] = jnp.zeros_like(dskip_ref)
-
+        for ref in (dstate, next_v, next_k, next_lags, chan_sums, key_sums, head_sums):
+            ref[...] = jnp.zeros_like(ref)
+
+    docs = Docs(meta_ref, i, span)
+    rows = iota((CHUNK, CHUNK), 0)
+    cols = iota((CHUNK, CHUNK), 1)
+    raw = raw_ref[...]
+    dt = jax.nn.softplus(raw)
     cum = cum_ref[...]
-    dt = dt_ref[...]
-    last = cum[CHUNK - 1 :, :]
-    doc = doc_ref[...]
-    doc_t = doc_t_ref[...]
-    flow = flow_ref[...]
-    rows = lax.broadcasted_iota(jnp.int32, (CHUNK, CHUNK), 0)
-    cols = lax.broadcasted_iota(jnp.int32, (CHUNK, CHUNK), 1)
-    bias = jnp.where((doc == doc_t) & (cols >= rows), 0.0, -1e30)
-    carry_w = flow * jnp.exp(cum)
-    final_d = jnp.where(doc == doc[CHUNK - 1 :, :], jnp.exp(last - cum), 0.0)
+    cum_t = cum.T
+    count = docs.count.astype(f32)
+    head_total = count * P_SIZE
+
+    def column(row):
+        return jnp.broadcast_to(row, (CHUNK, CHUNK)).T
+
+    inv = lax.rsqrt(column(sums_ref[pl.ds(i, 1), :]) / head_total + epsilon)
+    pull = inv * inv * inv * column(sums_ref[pl.ds(chunks + i, 1), :]) / head_total
+
+    bias = jnp.where((docs.doc == docs.row()) & (cols >= rows), 0.0, -1e30)
+    carry_w = docs.flow() * jnp.exp(cum)
+    final_d = docs.tail() * jnp.exp(cum[CHUNK - 1 :, :] - cum)
     final_w = final_d * dt
     gain = carry_w[CHUNK - 1 :, :]
     low = cols < P_SIZE
@@ -115,16 +232,27 @@
     dscores_t = jnp.zeros((CHUNK, CHUNK), f32)
     dwrite = jnp.zeros((CHUNK, N), f32)
     dread = jnp.zeros((CHUNK, N), f32)
-    end_row = lax.broadcasted_iota(jnp.int32, (CHUNK, 1), 0) == CHUNK - 1
-    dcum_cols = []
+    end_row = iota((CHUNK, 1), 0) == CHUNK - 1
+    dcum = jnp.zeros((CHUNK, LANES), f32)
+    ddt = jnp.zeros((CHUNK, LANES), f32)
     dcum_rows = []
-    ddt_cols = []
     for pair in range(heads // 2):
         first = 2 * pair
         lanes = slice(pair * 128, pair * 128 + 128)
-        x = val_ref[:, lanes]
-        xf = x.astype(f32)
-        dy = dy_ref[:, lanes]
+        gate = proj_ref[:, lanes]
+        sig = jax.nn.sigmoid(gate)
+        silu = gate * sig
+        masked = y_ref[:, lanes]
+        gated = masked * silu
+        norm_gain = chan_ref[5:6, lanes]
+        gm = grad_ref[:, lanes]
+        unit = gated * inv
+        mixed_ref[:, lanes] = (unit * norm_gain).astype(bf16)
+        chan_sums[5:6, lanes] += jnp.sum(gm * unit, axis=0, keepdims=True)
+        grad_gated = inv * (gm * norm_gain) - pull * gated
+        cols_ref[:, lanes] = (grad_gated * masked * silu_slope(gate, sig)).astype(bf16)
+        dy = jnp.where(chan_ref[7:8, lanes] < count, grad_gated * silu, 0.0)
+        xf = val_ref[:, lanes].astype(f32)
         dyb = dy.astype(bf16)
         x_stack = jnp.concatenate(
             [jnp.where(low, xf, 0.0).astype(bf16), jnp.where(low, 0.0, xf).astype(bf16)], axis=0
@@ -146,7 +274,7 @@
         weights = []
         for which, h in enumerate((first, first + 1)):
             col = dt[:, h : h + 1]
-            decay = jnp.exp(cum_t_ref[h : h + 1, :] - cum[:, h : h + 1] + bias)
+            decay = jnp.exp(cum_t[h : h + 1, :] - cum[:, h : h + 1] + bias)
             weighted = decay * col
             weights.append((weighted * scores_t).astype(bf16))
             dw = dweights[which * CHUNK : (which + 1) * CHUNK]
@@ -162,82 +290,122 @@
             at_end = jnp.sum(push, axis=0, keepdims=True) + gain[:, h : h + 1] * jnp.sum(
                 jnp.where(half_row, gain_prod, 0.0), axis=1, keepdims=True
             )
-            ddt_cols.append(ddt_in + final_d[:, h : h + 1] * final_sum)
-            dcum_cols.append(
-                carry_w[:, h : h + 1] * carry_sum - push - col * ddt_in + jnp.where(end_row, at_end, 0.0)
+            here = cols == h
+            ddt = jnp.where(here, ddt_in + final_d[:, h : h + 1] * final_sum, ddt)
+            dcum = jnp.where(
+                here,
+                carry_w[:, h : h + 1] * carry_sum - push - col * ddt_in + jnp.where(end_row, at_end, 0.0),
+                dcum,
             )
         dx = mm(jnp.concatenate(weights, axis=1), dy_stack, NN)
-        dval_ref[:, lanes] = dx + final_p * pushed + skip_ref[:, lanes] * dy
-        dskip_ref[:, lanes] += jnp.sum(dy * xf, axis=0, keepdims=True)
+        dv[:, lanes] = dx + final_p * pushed + chan_ref[6:7, lanes] * dy
+        chan_sums[6:7, lanes] += jnp.sum(dy * xf, axis=0, keepdims=True)
         dwrite = dwrite + mm((final_p * xf).astype(bf16), gradb, NT)
         carry_dy = (carry_p * dy).astype(bf16)
         dread = dread + mm(carry_dy, old, NT)
         dstate[:, lanes] = pair_cols(low_row, gain, first) * grad + mm(read_t, carry_dy, NN)
     dsb = dscores_t.astype(bf16)
-    dkey_ref[:, :N] = dwrite + mm(dsb, read, NN)
-    dkey_ref[:, N:] = dread + mm(dsb, write, TN)
-    dcum_ref[...] = jnp.concatenate(dcum_cols, axis=1)
-    dcum_t_ref[...] = jnp.concatenate(dcum_rows, axis=0)
-    ddt_ref[...] = jnp.concatenate(ddt_cols, axis=1)
-
-
-def scan_forward(val, keys, cum, cum_t, dt, dt_t, doc, doc_t, flow, skip):
-    length = val.shape[0]
-    heads = cum.shape[1]
+    dkeys = jnp.concatenate([dwrite + mm(dsb, read, NN), dread + mm(dsb, write, TN)], axis=1)
+
+    extra = jnp.concatenate(dcum_rows + [jnp.zeros((LANES - heads, CHUNK), f32)], axis=0)
+    dlog = mm((cols >= rows).astype(f32), dcum + extra.T, NN, exact)
+    rate = head_ref[1:2, :]
+    grad_step = (ddt - rate * dlog) * jax.nn.sigmoid(raw)
+    head_sums[:1, :] += jnp.sum(grad_step, axis=0, keepdims=True)
+    head_sums[1:2, :] -= jnp.sum(dt * rate * dlog, axis=0, keepdims=True)
+    chosen = (rows == head_ref[2:3, :].astype(jnp.int32)).astype(bf16)
+    key_cols_ref[:, KEYS:] = mm(grad_step.astype(bf16), chosen, NT).astype(bf16)
+
+    lags = [docs.lag(by) for by in range(1, CONV)]
+
+    def convolve_back(dact, total, rows_in, after, weight, sums):
+        dconv = dact * silu_slope(total, jax.nn.sigmoid(total))
+        grad_in = weight[CONV - 1 :] * dconv
+        sums[CONV : CONV + 1, :] += jnp.sum(dconv, axis=0, keepdims=True)
+        sums[CONV - 1 : CONV, :] += jnp.sum(dconv * rows_in, axis=0, keepdims=True)
+        for by in range(1, CONV):
+            at = CONV - 1 - by
+            moved = shift_up(dconv * lags[by - 1], after[...] * next_lags[:, by - 1 : by], by)
+            grad_in = grad_in + weight[at : at + 1] * moved
+            sums[at : at + 1, :] += jnp.sum(moved * rows_in, axis=0, keepdims=True)
+        after[...] = dconv[:8]
+        return grad_in.astype(bf16)
+
+    rows_v = proj_ref[:, inner:].astype(bf16).astype(f32)
+    cols_ref[:, inner:] = convolve_back(dv[...], vsum_ref[...], rows_v, next_v, chan_ref[:CONV, :], chan_sums)
+    rows_k = key_in_ref[:, :KEYS].astype(bf16).astype(f32)
+    key_cols_ref[:, :KEYS] = convolve_back(
+        dkeys, ksum_ref[...], rows_k, next_k, conv_k_ref[:CONV, :], key_sums
+    )
+    for by in range(1, CONV):
+        next_lags[:, by - 1 : by] = lags[by - 1][:8]
+
+
+def mixer_forward(meta, projected, key_out, grad_mixed, chan, conv_k, head_vec, span, heads):
+    length = projected.shape[0]
     inner = heads * P_SIZE
-    steps = length // CHUNK
+    chunks = length // CHUNK
     row = lambda width: pl.BlockSpec((CHUNK, width), lambda i: (i, 0))
-    lane = lambda height: pl.BlockSpec((height, CHUNK), lambda i: (0, i))
+    all_of = lambda *shape: pl.BlockSpec(shape, lambda i: (0,) * len(shape))
+    out = lambda width, dtype: jax.ShapeDtypeStruct((length, width), dtype)
     return pl.pallas_call(
-        scan_forward_kernel,
-        grid=(steps,),
+        partial(forward_kernel, span=span, heads=heads),
+        grid=(chunks,),
         in_specs=[
-            row(inner), row(KEYS), row(heads), lane(heads), row(heads), lane(heads), row(1), lane(1), row(1),
-            pl.BlockSpec((1, inner), lambda i: (0, 0)),
+            pl.BlockSpec(memory_space=pltpu.SMEM), row(2 * inner), row(KEYS + STEP_PAD), row(inner),
+            all_of(8, inner), all_of(8, KEYS), all_of(8, LANES),
         ],
-        out_specs=[row(inner), pl.BlockSpec((1, N, inner), lambda i: (i, 0, 0))],
+        out_specs=[
+            row(inner), row(KEYS), row(inner), row(KEYS), row(LANES), row(LANES), row(inner),
+            pl.BlockSpec((1, N, inner), lambda i: (i, 0, 0)), all_of(2 * chunks, LANES),
+        ],
         out_shape=[
-            jax.ShapeDtypeStruct((length, inner), f32),
-            jax.ShapeDtypeStruct((steps, N, inner), bf16),
+            out(inner, bf16), out(KEYS, bf16), out(inner, f32), out(KEYS, f32), out(LANES, f32), out(LANES, f32),
+            out(inner, f32), jax.ShapeDtypeStruct((chunks, N, inner), bf16),
+            jax.ShapeDtypeStruct((2 * chunks, LANES), f32),
         ],
-        scratch_shapes=[pltpu.VMEM((N, inner), f32)],
-        compiler_params=pltpu.CompilerParams(vmem_limit_bytes=40 * 2**20),
+        scratch_shapes=[pltpu.VMEM((N, inner), f32), pltpu.VMEM((8, inner), f32), pltpu.VMEM((8, KEYS), f32)],
+        compiler_params=pltpu.CompilerParams(vmem_limit_bytes=32 * 2**20),
         cost_estimate=pl.CostEstimate(
-            flops=length * inner * 1024, bytes_accessed=length * inner * 10, transcendentals=length * heads * CHUNK
+            flops=length * inner * 1024, bytes_accessed=length * inner * 24, transcendentals=length * heads * CHUNK
         ),
-    )(val, keys, cum, cum_t, dt, dt_t, doc, doc_t, flow, skip)
-
-
-def scan_backward(val, keys, cum, cum_t, dt, doc, doc_t, flow, skip, states, dy):
-    length = val.shape[0]
-    heads = cum.shape[1]
+        name="mixer_forward",
+    )(meta, projected, key_out, grad_mixed, chan, conv_k, head_vec)
+
+
+def mixer_backward(meta, projected, key_out, grad_mixed, chan, conv_k, head_vec, kept, sums, span, heads):
+    length = projected.shape[0]
     inner = heads * P_SIZE
-    steps = length // CHUNK
-    row = lambda width: pl.BlockSpec((CHUNK, width), lambda i: (steps - 1 - i, 0))
-    lane = lambda height: pl.BlockSpec((height, CHUNK), lambda i: (0, steps - 1 - i))
-    whole = pl.BlockSpec((1, inner), lambda i: (0, 0))
+    chunks = length // CHUNK
+    row = lambda width: pl.BlockSpec((CHUNK, width), lambda i: (chunks - 1 - i, 0))
+    all_of = lambda *shape: pl.BlockSpec(shape, lambda i: (0,) * len(shape))
+    out = lambda width: jax.ShapeDtypeStruct((length, width), bf16)
     return pl.pallas_call(
-        scan_backward_kernel,
-        grid=(steps,),
+        partial(backward_kernel, span=span, heads=heads),
+        grid=(chunks,),
         in_specs=[
-            row(inner), row(KEYS), row(heads), lane(heads), row(heads), row(1), lane(1), row(1), whole,
-            pl.BlockSpec((1, N, inner), lambda i: (steps - 1 - i, 0, 0)), row(inner),
+            pl.BlockSpec(memory_space=pltpu.SMEM), row(2 * inner), row(KEYS + STEP_PAD), row(inner),
+            all_of(8, inner), all_of(8, KEYS), all_of(8, LANES),
+            row(inner), row(KEYS), row(inner), row(KEYS), row(LANES), row(LANES), row(inner),
+            pl.BlockSpec((1, N, inner), lambda i: (chunks - 1 - i, 0, 0)), all_of(2 * chunks, LANES),
         ],
-        out_specs=[row(inner), row(KEYS), row(heads), lane(heads), row(heads), whole],
+        out_specs=[
+            row(inner), row(2 * inner), row(KEYS + STEP_PAD), all_of(8, inner), all_of(8, KEYS), all_of(8, LANES),
+        ],
         out_shape=[
-            jax.ShapeDtypeStruct((length, inner), f32),
-            jax.ShapeDtypeStruct((length, KEYS), f32),
-            jax.ShapeDtypeStruct((length, heads), f32),
-            jax.ShapeDtypeStruct((heads, length), f32),
-            jax.ShapeDtypeStruct((length, heads), f32),
-            jax.ShapeDtypeStruct((1, inner), f32),
+            out(inner), out(2 * inner), out(KEYS + STEP_PAD), jax.ShapeDtypeStruct((8, inner), f32),
+            jax.ShapeDtypeStruct((8, KEYS), f32), jax.ShapeDtypeStruct((8, LANES), f32),
         ],
-        scratch_shapes=[pltpu.VMEM((N, inner), f32)],
-        compiler_params=pltpu.CompilerParams(vmem_limit_bytes=40 * 2**20),
+        scratch_shapes=[
+            pltpu.VMEM((N, inner), f32), pltpu.VMEM((CHUNK, inner), f32), pltpu.VMEM((8, inner), f32),
+            pltpu.VMEM((8, KEYS), f32), pltpu.VMEM((8, LANES), f32),
+        ],
+        compiler_params=pltpu.CompilerParams(vmem_limit_bytes=32 * 2**20),
         cost_estimate=pl.CostEstimate(
-            flops=length * inner * 3072, bytes_accessed=length * inner * 14, transcendentals=length * heads * CHUNK
+            flops=length * inner * 3072, bytes_accessed=length * inner * 30, transcendentals=length * heads * CHUNK
         ),
-    )(val, keys, cum, cum_t, dt, doc, doc_t, flow, skip, states, dy)
+        name="mixer_backward",
+    )(meta, projected, key_out, grad_mixed, chan, conv_k, head_vec, *kept, sums)
 
 
 MESH = pl.DeviceIdType.MESH
@@ -484,8 +652,8 @@
     mover.close()
 
 
-def remote_params(identity):
-    return pltpu.CompilerParams(collective_id=identity, has_side_effects=True, vmem_limit_bytes=58 * 2**20)
+def remote_params(identity, mib):
+    return pltpu.CompilerParams(collective_id=identity, has_side_effects=True, vmem_limit_bytes=mib * 2**20)
 
 
 def sems(copies, kept):
@@ -513,7 +681,7 @@
         in_specs=[HBM] * 6,
         out_specs=[HBM] * 6,
         scratch_shapes=sems(copies, runs + 5),
-        compiler_params=remote_params(0),
+        compiler_params=remote_params(0, 4),
         name="gather_all",
     )(in_w, keys, out_w, rows, cot, meta)
 
@@ -541,7 +709,7 @@
         in_specs=[VMEM],
         out_specs=VMEM,
         scratch_shapes=[pltpu.VMEM((count,) + part.shape, f32)] + sems(count, 1),
-        compiler_params=remote_params(1),
+        compiler_params=remote_params(1, 4),
         name="cube_total",
     )(part)
 
@@ -778,41 +946,9 @@
             vm(max(far - 1, 1), *kblock[1:]), vm(peers - 1, far, *kblock), boxes(small), boxes(conv),
         ]
         + sems(copies, kept),
-        compiler_params=remote_params(2),
+        compiler_params=remote_params(2, 58),
         name="scatter_all",
     )(branch, grads, gw, go, gk, small, conv)
-
-
-def doc_index(places, doc_ends):
-    return jnp.sum((places[:, None] >= doc_ends[None, :-1]).astype(jnp.int32), axis=1)
-
-
-def moved_down(rows, by):
-    return jnp.concatenate([jnp.zeros((by,) + rows.shape[1:], rows.dtype), rows[: rows.shape[0] - by]], axis=0)
-
-
-def moved_up(rows, by):
-    return jnp.concatenate([rows[by:], jnp.zeros((by,) + rows.shape[1:], rows.dtype)], axis=0)
-
-
-def convolve(conv_in, weight, bias, masks):
-    total = jnp.broadcast_to(bias[None, :], conv_in.shape)
-    for k in range(CONV):
-        total = total + weight[k][None, :] * moved_down(conv_in, CONV - 1 - k).astype(f32) * masks[k][:, None]
-    return total
-
-
-def convolve_back(dact, conv_in, conv_sum, weight, masks):
-    sig = jax.nn.sigmoid(conv_sum)
-    dconv = dact * (sig * (1.0 + conv_sum * (1.0 - sig)))
-    sums = []
-    grad_in = jnp.zeros_like(dconv)
-    for k in range(CONV):
-        taken = dconv * masks[k][:, None]
-        sums.append(jnp.sum(taken * moved_down(conv_in, CONV - 1 - k).astype(f32), axis=0))
-        grad_in = grad_in + weight[k][None, :] * moved_up(taken, CONV - 1 - k)
-    sums.append(jnp.sum(dconv, axis=0))
-    return grad_in.astype(bf16), jnp.stack(sums)
 
 
 def body(
@@ -834,8 +970,7 @@
 
     def own(vector):
         part = vector.reshape(-1, peers, outer, near, vector.shape[-1] // (peers * outer * near))
-        part = lax.dynamic_index_in_dim(part, me.s, 1, False)
-        part = lax.dynamic_index_in_dim(part, me.zl, 2, False)
+        part = lax.dynamic_slice(part, (0, me.s, 0, me.zl, 0), (part.shape[0], 1, outer, 1, part.shape[4]))
         return part.reshape(vector.shape[:-1] + (-1,))
 
     def spread(part):
@@ -849,99 +984,54 @@
     )
     inv_rms = lax.rsqrt(jnp.mean(seq_rows * seq_rows, axis=1, keepdims=True) + epsilon)
     normed = (seq_rows * inv_rms * pre_gain[None, :]).astype(bf16)
-    meta = jnp.zeros((8, 128), jnp.int32)
-    meta = meta.at[0, :DOCS].set(doc_lengths[0]).at[1, 0].set(head_width[0])
+    meta = jnp.pad(jnp.concatenate([doc_lengths[0], head_width])[None], ((0, 7), (0, 123)))
     in_w, key_w, out_w, normed, cot_all, meta = gather(in_weight, key_send, out_weight, normed, cot_rows, meta)
     in_w = in_w.reshape(width, 2 * inner)
     key_w = key_w.reshape(width, -1)
     out_w = out_w.reshape(inner, width)
     normed = normed.reshape(length, width)
     cot_all = cot_all.reshape(length, width)
-
-    places = jnp.arange(span, dtype=jnp.int32)
-    doc_ids = jnp.concatenate(
-        [doc_index(places, jnp.cumsum(meta[i, 0, :DOCS])) + i * DOCS for i in range(near)]
+    meta = meta[:, 0, :8]
+
+    head_ids = jnp.arange(H, dtype=f32)
+    chan = own(
+        jnp.concatenate(
+            [
+                conv_weight[:, :E],
+                conv_bias[None, :E],
+                norm_gain[None],
+                jnp.repeat(skip_gain, P_SIZE)[None],
+                jnp.repeat(head_ids, P_SIZE)[None],
+            ],
+            axis=0,
+        )
     )
-    before = jnp.concatenate([jnp.full((1,), -1, jnp.int32), doc_ids[CHUNK - 1 : -1 : CHUNK]])
-    flow = (doc_ids == jnp.repeat(before, CHUNK)).astype(f32)[:, None]
-    doc = doc_ids[:, None]
-    doc_t = doc_ids[None, :]
-    counts = meta[:, 1, 0]
-    head_total = jnp.repeat((counts * P_SIZE).astype(f32), span)[:, None]
-    my_heads = own(jnp.arange(H, dtype=jnp.int32))
-    head_mask = jnp.repeat((my_heads[None, :] < counts[:, None]).astype(f32), P_SIZE, axis=1)
-    head_mask = jnp.repeat(head_mask, span, axis=0)
-    masks = []
-    for k in range(CONV):
-        lag = CONV - 1 - k
-        masks.append((jnp.concatenate([jnp.full((lag,), -1, jnp.int32), doc_ids[: length - lag]]) == doc_ids).astype(f32))
-
-    conv_all = jnp.concatenate([conv_weight, conv_bias[None]], axis=0)
-    conv_v = own(conv_all[:, :E])
-    conv_k = conv_all[:, E:]
-    step_b = own(step_bias)
-    rate = jnp.exp(own(decay_log))
-    skip = jnp.repeat(own(skip_gain), P_SIZE)[None, :]
-    gain = own(norm_gain)[None, :]
+    conv_k = jnp.concatenate([conv_weight[:, E:], conv_bias[None, E:], jnp.zeros((3, KEYS), f32)], axis=0)
+    head_vec = own(jnp.stack([step_bias, jnp.exp(decay_log), head_ids + 1.0]))
+    head_vec = jnp.pad(head_vec, ((0, 5), (0, LANES - heads))) - jnp.where(jnp.arange(8) == 2, 1.0, 0.0)[:, None]
 
     projected = mm(normed, in_w, NN)
-    gate = projected[:, :inner]
-    value_in = projected[:, inner:].astype(bf16)
     key_out = mm(normed, key_w, NN)
-    key_in = key_out[:, :KEYS].astype(bf16)
-    step_raw = own(key_out[:, KEYS : KEYS + H]) + step_b[None, :]
-    value_sum = convolve(value_in, conv_v[:CONV], conv_v[CONV], masks)
-    values = jax.nn.silu(value_sum).astype(bf16)
-    key_sum = convolve(key_in, conv_k[:CONV], conv_k[CONV], masks)
-    keys = jax.nn.silu(key_sum).astype(bf16)
-    dt = jax.nn.softplus(step_raw)
-    log_decay = -dt * rate[None, :]
-    cum = jnp.cumsum(log_decay.reshape(-1, CHUNK, heads), axis=1).reshape(length, heads)
-    y, states = scan_forward(values, keys, cum, cum.T, dt, dt.T, doc, doc_t, flow, skip)
     grad_mixed = mm(cot_all, out_w, NT)
-    sig_gate = jax.nn.sigmoid(gate)
-    silu_gate = gate * sig_gate
-    masked = y * head_mask
-    gated = masked * silu_gate
-    scaled = grad_mixed * gain
-    part = jnp.stack([jnp.sum(gated * gated, axis=1), jnp.sum(scaled * gated, axis=1)])
-    sums = cube_total(part.reshape(-1, 128)).reshape(2, length, 1)
-    inv = lax.rsqrt(sums[0] / head_total + epsilon)
-    pull = inv * inv * inv * sums[1] / head_total
-    mixed = (gated * inv * gain).astype(bf16)
+    mixer_args = (meta, projected, key_out, grad_mixed, chan, conv_k, head_vec)
+    *kept, part = mixer_forward(*mixer_args, span, heads)
+    sums = cube_total(part)
+    mixed, grad_cols, key_cols, chan_sums, key_sums, head_sums = mixer_backward(
+        *mixer_args, kept, sums, span, heads
+    )
     branch = mm(mixed, out_w, NN).astype(bf16)
-
     grad_out = mm(mixed, cot_all, TN).astype(bf16)
-    grad_norm_gain = jnp.sum(grad_mixed * gated * inv, axis=0)
-    grad_gated = inv * scaled - pull * gated
-    dy = grad_gated * silu_gate * head_mask
-    grad_gate = (grad_gated * masked * (sig_gate * (1.0 + gate * (1.0 - sig_gate)))).astype(bf16)
-    dvalues, dkeys, dcum, dcum_t, ddt, dskip = scan_backward(
-        values, keys, cum, cum.T, dt, doc, doc_t, flow, skip, states, dy
-    )
-    dcum = (dcum + dcum_t.T).reshape(-1, CHUNK, heads)
-    dlog = lax.cumsum(dcum, axis=1, reverse=True).reshape(length, heads)
-    grad_dt = ddt - rate[None, :] * dlog
-    grad_decay_log = -jnp.sum(dt * rate[None, :] * dlog, axis=0)
-    grad_step = grad_dt * jax.nn.sigmoid(step_raw)
-    grad_step_bias = jnp.sum(grad_step, axis=0)
-    grad_skip = jnp.sum(dskip.reshape(heads, P_SIZE), axis=1)
-    grad_value_in, sums_v = convolve_back(dvalues, value_in, value_sum, conv_v[:CONV], masks)
-    grad_key_in, sums_k = convolve_back(dkeys, key_in, key_sum, conv_k[:CONV], masks)
-    grad_cols = jnp.concatenate([grad_gate, grad_value_in], axis=1)
-    step_cols = jnp.pad(spread(grad_step.astype(bf16)), ((0, 0), (0, STEP_PAD - H)))
-    key_cols = jnp.concatenate([grad_key_in, step_cols], axis=1)
     grad_in = mm(normed, grad_cols, TN).astype(bf16)
     grad_keys = mm(normed, key_cols, TN).astype(bf16)
     grad_normed = mm(grad_cols, in_w, NT) + mm(key_cols, key_w, NT)
     grad_pre_gain = jnp.sum(grad_normed * normed.astype(f32), axis=0) / pre_gain
 
-    small = jnp.concatenate(
-        [grad_pre_gain, spread(grad_norm_gain), spread(grad_step_bias), spread(grad_decay_log), spread(grad_skip)]
-    )
+    grad_skip = jnp.sum(chan_sums[6].reshape(heads, P_SIZE), axis=1)
+    head_sums = spread(jnp.concatenate([head_sums[:2, :heads], grad_skip[None]], axis=0))
+    chan_sums = spread(chan_sums[:6])
+    small = jnp.concatenate([grad_pre_gain, chan_sums[5], head_sums.reshape(-1)])
     small = jnp.pad(small, (0, -small.shape[0] % 1024)).reshape(-1, 128)
-    conv_sums = jnp.concatenate([spread(sums_v), sums_k], axis=1)
-    conv_sums = jnp.pad(conv_sums, ((0, 8 - conv_sums.shape[0]), (0, 0)))
+    conv_sums = jnp.pad(jnp.concatenate([chan_sums[:5], key_sums[:5]], axis=1), ((0, 3), (0, 0)))
     rows_of = lambda part: part.reshape(near, peers, tokens, width)
     blocks = (peers, far, near, 2, rows)
     branch, grad_normed, grad_in, grad_out_weight, grad_keys, small, conv_sums = scatter(

time: 423 us -> 359 us (0.85); the launches traced: 418 us -> 359 us
  other arithmetic: 63.9 us -> 11.2 us
  Pallas kernels: 267 us -> 287 us
  local copies, waits for them, and re-layouts: 37.2 us -> 20 us
  matrix products: 47.2 us -> 38.6 us
    another operation x5 -> x1, other arithmetic: 25.7 us -> 0.03 us  [body(): head_vec = own(jnp.stack([step_bias, jnp.exp(decay_log), head_ids + 1.0]))]
    pallas_call x2, Pallas kernels: 21.2 us -> 39.9 us  [the longest x1 26.2 us: mixer_backward(): pl.pallas_call(partial(backward_kernel, span=span, heads=heads), grid=(ch...]
    pallas_call x1, Pallas kernels: 102 us -> 116 us  [gather(): pl.pallas_call(gather_kernel, out_shape=[shape((peers, far, near, 2), (in...]
    pallas_call x1, Pallas kernels: 19.2 us -> 7.45 us  [cube_total(): pl.pallas_call(total_kernel, out_shape=jax.ShapeDtypeStruct(part.shape, f...]
    convert_element_type x9 -> x0, other arithmetic: 11.3 us -> none  [the longest x1 3.38 us: body(): values = jax.nn.silu(value_sum).astype(bf16)]
    reduce_sum x9 -> x1, other arithmetic: 10.8 us -> 0.12 us  [body(): grad_skip = jnp.sum(chan_sums[6].reshape(heads, P_SIZE), axis=1)]
    dot_general x9, matrix products: 47.2 us -> 38.6 us  [mm(): lax.dot_general(a, b, (dims, ((), ())), precision=precision, preferred_el...]
    reshape x18 -> x0, local copies, waits for them, and re-layouts: 6.32 us -> none  [the longest x6 3.12 us: own(): vector.reshape(-1, peers, outer, near, vector.shape[-1] // (peers * outer...]
where the time goes in v4:
time: 359 us
  Pallas kernels  287 us (80%)
  matrix products  38.6 us (11%)
  local copies, waits for them, and re-layouts  20 us (6%)
  other arithmetic  11.2 us (3%)
    pallas_call x1, Pallas kernels, scatter(): pl.pallas_call(scatter_kernel, out_shape=[jax.ShapeDtypeStruct((tokens, w...  124 us
    pallas_call x1, Pallas kernels, gather(): pl.pallas_call(gather_kernel, out_shape=[shape((peers, far, near, 2), (in...  116 us
    dot_general x9, matrix products, mm(): lax.dot_general(a, b, (dims, ((), ())), precision=precision, preferred_el...  38.6 us
    pallas_call x1, Pallas kernels, mixer_backward(): pl.pallas_call(partial(backward_kernel, span=span, heads=heads), grid=(ch...  26.2 us
    pallas_call x1, Pallas kernels, mixer_forward(): pl.pallas_call(partial(forward_kernel, span=span, heads=heads), grid=(chu...  13.7 us
    pallas_call x1, Pallas kernels, cube_total(): pl.pallas_call(total_kernel, out_shape=jax.ShapeDtypeStruct(part.shape, f...  7.45 us

profile of v4, /device:TPU:0, one launch (start us, length us, event | category | flops | bytes accessed | tf_op | source)
XLA Modules:
  0.0 358.5 jit_solution(5131289673032682843)
XLA Ops:
  0.7 0.8 slice.90
  1.7 0.7 broadcast_in_dim.52
  2.7 0.7 slice.91
  3.5 0.7 concatenate.43
  4.3 0.1 concatenate.45
  4.4 0.7 exp.3
  5.2 0.7 stack.10
  6.1 1.2 fusion
  7.4 1.2 fusion.2.rows_ref
  8.6 0.8 slice.88
  9.5 0.7 maximum_maximum_fusion.key_ref
  10.9 0.7 add_bitcast_fusion
  11.6 1.0 copy-done.2
  12.6 1.2 copy-done.4
  13.9 1.0 copy-done.5
  14.9 116.0 %gather_all.1 = (bf16[4,2,2,2,64,1024]{5,4,3,2,1,0:T(8,128)(2,1)S(1)}, bf16[4,2,2,2,64,384]{5,4,3,2,1,0:T(8,128)(2,1)S(1)}, bf16[2,2,128,2048]{3,2,1,0:T(8,128)(...) custom-call(bf16[64,8448]{1,0:T(8,128)(2,1)S(1)} %copy-done.4, ...), custom_call_target="tpu_custom_call" | custom-call | tf_op jit(solution)/shard_map/gather_all/pallas_call | solution.py:671
  130.9 2.3 fusion.16.key_ref.key_in_ref
  133.3 4.5 %fusion.15.proj_ref = f32[1024,1024]{1,0:T(8,128)S(1)} fusion(bf16[1024,2048]{1,0:T(8,128)(2,1)S(1)} %bitcast.65, bf16[2048,1024]{1,0:T(8,128)(2,1)S(1)} %bitcast.79), kind=kOutput, calls=%fused_computation.50 | convolution fusion | flops 4294967296 | bytes 12582912 | tf_op jit(solution)/shard_map/dot_general | solution.py:26
  137.8 2.4 fusion.17.grad_ref
  140.4 13.7 %mixer_forward.1 = (bf16[1024,512]{1,0:T(8,128)(2,1)S(1)}, bf16[1024,256]{1,0:T(8,128)(2,1)S(1)}, f32[1024,512]{1,0:T(8,128)S(1)}, f32[1024,256]{1,0:T(8,128)S(1...) custom-call(s32[2,8]{1,0:T(2,128)S(1)} %bitcast.74, ...), custom_call_target="tpu_custom_call" | custom-call | flops 536870912 | bytes 12582912 | tf_op jit(solution)/shard_map/mixer_forward/pallas_call | solution.py:351
  154.1 7.5 %cube_total.1.sums_ref = f32[16,128]{1,0:T(8,128)S(1)} custom-call(f32[16,128]{1,0:T(8,128)S(1)} %get-tuple-element.54.part_ref), custom_call_target="tpu_custom_call" | custom-call | tf_op jit(solution)/shard_map/cube_total/pallas_call | solution.py:706
  161.5 26.2 %mixer_backward.1 = (bf16[1024,512]{1,0:T(8,128)(2,1)S(1)}, bf16[1024,1024]{1,0:T(8,128)(2,1)S(1)}, bf16[1024,384]{1,0:T(8,128)(2,1)S(1)}, f32[8,512]{1,0:T(8,12...) custom-call(s32[2,8]{1,0:T(2,128)S(1)} %bitcast.75, f32[1024,1024]{1,0:T(8,128)S(1)} %fusion.15.proj_ref, ...), custom_call_target="tpu_custom_call" | custom-call | flops 1610612736 | bytes 15728640 | tf_op jit(solution)/shard_map/mixer_backward/pallas_call | solution.py:383
  187.7 1.3 copy-done.11
  189.2 0.6 slice.115
  189.8 1.6 slice.99
  191.4 1.6 select_maximum_fusion.u_ref
  193.1 0.1 reduce_sum.38
  193.5 0.1 reshape_reshape.3
  193.6 7.2 %fusion.18 = f32[1024,2048]{1,0:T(8,128)S(1)} fusion(bf16[1024,1024]{1,0:T(8,128)(2,1)} %copy-done.11, bf16[2048,1024]{1,0:T(8,128)(2,1)} %bitcast.80), kind=kOutput, calls=%fused_computation.53 | convolution fusion | flops 4294967296 | bytes 14680064 | tf_op jit(solution)/shard_map/dot_general | solution.py:26
  200.8 4.5 %multiply_reduce_fusion = (f32[2048]{0:T(1024)S(1)}, bf16[1024,2048]{1,0:T(8,128)(2,1)}) fusion(bf16[2,4,128,2048]{3,2,1,0:T(8,128)(2,1)S(1)} %copy-done.1, f32[1024,2048]{1,0:T(8,128)S(1)} %fusion.18, bf16[1024,384]{1,0:T(8,128)(2,1)S(1)} %get-tuple-element.57, bf16[2048,384]{1,0:T(8,128)(2,1)S(1)} %bitcast.70), kind=kOutput, calls=%fused_computation | convolution fusion | flops 1621096448 | bytes 19144704 | tf_op jit(solution)/shard_map/dot_general | solution.py:26
  205.3 0.6 fusion.9.v_ref
  205.9 6.1 %convolution_convert_fusion.1 = bf16[2048,1024]{1,0:T(8,128)(2,1)} fusion(bf16[1024,2048]{1,0:T(8,128)(2,1)S(1)} %bitcast.66, bf16[1024,1024]{1,0:T(8,128)(2,1)S(1)} %copy-done.12), kind=kOutput, calls=%fused_computation.3 | convolution fusion | flops 4297064448 | bytes 10485760 | tf_op jit(solution)/shard_map/dot_general | solution.py:26
  212.0 3.8 %convolution_convert_fusion.2 = bf16[512,2048]{1,0:T(8,128)(2,1)} fusion(bf16[1024,512]{1,0:T(8,128)(2,1)S(1)} %get-tuple-element.55, bf16[1024,2048]{1,0:T(8,128)(2,1)S(1)} %bitcast.78), kind=kOutput, calls=%fused_computation.4 | convolution fusion | flops 2148532224 | bytes 7340032 | tf_op jit(solution)/shard_map/dot_general | solution.py:26
  215.8 3.6 convolution_convert_fusion.3
  219.4 4.3 %convolution_convert_fusion = bf16[1024,2048]{1,0:T(8,128)(2,1)} fusion(bf16[1024,512]{1,0:T(8,128)(2,1)S(1)} %get-tuple-element.55, bf16[512,2048]{1,0:T(8,128)(2,1)S(1)} %bitcast.82), kind=kOutput, calls=%fused_computation.2 | convolution fusion | flops 2149580800 | bytes 7340032 | tf_op jit(solution)/shard_map/dot_general | solution.py:26
  223.7 123.7 %scatter_all.1 = (f32[128,2048]{1,0:T(8,128)}, f32[128,2048]{1,0:T(8,128)}, bf16[64,8192]{1,0:T(8,128)(2,1)}, f32[128,2048]{1,0:T(8,128)}, f32[64,384]{1,0:T(8,1...) custom-call(bf16[2,4,128,2048]{3,2,1,0:T(8,128)(2,1)} %bitcast.85, bf16[2,4,128,2048]{3,2,1,0:T(8,128)(2,1)} %bitcast.83, ...), custom_call_target="tpu_custom_call" | custom-call | tf_op jit(solution)/shard_map/scatter_all/pallas_call | solution.py:927
  347.4 1.5 convert_element_type.53
  348.9 0.8 slice.103
  349.8 1.5 pad_maximum_fusion
  351.3 0.2 fusion.4
  351.5 1.5 fusion.7
  353.1 0.6 slice.105
  353.7 1.4 slice.104
  355.1 0.7 slice_reduce_fusion
  355.8 0.6 slice_bitcast_fusion
  356.4 0.6 slice_bitcast_fusion.1
  357.0 0.6 fusion.14
  357.6 1.0 copy.43
  (86 shorter events, 1.6 us)
Async XLA Ops:
  7.4 125.9 %copy-start.20 = (f32[128]{0:T(128)}, f32[128]{0:T(128)S(1)}, u32[]{:S(2)}) copy-start(f32[128]{0:T(128)S(1)} %fusion) | copy-start | bytes 1540
  11.6 1.0 copy-start.2
  12.6 1.2 copy-start.4
  13.9 1.0 copy-start.5
  130.9 2.4 copy-start
  130.9 6.9 %copy-start.8 = (bf16[4,2,2,2,64,1024]{5,4,3,2,1,0:T(8,128)(2,1)}, bf16[4,2,2,2,64,1024]{5,4,3,2,1,0:T(8,128)(2,1)S(1)}, u32[]{:S(2)}) copy-start(bf16[4,2,2,2,64,1024]{5,4,3,2,1,0:T(8,128)(2,1)S(1)} %get-tuple-element.42) | copy-start | bytes 12582916
  130.9 6.9 %copy-start.6 = (bf16[2,4,128,2048]{3,2,1,0:T(8,128)(2,1)}, bf16[2,4,128,2048]{3,2,1,0:T(8,128)(2,1)S(1)}, u32[]{:S(2)}) copy-start(bf16[2,4,128,2048]{3,2,1,0:T(8,128)(2,1)S(1)} %get-tuple-element.44) | copy-start | bytes 12582916
  130.9 6.9 %copy-start.9 = (bf16[2,2,128,2048]{3,2,1,0:T(8,128)(2,1)}, bf16[2,2,128,2048]{3,2,1,0:T(8,128)(2,1)S(1)}, u32[]{:S(2)}) copy-start(bf16[2,2,128,2048]{3,2,1,0:T(8,128)(2,1)S(1)} %get-tuple-element.45) | copy-start | bytes 6291460
  137.8 2.5 slice-start
  137.8 2.5 slice-start.1
  187.7 1.3 copy-start.11
  193.6 7.2 %copy-start.1 = (bf16[2,4,128,2048]{3,2,1,0:T(8,128)(2,1)S(1)}, bf16[2,4,128,2048]{3,2,1,0:T(8,128)(2,1)}, u32[]{:S(2)}) copy-start(bf16[2,4,128,2048]{3,2,1,0:T(8,128)(2,1)} %copy-done) | copy-start | bytes 12582916
  200.8 4.5 %copy-start.17 = (f32[2048]{0:T(1024)S(1)}, f32[2048]{0:T(1024)}, u32[]{:S(2)}) copy-start(f32[2048]{0:T(1024)} %param.18) | copy-start | bytes 24580
  200.8 5.1 %copy-start.12 = (bf16[1024,1024]{1,0:T(8,128)(2,1)S(1)}, bf16[1024,1024]{1,0:T(8,128)(2,1)}, u32[]{:S(2)}) copy-start(bf16[1024,1024]{1,0:T(8,128)(2,1)} %copy-done.11) | copy-start | bytes 6291460
  205.9 6.1 %copy-start.7 = (bf16[2,4,128,2048]{3,2,1,0:T(8,128)(2,1)S(1)}, bf16[2,4,128,2048]{3,2,1,0:T(8,128)(2,1)}, u32[]{:S(2)}) copy-start(bf16[2,4,128,2048]{3,2,1,0:T(8,128)(2,1)} %copy-done.6) | copy-start | bytes 12582916
  215.8 3.6 copy-start.10
  347.4 3.9 %copy-start.13 = (bf16[1,128,2048]{2,1,0:T(8,128)(2,1)S(1)}, bf16[1,128,2048]{2,1,0:T(8,128)(2,1)}, u32[]{:S(2)}) copy-start(bf16[1,128,2048]{2,1,0:T(8,128)(2,1)} %param.14) | copy-start | bytes 1572868
  347.4 3.9 %copy-start.14 = (f32[128,2048]{1,0:T(8,128)S(1)}, f32[128,2048]{1,0:T(8,128)}, u32[]{:S(2)}) copy-start(f32[128,2048]{1,0:T(8,128)} %get-tuple-element.62) | copy-start | bytes 3145732
  347.4 4.1 %copy-start.21 = (f32[128]{0:T(128)S(1)}, f32[128]{0:T(128)}, u32[]{:S(2)}) copy-start(f32[128]{0:T(128)} %copy-done.20) | copy-start | bytes 1540
  347.4 4.1 %copy-start.3 = (bf16[1,128,2048]{2,1,0:T(8,128)(2,1)S(1)}, bf16[1,128,2048]{2,1,0:T(8,128)(2,1)}, u32[]{:S(2)}) copy-start(bf16[1,128,2048]{2,1,0:T(8,128)(2,1)} %param.15) | copy-start | bytes 1572868
  347.4 4.1 %copy-start.16 = (f32[128,2048]{1,0:T(8,128)S(1)}, f32[128,2048]{1,0:T(8,128)}, u32[]{:S(2)}) copy-start(f32[128,2048]{1,0:T(8,128)} %get-tuple-element.61) | copy-start | bytes 3145732
  351.3 1.8 copy-start.18
  351.3 4.5 %copy-start.19 = (f32[56,128]{1,0:T(8,128)S(1)}, f32[56,128]{1,0:T(8,128)}, u32[]{:S(2)}) copy-start(f32[56,128]{1,0:T(8,128)} %get-tuple-element.63) | copy-start | bytes 86020
  351.3 6.3 %copy-start.15 = (f32[128,2048]{1,0:T(8,128)S(1)}, f32[128,2048]{1,0:T(8,128)}, u32[]{:S(2)}) copy-start(f32[128,2048]{1,0:T(8,128)} %get-tuple-element.99) | copy-start | bytes 3145732

commit v5 on v4

--- a/solution.py
+++ b/solution.py
@@ -96,8 +96,8 @@
 
 
 def forward_kernel(
-    meta_ref, proj_ref, key_ref, grad_ref, chan_ref, conv_k_ref, head_ref,
-    val_out, key_out, vsum_ref, ksum_ref, raw_ref, cum_ref, y_ref, state_ref, sums_ref,
+    meta_ref, proj_ref, grad_ref, chan_ref, conv_k_ref, head_ref,
+    val_out, key_out, vsum_ref, ksum_ref, raw_ref, cum_ref, y_ref, gated_ref, state_ref, sums_ref,
     state, last_v, last_k,
     *, span, heads,
 ):
@@ -121,12 +121,12 @@
             total = total + weight[at : at + 1] * (shift_down(rows, before, by) * lags[by - 1])
         return total
 
-    rows_v = proj_ref[:, inner:].astype(bf16).astype(f32)
+    rows_v = proj_ref[:, inner : 2 * inner].astype(bf16).astype(f32)
     vsum = convolve(rows_v, last_v[...], chan_ref[:CONV, :], chan_ref[CONV : CONV + 1, :])
     last_v[...] = rows_v[CHUNK - 8 :]
     vsum_ref[...] = vsum
     val_out[...] = (vsum * jax.nn.sigmoid(vsum)).astype(bf16)
-    rows_k = key_ref[:, :KEYS].astype(bf16).astype(f32)
+    rows_k = proj_ref[:, 2 * inner : 2 * inner + KEYS].astype(bf16).astype(f32)
     ksum = convolve(rows_k, last_k[...], conv_k_ref[:CONV, :], conv_k_ref[CONV : CONV + 1, :])
     last_k[...] = rows_k[CHUNK - 8 :]
     ksum_ref[...] = ksum
@@ -136,7 +136,7 @@
     rows = iota((CHUNK, CHUNK), 0)
     cols = iota((CHUNK, CHUNK), 1)
     chosen = (rows == head_ref[2:3, :].astype(jnp.int32)).astype(f32)
-    raw = mm(key_ref[:, KEYS:], chosen, NN, exact) + head_ref[:1, :]
+    raw = mm(proj_ref[:, 2 * inner + KEYS :], chosen, NN, exact) + head_ref[:1, :]
     raw_ref[...] = raw
     dt = jax.nn.softplus(raw)
     cum = mm((rows >= cols).astype(f32), -dt * head_ref[1:2, :], NN, exact)
@@ -180,25 +180,29 @@
         )
         gate = proj_ref[:, lanes]
         gated = y * (gate * jax.nn.sigmoid(gate))
+        gated_ref[:, lanes] = gated
         square = square + gated * gated
         cross = cross + gated * (grad_ref[:, lanes] * chan_ref[5:6, lanes])
-    sums_ref[pl.ds(i, 1), :] = jnp.sum(square.T, axis=0, keepdims=True)
-    sums_ref[pl.ds(chunks + i, 1), :] = jnp.sum(cross.T, axis=0, keepdims=True)
+    share = 1.0 / (count * P_SIZE)
+    sums_ref[pl.ds(i, 1), :] = jnp.sum(square.T, axis=0, keepdims=True) * share
+    sums_ref[pl.ds(chunks + i, 1), :] = jnp.sum(cross.T, axis=0, keepdims=True) * share
 
 
 def backward_kernel(
-    meta_ref, proj_ref, key_in_ref, grad_ref, chan_ref, conv_k_ref, head_ref,
-    val_ref, key_ref, vsum_ref, ksum_ref, raw_ref, cum_ref, y_ref, state_ref, sums_ref,
-    mixed_ref, cols_ref, key_cols_ref, chan_sums, key_sums, head_sums,
-    dstate, dv, next_v, next_k, next_lags,
-    *, span, heads,
+    meta_ref, proj_ref, grad_ref, chan_ref, conv_k_ref, head_ref,
+    val_ref, key_ref, vsum_ref, ksum_ref, raw_ref, cum_ref, y_ref, state_ref, sums_ref, branch_ref, go_ref,
+    cols_ref, chan_sums, key_sums, head_sums, b_out, o_out,
+    dstate, dv, next_v, next_k, next_lags, *early_refs,
+    span, heads,
 ):
     chunks = pl.num_programs(0)
     i = chunks - 1 - pl.program_id(0)
     inner = heads * P_SIZE
+    early = Early(branch_ref, go_ref, (b_out, o_out) + early_refs)
 
     @pl.when(pl.program_id(0) == 0)
     def _():
+        early.start()
         for ref in (dstate, next_v, next_k, next_lags, chan_sums, key_sums, head_sums):
             ref[...] = jnp.zeros_like(ref)
 
@@ -210,13 +214,12 @@
     cum = cum_ref[...]
     cum_t = cum.T
     count = docs.count.astype(f32)
-    head_total = count * P_SIZE
 
     def column(row):
         return jnp.broadcast_to(row, (CHUNK, CHUNK)).T
 
-    inv = lax.rsqrt(column(sums_ref[pl.ds(i, 1), :]) / head_total + epsilon)
-    pull = inv * inv * inv * column(sums_ref[pl.ds(chunks + i, 1), :]) / head_total
+    inv = lax.rsqrt(column(sums_ref[pl.ds(i, 1), :]) + epsilon)
+    pull = inv * inv * inv * column(sums_ref[pl.ds(chunks + i, 1), :])
 
     bias = jnp.where((docs.doc == docs.row()) & (cols >= rows), 0.0, -1e30)
     carry_w = docs.flow() * jnp.exp(cum)
@@ -247,7 +250,6 @@
         norm_gain = chan_ref[5:6, lanes]
         gm = grad_ref[:, lanes]
         unit = gated * inv
-        mixed_ref[:, lanes] = (unit * norm_gain).astype(bf16)
         chan_sums[5:6, lanes] += jnp.sum(gm * unit, axis=0, keepdims=True)
         grad_gated = inv * (gm * norm_gain) - pull * gated
         cols_ref[:, lanes] = (grad_gated * masked * silu_slope(gate, sig)).astype(bf16)
@@ -314,7 +316,7 @@
     head_sums[:1, :] += jnp.sum(grad_step, axis=0, keepdims=True)
     head_sums[1:2, :] -= jnp.sum(dt * rate * dlog, axis=0, keepdims=True)
     chosen = (rows == head_ref[2:3, :].astype(jnp.int32)).astype(bf16)
-    key_cols_ref[:, KEYS:] = mm(grad_step.astype(bf16), chosen, NT).astype(bf16)
+    cols_ref[:, 2 * inner + KEYS :] = mm(grad_step.astype(bf16), chosen, NT).astype(bf16)
 
     lags = [docs.lag(by) for by in range(1, CONV)]
 
@@ -331,17 +333,25 @@
         after[...] = dconv[:8]
         return grad_in.astype(bf16)
 
-    rows_v = proj_ref[:, inner:].astype(bf16).astype(f32)
-    cols_ref[:, inner:] = convolve_back(dv[...], vsum_ref[...], rows_v, next_v, chan_ref[:CONV, :], chan_sums)
-    rows_k = key_in_ref[:, :KEYS].astype(bf16).astype(f32)
-    key_cols_ref[:, :KEYS] = convolve_back(
+    rows_v = proj_ref[:, inner : 2 * inner].astype(bf16).astype(f32)
+    cols_ref[:, inner : 2 * inner] = convolve_back(dv[...], vsum_ref[...], rows_v, next_v, chan_ref[:CONV, :], chan_sums)
+    rows_k = proj_ref[:, 2 * inner : 2 * inner + KEYS].astype(bf16).astype(f32)
+    cols_ref[:, 2 * inner : 2 * inner + KEYS] = convolve_back(
         dkeys, ksum_ref[...], rows_k, next_k, conv_k_ref[:CONV, :], key_sums
     )
     for by in range(1, CONV):
         next_lags[:, by - 1 : by] = lags[by - 1][:8]
 
-
-def mixer_forward(meta, projected, key_out, grad_mixed, chan, conv_k, head_vec, span, heads):
+    @pl.when(pl.program_id(0) == 1)
+    def _():
+        early.middle()
+
+    @pl.when(pl.program_id(0) == chunks - 1)
+    def _():
+        early.end()
+
+
+def mixer_forward(meta, projected, grad_mixed, chan, conv_k, head_vec, span, heads):
     length = projected.shape[0]
     inner = heads * P_SIZE
     chunks = length // CHUNK
@@ -352,31 +362,37 @@
         partial(forward_kernel, span=span, heads=heads),
         grid=(chunks,),
         in_specs=[
-            pl.BlockSpec(memory_space=pltpu.SMEM), row(2 * inner), row(KEYS + STEP_PAD), row(inner),
+            pl.BlockSpec(memory_space=pltpu.SMEM), row(2 * inner + KEYS + STEP_PAD), row(inner),
             all_of(8, inner), all_of(8, KEYS), all_of(8, LANES),
         ],
         out_specs=[
-            row(inner), row(KEYS), row(inner), row(KEYS), row(LANES), row(LANES), row(inner),
+            row(inner), row(KEYS), row(inner), row(KEYS), row(LANES), row(LANES), row(inner), row(inner),
             pl.BlockSpec((1, N, inner), lambda i: (i, 0, 0)), all_of(2 * chunks, LANES),
         ],
         out_shape=[
             out(inner, bf16), out(KEYS, bf16), out(inner, f32), out(KEYS, f32), out(LANES, f32), out(LANES, f32),
-            out(inner, f32), jax.ShapeDtypeStruct((chunks, N, inner), bf16),
+            out(inner, f32), out(inner, f32), jax.ShapeDtypeStruct((chunks, N, inner), bf16),
             jax.ShapeDtypeStruct((2 * chunks, LANES), f32),
         ],
         scratch_shapes=[pltpu.VMEM((N, inner), f32), pltpu.VMEM((8, inner), f32), pltpu.VMEM((8, KEYS), f32)],
-        compiler_params=pltpu.CompilerParams(vmem_limit_bytes=32 * 2**20),
+        compiler_params=pltpu.CompilerParams(vmem_limit_bytes=16 * 2**20),
         cost_estimate=pl.CostEstimate(
             flops=length * inner * 1024, bytes_accessed=length * inner * 24, transcendentals=length * heads * CHUNK
         ),
         name="mixer_forward",
-    )(meta, projected, key_out, grad_mixed, chan, conv_k, head_vec)
-
-
-def mixer_backward(meta, projected, key_out, grad_mixed, chan, conv_k, head_vec, kept, sums, span, heads):
+    )(meta, projected, grad_mixed, chan, conv_k, head_vec)
+
+
+def mixer_backward(meta, projected, grad_mixed, chan, conv_k, head_vec, kept, sums, branch, grad_out, span, heads):
     length = projected.shape[0]
     inner = heads * P_SIZE
     chunks = length // CHUNK
+    me = Place()
+    near, peers, tokens, width = branch.shape
+    far = me.far
+    part = grad_out.shape[2:]
+    copies = near * peers // 2 + 2 * far - 1
+    vm = lambda *shape: pltpu.VMEM(shape, bf16)
     row = lambda width: pl.BlockSpec((CHUNK, width), lambda i: (chunks - 1 - i, 0))
     all_of = lambda *shape: pl.BlockSpec(shape, lambda i: (0,) * len(shape))
     out = lambda width: jax.ShapeDtypeStruct((length, width), bf16)
@@ -384,28 +400,33 @@
         partial(backward_kernel, span=span, heads=heads),
         grid=(chunks,),
         in_specs=[
-            pl.BlockSpec(memory_space=pltpu.SMEM), row(2 * inner), row(KEYS + STEP_PAD), row(inner),
+            pl.BlockSpec(memory_space=pltpu.SMEM), row(2 * inner + KEYS + STEP_PAD), row(inner),
             all_of(8, inner), all_of(8, KEYS), all_of(8, LANES),
             row(inner), row(KEYS), row(inner), row(KEYS), row(LANES), row(LANES), row(inner),
-            pl.BlockSpec((1, N, inner), lambda i: (chunks - 1 - i, 0, 0)), all_of(2 * chunks, LANES),
+            pl.BlockSpec((1, N, inner), lambda i: (chunks - 1 - i, 0, 0)), all_of(2 * chunks, LANES), HBM, HBM,
         ],
         out_specs=[
-            row(inner), row(2 * inner), row(KEYS + STEP_PAD), all_of(8, inner), all_of(8, KEYS), all_of(8, LANES),
+            row(2 * inner + KEYS + STEP_PAD), all_of(8, inner), all_of(8, KEYS), all_of(8, LANES),
+            VMEM, VMEM,
         ],
         out_shape=[
-            out(inner), out(2 * inner), out(KEYS + STEP_PAD), jax.ShapeDtypeStruct((8, inner), f32),
+            out(2 * inner + KEYS + STEP_PAD), jax.ShapeDtypeStruct((8, inner), f32),
             jax.ShapeDtypeStruct((8, KEYS), f32), jax.ShapeDtypeStruct((8, LANES), f32),
+            jax.ShapeDtypeStruct((near, peers // 2, tokens, width), bf16), jax.ShapeDtypeStruct(part, f32),
         ],
         scratch_shapes=[
             pltpu.VMEM((N, inner), f32), pltpu.VMEM((CHUNK, inner), f32), pltpu.VMEM((8, inner), f32),
             pltpu.VMEM((8, KEYS), f32), pltpu.VMEM((8, LANES), f32),
-        ],
-        compiler_params=pltpu.CompilerParams(vmem_limit_bytes=32 * 2**20),
+            vm(near, peers // 2, tokens, width), vm(near, peers // 2, tokens, width),
+            vm(far, *part), vm(far, *part), vm(max(far - 1, 1), *part),
+        ]
+        + sems(copies, near * peers // 2 + far),
+        compiler_params=remote_params(3, 32),
         cost_estimate=pl.CostEstimate(
             flops=length * inner * 3072, bytes_accessed=length * inner * 30, transcendentals=length * heads * CHUNK
         ),
         name="mixer_backward",
-    )(meta, projected, key_out, grad_mixed, chan, conv_k, head_vec, *kept, sums)
+    )(meta, projected, grad_mixed, chan, conv_k, head_vec, *kept, sums, branch, grad_out)
 
 
 MESH = pl.DeviceIdType.MESH
@@ -470,20 +491,27 @@
         self.sent, self.kept = 0, 0
         self.open = []
 
-    def put(self, src, dst, device):
+    def plan(self, src, dst, device):
         copy = pltpu.make_async_remote_copy(
             src_ref=src, dst_ref=dst, send_sem=self.send.at[self.sent], recv_sem=self.recv.at[self.sent],
             device_id=device, device_id_type=MESH,
         )
-        copy.start()
         self.sent += 1
         self.open.append(copy)
         return copy
 
+    def put(self, src, dst, device):
+        copy = self.plan(src, dst, device)
+        copy.start()
+        return copy
+
+    def plan_keep(self, src, dst):
+        self.kept += 1
+        return pltpu.make_async_copy(src, dst, self.local.at[self.kept - 1])
+
     def keep(self, src, dst):
-        copy = pltpu.make_async_copy(src, dst, self.local.at[self.kept])
+        copy = self.plan_keep(src, dst)
         copy.start()
-        self.kept += 1
         return copy
 
     def close(self):
@@ -522,10 +550,12 @@
 
 def gather_kernel(
     in_ref, key_ref, out_ref, rows_ref, cot_ref, meta_ref,
-    w_ref, k_ref, o_ref, x_ref, ct_ref, m_ref, send, recv, local,
+    w_ref, o_ref, x_ref, ct_ref, m_ref, send, recv, local,
 ):
     me = Place()
     s, zl, zh, c = me.s, me.zl, me.zh, me.c
+    columns = w_ref.shape[-1] - key_ref.shape[-1]
+    mine, shared = pl.ds(0, columns), pl.ds(columns, key_ref.shape[-1])
     cube, far, sibling = me.partners()
     greet(cube + far + sibling)
     mover = Mover(send, recv, local)
@@ -561,14 +591,14 @@
             copy.wait_recv()
 
     def key_path():
-        block = k_ref.at[s, zh, zl, c]
+        block = w_ref.at[s, zh, zl, c, :, shared]
         own = mover.keep(key_ref, block)
         copies = [mover.put(key_ref, block, me.at(zh=o)) for o in range(1, me.far)]
         yield
         own.wait()
         for copy in copies:
             copy.wait_recv()
-        block = k_ref.at[s, :, zl, c]
+        block = w_ref.at[s, :, zl, c, :, shared]
         copies = [mover.put(block, block, me.at(zl=o)) for o in range(1, me.near)]
         yield
         for copy in copies:
@@ -577,13 +607,13 @@
         for bit in bits:
             copies = []
             for h in held:
-                block = k_ref.at[flip(s, h), :, :, c]
+                block = w_ref.at[flip(s, h), :, :, c, :, shared]
                 copies.append(mover.put(block, block, me.at(s=bit)))
             held = held + [h ^ bit for h in held]
             yield
             for copy in copies:
                 copy.wait_recv()
-        block = k_ref.at[:, :, :, c]
+        block = w_ref.at[:, :, :, c, :, shared]
         copy = mover.put(block, block, me.at(c=1))
         yield
         copy.wait_recv()
@@ -611,7 +641,7 @@
         for step in range(me.peers):
             for o in range(me.near):
                 to_s, to_zl = flip(s, step), flip(zl, o)
-                for src, dst in me.column_runs(to_s, to_zl, w_ref.shape[-1]):
+                for src, dst in me.column_runs(to_s, to_zl, columns):
                     src = in_ref.at[:, src]
                     dst = w_ref.at[s, zh, zl, c, :, dst]
                     if step or o:
@@ -627,13 +657,13 @@
                     copy.wait()
                 else:
                     copy.wait_recv()
-            block = w_ref.at[flip(s, step), zh, :, c]
+            block = w_ref.at[flip(s, step), zh, :, c, :, mine]
             copies = [(o, mover.put(block, block, me.at(zh=o))) for o in range(1, me.far)]
             pieces.append((step, copies, mover.put(block, block, me.at(c=1))))
         last = []
         for step, copies, first in pieces:
             last.append(first)
-            last += yield from spread_path(copies, lambda h, step=step: w_ref.at[flip(s, step), h, :, c])
+            last += yield from spread_path(copies, lambda h, step=step: w_ref.at[flip(s, step), h, :, c, :, mine])
         yield
         for copy in last:
             copy.wait_recv()
@@ -671,22 +701,21 @@
     return pl.pallas_call(
         gather_kernel,
         out_shape=[
-            shape((peers, far, near, 2), (in_w.shape[0], columns)),
-            shape((peers, far, near, 2), keys.shape),
+            shape((peers, far, near, 2), (in_w.shape[0], columns + keys.shape[1])),
             shape((far, 2), out_w.shape),
             shape((near, peers), rows.shape),
             shape((near, peers), cot.shape),
             jax.ShapeDtypeStruct((near,) + meta.shape, meta.dtype),
         ],
         in_specs=[HBM] * 6,
-        out_specs=[HBM] * 6,
+        out_specs=[HBM] * 5,
         scratch_shapes=sems(copies, runs + 5),
         compiler_params=remote_params(0, 4),
         name="gather_all",
     )(in_w, keys, out_w, rows, cot, meta)
 
 
-def total_kernel(part_ref, sum_ref, box, send, recv, local):
+def total_kernel(part_ref, gated_ref, chan_ref, sum_ref, mixed_ref, box, send, recv, local):
     me = Place()
     cube = me.partners()[0]
     greet(cube)
@@ -697,21 +726,32 @@
         copy.wait_recv()
         total = total + box[i]
     sum_ref[...] = total
+    chunks = part_ref.shape[0] // 2
+
+    def step(i, carry):
+        at = pl.ds(pl.multiple_of(i * CHUNK, CHUNK), CHUNK)
+        inv = lax.rsqrt(jnp.broadcast_to(sum_ref[pl.ds(i, 1), :], (CHUNK, CHUNK)).T + epsilon)
+        for lane in range(0, gated_ref.shape[1], LANES):
+            lanes = slice(lane, lane + LANES)
+            mixed_ref[at, lanes] = (gated_ref[at, lanes] * inv * chan_ref[5:6, lanes]).astype(bf16)
+        return carry
+
+    lax.fori_loop(0, chunks, step, 0)
     mover.close()
 
 
-def cube_total(part):
+def cube_total(part, gated, chan):
     me = Place()
     count = me.peers * me.near - 1
     return pl.pallas_call(
         total_kernel,
-        out_shape=jax.ShapeDtypeStruct(part.shape, f32),
-        in_specs=[VMEM],
-        out_specs=VMEM,
+        out_shape=[jax.ShapeDtypeStruct(part.shape, f32), jax.ShapeDtypeStruct(gated.shape, bf16)],
+        in_specs=[VMEM] * 3,
+        out_specs=[VMEM] * 2,
         scratch_shapes=[pltpu.VMEM((count,) + part.shape, f32)] + sems(count, 1),
-        compiler_params=remote_params(1, 4),
+        compiler_params=remote_params(1, 12),
         name="cube_total",
-    )(part)
+    )(part, gated, chan)
 
 
 def add_rows(out, parts):
@@ -734,9 +774,8 @@
 
 
 def scatter_kernel(
-    bp_ref, gn_ref, gw_ref, go_ref, gk_ref, v_ref, u_ref,
-    ob_ref, og_ref, ow_ref, oo_ref, ok_ref, ov_ref, ou_ref,
-    b_own, b_box, b_near, n_own, n_box, n_near, w_own, w_box, w_far, o_own, o_box, o_far,
+    gn_ref, gw_ref, b_ref, v_ref, u_ref, og_ref, ow_ref, ob_ref, ok_ref, ov_ref, ou_ref,
+    n_own, n_box, n_near, b_own, b_box, b_near, w_own, w_box, w_far,
     k_own, k_box, k_near, k_far, k_bits, v_box, u_box, send, recv, local,
 ):
     me = Place()
@@ -745,17 +784,24 @@
     greet(cube + far + sibling)
     mover = Mover(send, recv, local)
     bits = bits_of(me.peers)
-
-    def rows_path(src, own, box, near_box, out, order, near, arrivals):
+    columns = w_own.shape[-1]
+    mine, shared = pl.ds(0, columns), pl.ds(columns, k_own.shape[-1])
+
+    def rows_path(src, own, box, near_box, out, order, near, arrivals, done=0):
         own, box = own.at[near], box.at[near]
-        at_zl = src.at[flip(zl, near)]
-        todo = combos(order[1:])
         copies, loads = [], []
-        for j, o in enumerate(todo):
-            copies.append(mover.put(at_zl.at[flip(s, order[0] ^ o)], box.at[j], me.at(s=order[0])))
-            loads.append(mover.keep(at_zl.at[flip(s, o)], own.at[j]))
+        if done:
+            half = me.peers // 4
+            for j in range(half):
+                copies.append(mover.put(src.at[near, j], box.at[j], me.at(s=order[1])))
+                loads.append(mover.keep(src.at[near, half + j], own.at[half + j]))
+        else:
+            at_zl = src.at[flip(zl, near)]
+            for j, o in enumerate(combos(order[1:])):
+                copies.append(mover.put(at_zl.at[flip(s, order[0] ^ o)], box.at[j], me.at(s=order[0])))
+                loads.append(mover.keep(at_zl.at[flip(s, o)], own.at[j]))
         base = 0
-        for i, bit in enumerate(order):
+        for i in range(done, len(order)):
             rest = order[i + 1 :]
             count = 1 << len(rest)
             offset = (1 << (len(order) - 1)) - count
@@ -763,7 +809,7 @@
             for j in range(count):
                 yield
                 copies[j].wait_recv()
-                if i == 0:
+                if i == done:
                     loads[j].wait()
                 if rest or near:
                     add_rows(own.at[offset + j], [own.at[offset + j], box.at[base + j]])
@@ -786,8 +832,8 @@
         order = [(o, k) for o in range(1, me.far) for k in range(me.peers)] + [(0, k) for k in range(me.peers)]
         loads, copies = {}, {}
         for o, k in order:
-            copies[o, k] = mover.put(gw_ref.at[flip(s, k), flip(zh, o), :, 1 - c], w_box.at[o, k], me.at(c=1))
-            loads[o, k] = mover.keep(gw_ref.at[flip(s, k), flip(zh, o), :, c], w_own.at[o, k])
+            copies[o, k] = mover.put(gw_ref.at[flip(s, k), flip(zh, o), :, 1 - c, :, mine], w_box.at[o, k], me.at(c=1))
+            loads[o, k] = mover.keep(gw_ref.at[flip(s, k), flip(zh, o), :, c, :, mine], w_own.at[o, k])
         far_copies = {}
         for o, k in order:
             yield
@@ -804,8 +850,8 @@
             parts = [w_own.at[0, k], w_box.at[0, k]] + [w_far.at[o - 1, k] for o in range(1, me.far)]
             add_rows(w_own.at[0, k], parts)
             for o in range(me.near):
-                for whole, mine in me.column_runs(s, zl, w_own.shape[-1]):
-                    src = w_own.at[0, k, flip(zl, o), :, mine]
+                for whole, part in me.column_runs(s, zl, columns):
+                    src = w_own.at[0, k, flip(zl, o), :, part]
                     if k or o:
                         ends.append(mover.put(src, ow_ref.at[:, whole], me.at(s=k, zl=o)))
                     else:
@@ -816,32 +862,12 @@
         for copy in ends:
             copy.wait_recv()
 
-    def out_path():
-        order = list(range(1, me.far)) + [0]
-        copies, loads = {}, {}
-        for o in order:
-            copies[o] = mover.put(go_ref.at[flip(zh, o), 1 - c], o_box.at[o], me.at(c=1))
-            loads[o] = mover.keep(go_ref.at[flip(zh, o), c], o_own.at[o])
-        yield
-        far_copies = {}
-        for o in order:
-            loads[o].wait()
-            copies[o].wait_recv()
-            if o:
-                add_rows(o_own.at[o], [o_own.at[o], o_box.at[o]])
-                far_copies[o] = mover.put(o_own.at[o], o_far.at[o - 1], me.at(zh=o))
-        for _ in range(2 * me.peers + 4):
-            yield
-        for o in range(1, me.far):
-            far_copies[o].wait_recv()
-        add_rows(oo_ref, [o_own.at[0], o_box.at[0]] + [o_far.at[o - 1] for o in range(1, me.far)])
-
     def key_path():
         blocks = combos(bits)
         copies, loads = [], []
         for j, o in enumerate(blocks):
-            copies.append(mover.put(gk_ref.at[flip(s, o), :, :, 1 - c], k_box.at[j], me.at(c=1)))
-            loads.append(mover.keep(gk_ref.at[flip(s, o), :, :, c], k_own.at[j]))
+            copies.append(mover.put(gw_ref.at[flip(s, o), :, :, 1 - c, :, shared], k_box.at[j], me.at(c=1)))
+            loads.append(mover.keep(gw_ref.at[flip(s, o), :, :, c, :, shared], k_own.at[j]))
         half = me.peers // 2
         sent = []
         for j in range(me.peers):
@@ -891,64 +917,110 @@
         for _, box, out in pairs:
             out[...] = box[2 * len(turns)]
 
-    arrivals_n, arrivals_b = [], []
-    orders = (bits[::-1], bits)
-    grads = (gn_ref, n_own, n_box, n_near, og_ref, orders[0])
-    branch = (bp_ref, b_own, b_box, b_near, ob_ref, orders[1])
-    near_n = [rows_path(*grads, o, arrivals_n) for o in range(1, me.near)]
-    near_b = [rows_path(*branch, o, arrivals_b) for o in range(1, me.near)]
-    own_n, own_b = rows_path(*grads, 0, arrivals_n), rows_path(*branch, 0, arrivals_b)
-    near, own = near_n + near_b, [own_n, own_b]
-    weights, keys, small, outs = weight_path(), key_path(), small_path(), out_path()
-    turn([weights] + near + own + [keys, small, outs])
-    turn([weights] * (me.far * me.peers) + [outs, keys] * me.peers)
-    run_paths(near + [keys, small] + own + [weights, outs])
+    coming_n, coming_b = [], []
+    grads = (gn_ref, n_own, n_box, n_near, og_ref)
+    branch = (b_ref, b_own, b_box, b_near, ob_ref)
+    orders = lambda o: bits if o else bits[::-1]
+    near_n = [rows_path(*grads, orders(o), o, coming_n) for o in range(1, me.near)]
+    near_b = [rows_path(*branch, orders(o), o, coming_b, 1) for o in range(1, me.near)]
+    own_n = rows_path(*grads, orders(0), 0, coming_n)
+    own_b = rows_path(*branch, orders(0), 0, coming_b, 1)
+    weights, keys, small = weight_path(), key_path(), small_path()
+    turn([weights] + near_b + near_n + [own_n, keys, own_b, small])
+    turn([weights] * (me.far * me.peers) + [keys] * me.peers)
+    run_paths(near_b + near_n + [keys, small, own_b, own_n, weights])
     mover.close()
 
 
-def scatter(branch, grads, gw, go, gk, small, conv):
+def scatter(grads, gw, branch, small, conv):
     me = Place()
     peers, near, far = me.peers, me.near, me.far
-    tokens, width = branch.shape[2:]
+    tokens, width = grads.shape[2:]
     stages = len(bits_of(peers)) + len(bits_of(near)) + len(bits_of(far)) + 1
     vm = lambda *shape: pltpu.VMEM(shape, bf16)
     boxes = lambda part: pltpu.VMEM((2 * stages + 1,) + part.shape, f32)
-    rows_scratch = [
-        vm(near, peers // 2, tokens, width), vm(near, peers - 1, tokens, width), vm(max(near - 1, 1), tokens, width)
-    ]
-    block = gw.shape[2:3] + gw.shape[4:]
-    kblock = gk.shape[2:3] + gk.shape[4:]
-    oblock = go.shape[2:]
+    keys = KEYS + STEP_PAD
+    rows = gw.shape[4]
+    block = (near, rows, gw.shape[5] - keys)
+    kblock = (near, rows, keys)
     runs = 2 * (far if near > 1 else 1)
-    copies = 2 * (peers * near - 1) + (2 * far - 1) * peers + runs * (peers * near - 1) + 2 * far - 1
-    copies += 2 * peers - 1 + near - 1 + far - 1 + 2 * stages
-    kept = peers * near + far * peers + runs + far + peers
+    copies = peers * near - 1 + (2 * far - 1) * peers + runs * (peers * near - 1)
+    copies += 2 * peers - 1 + near - 1 + far - 1 + 2 * stages + peers // 2 * near - 1
+    kept = peers * near + far * peers + runs + peers + near * peers // 4
     same = lambda part: jax.ShapeDtypeStruct(part.shape, part.dtype)
     return pl.pallas_call(
         scatter_kernel,
         out_shape=[
             jax.ShapeDtypeStruct((tokens, width), f32),
+            jax.ShapeDtypeStruct((rows, 2 * E), bf16),
             jax.ShapeDtypeStruct((tokens, width), f32),
-            jax.ShapeDtypeStruct((block[1], 2 * E), bf16),
-            jax.ShapeDtypeStruct(oblock, f32),
-            jax.ShapeDtypeStruct(kblock[1:], f32),
+            jax.ShapeDtypeStruct((rows, keys), f32),
             same(small),
             same(conv),
         ],
-        in_specs=[HBM] * 5 + [VMEM] * 2,
-        out_specs=[VMEM, VMEM, HBM, VMEM, VMEM, VMEM, VMEM],
-        scratch_shapes=rows_scratch
-        + rows_scratch
-        + [vm(far, peers, *block), vm(far, peers, *block), vm(max(far - 1, 1), peers, *block)]
-        + [vm(far, *oblock), vm(far, *oblock), vm(max(far - 1, 1), *oblock)]
-        + [
+        in_specs=[HBM] * 3 + [VMEM] * 2,
+        out_specs=[VMEM, HBM, VMEM, VMEM, VMEM, VMEM],
+        scratch_shapes=[
+            vm(near, peers // 2, tokens, width), vm(near, peers - 1, tokens, width), vm(max(near - 1, 1), tokens, width),
+            vm(near, peers // 2, tokens, width), vm(near, peers // 2 - 1, tokens, width), vm(max(near - 1, 1), tokens, width),
+            vm(far, peers, *block), vm(far, peers, *block), vm(max(far - 1, 1), peers, *block),
             vm(peers, far, *kblock), vm(peers, far, *kblock), vm(max(near - 1, 1), far, *kblock[1:]),
             vm(max(far - 1, 1), *kblock[1:]), vm(peers - 1, far, *kblock), boxes(small), boxes(conv),
         ]
         + sems(copies, kept),
-        compiler_params=remote_params(2, 58),
+        compiler_params=remote_params(2, 40),
+        cost_estimate=pl.CostEstimate(flops=0, bytes_accessed=250 * 10**6, transcendentals=0),
         name="scatter_all",
-    )(branch, grads, gw, go, gk, small, conv)
+    )(grads, gw, branch, small, conv)
+
+
+class Early:
+    def __init__(self, b_ref, go_ref, refs):
+        self.b_out, self.o_out, self.b_own, self.b_box, self.o_own, self.o_box, self.o_far, send, recv, local = refs
+        me = self.me = Place()
+        mover = self.mover = Mover(send, recv, local)
+        bits = bits_of(me.peers)
+        self.rows, self.outs, self.far = [], [], []
+        for o in range(me.near):
+            order = bits if o else bits[::-1]
+            at_zl = b_ref.at[flip(me.zl, o)]
+            for j, left in enumerate(combos(order[1:])):
+                put = mover.plan(at_zl.at[flip(me.s, order[0] ^ left)], self.b_box.at[o, j], me.at(s=order[0]))
+                self.rows.append((put, mover.plan_keep(at_zl.at[flip(me.s, left)], self.b_own.at[o, j]), (o, j)))
+        for o in range(me.far):
+            put = mover.plan(go_ref.at[flip(me.zh, o), 1 - me.c], self.o_box.at[o], me.at(c=1))
+            self.outs.append((put, mover.plan_keep(go_ref.at[flip(me.zh, o), me.c], self.o_own.at[o])))
+        for o in range(1, me.far):
+            self.far.append(mover.plan(self.o_own.at[o], self.o_far.at[o - 1], me.at(zh=o)))
+
+    def start(self):
+        _, far, sibling = self.me.partners()
+        bits = bits_of(self.me.peers)
+        greet([self.me.at(s=bit) for bit in sorted({bits[0], bits[-1]})] + far + sibling)
+        for put, load in self.outs:
+            put.start()
+            load.start()
+        for put, load, _ in self.rows:
+            put.start()
+            load.start()
+
+    def middle(self):
+        for o, (put, load) in enumerate(self.outs):
+            load.wait()
+            put.wait_recv()
+            if o:
+                add_rows(self.o_own.at[o], [self.o_own.at[o], self.o_box.at[o]])
+                self.far[o - 1].start()
+
+    def end(self):
+        for put, load, at in self.rows:
+            load.wait()
+            put.wait_recv()
+            add_rows(self.b_out.at[at], [self.b_own.at[at], self.b_box.at[at]])
+        for put in self.far:
+            put.wait_recv()
+        add_rows(self.o_out, [self.o_own.at[0], self.o_box.at[0]] + [self.o_far.at[o] for o in range(self.me.far - 1)])
+        self.mover.close()
 
 
 def body(
@@ -985,9 +1057,8 @@
     inv_rms = lax.rsqrt(jnp.mean(seq_rows * seq_rows, axis=1, keepdims=True) + epsilon)
     normed = (seq_rows * inv_rms * pre_gain[None, :]).astype(bf16)
     meta = jnp.pad(jnp.concatenate([doc_lengths[0], head_width])[None], ((0, 7), (0, 123)))
-    in_w, key_w, out_w, normed, cot_all, meta = gather(in_weight, key_send, out_weight, normed, cot_rows, meta)
-    in_w = in_w.reshape(width, 2 * inner)
-    key_w = key_w.reshape(width, -1)
+    in_w, out_w, normed, cot_all, meta = gather(in_weight, key_send, out_weight, normed, cot_rows, meta)
+    in_w = in_w.reshape(width, -1)
     out_w = out_w.reshape(inner, width)
     normed = normed.reshape(length, width)
     cot_all = cot_all.reshape(length, width)
@@ -1011,19 +1082,18 @@
     head_vec = jnp.pad(head_vec, ((0, 5), (0, LANES - heads))) - jnp.where(jnp.arange(8) == 2, 1.0, 0.0)[:, None]
 
     projected = mm(normed, in_w, NN)
-    key_out = mm(normed, key_w, NN)
     grad_mixed = mm(cot_all, out_w, NT)
-    mixer_args = (meta, projected, key_out, grad_mixed, chan, conv_k, head_vec)
-    *kept, part = mixer_forward(*mixer_args, span, heads)
-    sums = cube_total(part)
-    mixed, grad_cols, key_cols, chan_sums, key_sums, head_sums = mixer_backward(
-        *mixer_args, kept, sums, span, heads
-    )
+    mixer_args = (meta, projected, grad_mixed, chan, conv_k, head_vec)
+    *kept, gated, states, part = mixer_forward(*mixer_args, span, heads)
+    sums, mixed = cube_total(part, gated, chan)
     branch = mm(mixed, out_w, NN).astype(bf16)
     grad_out = mm(mixed, cot_all, TN).astype(bf16)
+    grad_cols, chan_sums, key_sums, head_sums, branch, grad_out_weight = mixer_backward(
+        *mixer_args, (*kept, states), sums, branch.reshape(near, peers, tokens, width),
+        grad_out.reshape(far, 2, -1, width), span, heads,
+    )
     grad_in = mm(normed, grad_cols, TN).astype(bf16)
-    grad_keys = mm(normed, key_cols, TN).astype(bf16)
-    grad_normed = mm(grad_cols, in_w, NT) + mm(key_cols, key_w, NT)
+    grad_normed = mm(grad_cols, in_w, NT)
     grad_pre_gain = jnp.sum(grad_normed * normed.astype(f32), axis=0) / pre_gain
 
     grad_skip = jnp.sum(chan_sums[6].reshape(heads, P_SIZE), axis=1)
@@ -1032,14 +1102,10 @@
     small = jnp.concatenate([grad_pre_gain, chan_sums[5], head_sums.reshape(-1)])
     small = jnp.pad(small, (0, -small.shape[0] % 1024)).reshape(-1, 128)
     conv_sums = jnp.pad(jnp.concatenate([chan_sums[:5], key_sums[:5]], axis=1), ((0, 3), (0, 0)))
-    rows_of = lambda part: part.reshape(near, peers, tokens, width)
-    blocks = (peers, far, near, 2, rows)
-    branch, grad_normed, grad_in, grad_out_weight, grad_keys, small, conv_sums = scatter(
-        rows_of(branch),
-        rows_of(grad_normed.astype(bf16)),
-        grad_in.reshape(blocks + (2 * inner,)),
-        grad_out.reshape(far, 2, -1, width),
-        grad_keys.reshape(blocks + (KEYS + STEP_PAD,)),
+    grad_normed, grad_in, branch, grad_keys, small, conv_sums = scatter(
+        grad_normed.astype(bf16).reshape(near, peers, tokens, width),
+        grad_in.reshape(peers, far, near, 2, rows, -1),
+        branch,
         small,
         conv_sums,
     )

time: 359 us -> 322 us (0.90)
  Pallas kernels: 287 us -> 259 us
    pallas_call x1, Pallas kernels: 124 us -> 87.2 us  [scatter(): pl.pallas_call(scatter_kernel, out_shape=[jax.ShapeDtypeStruct((tokens, w...]
    pallas_call x1, Pallas kernels: 26.2 us -> 33.3 us  [mixer_backward(): pl.pallas_call(partial(backward_kernel, span=span, heads=heads), grid=(ch...]
    dot_general x9 -> x6, matrix products: 38.6 us -> 35.1 us  [mm(): lax.dot_general(a, b, (dims, ((), ())), precision=precision, preferred_el...]
where the time goes in v5:
time: 322 us; the launch traced here: 321 us
  Pallas kernels  259 us (80%)
  matrix products  35.1 us (11%)
  local copies, waits for them, and re-layouts  17.7 us (5%)
  other arithmetic  7.69 us (2%)
    pallas_call x1, Pallas kernels, gather(): pl.pallas_call(gather_kernel, out_shape=[shape((peers, far, near, 2), (in...  116 us
    pallas_call x1, Pallas kernels, scatter(): pl.pallas_call(scatter_kernel, out_shape=[jax.ShapeDtypeStruct((tokens, w...  87.2 us
    dot_general x6, matrix products, mm(): lax.dot_general(a, b, (dims, ((), ())), precision=precision, preferred_el...  35.1 us
    pallas_call x1, Pallas kernels, mixer_backward(): pl.pallas_call(partial(backward_kernel, span=span, heads=heads), grid=(ch...  33.3 us
    pallas_call x1, Pallas kernels, mixer_forward(): pl.pallas_call(partial(forward_kernel, span=span, heads=heads), grid=(chu...  13.6 us
    pallas_call x1, Pallas kernels, cube_total(): pl.pallas_call(total_kernel, out_shape=[jax.ShapeDtypeStruct(part.shape,...  8.65 us
    unnamed x28, local copies, waits for them, and re-layouts  6.46 us

profile of v5, /device:TPU:0, one launch (start us, length us, event | category | flops | bytes accessed | tf_op | source)
XLA Modules:
  0.0 321.0 jit_solution(7731385128511269506)
XLA Ops:
  0.7 0.8 slice.90
  1.7 0.7 broadcast_in_dim.52
  2.5 0.1 broadcast_in_dim.54
  2.6 0.1 concatenate.44
  2.7 0.7 slice.91
  3.5 0.7 concatenate.43
  4.3 0.1 concatenate.45
  4.4 0.7 exp.3
  5.1 0.1 stack.11
  5.2 0.7 stack.10
  6.0 0.1 reshape.164
  6.1 1.2 fusion
  7.4 1.2 fusion.2.rows_ref
  8.6 0.8 slice.88
  9.5 0.7 maximum_maximum_fusion.key_ref
  10.9 0.7 add_bitcast_fusion
  11.6 1.0 copy-done.1
  12.6 1.2 copy-done.3
  13.9 1.0 copy-done.4
  14.9 116.0 %gather_all.1 = (bf16[4,2,2,2,64,1408]{5,4,3,2,1,0:T(8,128)(2,1)S(1)}, bf16[2,2,128,2048]{3,2,1,0:T(8,128)(2,1)S(1)}, bf16[2,4,128,2048]{3,2,1,0:T(8,128)(2,1)S(...) custom-call(bf16[64,8448]{1,0:T(8,128)(2,1)S(1)} %copy-done.3, ...), custom_call_target="tpu_custom_call" | custom-call | tf_op jit(solution)/shard_map/gather_all/pallas_call | solution.py:701
  130.9 6.7 %fusion.15.proj_ref = f32[1024,1408]{1,0:T(8,128)S(1)} fusion(bf16[1024,2048]{1,0:T(8,128)(2,1)S(1)} %bitcast.68, bf16[2048,1408]{1,0:T(8,128)(2,1)S(1)} %bitcast.66), kind=kOutput, calls=%fused_computation.48 | convolution fusion | flops 5905580032 | bytes 15728640 | tf_op jit(solution)/shard_map/dot_general | solution.py:26
  137.6 2.4 fusion.16.grad_ref
  140.2 13.6 %mixer_forward.1 = (bf16[1024,512]{1,0:T(8,128)(2,1)S(1)}, bf16[1024,256]{1,0:T(8,128)(2,1)S(1)}, f32[1024,512]{1,0:T(8,128)S(1)}, f32[1024,256]{1,0:T(8,128)S(1...) custom-call(s32[2,8]{1,0:T(2,128)S(1)} %bitcast.63, ...), custom_call_target="tpu_custom_call" | custom-call | flops 536870912 | bytes 12582912 | tf_op jit(solution)/shard_map/mixer_forward/pallas_call | solution.py:361
  153.8 8.6 %cube_total.1 = (f32[16,128]{1,0:T(8,128)S(1)}, bf16[1024,512]{1,0:T(8,128)(2,1)S(1)}) custom-call(f32[16,128]{1,0:T(8,128)S(1)} %get-tuple-element.54.part_ref, f32[1024,512]{1,0:T(8,128)S(1)} %get-tuple-element.55.gated_ref, f32[8,512]{1,0:T(8,128)S(1)} %bitcast.60), custom_call_target="tpu_custom_call" | custom-call | tf_op jit(solution)/shard_map/cube_total/pallas_call | solution.py:746
  162.4 2.4 convolution_convert_fusion.2
  164.9 4.3 %convolution_convert_fusion.1 = bf16[1024,2048]{1,0:T(8,128)(2,1)} fusion(bf16[1024,512]{1,0:T(8,128)(2,1)S(1)} %get-tuple-element.57, bf16[512,2048]{1,0:T(8,128)(2,1)S(1)} %bitcast.73), kind=kOutput, calls=%fused_computation.2 | convolution fusion | flops 2149580800 | bytes 7340032 | tf_op jit(solution)/shard_map/dot_general | solution.py:26
  169.2 33.3 %mixer_backward.1 = (bf16[1024,1408]{1,0:T(8,128)(2,1)S(1)}, f32[8,512]{1,0:T(8,128)S(1)}, f32[8,256]{1,0:T(8,128)S(1)}, f32[8,128]{1,0:T(8,128)S(1)}, bf16[2,2,...) custom-call(s32[2,8]{1,0:T(2,128)S(1)} %bitcast.64, f32[1024,1408]{1,0:T(8,128)} %copy-done, ...), custom_call_target="tpu_custom_call" | custom-call | flops 1610612736 | bytes 15728640 | tf_op jit(solution)/shard_map/mixer_backward/pallas_call | solution.py:399
  202.5 1.6 copy-done.8
  204.3 0.5 copy-done.11
  205.0 0.1 reduce_sum.38
  205.1 0.1 concatenate.48
  205.2 0.1 concatenate.47
  205.4 0.1 reshape_reshape.3
  205.5 0.7 slice.114
  206.2 10.7 %multiply_reduce_fusion = (f32[2048]{0:T(1024)S(1)}, bf16[1024,2048]{1,0:T(8,128)(2,1)S(1)}) fusion(bf16[2,4,128,2048]{3,2,1,0:T(8,128)(2,1)} %copy-done.6, bf16[1024,1408]{1,0:T(8,128)(2,1)} %copy-done.8, bf16[2048,1408]{1,0:T(8,128)(2,1)} %bitcast.67), kind=kOutput, calls=%fused_computation | convolution fusion | flops 5913966592 | bytes 17047552 | tf_op jit(solution)/shard_map/dot_general | solution.py:26
  217.0 8.7 %convolution_convert_fusion = bf16[2048,1408]{1,0:T(8,128)(2,1)} fusion(bf16[1024,2048]{1,0:T(8,128)(2,1)S(1)} %bitcast.69, bf16[1024,1408]{1,0:T(8,128)(2,1)S(1)} %copy-done.9), kind=kOutput, calls=%fused_computation.1 | convolution fusion | flops 5908463616 | bytes 12845056 | tf_op jit(solution)/shard_map/dot_general | solution.py:26
  225.7 87.2 %scatter_all.1 = (f32[128,2048]{1,0:T(8,128)S(1)}, bf16[64,8192]{1,0:T(8,128)(2,1)S(1)}, f32[128,2048]{1,0:T(8,128)S(1)}, f32[64,384]{1,0:T(8,128)S(1)}, f32[56,128]{1,0:T(8,128)S(1)}, /*index=5*/f32[8,4352]{1,0:T(8,128)S(1)}) custom-call(bf16[2,4,128,2048]{3,2,1,0:T(8,128)(2,1)S(1)} %bitcast.56, bf16[4,2,2,2,64,1408]{5,4,3,2,1,0:T(8,128)(2,1)} %bitcast.74, ...), custom_call_target="tpu_custom_call" | custom-call | bytes 250000000 | tf_op jit(solution)/shard_map/scatter_all/pallas_call | solution.py:951
  312.9 0.1 convert_element_type.49
  313.1 1.5 pad_maximum_fusion
  314.6 0.2 fusion.4
  314.8 1.5 fusion.7
  316.4 0.6 slice.105
  317.0 0.6 slice.104
  317.6 0.7 slice_reduce_fusion
  318.3 0.6 slice_bitcast_fusion
  318.9 0.6 slice_bitcast_fusion.1
  319.5 0.6 fusion.14
  320.1 1.0 copy.43
  (65 shorter events, 1.2 us)
Async XLA Ops:
  11.6 1.0 copy-start.1
  12.6 1.2 copy-start.3
  13.9 1.0 copy-start.4
  130.9 6.7 %copy-start.5 = (bf16[4,2,2,2,64,1408]{5,4,3,2,1,0:T(8,128)(2,1)}, bf16[4,2,2,2,64,1408]{5,4,3,2,1,0:T(8,128)(2,1)S(1)}, u32[]{:S(2)}) copy-start(bf16[4,2,2,2,64,1408]{5,4,3,2,1,0:T(8,128)(2,1)S(1)} %get-tuple-element.43) | copy-start | bytes 17301508
  130.9 6.7 %copy-start.6 = (bf16[2,4,128,2048]{3,2,1,0:T(8,128)(2,1)}, bf16[2,4,128,2048]{3,2,1,0:T(8,128)(2,1)S(1)}, u32[]{:S(2)}) copy-start(bf16[2,4,128,2048]{3,2,1,0:T(8,128)(2,1)S(1)} %get-tuple-element.42) | copy-start | bytes 12582916
  137.6 2.6 copy-start
  137.6 2.5 slice-start
  137.6 2.5 slice-start.1
  202.5 1.6 copy-start.8
  204.2 0.6 copy-start.11
  206.2 10.7 %copy-start.12 = (f32[2048]{0:T(1024)S(1)}, f32[2048]{0:T(1024)}, u32[]{:S(2)}) copy-start(f32[2048]{0:T(1024)} %param.18) | copy-start | bytes 24580
  206.2 10.7 %copy-start.7 = (bf16[2,4,128,2048]{3,2,1,0:T(8,128)(2,1)S(1)}, bf16[2,4,128,2048]{3,2,1,0:T(8,128)(2,1)}, u32[]{:S(2)}) copy-start(bf16[2,4,128,2048]{3,2,1,0:T(8,128)(2,1)} %copy-done.6) | copy-start | bytes 12582916
  206.2 10.7 %copy-start.9 = (bf16[1024,1408]{1,0:T(8,128)(2,1)S(1)}, bf16[1024,1408]{1,0:T(8,128)(2,1)}, u32[]{:S(2)}) copy-start(bf16[1024,1408]{1,0:T(8,128)(2,1)} %copy-done.8) | copy-start | bytes 8650756
  312.9 1.7 copy-start.10
  312.9 1.9 copy-start.2

commit v6 on v5

--- a/solution.py
+++ b/solution.py
@@ -95,9 +95,45 @@
     return sig * (1.0 + v * (1.0 - sig))
 
 
+def own_parameters(chan_ref, head_ref, conv_ref, bias_ref, norm_ref, step_b_ref, decay_ref, skip_ref, heads):
+    me = Place()
+    inner = heads * P_SIZE
+    for whole, part in me.channel_runs(inner):
+        chan_ref[:CONV, part] = conv_ref[:, whole]
+        chan_ref[CONV : CONV + 1, part] = bias_ref[:, whole]
+        chan_ref[5:6, part] = norm_ref[:, whole]
+    ids = me.heads_at(iota((1, inner), 1), P_SIZE, inner)
+    chosen = (iota((H, inner), 0) == ids).astype(f32)
+    chan_ref[6:7, :] = mm(jnp.broadcast_to(skip_ref[...], (8, H)), chosen, NN, exact)[:1]
+    chan_ref[7:8, :] = ids.astype(f32)
+    lanes = iota((1, LANES), 1)
+    ids = jnp.where(lanes < heads, me.heads_at(lanes, 1, heads), -1)
+    chosen = (iota((H, LANES), 0) == ids).astype(f32)
+    head_ref[...] = jnp.zeros_like(head_ref)
+    head_ref[:1, :] = mm(jnp.broadcast_to(step_b_ref[...], (8, H)), chosen, NN, exact)[:1]
+    head_ref[1:2, :] = mm(jnp.broadcast_to(jnp.exp(decay_ref[...]), (8, H)), chosen, NN, exact)[:1]
+    head_ref[2:3, :] = ids.astype(f32)
+
+
+def whole_sums(out_ref, chan_sums, key_sums, head_sums, head_ref, chan_ref, heads):
+    me = Place()
+    inner = heads * P_SIZE
+    out_ref[...] = jnp.zeros_like(out_ref)
+    for whole, part in me.channel_runs(inner):
+        out_ref[:6, whole] = chan_sums[:6, part]
+    out_ref[:5, E:] = key_sums[:5, :]
+    chosen = (iota((H, LANES), 0) == head_ref[2:3, :].astype(jnp.int32)).astype(f32)
+    steps = mm(head_sums[...], chosen, NT, exact)
+    chosen = (iota((H, inner), 0) == chan_ref[7:8, :].astype(jnp.int32)).astype(f32)
+    skips = mm(chan_sums[...], chosen, NT, exact)
+    out_ref[7:8, :H] = steps[:1]
+    out_ref[7:8, LANES : LANES + H] = steps[1:2]
+    out_ref[7:8, 2 * LANES : 2 * LANES + H] = skips[6:7]
+
+
 def forward_kernel(
-    meta_ref, proj_ref, grad_ref, chan_ref, conv_k_ref, head_ref,
-    val_out, key_out, vsum_ref, ksum_ref, raw_ref, cum_ref, y_ref, gated_ref, state_ref, sums_ref,
+    meta_ref, proj_ref, grad_ref, conv_ref, bias_ref, norm_ref, step_b_ref, decay_ref, skip_ref,
+    val_out, key_out, vsum_ref, ksum_ref, raw_ref, cum_ref, y_ref, gated_ref, state_ref, sums_ref, chan_ref, head_ref,
     state, last_v, last_k,
     *, span, heads,
 ):
@@ -107,6 +143,7 @@
 
     @pl.when(i == 0)
     def _():
+        own_parameters(chan_ref, head_ref, conv_ref, bias_ref, norm_ref, step_b_ref, decay_ref, skip_ref, heads)
         state[...] = jnp.zeros_like(state)
         last_v[...] = jnp.zeros_like(last_v)
         last_k[...] = jnp.zeros_like(last_k)
@@ -127,7 +164,7 @@
     vsum_ref[...] = vsum
     val_out[...] = (vsum * jax.nn.sigmoid(vsum)).astype(bf16)
     rows_k = proj_ref[:, 2 * inner : 2 * inner + KEYS].astype(bf16).astype(f32)
-    ksum = convolve(rows_k, last_k[...], conv_k_ref[:CONV, :], conv_k_ref[CONV : CONV + 1, :])
+    ksum = convolve(rows_k, last_k[...], conv_ref[:, E:], bias_ref[:, E:])
     last_k[...] = rows_k[CHUNK - 8 :]
     ksum_ref[...] = ksum
     keys = (ksum * jax.nn.sigmoid(ksum)).astype(bf16)
@@ -189,10 +226,10 @@
 
 
 def backward_kernel(
-    meta_ref, proj_ref, grad_ref, chan_ref, conv_k_ref, head_ref,
+    meta_ref, proj_ref, grad_ref, chan_ref, conv_ref, head_ref,
     val_ref, key_ref, vsum_ref, ksum_ref, raw_ref, cum_ref, y_ref, state_ref, sums_ref, branch_ref, go_ref,
-    cols_ref, chan_sums, key_sums, head_sums, b_out, o_out,
-    dstate, dv, next_v, next_k, next_lags, *early_refs,
+    cols_ref, all_sums, b_out, o_out,
+    chan_sums, key_sums, head_sums, dstate, dv, next_v, next_k, next_lags, *early_refs,
     span, heads,
 ):
     chunks = pl.num_programs(0)
@@ -337,21 +374,22 @@
     cols_ref[:, inner : 2 * inner] = convolve_back(dv[...], vsum_ref[...], rows_v, next_v, chan_ref[:CONV, :], chan_sums)
     rows_k = proj_ref[:, 2 * inner : 2 * inner + KEYS].astype(bf16).astype(f32)
     cols_ref[:, 2 * inner : 2 * inner + KEYS] = convolve_back(
-        dkeys, ksum_ref[...], rows_k, next_k, conv_k_ref[:CONV, :], key_sums
+        dkeys, ksum_ref[...], rows_k, next_k, conv_ref[:, E:], key_sums
     )
     for by in range(1, CONV):
         next_lags[:, by - 1 : by] = lags[by - 1][:8]
 
-    @pl.when(pl.program_id(0) == 1)
+    @pl.when(pl.program_id(0) == 0)
     def _():
         early.middle()
 
     @pl.when(pl.program_id(0) == chunks - 1)
     def _():
+        whole_sums(all_sums, chan_sums, key_sums, head_sums, head_ref, chan_ref, heads)
         early.end()
 
 
-def mixer_forward(meta, projected, grad_mixed, chan, conv_k, head_vec, span, heads):
+def mixer_forward(meta, projected, grad_mixed, params, span, heads):
     length = projected.shape[0]
     inner = heads * P_SIZE
     chunks = length // CHUNK
@@ -363,16 +401,18 @@
         grid=(chunks,),
         in_specs=[
             pl.BlockSpec(memory_space=pltpu.SMEM), row(2 * inner + KEYS + STEP_PAD), row(inner),
-            all_of(8, inner), all_of(8, KEYS), all_of(8, LANES),
-        ],
+        ]
+        + [all_of(*part.shape) for part in params],
         out_specs=[
             row(inner), row(KEYS), row(inner), row(KEYS), row(LANES), row(LANES), row(inner), row(inner),
             pl.BlockSpec((1, N, inner), lambda i: (i, 0, 0)), all_of(2 * chunks, LANES),
+            all_of(8, inner), all_of(8, LANES),
         ],
         out_shape=[
             out(inner, bf16), out(KEYS, bf16), out(inner, f32), out(KEYS, f32), out(LANES, f32), out(LANES, f32),
             out(inner, f32), out(inner, f32), jax.ShapeDtypeStruct((chunks, N, inner), bf16),
-            jax.ShapeDtypeStruct((2 * chunks, LANES), f32),
+            jax.ShapeDtypeStruct((2 * chunks, LANES), f32), jax.ShapeDtypeStruct((8, inner), f32),
+            jax.ShapeDtypeStruct((8, LANES), f32),
         ],
         scratch_shapes=[pltpu.VMEM((N, inner), f32), pltpu.VMEM((8, inner), f32), pltpu.VMEM((8, KEYS), f32)],
         compiler_params=pltpu.CompilerParams(vmem_limit_bytes=16 * 2**20),
@@ -380,10 +420,10 @@
             flops=length * inner * 1024, bytes_accessed=length * inner * 24, transcendentals=length * heads * CHUNK
         ),
         name="mixer_forward",
-    )(meta, projected, grad_mixed, chan, conv_k, head_vec)
-
-
-def mixer_backward(meta, projected, grad_mixed, chan, conv_k, head_vec, kept, sums, branch, grad_out, span, heads):
+    )(meta, projected, grad_mixed, *params)
+
+
+def mixer_backward(meta, projected, grad_mixed, chan, conv, head_vec, kept, sums, branch, grad_out, span, heads):
     length = projected.shape[0]
     inner = heads * P_SIZE
     chunks = length // CHUNK
@@ -401,20 +441,19 @@
         grid=(chunks,),
         in_specs=[
             pl.BlockSpec(memory_space=pltpu.SMEM), row(2 * inner + KEYS + STEP_PAD), row(inner),
-            all_of(8, inner), all_of(8, KEYS), all_of(8, LANES),
+            all_of(8, inner), all_of(*conv.shape), all_of(8, LANES),
             row(inner), row(KEYS), row(inner), row(KEYS), row(LANES), row(LANES), row(inner),
             pl.BlockSpec((1, N, inner), lambda i: (chunks - 1 - i, 0, 0)), all_of(2 * chunks, LANES), HBM, HBM,
         ],
         out_specs=[
-            row(2 * inner + KEYS + STEP_PAD), all_of(8, inner), all_of(8, KEYS), all_of(8, LANES),
-            VMEM, VMEM,
+            row(2 * inner + KEYS + STEP_PAD), all_of(8, conv.shape[1]), VMEM, VMEM,
         ],
         out_shape=[
-            out(2 * inner + KEYS + STEP_PAD), jax.ShapeDtypeStruct((8, inner), f32),
-            jax.ShapeDtypeStruct((8, KEYS), f32), jax.ShapeDtypeStruct((8, LANES), f32),
+            out(2 * inner + KEYS + STEP_PAD), jax.ShapeDtypeStruct((8, conv.shape[1]), f32),
             jax.ShapeDtypeStruct((near, peers // 2, tokens, width), bf16), jax.ShapeDtypeStruct(part, f32),
         ],
         scratch_shapes=[
+            pltpu.VMEM((8, inner), f32), pltpu.VMEM((8, KEYS), f32), pltpu.VMEM((8, LANES), f32),
             pltpu.VMEM((N, inner), f32), pltpu.VMEM((CHUNK, inner), f32), pltpu.VMEM((8, inner), f32),
             pltpu.VMEM((8, KEYS), f32), pltpu.VMEM((8, LANES), f32),
             vm(near, peers // 2, tokens, width), vm(near, peers // 2, tokens, width),
@@ -426,7 +465,7 @@
             flops=length * inner * 3072, bytes_accessed=length * inner * 30, transcendentals=length * heads * CHUNK
         ),
         name="mixer_backward",
-    )(meta, projected, grad_mixed, chan, conv_k, head_vec, *kept, sums, branch, grad_out)
+    )(meta, projected, grad_mixed, chan, conv, head_vec, *kept, sums, branch, grad_out)
 
 
 MESH = pl.DeviceIdType.MESH
@@ -463,6 +502,20 @@
     def at(self, s=0, zl=0, zh=0, c=0):
         return (flip(self.s, s), (flip(self.zh, zh) * self.near + flip(self.zl, zl)) * 2 + flip(self.c, c))
 
+    def heads_at(self, index, per, width):
+        outer = self.far if self.near > 1 else 1
+        run = width // outer
+        return (((self.s * outer + index // run) * self.near + self.zl) * run + index % run) // per
+
+    def channel_runs(self, width):
+        outer = self.far if self.near > 1 else 1
+        run = width // outer
+        runs = []
+        for i in range(outer):
+            first = ((self.s * outer + i) * self.near + self.zl) * run
+            runs.append((pl.ds(pl.multiple_of(first, 128), run), slice(i * run, (i + 1) * run)))
+        return runs
+
     def column_runs(self, s, zl, width):
         outer = self.far if self.near > 1 else 1
         run = width // (2 * outer)
@@ -549,13 +602,13 @@
 
 
 def gather_kernel(
-    in_ref, key_ref, out_ref, rows_ref, cot_ref, meta_ref,
+    in_ref, steps_ref, out_ref, rows_ref, cot_ref, meta_ref,
     w_ref, o_ref, x_ref, ct_ref, m_ref, send, recv, local,
 ):
     me = Place()
     s, zl, zh, c = me.s, me.zl, me.zh, me.c
-    columns = w_ref.shape[-1] - key_ref.shape[-1]
-    mine, shared = pl.ds(0, columns), pl.ds(columns, key_ref.shape[-1])
+    columns = w_ref.shape[-1] - KEYS - STEP_PAD
+    mine, shared = pl.ds(0, columns), pl.ds(columns, KEYS + STEP_PAD)
     cube, far, sibling = me.partners()
     greet(cube + far + sibling)
     mover = Mover(send, recv, local)
@@ -591,11 +644,16 @@
             copy.wait_recv()
 
     def key_path():
-        block = w_ref.at[s, zh, zl, c, :, shared]
-        own = mover.keep(key_ref, block)
-        copies = [mover.put(key_ref, block, me.at(zh=o)) for o in range(1, me.far)]
+        block = w_ref.at[s, zh, zl, c]
+        parts = [
+            (in_ref.at[:, pl.ds(2 * E, KEYS)], block.at[:, pl.ds(columns, KEYS)]),
+            (steps_ref, block.at[:, pl.ds(columns + KEYS, STEP_PAD)]),
+        ]
+        own = [mover.keep(*part) for part in parts]
+        copies = [mover.put(*part, me.at(zh=o)) for o in range(1, me.far) for part in parts]
         yield
-        own.wait()
+        for copy in own:
+            copy.wait()
         for copy in copies:
             copy.wait_recv()
         block = w_ref.at[s, :, zl, c, :, shared]
@@ -690,18 +748,18 @@
     return [pltpu.SemaphoreType.DMA((copies,)), pltpu.SemaphoreType.DMA((copies,)), pltpu.SemaphoreType.DMA((kept,))]
 
 
-def gather(in_w, keys, out_w, rows, cot, meta):
+def gather(in_w, steps, out_w, rows, cot, meta):
     me = Place()
     peers, near, far = me.peers, me.near, me.far
     shape = lambda lead, part: jax.ShapeDtypeStruct(lead + part, bf16)
     columns = 2 * E // (peers * near)
     runs = 2 * (far if near > 1 else 1)
     copies = runs * (peers * near - 1) + (peers + 1) * (2 * far - 1) + 2 * (near * peers - 1)
-    copies += 2 * near + peers + far - 3
+    copies += 2 * near + peers + 2 * far - 4
     return pl.pallas_call(
         gather_kernel,
         out_shape=[
-            shape((peers, far, near, 2), (in_w.shape[0], columns + keys.shape[1])),
+            shape((peers, far, near, 2), (in_w.shape[0], columns + KEYS + STEP_PAD)),
             shape((far, 2), out_w.shape),
             shape((near, peers), rows.shape),
             shape((near, peers), cot.shape),
@@ -709,10 +767,10 @@
         ],
         in_specs=[HBM] * 6,
         out_specs=[HBM] * 5,
-        scratch_shapes=sems(copies, runs + 5),
-        compiler_params=remote_params(0, 4),
+        scratch_shapes=sems(copies, runs + 6),
+        compiler_params=remote_params(0, 58),
         name="gather_all",
-    )(in_w, keys, out_w, rows, cot, meta)
+    )(in_w, steps, out_w, rows, cot, meta)
 
 
 def total_kernel(part_ref, gated_ref, chan_ref, sum_ref, mixed_ref, box, send, recv, local):
@@ -774,9 +832,9 @@
 
 
 def scatter_kernel(
-    gn_ref, gw_ref, b_ref, v_ref, u_ref, og_ref, ow_ref, ob_ref, ok_ref, ov_ref, ou_ref,
+    gn_ref, gw_ref, b_ref, u_ref, p_ref, gain_ref, og_ref, ow_ref, ob_ref, ok_ref, ou_ref,
     n_own, n_box, n_near, b_own, b_box, b_near, w_own, w_box, w_far,
-    k_own, k_box, k_near, k_far, k_bits, v_box, u_box, send, recv, local,
+    k_own, k_box, k_near, k_far, k_bits, u_box, send, recv, local,
 ):
     me = Place()
     s, zl, zh, c = me.s, me.zl, me.zh, me.c
@@ -905,17 +963,14 @@
     def small_path():
         turns = [me.at(c=1)] + [me.at(zl=o) for o in bits_of(me.near)]
         turns += [me.at(s=o) for o in bits] + [me.at(zh=o) for o in bits_of(me.far)]
-        pairs = [(v_ref, v_box, ov_ref), (u_ref, u_box, ou_ref)]
-        for src, box, _ in pairs:
-            box[0] = src[...]
+        u_box[0] = u_ref[...]
+        u_box[0, 6:7, : p_ref.shape[1]] = p_ref[...] / gain_ref[...]
         for i, device in enumerate(turns):
-            copies = [mover.put(box.at[2 * i], box.at[2 * i + 1], device) for _, box, _ in pairs]
+            copy = mover.put(u_box.at[2 * i], u_box.at[2 * i + 1], device)
             yield
-            for copy, (_, box, _) in zip(copies, pairs):
-                copy.wait_recv()
-                box[2 * i + 2] = box[2 * i] + box[2 * i + 1]
-        for _, box, out in pairs:
-            out[...] = box[2 * len(turns)]
+            copy.wait_recv()
+            u_box[2 * i + 2] = u_box[2 * i] + u_box[2 * i + 1]
+        ou_ref[...] = u_box[2 * len(turns)]
 
     coming_n, coming_b = [], []
     grads = (gn_ref, n_own, n_box, n_near, og_ref)
@@ -926,13 +981,14 @@
     own_n = rows_path(*grads, orders(0), 0, coming_n)
     own_b = rows_path(*branch, orders(0), 0, coming_b, 1)
     weights, keys, small = weight_path(), key_path(), small_path()
-    turn([weights] + near_b + near_n + [own_n, keys, own_b, small])
-    turn([weights] * (me.far * me.peers) + [keys] * me.peers)
-    run_paths(near_b + near_n + [keys, small, own_b, own_n, weights])
+    turn(near_b + near_n + [weights, own_n, keys, own_b, small])
+    turn([weights] * (me.far * me.peers) + [keys] * me.peers + [small])
+    turn(near_b + near_n + [keys, own_b, small] + near_b + near_n + [keys, small, keys, own_b, own_n])
+    run_paths(near_b + near_n + [keys, small, weights, own_b, own_n])
     mover.close()
 
 
-def scatter(grads, gw, branch, small, conv):
+def scatter(grads, gw, branch, small, products, gain):
     me = Place()
     peers, near, far = me.peers, me.near, me.far
     tokens, width = grads.shape[2:]
@@ -945,7 +1001,7 @@
     kblock = (near, rows, keys)
     runs = 2 * (far if near > 1 else 1)
     copies = peers * near - 1 + (2 * far - 1) * peers + runs * (peers * near - 1)
-    copies += 2 * peers - 1 + near - 1 + far - 1 + 2 * stages + peers // 2 * near - 1
+    copies += 2 * peers - 1 + near - 1 + far - 1 + stages + peers // 2 * near - 1
     kept = peers * near + far * peers + runs + peers + near * peers // 4
     same = lambda part: jax.ShapeDtypeStruct(part.shape, part.dtype)
     return pl.pallas_call(
@@ -956,22 +1012,21 @@
             jax.ShapeDtypeStruct((tokens, width), f32),
             jax.ShapeDtypeStruct((rows, keys), f32),
             same(small),
-            same(conv),
         ],
-        in_specs=[HBM] * 3 + [VMEM] * 2,
-        out_specs=[VMEM, HBM, VMEM, VMEM, VMEM, VMEM],
+        in_specs=[HBM] * 3 + [VMEM] * 3,
+        out_specs=[VMEM, HBM, VMEM, VMEM, VMEM],
         scratch_shapes=[
             vm(near, peers // 2, tokens, width), vm(near, peers - 1, tokens, width), vm(max(near - 1, 1), tokens, width),
             vm(near, peers // 2, tokens, width), vm(near, peers // 2 - 1, tokens, width), vm(max(near - 1, 1), tokens, width),
             vm(far, peers, *block), vm(far, peers, *block), vm(max(far - 1, 1), peers, *block),
             vm(peers, far, *kblock), vm(peers, far, *kblock), vm(max(near - 1, 1), far, *kblock[1:]),
-            vm(max(far - 1, 1), *kblock[1:]), vm(peers - 1, far, *kblock), boxes(small), boxes(conv),
+            vm(max(far - 1, 1), *kblock[1:]), vm(peers - 1, far, *kblock), boxes(small),
         ]
         + sems(copies, kept),
         compiler_params=remote_params(2, 40),
         cost_estimate=pl.CostEstimate(flops=0, bytes_accessed=250 * 10**6, transcendentals=0),
         name="scatter_all",
-    )(grads, gw, branch, small, conv)
+    )(grads, gw, branch, small, products, gain)
 
 
 class Early:
@@ -1023,107 +1078,127 @@
         self.mover.close()
 
 
+def prepare_kernel(x_ref, gain_ref, step_ref, lengths_ref, width_ref, normed_ref, inv_ref, steps_ref, meta_ref):
+    x = x_ref[0].astype(f32)
+    inv = lax.rsqrt(jnp.mean(x * x, axis=1, keepdims=True) + epsilon)
+    normed_ref[...] = (x * inv * gain_ref[...]).astype(bf16)
+    inv_ref[...] = jnp.broadcast_to(inv, inv_ref.shape)
+    steps_ref[...] = jnp.zeros_like(steps_ref)
+    steps_ref[:, :H] = step_ref[...]
+    lanes = iota(meta_ref.shape, 1)
+    meta = jnp.where(lanes == DOCS, width_ref[0], 0)
+    for i in range(DOCS):
+        meta = jnp.where(lanes == i, lengths_ref[0, i], meta)
+    meta_ref[...] = meta
+
+
+def prepare(inputs, gain, step_weight, doc_lengths, head_width):
+    tokens, width = inputs.shape[1:]
+    smem = pl.BlockSpec(memory_space=pltpu.SMEM)
+    return pl.pallas_call(
+        prepare_kernel,
+        out_shape=[
+            jax.ShapeDtypeStruct((tokens, width), bf16),
+            jax.ShapeDtypeStruct((tokens, LANES), f32),
+            jax.ShapeDtypeStruct((step_weight.shape[0], STEP_PAD), bf16),
+            jax.ShapeDtypeStruct((8, LANES), jnp.int32),
+        ],
+        in_specs=[VMEM] * 3 + [smem] * 2,
+        out_specs=[VMEM] * 4,
+        compiler_params=pltpu.CompilerParams(vmem_limit_bytes=16 * 2**20),
+        name="prepare",
+    )(inputs, gain, step_weight, doc_lengths, head_width)
+
+
+def finish_kernel(
+    x_ref, cot_ref, gain_ref, inv_ref, og_ref, ob_ref, ow_ref, ok_ref, u_ref,
+    out_ref, gx_ref, gw_ref, gs_ref, gc_ref, gb_ref, gp_ref, gn_ref, g0_ref, g1_ref, g2_ref,
+):
+    x = x_ref[0].astype(f32)
+    out_ref[0] = (x + ob_ref[...]).astype(bf16)
+    inv = inv_ref[:, :1]
+    scaled = og_ref[...] * gain_ref[...]
+    dot = jnp.mean(scaled * x, axis=1, keepdims=True)
+    gx_ref[0] = inv * scaled - x * (inv * inv * inv * dot) + cot_ref[0].astype(f32)
+    gw_ref[:, : 2 * E] = ow_ref[...].astype(f32)
+    gw_ref[:, 2 * E :] = ok_ref[:, :KEYS]
+    gs_ref[...] = ok_ref[:, KEYS : KEYS + H]
+    gc_ref[...] = u_ref[:CONV, :]
+    gb_ref[...] = u_ref[CONV : CONV + 1, :]
+    gn_ref[...] = u_ref[5:6, :E]
+    gp_ref[...] = u_ref[6:7, : gp_ref.shape[1]]
+    for i, ref in enumerate((g0_ref, g1_ref, g2_ref)):
+        ref[...] = u_ref[7:8, i * LANES : i * LANES + H]
+
+
+def finish(inputs, cotangent, gain, inv, sums):
+    tokens, width = inputs.shape[1:]
+    og, ow, ob, ok, u = sums
+    shape = lambda *dims: jax.ShapeDtypeStruct(dims, f32)
+    rows = ow.shape[0]
+    return pl.pallas_call(
+        finish_kernel,
+        out_shape=[
+            jax.ShapeDtypeStruct(inputs.shape, bf16), shape(*inputs.shape), shape(rows, 2 * E + KEYS), shape(rows, H),
+            shape(CONV, E + KEYS), shape(1, E + KEYS), shape(1, width), shape(1, E), shape(1, H), shape(1, H), shape(1, H),
+        ],
+        in_specs=[VMEM] * 9,
+        out_specs=[VMEM] * 11,
+        compiler_params=pltpu.CompilerParams(vmem_limit_bytes=32 * 2**20),
+        name="finish",
+    )(inputs, cotangent, gain, inv, og, ob, ow, ok, u)
+
+
 def body(
     inputs, cotangent, doc_lengths, head_width, pre_gain, in_weight, step_weight, conv_weight, conv_bias,
     step_bias, decay_log, skip_gain, norm_gain, out_weight,
 ):
     me = Place()
     peers, near, far = me.peers, me.near, me.far
-    outer = far if near > 1 else 1
-    tokens = inputs.shape[1]
-    width = inputs.shape[2]
+    tokens, width = inputs.shape[1:]
     span = tokens * peers
     length = span * near
     heads = H // (peers * near)
     inner = heads * P_SIZE
     rows = in_weight.shape[0]
-    seq_rows = inputs[0].astype(f32)
-    cot_rows = cotangent[0]
-
-    def own(vector):
-        part = vector.reshape(-1, peers, outer, near, vector.shape[-1] // (peers * outer * near))
-        part = lax.dynamic_slice(part, (0, me.s, 0, me.zl, 0), (part.shape[0], 1, outer, 1, part.shape[4]))
-        return part.reshape(vector.shape[:-1] + (-1,))
-
-    def spread(part):
-        lead = part.shape[:-1]
-        part = part.reshape(-1, 1, outer, 1, part.shape[-1] // outer)
-        full = jnp.zeros((part.shape[0], peers, outer, near, part.shape[-1]), part.dtype)
-        return lax.dynamic_update_slice(full, part, (0, me.s, 0, me.zl, 0)).reshape(lead + (-1,))
-
-    key_send = jnp.concatenate(
-        [in_weight[:, 2 * E :], step_weight, jnp.zeros((rows, STEP_PAD - H), bf16)], axis=1
-    )
-    inv_rms = lax.rsqrt(jnp.mean(seq_rows * seq_rows, axis=1, keepdims=True) + epsilon)
-    normed = (seq_rows * inv_rms * pre_gain[None, :]).astype(bf16)
-    meta = jnp.pad(jnp.concatenate([doc_lengths[0], head_width])[None], ((0, 7), (0, 123)))
-    in_w, out_w, normed, cot_all, meta = gather(in_weight, key_send, out_weight, normed, cot_rows, meta)
+    row = lambda vector: vector[None, :]
+
+    normed, inv, steps, meta = prepare(inputs, row(pre_gain), step_weight, doc_lengths, head_width)
+    in_w, out_w, normed, cot_all, meta = gather(in_weight, steps, out_weight, normed, cotangent[0], meta)
     in_w = in_w.reshape(width, -1)
     out_w = out_w.reshape(inner, width)
     normed = normed.reshape(length, width)
     cot_all = cot_all.reshape(length, width)
     meta = meta[:, 0, :8]
 
-    head_ids = jnp.arange(H, dtype=f32)
-    chan = own(
-        jnp.concatenate(
-            [
-                conv_weight[:, :E],
-                conv_bias[None, :E],
-                norm_gain[None],
-                jnp.repeat(skip_gain, P_SIZE)[None],
-                jnp.repeat(head_ids, P_SIZE)[None],
-            ],
-            axis=0,
-        )
-    )
-    conv_k = jnp.concatenate([conv_weight[:, E:], conv_bias[None, E:], jnp.zeros((3, KEYS), f32)], axis=0)
-    head_vec = own(jnp.stack([step_bias, jnp.exp(decay_log), head_ids + 1.0]))
-    head_vec = jnp.pad(head_vec, ((0, 5), (0, LANES - heads))) - jnp.where(jnp.arange(8) == 2, 1.0, 0.0)[:, None]
-
+    params = (conv_weight, row(conv_bias), row(norm_gain), row(step_bias), row(decay_log), row(skip_gain))
     projected = mm(normed, in_w, NN)
     grad_mixed = mm(cot_all, out_w, NT)
-    mixer_args = (meta, projected, grad_mixed, chan, conv_k, head_vec)
-    *kept, gated, states, part = mixer_forward(*mixer_args, span, heads)
+    *kept, gated, states, part, chan, head_vec = mixer_forward(meta, projected, grad_mixed, params, span, heads)
     sums, mixed = cube_total(part, gated, chan)
     branch = mm(mixed, out_w, NN).astype(bf16)
     grad_out = mm(mixed, cot_all, TN).astype(bf16)
-    grad_cols, chan_sums, key_sums, head_sums, branch, grad_out_weight = mixer_backward(
-        *mixer_args, (*kept, states), sums, branch.reshape(near, peers, tokens, width),
-        grad_out.reshape(far, 2, -1, width), span, heads,
+    grad_cols, small, branch, grad_out_weight = mixer_backward(
+        meta, projected, grad_mixed, chan, conv_weight, head_vec, (*kept, states), sums,
+        branch.reshape(near, peers, tokens, width), grad_out.reshape(far, 2, -1, width), span, heads,
     )
     grad_in = mm(normed, grad_cols, TN).astype(bf16)
     grad_normed = mm(grad_cols, in_w, NT)
-    grad_pre_gain = jnp.sum(grad_normed * normed.astype(f32), axis=0) / pre_gain
-
-    grad_skip = jnp.sum(chan_sums[6].reshape(heads, P_SIZE), axis=1)
-    head_sums = spread(jnp.concatenate([head_sums[:2, :heads], grad_skip[None]], axis=0))
-    chan_sums = spread(chan_sums[:6])
-    small = jnp.concatenate([grad_pre_gain, chan_sums[5], head_sums.reshape(-1)])
-    small = jnp.pad(small, (0, -small.shape[0] % 1024)).reshape(-1, 128)
-    conv_sums = jnp.pad(jnp.concatenate([chan_sums[:5], key_sums[:5]], axis=1), ((0, 3), (0, 0)))
-    grad_normed, grad_in, branch, grad_keys, small, conv_sums = scatter(
+    products = jnp.sum(grad_normed * normed.astype(f32), axis=0)
+    summed = scatter(
         grad_normed.astype(bf16).reshape(near, peers, tokens, width),
         grad_in.reshape(peers, far, near, 2, rows, -1),
         branch,
         small,
-        conv_sums,
+        row(products),
+        row(pre_gain),
     )
-    output = (seq_rows + branch).astype(bf16)[None]
-    scaled_in = grad_normed * pre_gain[None, :]
-    dot = jnp.mean(scaled_in * seq_rows, axis=1, keepdims=True)
-    grad_seq = inv_rms * scaled_in - seq_rows * (inv_rms * inv_rms * inv_rms * dot)
-    grad_inputs = (grad_seq + cot_rows.astype(f32))[None]
-    grad_in_weight = jnp.concatenate([grad_in.astype(f32), grad_keys[:, :KEYS]], axis=1)
-    grad_step_weight = grad_keys[:, KEYS : KEYS + H]
-    small = small.reshape(-1)
-    parts = []
-    for size in (width, E, H, H, H):
-        parts.append(small[:size])
-        small = small[size:]
+    outs = finish(inputs, cotangent, row(pre_gain), inv, summed)
+    output, grad_inputs, grad_in_weight, grad_step_weight, grad_conv_weight = outs[:5]
+    grad_conv_bias, grad_pre_gain, grad_norm_gain, grad_step_bias, grad_decay_log, grad_skip = [o[0] for o in outs[5:]]
     return (
-        output, grad_inputs, parts[0], grad_in_weight, grad_step_weight, conv_sums[:CONV], conv_sums[CONV],
-        parts[2], parts[3], parts[4], parts[1], grad_out_weight,
+        output, grad_inputs, grad_pre_gain, grad_in_weight, grad_step_weight, grad_conv_weight, grad_conv_bias,
+        grad_step_bias, grad_decay_log, grad_skip, grad_norm_gain, grad_out_weight,
     )
 
 

time: 322 us -> 301 us (0.935)
  local copies, waits for them, and re-layouts: 17.7 us -> 7.92 us
  other arithmetic: 7.69 us -> 0.65 us
    pallas_call x1, Pallas kernels: 116 us -> 102 us  [gather(): pl.pallas_call(gather_kernel, out_shape=[shape((peers, far, near, 2), (in...]
    pallas_call x1, Pallas kernels: 8.65 us -> 19 us  [cube_total(): pl.pallas_call(total_kernel, out_shape=[jax.ShapeDtypeStruct(part.shape,...]
    slice x20 -> x0, local copies, waits for them, and re-layouts: 6.88 us -> none  [the longest x3 1.79 us: body(): parts.append(small[:size])]
    unnamed x28 -> x43, local copies, waits for them, and re-layouts: 6.46 us -> 6.48 us
where the time goes in v6:
time: 301 us
  Pallas kernels  256 us (85%)
  matrix products  35 us (12%)
  local copies, waits for them, and re-layouts  7.92 us (3%)
    pallas_call x1, Pallas kernels, gather(): pl.pallas_call(gather_kernel, out_shape=[shape((peers, far, near, 2), (in...  102 us
    pallas_call x1, Pallas kernels, scatter(): pl.pallas_call(scatter_kernel, out_shape=[jax.ShapeDtypeStruct((tokens, w...  85.5 us
    dot_general x6, matrix products, mm(): lax.dot_general(a, b, (dims, ((), ())), precision=precision, preferred_el...  35 us
    pallas_call x1, Pallas kernels, mixer_backward(): pl.pallas_call(partial(backward_kernel, span=span, heads=heads), grid=(ch...  31.9 us
    pallas_call x1, Pallas kernels, cube_total(): pl.pallas_call(total_kernel, out_shape=[jax.ShapeDtypeStruct(part.shape,...  19 us
    pallas_call x1, Pallas kernels, mixer_forward(): pl.pallas_call(partial(forward_kernel, span=span, heads=heads), grid=(chu...  14.3 us
    unnamed x43, local copies, waits for them, and re-layouts  6.48 us

profile of v6, /device:TPU:0, one launch (start us, length us, event | category | flops | bytes accessed | tf_op | source)
XLA Modules:
  0.0 300.7 jit_solution(12849239630676149503)
XLA Ops:
  1.3 0.7 broadcast_in_dim.24.bias_ref
  2.0 0.0 copy-start.1
  2.0 1.0 copy-done.1
  3.1 0.0 copy-start.6
  3.1 0.7 copy-done.6
  3.8 0.0 copy-start.10
  3.8 0.7 copy-done.10
  4.5 0.0 copy-start.15
  4.5 0.7 copy-done.15
  5.2 0.8 prepare.1
  5.9 0.0 copy-start.4
  5.9 0.8 copy-done.4
  6.7 0.6 copy-done.9
  7.3 0.6 copy-done.11
  7.9 101.9 %gather_all.1 = (bf16[4,2,2,2,64,1408]{5,4,3,2,1,0:T(8,128)(2,1)}, bf16[2,2,128,2048]{3,2,1,0:T(8,128)(2,1)}, bf16[2,4,128,2048]{3,2,1,0:T(8,128)(2,1)}, bf16[2,4,128,2048]{3,2,1,0:T(8,128)(2,1)}, s32[2,8,128]{2,1,0:T(8,128)}) custom-call(bf16[64,8448]{1,0:T(8,128)(2,1)} %in_ref.1, bf16[64,128]{1,0:T(8,128)(2,1)} %copy-done.9, bf16[128,2048]{1,0:T(8,128)(2,1)} %out_ref.1, ...), custom_call_target="tpu_custom_call" | custom-call | tf_op jit(solution)/shard_map/gather_all/pallas_call | solution.py:759
  109.8 0.7 slice.3
  110.5 5.4 %fusion.1.grad_ref = f32[1024,512]{1,0:T(8,128)S(1)} fusion(bf16[1024,2048]{1,0:T(8,128)(2,1)} %bitcast.53, bf16[512,2048]{1,0:T(8,128)(2,1)} %bitcast.55), kind=kOutput, calls=%fused_computation.5 | convolution fusion | flops 2147483648 | bytes 8388608 | tf_op jit(solution)/shard_map/dot_general | solution.py:26
  115.9 0.0 copy-done.16
  115.9 0.4 copy-done.17
  116.3 0.0 copy-start.14
  116.3 6.6 %fusion.proj_ref = f32[1024,1408]{1,0:T(8,128)S(1)} fusion(bf16[1024,2048]{1,0:T(8,128)(2,1)S(1)} %bitcast.51, bf16[2048,1408]{1,0:T(8,128)(2,1)S(1)} %bitcast.49), kind=kOutput, calls=%fused_computation.4 | convolution fusion | flops 5905580032 | bytes 15728640 | tf_op jit(solution)/shard_map/dot_general | solution.py:26
  123.0 0.0 copy-done.5
  123.0 0.0 copy-done.8
  123.0 0.0 copy-done.12
  123.0 0.0 copy-done.13
  123.0 0.0 copy-done.14
  123.0 0.0 copy-start
  123.0 0.0 copy-start.19
  123.0 14.3 %mixer_forward.1 = (bf16[1024,512]{1,0:T(8,128)(2,1)S(1)}, bf16[1024,256]{1,0:T(8,128)(2,1)S(1)}, f32[1024,512]{1,0:T(8,128)S(1)}, f32[1024,256]{1,0:T(8,128)S(1...) custom-call(s32[2,8]{1,0:T(2,128)S(1)} %bitcast.41, ...), custom_call_target="tpu_custom_call" | custom-call | flops 536870912 | bytes 12582912 | tf_op jit(solution)/shard_map/mixer_forward/pallas_call | solution.py:399
  137.3 19.0 %cube_total.1 = (f32[16,128]{1,0:T(8,128)S(1)}, bf16[1024,512]{1,0:T(8,128)(2,1)S(1)}) custom-call(f32[16,128]{1,0:T(8,128)S(1)} %get-tuple-element.74.part_ref, f32[1024,512]{1,0:T(8,128)S(1)} %get-tuple-element.75.gated_ref, f32[8,512]{1,0:T(8,128)S(1)} %get-tuple-element.64.chan_ref), custom_call_target="tpu_custom_call" | custom-call | tf_op jit(solution)/shard_map/cube_total/pallas_call | solution.py:804
  156.3 0.0 copy-done
  156.3 0.0 copy-done.19
  156.3 0.0 copy-start.20
  156.3 2.4 convolution_convert_fusion.2
  158.7 0.0 copy-done.20
  158.7 4.4 %convolution_convert_fusion.1 = bf16[1024,2048]{1,0:T(8,128)(2,1)} fusion(bf16[1024,512]{1,0:T(8,128)(2,1)S(1)} %get-tuple-element.77, bf16[512,2048]{1,0:T(8,128)(2,1)S(1)} %bitcast.56), kind=kOutput, calls=%fused_computation.2 | convolution fusion | flops 2149580800 | bytes 7340032 | tf_op jit(solution)/shard_map/dot_general | solution.py:26
  163.2 31.9 %mixer_backward.1 = (bf16[1024,1408]{1,0:T(8,128)(2,1)S(1)}, f32[8,4352]{1,0:T(8,128)S(1)}, bf16[2,2,128,2048]{3,2,1,0:T(8,128)(2,1)S(1)}, f32[128,2048]{1,0:T(8,128)S(1)}) custom-call(s32[2,8]{1,0:T(2,128)S(1)} %bitcast.42, f32[1024,1408]{1,0:T(8,128)} %copy-done, f32[1024,512]{1,0:T(8,128)S(1)} %fusion.1.grad_ref, ...), custom_call_target="tpu_custom_call" | custom-call | flops 1610612736 | bytes 15728640 | tf_op jit(solution)/shard_map/mixer_backward/pallas_call | solution.py:439
  195.1 0.0 copy-done.18
  195.1 7.3 %multiply_reduce_fusion = (f32[2048]{0:T(1024)S(1)}, bf16[1024,2048]{1,0:T(8,128)(2,1)S(1)}) fusion(bf16[2,4,128,2048]{3,2,1,0:T(8,128)(2,1)S(1)} %copy-done.18, bf16[1024,1408]{1,0:T(8,128)(2,1)S(1)} %get-tuple-element.78, bf16[2048,1408]{1,0:T(8,128)(2,1)S(1)} %bitcast.50), kind=kOutput, calls=%fused_computation | convolution fusion | flops 5913966592 | bytes 17047552 | tf_op jit(solution)/shard_map/dot_general | solution.py:26
  202.4 0.0 copy-start.7
  202.4 8.9 %convolution_convert_fusion = bf16[2048,1408]{1,0:T(8,128)(2,1)} fusion(bf16[1024,2048]{1,0:T(8,128)(2,1)S(1)} %bitcast.52, bf16[1024,1408]{1,0:T(8,128)(2,1)S(1)} %get-tuple-element.78), kind=kOutput, calls=%fused_computation.1 | convolution fusion | flops 5908463616 | bytes 12845056 | tf_op jit(solution)/shard_map/dot_general | solution.py:26
  211.3 0.0 copy-done.7
  211.3 85.5 %scatter_all.1 = (f32[128,2048]{1,0:T(8,128)S(1)}, bf16[64,8192]{1,0:T(8,128)(2,1)S(1)}, f32[128,2048]{1,0:T(8,128)S(1)}, f32[64,384]{1,0:T(8,128)S(1)}, f32[8,4352]{1,0:T(8,128)S(1)}) custom-call(bf16[2,4,128,2048]{3,2,1,0:T(8,128)(2,1)S(1)} %bitcast.34, bf16[4,2,2,2,64,1408]{5,4,3,2,1,0:T(8,128)(2,1)} %bitcast.47, ...), custom_call_target="tpu_custom_call" | custom-call | bytes 250000000 | tf_op jit(solution)/shard_map/scatter_all/pallas_call | solution.py:1007
  296.8 0.0 copy-done.2
  296.8 0.0 copy-done.3
  296.8 2.3 finish.1
  299.1 0.7 reduce
  299.8 1.0 copy.28
  (11 shorter events, 0.0 us)
Async XLA Ops:
  2.0 1.0 copy-start.1
  3.1 0.7 copy-start.6
  3.8 0.7 copy-start.10
  4.5 0.7 copy-start.15
  5.9 0.8 copy-start.4
  6.7 0.6 copy-start.9
  7.3 0.6 copy-start.11
  110.5 5.4 %copy-start.16 = (bf16[4,2,2,2,64,1408]{5,4,3,2,1,0:T(8,128)(2,1)S(1)}, bf16[4,2,2,2,64,1408]{5,4,3,2,1,0:T(8,128)(2,1)}, u32[]{:S(2)}) copy-start(bf16[4,2,2,2,64,1408]{5,4,3,2,1,0:T(8,128)(2,1)} %get-tuple-element.61) | copy-start | bytes 17301508
  110.5 5.7 %copy-start.17 = (bf16[2,4,128,2048]{3,2,1,0:T(8,128)(2,1)S(1)}, bf16[2,4,128,2048]{3,2,1,0:T(8,128)(2,1)}, u32[]{:S(2)}) copy-start(bf16[2,4,128,2048]{3,2,1,0:T(8,128)(2,1)} %get-tuple-element.60) | copy-start | bytes 12582916
  116.3 6.7 %copy-start.5 = (f32[4,4352]{1,0:T(4,128)S(1)}, f32[4,4352]{1,0:T(4,128)}, u32[]{:S(2)}) copy-start(f32[4,4352]{1,0:T(4,128)} %conv_ref.3) | copy-start | bytes 208900
  116.3 6.7 %copy-start.8 = (f32[4096]{0:T(1024)S(1)}, f32[4096]{0:T(1024)}, u32[]{:S(2)}) copy-start(f32[4096]{0:T(1024)} %param.26) | copy-start | bytes 49156
  116.3 6.7 %copy-start.12 = (f32[64]{0:T(128)S(1)}, f32[64]{0:T(128)}, u32[]{:S(2)}) copy-start(f32[64]{0:T(128)} %param.23) | copy-start | bytes 772
  116.3 6.7 %copy-start.13 = (f32[64]{0:T(128)S(1)}, f32[64]{0:T(128)}, u32[]{:S(2)}) copy-start(f32[64]{0:T(128)} %param.24) | copy-start | bytes 772
  116.3 6.7 %copy-start.14 = (f32[64]{0:T(128)S(1)}, f32[64]{0:T(128)}, u32[]{:S(2)}) copy-start(f32[64]{0:T(128)} %param.25) | copy-start | bytes 772
  123.0 33.3 %copy-start = (f32[1024,1408]{1,0:T(8,128)}, f32[1024,1408]{1,0:T(8,128)S(1)}, u32[]{:S(2)}) copy-start(f32[1024,1408]{1,0:T(8,128)S(1)} %fusion.proj_ref) | copy-start | bytes 17301508
  123.0 33.3 %copy-start.19 = (bf16[2,4,128,2048]{3,2,1,0:T(8,128)(2,1)S(1)}, bf16[2,4,128,2048]{3,2,1,0:T(8,128)(2,1)}, u32[]{:S(2)}) copy-start(bf16[2,4,128,2048]{3,2,1,0:T(8,128)(2,1)} %get-tuple-element.62) | copy-start | bytes 12582916
  156.3 2.4 copy-start.20
  163.2 31.9 %copy-start.18 = (bf16[2,4,128,2048]{3,2,1,0:T(8,128)(2,1)S(1)}, bf16[2,4,128,2048]{3,2,1,0:T(8,128)(2,1)}, u32[]{:S(2)}) copy-start(bf16[2,4,128,2048]{3,2,1,0:T(8,128)(2,1)} %get-tuple-element.60) | copy-start | bytes 12582916
  202.4 8.9 %copy-start.7 = (f32[2048]{0:T(1024)S(1)}, f32[2048]{0:T(1024)}, u32[]{:S(2)}) copy-start(f32[2048]{0:T(1024)} %param.18) | copy-start | bytes 24580
  211.3 85.5 %copy-start.2 = (bf16[1,128,2048]{2,1,0:T(8,128)(2,1)S(1)}, bf16[1,128,2048]{2,1,0:T(8,128)(2,1)}, u32[]{:S(2)}) copy-start(bf16[1,128,2048]{2,1,0:T(8,128)(2,1)} %x_ref.3) | copy-start | bytes 1572868
  211.3 85.5 %copy-start.3 = (bf16[1,128,2048]{2,1,0:T(8,128)(2,1)S(1)}, bf16[1,128,2048]{2,1,0:T(8,128)(2,1)}, u32[]{:S(2)}) copy-start(bf16[1,128,2048]{2,1,0:T(8,128)(2,1)} %cot_ref.1) | copy-start | bytes 1572868

commit v7 on v6

--- a/solution.py
+++ b/solution.py
@@ -132,21 +132,27 @@
 
 
 def forward_kernel(
-    meta_ref, proj_ref, grad_ref, conv_ref, bias_ref, norm_ref, step_b_ref, decay_ref, skip_ref,
+    meta_ref, proj_ref, conv_ref, bias_ref, norm_ref, step_b_ref, decay_ref, skip_ref, cot_in, out_in,
     val_out, key_out, vsum_ref, ksum_ref, raw_ref, cum_ref, y_ref, gated_ref, state_ref, sums_ref, chan_ref, head_ref,
-    state, last_v, last_k,
+    cot_out, out_out, state, last_v, last_k, send, recv,
     *, span, heads,
 ):
     i = pl.program_id(0)
     chunks = pl.num_programs(0)
     inner = heads * P_SIZE
+    late = Late(cot_in, cot_out, out_in, out_out, send, recv)
 
     @pl.when(i == 0)
     def _():
+        late.start()
         own_parameters(chan_ref, head_ref, conv_ref, bias_ref, norm_ref, step_b_ref, decay_ref, skip_ref, heads)
         state[...] = jnp.zeros_like(state)
         last_v[...] = jnp.zeros_like(last_v)
         last_k[...] = jnp.zeros_like(last_k)
+
+    @pl.when(i == chunks - 1)
+    def _():
+        late.middle()
 
     docs = Docs(meta_ref, i, span)
     lags = [docs.lag(by) for by in range(1, CONV)]
@@ -193,7 +199,6 @@
     write_t = write.astype(f32).T.astype(bf16)
     scores = mm(read, write, NT)
     square = jnp.zeros((CHUNK, LANES), f32)
-    cross = jnp.zeros((CHUNK, LANES), f32)
     count = docs.count.astype(f32)
     for pair in range(heads // 2):
         first = 2 * pair
@@ -219,10 +224,13 @@
         gated = y * (gate * jax.nn.sigmoid(gate))
         gated_ref[:, lanes] = gated
         square = square + gated * gated
-        cross = cross + gated * (grad_ref[:, lanes] * chan_ref[5:6, lanes])
     share = 1.0 / (count * P_SIZE)
     sums_ref[pl.ds(i, 1), :] = jnp.sum(square.T, axis=0, keepdims=True) * share
-    sums_ref[pl.ds(chunks + i, 1), :] = jnp.sum(cross.T, axis=0, keepdims=True) * share
+    sums_ref[pl.ds(chunks + i, 1), :] = jnp.full((1, LANES), share, f32)
+
+    @pl.when(i == chunks - 1)
+    def _():
+        late.end()
 
 
 def backward_kernel(
@@ -389,10 +397,11 @@
         early.end()
 
 
-def mixer_forward(meta, projected, grad_mixed, params, span, heads):
+def mixer_forward(meta, projected, params, cot, out_w, span, heads):
     length = projected.shape[0]
     inner = heads * P_SIZE
     chunks = length // CHUNK
+    copies = sum(len(left_over(cot_order(o))) for o in range(cot.shape[0])) + 2 * (out_w.shape[0] - 1)
     row = lambda width: pl.BlockSpec((CHUNK, width), lambda i: (i, 0))
     all_of = lambda *shape: pl.BlockSpec(shape, lambda i: (0,) * len(shape))
     out = lambda width, dtype: jax.ShapeDtypeStruct((length, width), dtype)
@@ -400,27 +409,31 @@
         partial(forward_kernel, span=span, heads=heads),
         grid=(chunks,),
         in_specs=[
-            pl.BlockSpec(memory_space=pltpu.SMEM), row(2 * inner + KEYS + STEP_PAD), row(inner),
+            pl.BlockSpec(memory_space=pltpu.SMEM), row(2 * inner + KEYS + STEP_PAD),
         ]
-        + [all_of(*part.shape) for part in params],
+        + [all_of(*part.shape) for part in params]
+        + [HBM] * 2,
         out_specs=[
             row(inner), row(KEYS), row(inner), row(KEYS), row(LANES), row(LANES), row(inner), row(inner),
             pl.BlockSpec((1, N, inner), lambda i: (i, 0, 0)), all_of(2 * chunks, LANES),
-            all_of(8, inner), all_of(8, LANES),
+            all_of(8, inner), all_of(8, LANES), HBM, HBM,
         ],
         out_shape=[
             out(inner, bf16), out(KEYS, bf16), out(inner, f32), out(KEYS, f32), out(LANES, f32), out(LANES, f32),
             out(inner, f32), out(inner, f32), jax.ShapeDtypeStruct((chunks, N, inner), bf16),
             jax.ShapeDtypeStruct((2 * chunks, LANES), f32), jax.ShapeDtypeStruct((8, inner), f32),
-            jax.ShapeDtypeStruct((8, LANES), f32),
+            jax.ShapeDtypeStruct((8, LANES), f32), jax.ShapeDtypeStruct(cot.shape, bf16),
+            jax.ShapeDtypeStruct(out_w.shape, bf16),
         ],
-        scratch_shapes=[pltpu.VMEM((N, inner), f32), pltpu.VMEM((8, inner), f32), pltpu.VMEM((8, KEYS), f32)],
-        compiler_params=pltpu.CompilerParams(vmem_limit_bytes=16 * 2**20),
+        input_output_aliases={2 + len(params): 12, 3 + len(params): 13},
+        scratch_shapes=[pltpu.VMEM((N, inner), f32), pltpu.VMEM((8, inner), f32), pltpu.VMEM((8, KEYS), f32)]
+        + sems(copies, 1)[:2],
+        compiler_params=remote_params(4, 16),
         cost_estimate=pl.CostEstimate(
             flops=length * inner * 1024, bytes_accessed=length * inner * 24, transcendentals=length * heads * CHUNK
         ),
         name="mixer_forward",
-    )(meta, projected, grad_mixed, *params)
+    )(meta, projected, *params, cot, out_w)
 
 
 def mixer_backward(meta, projected, grad_mixed, chan, conv, head_vec, kept, sums, branch, grad_out, span, heads):
@@ -601,10 +614,56 @@
     return out
 
 
+def cot_order(near):
+    bits = bits_of(lax.axis_size("seq"))
+    return bits if near else bits[::-1]
+
+
+def left_over(order):
+    return [h for h in combos(order[:-1]) if len(order) > 1 and h & order[-2]]
+
+
+class Late:
+    def __init__(self, src, dst, out_src, out_dst, send, recv):
+        me = self.me = Place()
+        self.mover = Mover(send, recv, None)
+        self.copies, self.far, self.forward = [], [], []
+        for o in range(me.near):
+            order = cot_order(o)
+            for h in left_over(order):
+                at = (flip(me.zl, o), flip(me.s, h))
+                self.copies.append(self.mover.plan(src.at[at], dst.at[at], me.at(s=order[-1])))
+        half = out_src.shape[2] // 2
+        for o in range(1, me.far):
+            at = (me.zh, me.c, pl.ds(half, half))
+            self.far.append(self.mover.plan(out_src.at[at], out_dst.at[at], me.at(zh=o)))
+        for o in range(1, me.far):
+            at = (flip(me.zh, o), me.c, pl.ds(half, half))
+            self.forward.append(self.mover.plan(out_dst.at[at], out_dst.at[at], me.at(c=1)))
+
+    def start(self):
+        _, far, sibling = self.me.partners()
+        greet([self.me.at(s=bit) for bit in sorted({cot_order(o)[-1] for o in range(self.me.near)})] + far + sibling)
+        for copy in self.far + self.copies:
+            copy.start()
+
+    def middle(self):
+        for far, forward in zip(self.far, self.forward):
+            far.wait_recv()
+            forward.start()
+
+    def end(self):
+        for copy in self.copies + self.forward:
+            copy.wait_recv()
+        self.mover.close()
+
+
 def gather_kernel(
-    in_ref, steps_ref, out_ref, rows_ref, cot_ref, meta_ref,
-    w_ref, o_ref, x_ref, ct_ref, m_ref, send, recv, local,
+    in_ref, out_ref, cot_ref, inputs_ref, gain_ref, step_ref, lengths_ref, width_ref,
+    w_ref, o_ref, x_ref, ct_ref, m_ref, inv_ref, rows_ref, steps_ref, meta_ref, send, recv, local,
 ):
+    prepare(inputs_ref, gain_ref, step_ref, lengths_ref, width_ref, rows_ref, inv_ref, steps_ref, meta_ref)
+    cot_ref = cot_ref.at[0]
     me = Place()
     s, zl, zh, c = me.s, me.zl, me.zh, me.c
     columns = w_ref.shape[-1] - KEYS - STEP_PAD
@@ -614,7 +673,7 @@
     mover = Mover(send, recv, local)
     bits = bits_of(me.peers)
 
-    def plane_path(src, dst, order, near):
+    def plane_path(src, dst, order, near, skip=()):
         view = dst.at[flip(zl, near)]
         if near:
             copy = mover.put(src, dst.at[zl, s], me.at(zl=near))
@@ -626,6 +685,8 @@
         for bit in order:
             copies = []
             for h in held:
+                if bit == order[-1] and h in skip:
+                    continue
                 at = view.at[flip(s, h)]
                 copies.append(mover.put(at if near or h else src, at if near else dst.at[zl, flip(s, h)], me.at(s=bit)))
             held = held + [h ^ bit for h in held]
@@ -686,9 +747,10 @@
 
     def out_path():
         own = mover.keep(out_ref, o_ref.at[zh, c])
-        copies = [(o, mover.put(out_ref, o_ref.at[zh, c], me.at(zh=o))) for o in range(1, me.far)]
+        part = pl.ds(0, out_ref.shape[0] // 2)
+        copies = [(o, mover.put(out_ref.at[part], o_ref.at[zh, c, part], me.at(zh=o))) for o in range(1, me.far)]
         first = mover.put(out_ref, o_ref.at[zh, c], me.at(c=1))
-        last = yield from spread_path(copies, lambda h: o_ref.at[h, c])
+        last = yield from spread_path(copies, lambda h: o_ref.at[h, c, part])
         yield
         own.wait()
         for copy in last + [first]:
@@ -727,14 +789,12 @@
             copy.wait_recv()
 
     own_x = plane_path(rows_ref, x_ref, bits, 0)
-    own_c = plane_path(cot_ref, ct_ref, bits[::-1], 0)
-    near_x = [plane_path(rows_ref, x_ref, bits, o) for o in range(1, me.near)]
-    near_c = [plane_path(cot_ref, ct_ref, bits[::-1], o) for o in range(1, me.near)]
+    near_x = [plane_path(rows_ref, x_ref, bits[::-1], o) for o in range(1, me.near)]
+    own_c, *near_c = [plane_path(cot_ref, ct_ref, cot_order(o), o, left_over(cot_order(o))) for o in range(me.near)]
+    keys, weights, outs, extra = key_path(), weight_path(), out_path(), meta_path()
     near = near_x + near_c
-    keys, weights, outs = key_path(), weight_path(), out_path()
-    turn([own_x, own_c, weights] + near + [keys, outs])
-    extra = meta_path()
-    turn([extra, own_x, own_c] + [weights] * me.peers + [keys] + near + [keys])
+    turn([keys, own_x, own_c, weights] + near + [outs])
+    turn([keys, own_x, own_c, keys] + [weights] * me.peers + [keys] + near + [extra])
     turn([own_x, own_c] + near + [keys, outs, weights, keys, weights])
     run_paths([weights, extra, keys, outs, own_x, own_c] + near)
     mover.close()
@@ -748,68 +808,101 @@
     return [pltpu.SemaphoreType.DMA((copies,)), pltpu.SemaphoreType.DMA((copies,)), pltpu.SemaphoreType.DMA((kept,))]
 
 
-def gather(in_w, steps, out_w, rows, cot, meta):
+def prepare(x_ref, gain_ref, step_ref, lengths_ref, width_ref, normed_ref, inv_ref, steps_ref, meta_ref):
+    x = x_ref[0].astype(f32)
+    inv = lax.rsqrt(jnp.mean(x * x, axis=1, keepdims=True) + epsilon)
+    normed_ref[...] = (x * inv * gain_ref[...]).astype(bf16)
+    inv_ref[...] = jnp.broadcast_to(inv, inv_ref.shape)
+    steps_ref[...] = jnp.zeros_like(steps_ref)
+    steps_ref[:, :H] = step_ref[...]
+    lanes = iota(meta_ref.shape, 1)
+    meta = jnp.where(lanes == DOCS, width_ref[0], 0)
+    for i in range(DOCS):
+        meta = jnp.where(lanes == i, lengths_ref[0, i], meta)
+    meta_ref[...] = meta
+
+
+def gather(in_w, out_w, cot, inputs, gain, step_w, lengths, head_width):
     me = Place()
     peers, near, far = me.peers, me.near, me.far
     shape = lambda lead, part: jax.ShapeDtypeStruct(lead + part, bf16)
+    rows = inputs.shape[1:]
     columns = 2 * E // (peers * near)
     runs = 2 * (far if near > 1 else 1)
     copies = runs * (peers * near - 1) + (peers + 1) * (2 * far - 1) + 2 * (near * peers - 1)
+    copies -= sum(len(left_over(cot_order(o))) for o in range(near))
     copies += 2 * near + peers + 2 * far - 4
+    smem = pl.BlockSpec(memory_space=pltpu.SMEM)
     return pl.pallas_call(
         gather_kernel,
         out_shape=[
             shape((peers, far, near, 2), (in_w.shape[0], columns + KEYS + STEP_PAD)),
             shape((far, 2), out_w.shape),
-            shape((near, peers), rows.shape),
-            shape((near, peers), cot.shape),
-            jax.ShapeDtypeStruct((near,) + meta.shape, meta.dtype),
+            shape((near, peers), rows),
+            shape((near, peers), rows),
+            jax.ShapeDtypeStruct((near, 8, LANES), jnp.int32),
+            jax.ShapeDtypeStruct((rows[0], LANES), f32),
         ],
-        in_specs=[HBM] * 6,
-        out_specs=[HBM] * 5,
-        scratch_shapes=sems(copies, runs + 6),
+        in_specs=[HBM] * 3 + [VMEM] * 3 + [smem] * 2,
+        out_specs=[HBM] * 5 + [VMEM],
+        scratch_shapes=[
+            pltpu.VMEM(rows, bf16), pltpu.VMEM((in_w.shape[0], STEP_PAD), bf16), pltpu.VMEM((8, LANES), jnp.int32)
+        ]
+        + sems(copies, runs + 6),
         compiler_params=remote_params(0, 58),
         name="gather_all",
-    )(in_w, steps, out_w, rows, cot, meta)
-
-
-def total_kernel(part_ref, gated_ref, chan_ref, sum_ref, mixed_ref, box, send, recv, local):
+    )(in_w, out_w, cot, inputs, gain, step_w, lengths, head_width)
+
+
+def total_kernel(part_ref, gated_ref, chan_ref, grad_ref, sum_ref, mixed_ref, mine, box, send, recv, local):
     me = Place()
     cube = me.partners()[0]
     greet(cube)
     mover = Mover(send, recv, local)
-    copies = [mover.put(part_ref, box.at[i], device) for i, device in enumerate(cube)]
-    total = part_ref[...]
+    chunks = part_ref.shape[0] // 2
+    tiles = [slice(lane, lane + LANES) for lane in range(0, gated_ref.shape[1], LANES)]
+    mine[...] = part_ref[...]
+
+    def products(i, carry):
+        at = pl.ds(pl.multiple_of(i * CHUNK, CHUNK), CHUNK)
+        cross = jnp.zeros((CHUNK, LANES), f32)
+        for lanes in tiles:
+            cross = cross + gated_ref[at, lanes] * (grad_ref[at, lanes] * chan_ref[5:6, lanes])
+        row = pl.ds(chunks + i, 1)
+        mine[row, :] = jnp.sum(cross.T, axis=0, keepdims=True) * part_ref[row, :]
+        return carry
+
+    lax.fori_loop(0, chunks, products, 0)
+    copies = [mover.put(mine, box.at[i], device) for i, device in enumerate(cube)]
+    total = mine[...]
     for i, copy in enumerate(copies):
         copy.wait_recv()
         total = total + box[i]
     sum_ref[...] = total
-    chunks = part_ref.shape[0] // 2
-
-    def step(i, carry):
+
+    def mix(i, carry):
         at = pl.ds(pl.multiple_of(i * CHUNK, CHUNK), CHUNK)
         inv = lax.rsqrt(jnp.broadcast_to(sum_ref[pl.ds(i, 1), :], (CHUNK, CHUNK)).T + epsilon)
-        for lane in range(0, gated_ref.shape[1], LANES):
-            lanes = slice(lane, lane + LANES)
+        for lanes in tiles:
             mixed_ref[at, lanes] = (gated_ref[at, lanes] * inv * chan_ref[5:6, lanes]).astype(bf16)
         return carry
 
-    lax.fori_loop(0, chunks, step, 0)
+    lax.fori_loop(0, chunks, mix, 0)
     mover.close()
 
 
-def cube_total(part, gated, chan):
+def cube_total(part, gated, chan, grad):
     me = Place()
     count = me.peers * me.near - 1
     return pl.pallas_call(
         total_kernel,
         out_shape=[jax.ShapeDtypeStruct(part.shape, f32), jax.ShapeDtypeStruct(gated.shape, bf16)],
-        in_specs=[VMEM] * 3,
+        in_specs=[VMEM] * 4,
         out_specs=[VMEM] * 2,
-        scratch_shapes=[pltpu.VMEM((count,) + part.shape, f32)] + sems(count, 1),
+        scratch_shapes=[pltpu.VMEM(part.shape, f32), pltpu.VMEM((count,) + part.shape, f32)] + sems(count, 1),
         compiler_params=remote_params(1, 12),
         name="cube_total",
-    )(part, gated, chan)
+    )(part, gated, chan, grad)
 
 
 def add_rows(out, parts):
@@ -1078,38 +1171,6 @@
         self.mover.close()
 
 
-def prepare_kernel(x_ref, gain_ref, step_ref, lengths_ref, width_ref, normed_ref, inv_ref, steps_ref, meta_ref):
-    x = x_ref[0].astype(f32)
-    inv = lax.rsqrt(jnp.mean(x * x, axis=1, keepdims=True) + epsilon)
-    normed_ref[...] = (x * inv * gain_ref[...]).astype(bf16)
-    inv_ref[...] = jnp.broadcast_to(inv, inv_ref.shape)
-    steps_ref[...] = jnp.zeros_like(steps_ref)
-    steps_ref[:, :H] = step_ref[...]
-    lanes = iota(meta_ref.shape, 1)
-    meta = jnp.where(lanes == DOCS, width_ref[0], 0)
-    for i in range(DOCS):
-        meta = jnp.where(lanes == i, lengths_ref[0, i], meta)
-    meta_ref[...] = meta
-
-
-def prepare(inputs, gain, step_weight, doc_lengths, head_width):
-    tokens, width = inputs.shape[1:]
-    smem = pl.BlockSpec(memory_space=pltpu.SMEM)
-    return pl.pallas_call(
-        prepare_kernel,
-        out_shape=[
-            jax.ShapeDtypeStruct((tokens, width), bf16),
-            jax.ShapeDtypeStruct((tokens, LANES), f32),
-            jax.ShapeDtypeStruct((step_weight.shape[0], STEP_PAD), bf16),
-            jax.ShapeDtypeStruct((8, LANES), jnp.int32),
-        ],
-        in_specs=[VMEM] * 3 + [smem] * 2,
-        out_specs=[VMEM] * 4,
-        compiler_params=pltpu.CompilerParams(vmem_limit_bytes=16 * 2**20),
-        name="prepare",
-    )(inputs, gain, step_weight, doc_lengths, head_width)
-
-
 def finish_kernel(
     x_ref, cot_ref, gain_ref, inv_ref, og_ref, ob_ref, ow_ref, ok_ref, u_ref,
     out_ref, gx_ref, gw_ref, gs_ref, gc_ref, gb_ref, gp_ref, gn_ref, g0_ref, g1_ref, g2_ref,
@@ -1163,19 +1224,22 @@
     rows = in_weight.shape[0]
     row = lambda vector: vector[None, :]
 
-    normed, inv, steps, meta = prepare(inputs, row(pre_gain), step_weight, doc_lengths, head_width)
-    in_w, out_w, normed, cot_all, meta = gather(in_weight, steps, out_weight, normed, cotangent[0], meta)
+    in_w, out_w, normed, cot_all, meta, inv = gather(
+        in_weight, out_weight, cotangent, inputs, row(pre_gain), step_weight, doc_lengths, head_width
+    )
     in_w = in_w.reshape(width, -1)
-    out_w = out_w.reshape(inner, width)
     normed = normed.reshape(length, width)
-    cot_all = cot_all.reshape(length, width)
     meta = meta[:, 0, :8]
 
     params = (conv_weight, row(conv_bias), row(norm_gain), row(step_bias), row(decay_log), row(skip_gain))
     projected = mm(normed, in_w, NN)
+    *kept, gated, states, part, chan, head_vec, cot_all, out_w = mixer_forward(
+        meta, projected, params, cot_all, out_w, span, heads
+    )
+    out_w = out_w.reshape(inner, width)
+    cot_all = cot_all.reshape(length, width)
     grad_mixed = mm(cot_all, out_w, NT)
-    *kept, gated, states, part, chan, head_vec = mixer_forward(meta, projected, grad_mixed, params, span, heads)
-    sums, mixed = cube_total(part, gated, chan)
+    sums, mixed = cube_total(part, gated, chan, grad_mixed)
     branch = mm(mixed, out_w, NN).astype(bf16)
     grad_out = mm(mixed, cot_all, TN).astype(bf16)
     grad_cols, small, branch, grad_out_weight = mixer_backward(

time: 301 us -> 288 us (0.957)
  Pallas kernels: 256 us -> 247 us
  local copies, waits for them, and re-layouts: 7.92 us -> 2.48 us
    pallas_call x1, Pallas kernels: 19 us -> 7.91 us  [cube_total(): pl.pallas_call(total_kernel, out_shape=[jax.ShapeDtypeStruct(part.shape,...]
    unnamed x43 -> x31, local copies, waits for them, and re-layouts: 6.48 us -> 1.04 us
    pallas_call x1, Pallas kernels: 14.3 us -> 18.7 us  [mixer_forward(): pl.pallas_call(partial(forward_kernel, span=span, heads=heads), grid=(chu...]
where the time goes in v7:
time: 288 us; the launch traced here: 287 us
  Pallas kernels  247 us (86%)
  matrix products  35.7 us (12%)
    pallas_call x1, Pallas kernels, gather(): pl.pallas_call(gather_kernel, out_shape=[shape((peers, far, near, 2), (in...  102 us
    pallas_call x1, Pallas kernels, scatter(): pl.pallas_call(scatter_kernel, out_shape=[jax.ShapeDtypeStruct((tokens, w...  85.2 us
    dot_general x6, matrix products, mm(): lax.dot_general(a, b, (dims, ((), ())), precision=precision, preferred_el...  35.7 us
    pallas_call x1, Pallas kernels, mixer_backward(): pl.pallas_call(partial(backward_kernel, span=span, heads=heads), grid=(ch...  30.8 us
    pallas_call x1, Pallas kernels, mixer_forward(): pl.pallas_call(partial(forward_kernel, span=span, heads=heads), grid=(chu...  18.7 us
    pallas_call x1, Pallas kernels, cube_total(): pl.pallas_call(total_kernel, out_shape=[jax.ShapeDtypeStruct(part.shape,...  7.91 us

profile of v7, /device:TPU:0, one launch (start us, length us, event | category | flops | bytes accessed | tf_op | source)
XLA Modules:
  0.0 287.4 jit_solution(13790840821889962350)
XLA Ops:
  1.3 0.7 broadcast_in_dim.24.bias_ref
  2.0 102.0 %gather_all.1 = (bf16[4,2,2,2,64,1408]{5,4,3,2,1,0:T(8,128)(2,1)}, bf16[2,2,128,2048]{3,2,1,0:T(8,128)(2,1)}, bf16[2,4,128,2048]{3,2,1,0:T(8,128)(2,1)}, bf16[2,...) custom-call(bf16[64,8448]{1,0:T(8,128)(2,1)} %in_ref.1, bf16[128,2048]{1,0:T(8,128)(2,1)} %out_ref.1, ...), custom_call_target="tpu_custom_call" | custom-call | tf_op jit(solution)/shard_map/gather_all/pallas_call | solution.py:836
  104.0 0.7 slice.3
  104.7 0.0 copy-start.1
  104.7 0.0 copy-start.2
  104.7 0.0 copy-start.5
  104.7 0.0 copy-start.8
  104.7 0.0 copy-start.9
  104.7 0.0 copy-start.10
  104.7 0.0 copy-start.11
  104.7 10.6 %fusion.proj_ref = f32[1024,1408]{1,0:T(8,128)S(1)} fusion(bf16[1024,2048]{1,0:T(8,128)(2,1)} %bitcast.55, bf16[2048,1408]{1,0:T(8,128)(2,1)} %bitcast.51), kind=kOutput, calls=%fused_computation.4 | convolution fusion | flops 5905580032 | bytes 15728640 | tf_op jit(solution)/shard_map/dot_general | solution.py:26
  115.4 0.0 copy-done.1
  115.4 0.0 copy-done.2
  115.4 0.0 copy-done.5
  115.4 0.0 copy-done.8
  115.4 0.0 copy-done.9
  115.4 0.0 copy-done.10
  115.4 0.0 copy-done.11
  115.4 0.0 copy-start
  115.4 18.7 %mixer_forward.1 = (bf16[1024,512]{1,0:T(8,128)(2,1)S(1)}, bf16[1024,256]{1,0:T(8,128)(2,1)S(1)}, f32[1024,512]{1,0:T(8,128)S(1)}, f32[1024,256]{1,0:T(8,128)S(1...) custom-call(s32[2,8]{1,0:T(2,128)S(1)} %bitcast.43, ...), custom_call_target="tpu_custom_call", output_to_operand_aliasing={{12}: (8, {}), {13}: (9, {})} | custom-call | flops 536870912 | bytes 12582912 | tf_op jit(solution)/shard_map/mixer_forward/pallas_call | solution.py:408
  134.2 0.0 copy-done
  134.2 2.4 fusion.1.grad_ref
  136.6 7.9 %cube_total.1 = (f32[16,128]{1,0:T(8,128)S(1)}, bf16[1024,512]{1,0:T(8,128)(2,1)S(1)}) custom-call(f32[16,128]{1,0:T(8,128)S(1)} %get-tuple-element.72.part_ref, f32[1024,512]{1,0:T(8,128)S(1)} %get-tuple-element.73.gated_ref, f32[8,512]{1,0:T(8,128)S(1)} %get-tuple-element.62.chan_ref, f32[1024,512]{1,0:T(8,128)S(1)} %fusion.1.grad_ref), custom_call_target="tpu_custom_call" | custom-call | tf_op jit(solution)/shard_map/cube_total/pallas_call | solution.py:897
  144.5 2.5 convolution_convert_fusion.2
  147.0 0.0 slice-start
  147.0 4.3 %convolution_convert_fusion.1 = bf16[1024,2048]{1,0:T(8,128)(2,1)} fusion(bf16[1024,512]{1,0:T(8,128)(2,1)S(1)} %get-tuple-element.75, bf16[512,2048]{1,0:T(8,128)(2,1)S(1)} %bitcast.37), kind=kOutput, calls=%fused_computation.2 | convolution fusion | flops 2149580800 | bytes 7340032 | tf_op jit(solution)/shard_map/dot_general | solution.py:26
  151.3 0.0 slice-start.1
  151.3 0.0 copy-start.12
  151.3 30.8 %mixer_backward.1 = (bf16[1024,1408]{1,0:T(8,128)(2,1)S(1)}, f32[8,4352]{1,0:T(8,128)S(1)}, bf16[2,2,128,2048]{3,2,1,0:T(8,128)(2,1)S(1)}, f32[128,2048]{1,0:T(8,128)S(1)}) custom-call(s32[2,8]{1,0:T(2,128)S(1)} %bitcast.44, f32[1024,1408]{1,0:T(8,128)} %copy-done, f32[1024,512]{1,0:T(8,128)S(1)} %fusion.1.grad_ref, ...), custom_call_target="tpu_custom_call" | custom-call | flops 1610612736 | bytes 15728640 | tf_op jit(solution)/shard_map/mixer_backward/pallas_call | solution.py:452
  182.1 0.0 slice-done
  182.1 0.0 slice-done.1
  182.1 0.0 copy-done.12
  182.1 7.3 %multiply_reduce_fusion = (f32[2048]{0:T(1024)S(1)}, bf16[1024,2048]{1,0:T(8,128)(2,1)S(1)}) fusion(bf16[2,4,128,2048]{3,2,1,0:T(8,128)(2,1)S(1)} %copy-done.12, bf16[1024,1408]{1,0:T(8,128)(2,1)S(1)} %get-tuple-element.76, bf16[2048,1408]{1,0:T(8,128)(2,1)S(1)} %bitcast.54), kind=kOutput, calls=%fused_computation | convolution fusion | flops 5913966592 | bytes 17047552 | tf_op jit(solution)/shard_map/dot_general | solution.py:26
  189.4 0.0 copy-start.6
  189.4 8.7 %convolution_convert_fusion = bf16[2048,1408]{1,0:T(8,128)(2,1)} fusion(bf16[1024,2048]{1,0:T(8,128)(2,1)S(1)} %bitcast.56, bf16[1024,1408]{1,0:T(8,128)(2,1)S(1)} %get-tuple-element.76), kind=kOutput, calls=%fused_computation.1 | convolution fusion | flops 5908463616 | bytes 12845056 | tf_op jit(solution)/shard_map/dot_general | solution.py:26
  198.1 0.0 copy-done.6
  198.1 0.0 copy-start.3
  198.1 0.0 copy-start.4
  198.2 0.0 copy-start.7
  198.2 85.2 %scatter_all.1 = (f32[128,2048]{1,0:T(8,128)S(1)}, bf16[64,8192]{1,0:T(8,128)(2,1)S(1)}, f32[128,2048]{1,0:T(8,128)S(1)}, f32[64,384]{1,0:T(8,128)S(1)}, f32[8,4352]{1,0:T(8,128)S(1)}) custom-call(bf16[2,4,128,2048]{3,2,1,0:T(8,128)(2,1)S(1)} %bitcast.35, bf16[4,2,2,2,64,1408]{5,4,3,2,1,0:T(8,128)(2,1)} %bitcast.49, ...), custom_call_target="tpu_custom_call" | custom-call | bytes 250000000 | tf_op jit(solution)/shard_map/scatter_all/pallas_call | solution.py:1100
  283.4 0.0 copy-done.3
  283.4 0.0 copy-done.4
  283.4 0.0 copy-done.7
  283.4 2.3 finish.1
  285.7 0.7 reduce
  286.4 1.0 copy.32
  (1 shorter events, 0.0 us)
Async XLA Ops:
  104.7 10.7 %copy-start.1 = (bf16[2,4,128,2048]{3,2,1,0:T(8,128)(2,1)S(1)}, bf16[2,4,128,2048]{3,2,1,0:T(8,128)(2,1)}, u32[]{:S(2)}) copy-start(bf16[2,4,128,2048]{3,2,1,0:T(8,128)(2,1)} %get-tuple-element.58.cot_in) | copy-start | bytes 12582916
  104.7 10.7 %copy-start.2 = (bf16[2,2,128,2048]{3,2,1,0:T(8,128)(2,1)S(1)}, bf16[2,2,128,2048]{3,2,1,0:T(8,128)(2,1)}, u32[]{:S(2)}) copy-start(bf16[2,2,128,2048]{3,2,1,0:T(8,128)(2,1)} %get-tuple-element.59.out_in) | copy-start | bytes 6291460
  104.7 10.7 %copy-start.5 = (f32[4,4352]{1,0:T(4,128)S(1)}, f32[4,4352]{1,0:T(4,128)}, u32[]{:S(2)}) copy-start(f32[4,4352]{1,0:T(4,128)} %conv_ref.3) | copy-start | bytes 208900
  104.7 10.7 %copy-start.8 = (f32[4096]{0:T(1024)S(1)}, f32[4096]{0:T(1024)}, u32[]{:S(2)}) copy-start(f32[4096]{0:T(1024)} %param.26) | copy-start | bytes 49156
  104.7 10.7 %copy-start.9 = (f32[64]{0:T(128)S(1)}, f32[64]{0:T(128)}, u32[]{:S(2)}) copy-start(f32[64]{0:T(128)} %param.23) | copy-start | bytes 772
  104.7 10.7 %copy-start.10 = (f32[64]{0:T(128)S(1)}, f32[64]{0:T(128)}, u32[]{:S(2)}) copy-start(f32[64]{0:T(128)} %param.24) | copy-start | bytes 772
  104.7 10.7 %copy-start.11 = (f32[64]{0:T(128)S(1)}, f32[64]{0:T(128)}, u32[]{:S(2)}) copy-start(f32[64]{0:T(128)} %param.25) | copy-start | bytes 772
  115.4 18.8 %copy-start = (f32[1024,1408]{1,0:T(8,128)}, f32[1024,1408]{1,0:T(8,128)S(1)}, u32[]{:S(2)}) copy-start(f32[1024,1408]{1,0:T(8,128)S(1)} %fusion.proj_ref) | copy-start | bytes 17301508
  147.0 35.2 %slice-start = ((s8[5767168]{0:T(1024)(128)(4,1)}), s8[4194304]{0:T(1024)(128)(4,1)S(1)}, s32[]{:S(2)}) async-start(s8[5767168]{0:T(1024)(128)(4,1)} %bitcast.52), calls=%async_computation | async-start | bytes 8388608
  151.3 30.9 %slice-start.1 = ((s8[5767168]{0:T(1024)(128)(4,1)}), s8[1572864]{0:T(1024)(128)(4,1)S(1)}, s32[]{:S(2)}) async-start(s8[5767168]{0:T(1024)(128)(4,1)} %bitcast.52), calls=%async_computation.1 | async-start | bytes 3145728
  151.3 30.9 %copy-start.12 = (bf16[2,4,128,2048]{3,2,1,0:T(8,128)(2,1)S(1)}, bf16[2,4,128,2048]{3,2,1,0:T(8,128)(2,1)}, u32[]{:S(2)}) copy-start(bf16[2,4,128,2048]{3,2,1,0:T(8,128)(2,1)} %get-tuple-element.56) | copy-start | bytes 12582916
  189.4 8.7 %copy-start.6 = (f32[2048]{0:T(1024)S(1)}, f32[2048]{0:T(1024)}, u32[]{:S(2)}) copy-start(f32[2048]{0:T(1024)} %param.18) | copy-start | bytes 24580
  198.1 85.3 %copy-start.3 = (bf16[1,128,2048]{2,1,0:T(8,128)(2,1)S(1)}, bf16[1,128,2048]{2,1,0:T(8,128)(2,1)}, u32[]{:S(2)}) copy-start(bf16[1,128,2048]{2,1,0:T(8,128)(2,1)} %x_ref.1) | copy-start | bytes 1572868
  198.1 85.3 %copy-start.4 = (bf16[1,128,2048]{2,1,0:T(8,128)(2,1)S(1)}, bf16[1,128,2048]{2,1,0:T(8,128)(2,1)}, u32[]{:S(2)}) copy-start(bf16[1,128,2048]{2,1,0:T(8,128)(2,1)} %cot_ref.3) | copy-start | bytes 1572868
  198.2 85.3 %copy-start.7 = (f32[128,128]{1,0:T(8,128)S(1)}, f32[128,128]{1,0:T(8,128)}, u32[]{:S(2)}) copy-start(f32[128,128]{1,0:T(8,128)} %get-tuple-element.54.inv_ref) | copy-start | bytes 196612

commit v8 on v7

--- a/solution.py
+++ b/solution.py
@@ -132,9 +132,9 @@
 
 
 def forward_kernel(
-    meta_ref, proj_ref, conv_ref, bias_ref, norm_ref, step_b_ref, decay_ref, skip_ref, cot_in, out_in,
+    meta_ref, rows_ref, w_ref, conv_ref, bias_ref, norm_ref, step_b_ref, decay_ref, skip_ref, cot_in, out_in,
     val_out, key_out, vsum_ref, ksum_ref, raw_ref, cum_ref, y_ref, gated_ref, state_ref, sums_ref, chan_ref, head_ref,
-    cot_out, out_out, state, last_v, last_k, send, recv,
+    cot_out, out_out, proj_out, state, last_v, last_k, proj_v, send, recv,
     *, span, heads,
 ):
     i = pl.program_id(0)
@@ -149,6 +149,15 @@
         state[...] = jnp.zeros_like(state)
         last_v[...] = jnp.zeros_like(last_v)
         last_k[...] = jnp.zeros_like(last_k)
+
+    @pl.when(i % 2 == 0)
+    def _():
+        for lane in range(0, w_ref.shape[1], 256):
+            lanes = slice(lane, min(lane + 256, w_ref.shape[1]))
+            proj_v[:, lanes] = mm(rows_ref[...], w_ref[:, lanes], NN)
+
+    proj_ref = proj_v.at[pl.ds(pl.multiple_of(i % 2 * CHUNK, CHUNK), CHUNK)]
+    proj_out[...] = proj_ref[...]
 
     @pl.when(i == chunks - 1)
     def _():
@@ -397,8 +406,9 @@
         early.end()
 
 
-def mixer_forward(meta, projected, params, cot, out_w, span, heads):
-    length = projected.shape[0]
+def mixer_forward(meta, normed, in_w, params, cot, out_w, span, heads):
+    length = normed.shape[0]
+    columns = in_w.shape[1]
     inner = heads * P_SIZE
     chunks = length // CHUNK
     copies = sum(len(left_over(cot_order(o))) for o in range(cot.shape[0])) + 2 * (out_w.shape[0] - 1)
@@ -409,31 +419,33 @@
         partial(forward_kernel, span=span, heads=heads),
         grid=(chunks,),
         in_specs=[
-            pl.BlockSpec(memory_space=pltpu.SMEM), row(2 * inner + KEYS + STEP_PAD),
+            pl.BlockSpec(memory_space=pltpu.SMEM), pl.BlockSpec((2 * CHUNK, normed.shape[1]), lambda i: (i // 2, 0)),
+            all_of(*in_w.shape),
         ]
         + [all_of(*part.shape) for part in params]
         + [HBM] * 2,
         out_specs=[
             row(inner), row(KEYS), row(inner), row(KEYS), row(LANES), row(LANES), row(inner), row(inner),
             pl.BlockSpec((1, N, inner), lambda i: (i, 0, 0)), all_of(2 * chunks, LANES),
-            all_of(8, inner), all_of(8, LANES), HBM, HBM,
+            all_of(8, inner), all_of(8, LANES), HBM, HBM, row(columns),
         ],
         out_shape=[
             out(inner, bf16), out(KEYS, bf16), out(inner, f32), out(KEYS, f32), out(LANES, f32), out(LANES, f32),
             out(inner, f32), out(inner, f32), jax.ShapeDtypeStruct((chunks, N, inner), bf16),
             jax.ShapeDtypeStruct((2 * chunks, LANES), f32), jax.ShapeDtypeStruct((8, inner), f32),
             jax.ShapeDtypeStruct((8, LANES), f32), jax.ShapeDtypeStruct(cot.shape, bf16),
-            jax.ShapeDtypeStruct(out_w.shape, bf16),
+            jax.ShapeDtypeStruct(out_w.shape, bf16), out(columns, f32),
         ],
-        input_output_aliases={2 + len(params): 12, 3 + len(params): 13},
+        input_output_aliases={3 + len(params): 12, 4 + len(params): 13},
         scratch_shapes=[pltpu.VMEM((N, inner), f32), pltpu.VMEM((8, inner), f32), pltpu.VMEM((8, KEYS), f32)]
+        + [pltpu.VMEM((2 * CHUNK, columns), f32)]
         + sems(copies, 1)[:2],
-        compiler_params=remote_params(4, 16),
+        compiler_params=remote_params(4, 58),
         cost_estimate=pl.CostEstimate(
             flops=length * inner * 1024, bytes_accessed=length * inner * 24, transcendentals=length * heads * CHUNK
         ),
         name="mixer_forward",
-    )(meta, projected, *params, cot, out_w)
+    )(meta, normed, in_w, *params, cot, out_w)
 
 
 def mixer_backward(meta, projected, grad_mixed, chan, conv, head_vec, kept, sums, branch, grad_out, span, heads):
@@ -620,7 +632,7 @@
 
 
 def left_over(order):
-    return [h for h in combos(order[:-1]) if len(order) > 1 and h & order[-2]]
+    return combos(order[:-1])
 
 
 class Late:
@@ -633,12 +645,11 @@
             for h in left_over(order):
                 at = (flip(me.zl, o), flip(me.s, h))
                 self.copies.append(self.mover.plan(src.at[at], dst.at[at], me.at(s=order[-1])))
-        half = out_src.shape[2] // 2
         for o in range(1, me.far):
-            at = (me.zh, me.c, pl.ds(half, half))
+            at = (me.zh, me.c)
             self.far.append(self.mover.plan(out_src.at[at], out_dst.at[at], me.at(zh=o)))
         for o in range(1, me.far):
-            at = (flip(me.zh, o), me.c, pl.ds(half, half))
+            at = (flip(me.zh, o), me.c)
             self.forward.append(self.mover.plan(out_dst.at[at], out_dst.at[at], me.at(c=1)))
 
     def start(self):
@@ -747,14 +758,10 @@
 
     def out_path():
         own = mover.keep(out_ref, o_ref.at[zh, c])
-        part = pl.ds(0, out_ref.shape[0] // 2)
-        copies = [(o, mover.put(out_ref.at[part], o_ref.at[zh, c, part], me.at(zh=o))) for o in range(1, me.far)]
         first = mover.put(out_ref, o_ref.at[zh, c], me.at(c=1))
-        last = yield from spread_path(copies, lambda h: o_ref.at[h, c, part])
         yield
         own.wait()
-        for copy in last + [first]:
-            copy.wait_recv()
+        first.wait_recv()
 
     def weight_path():
         moves = {}
@@ -792,11 +799,10 @@
     near_x = [plane_path(rows_ref, x_ref, bits[::-1], o) for o in range(1, me.near)]
     own_c, *near_c = [plane_path(cot_ref, ct_ref, cot_order(o), o, left_over(cot_order(o))) for o in range(me.near)]
     keys, weights, outs, extra = key_path(), weight_path(), out_path(), meta_path()
-    near = near_x + near_c
-    turn([keys, own_x, own_c, weights] + near + [outs])
-    turn([keys, own_x, own_c, keys] + [weights] * me.peers + [keys] + near + [extra])
-    turn([own_x, own_c] + near + [keys, outs, weights, keys, weights])
-    run_paths([weights, extra, keys, outs, own_x, own_c] + near)
+    turn([keys, weights, own_x] + near_x + [own_c, outs, extra])
+    turn([keys] + near_x + near_c + [keys] + [weights] * me.peers + [keys] + near_x + [own_x, own_c] + near_c)
+    turn([keys, weights, keys, weights, weights, weights] + near_x + [own_x] + near_c)
+    run_paths([weights, extra, keys, outs, own_x, own_c] + near_x + near_c)
     mover.close()
 
 
@@ -1232,9 +1238,8 @@
     meta = meta[:, 0, :8]
 
     params = (conv_weight, row(conv_bias), row(norm_gain), row(step_bias), row(decay_log), row(skip_gain))
-    projected = mm(normed, in_w, NN)
-    *kept, gated, states, part, chan, head_vec, cot_all, out_w = mixer_forward(
-        meta, projected, params, cot_all, out_w, span, heads
+    *kept, gated, states, part, chan, head_vec, cot_all, out_w, projected = mixer_forward(
+        meta, normed, in_w, params, cot_all, out_w, span, heads
     )
     out_w = out_w.reshape(inner, width)
     cot_all = cot_all.reshape(length, width)

time: 288 us -> 279 us (0.969)
  matrix products: 35.7 us -> 28.3 us
  Pallas kernels: 247 us -> 244 us
    pallas_call x1, Pallas kernels: 102 us -> 84.3 us  [gather(): pl.pallas_call(gather_kernel, out_shape=[shape((peers, far, near, 2), (in...]
    pallas_call x1, Pallas kernels: 18.7 us -> 32.3 us  [mixer_forward(): pl.pallas_call(partial(forward_kernel, span=span, heads=heads), grid=(chu...]
    dot_general x6 -> x5, matrix products: 35.7 us -> 28.3 us  [mm(): lax.dot_general(a, b, (dims, ((), ())), precision=precision, preferred_el...]
where the time goes in v8:
time: 279 us; the launch traced here: 278 us
  Pallas kernels  244 us (87%)
  matrix products  28.3 us (10%)
  local copies, waits for them, and re-layouts  3.68 us (1%)
    pallas_call x1, Pallas kernels, scatter(): pl.pallas_call(scatter_kernel, out_shape=[jax.ShapeDtypeStruct((tokens, w...  85.7 us
    pallas_call x1, Pallas kernels, gather(): pl.pallas_call(gather_kernel, out_shape=[shape((peers, far, near, 2), (in...  84.3 us
    pallas_call x1, Pallas kernels, mixer_forward(): pl.pallas_call(partial(forward_kernel, span=span, heads=heads), grid=(chu...  32.3 us
    pallas_call x1, Pallas kernels, mixer_backward(): pl.pallas_call(partial(backward_kernel, span=span, heads=heads), grid=(ch...  31.6 us
    dot_general x5, matrix products, mm(): lax.dot_general(a, b, (dims, ((), ())), precision=precision, preferred_el...  28.3 us
    pallas_call x1, Pallas kernels, cube_total(): pl.pallas_call(total_kernel, out_shape=[jax.ShapeDtypeStruct(part.shape,...  7.85 us

profile of v8, /device:TPU:0, one launch (start us, length us, event | category | flops | bytes accessed | tf_op | source)
XLA Modules:
  0.0 278.3 jit_solution(5367551115401247341)
XLA Ops:
  1.3 1.3 broadcast_in_dim.24.bias_ref
  2.6 84.3 %gather_all.1 = (bf16[4,2,2,2,64,1408]{5,4,3,2,1,0:T(8,128)(2,1)}, bf16[2,2,128,2048]{3,2,1,0:T(8,128)(2,1)}, bf16[2,4,128,2048]{3,2,1,0:T(8,128)(2,1)}, bf16[2,...) custom-call(bf16[64,8448]{1,0:T(8,128)(2,1)} %in_ref.1, bf16[128,2048]{1,0:T(8,128)(2,1)} %out_ref.1, ...), custom_call_target="tpu_custom_call" | custom-call | tf_op jit(solution)/shard_map/gather_all/pallas_call | solution.py:842
  86.9 1.3 slice.3
  88.2 32.3 %mixer_forward.1 = (bf16[1024,512]{1,0:T(8,128)(2,1)}, bf16[1024,256]{1,0:T(8,128)(2,1)}, f32[1024,512]{1,0:T(8,128)}, f32[1024,256]{1,0:T(8,128)}, f32[1024,128...) custom-call(s32[2,8]{1,0:T(2,128)} %bitcast.36, ...), custom_call_target="tpu_custom_call", output_to_operand_aliasing={{12}: (9, {}), {13}: (10, {})} | custom-call | flops 536870912 | bytes 12582912 | tf_op jit(solution)/shard_map/mixer_forward/pallas_call | solution.py:418
  120.4 0.0 copy-start.4
  120.4 0.0 copy-start.14
  120.5 0.0 copy-start.16
  120.5 5.4 %fusion.grad_ref = f32[1024,512]{1,0:T(8,128)S(1)} fusion(bf16[1024,2048]{1,0:T(8,128)(2,1)} %bitcast.46, bf16[512,2048]{1,0:T(8,128)(2,1)} %bitcast.49), kind=kOutput, calls=%fused_computation.4 | convolution fusion | flops 2147483648 | bytes 8388608 | tf_op jit(solution)/shard_map/dot_general | solution.py:26
  125.8 0.0 copy-done.4
  125.8 0.0 copy-done.14
  125.8 0.0 copy-done.16
  125.9 0.0 copy-start.19
  125.9 7.9 %cube_total.1 = (f32[16,128]{1,0:T(8,128)S(1)}, bf16[1024,512]{1,0:T(8,128)(2,1)S(1)}) custom-call(f32[16,128]{1,0:T(8,128)S(1)} %copy-done.16, f32[1024,512]{1,0:T(8,128)S(1)} %copy-done.4, f32[8,512]{1,0:T(8,128)S(1)} %copy-done.14, f32[1024,512]{1,0:T(8,128)S(1)} %fusion.grad_ref), custom_call_target="tpu_custom_call" | custom-call | tf_op jit(solution)/shard_map/cube_total/pallas_call | solution.py:903
  133.7 0.0 copy-done.19
  133.7 0.0 copy-start.20
  133.7 2.5 convolution_convert_fusion.2
  136.2 0.0 copy-done.20
  136.2 0.0 copy-start
  136.2 0.0 copy-start.1
  136.2 0.0 copy-start.5
  136.2 0.0 copy-start.6
  136.3 0.0 copy-start.7
  136.3 0.0 copy-start.8
  136.3 0.0 copy-start.9
  136.3 0.0 copy-start.10
  136.3 0.0 copy-start.11
  136.3 0.0 copy-start.15
  136.3 0.0 copy-start.17
  136.3 0.0 slice-start
  136.3 4.5 %convolution_convert_fusion.1 = bf16[1024,2048]{1,0:T(8,128)(2,1)} fusion(bf16[1024,512]{1,0:T(8,128)(2,1)S(1)} %get-tuple-element.77, bf16[512,2048]{1,0:T(8,128)(2,1)S(1)} %bitcast.50), kind=kOutput, calls=%fused_computation.2 | convolution fusion | flops 2149580800 | bytes 7340032 | tf_op jit(solution)/shard_map/dot_general | solution.py:26
  140.9 0.0 copy-done
  140.9 0.0 copy-done.1
  140.9 0.0 copy-done.5
  140.9 0.0 copy-done.6
  140.9 0.0 copy-done.7
  140.9 0.0 copy-done.8
  140.9 0.0 copy-done.9
  140.9 0.0 slice-start.1
  140.9 0.0 copy-start.18
  141.0 31.6 %mixer_backward.1 = (bf16[1024,1408]{1,0:T(8,128)(2,1)S(1)}, f32[8,4352]{1,0:T(8,128)S(1)}, bf16[2,2,128,2048]{3,2,1,0:T(8,128)(2,1)S(1)}, f32[128,2048]{1,0:T(8,128)S(1)}) custom-call(s32[2,8]{1,0:T(2,128)S(1)} %bitcast.37, f32[1024,1408]{1,0:T(8,128)} %get-tuple-element.61.proj_ref, f32[1024,512]{1,0:T(8,128)S(1)} %fusion.grad_ref, ...), custom_call_target="tpu_custom_call" | custom-call | flops 1610612736 | bytes 15728640 | tf_op jit(solution)/shard_map/mixer_backward/pallas_call | solution.py:464
  172.6 7.3 %multiply_reduce_fusion = (f32[2048]{0:T(1024)S(1)}, bf16[1024,2048]{1,0:T(8,128)(2,1)S(1)}) fusion(bf16[2,4,128,2048]{3,2,1,0:T(8,128)(2,1)S(1)} %copy-done.18, bf16[1024,1408]{1,0:T(8,128)(2,1)S(1)} %get-tuple-element.78, bf16[2048,1408]{1,0:T(8,128)(2,1)S(1)} %bitcast.42), kind=kOutput, calls=%fused_computation | convolution fusion | flops 5913966592 | bytes 17047552 | tf_op jit(solution)/shard_map/dot_general | solution.py:26
  179.9 0.0 copy-start.12
  179.9 8.7 %convolution_convert_fusion = bf16[2048,1408]{1,0:T(8,128)(2,1)} fusion(bf16[1024,2048]{1,0:T(8,128)(2,1)S(1)} %bitcast.45, bf16[1024,1408]{1,0:T(8,128)(2,1)S(1)} %get-tuple-element.78), kind=kOutput, calls=%fused_computation.1 | convolution fusion | flops 5908463616 | bytes 12845056 | tf_op jit(solution)/shard_map/dot_general | solution.py:26
  188.6 0.0 copy-done.12
  188.6 85.7 %scatter_all.1 = (f32[128,2048]{1,0:T(8,128)S(1)}, bf16[64,8192]{1,0:T(8,128)(2,1)S(1)}, f32[128,2048]{1,0:T(8,128)S(1)}, f32[64,384]{1,0:T(8,128)S(1)}, f32[8,4352]{1,0:T(8,128)S(1)}) custom-call(bf16[2,4,128,2048]{3,2,1,0:T(8,128)(2,1)S(1)} %bitcast.31, bf16[4,2,2,2,64,1408]{5,4,3,2,1,0:T(8,128)(2,1)} %bitcast.43, ...), custom_call_target="tpu_custom_call" | custom-call | bytes 250000000 | tf_op jit(solution)/shard_map/scatter_all/pallas_call | solution.py:1106
  274.4 2.3 finish.1
  276.7 0.7 reduce
  277.3 1.0 copy.32
  (14 shorter events, 0.0 us)
Async XLA Ops:
  120.4 5.4 %copy-start.4 = (f32[1024,512]{1,0:T(8,128)S(1)}, f32[1024,512]{1,0:T(8,128)}, u32[]{:S(2)}) copy-start(f32[1024,512]{1,0:T(8,128)} %get-tuple-element.75.gated_ref) | copy-start | bytes 6291460
  120.4 5.4 %copy-start.14 = (f32[8,512]{1,0:T(8,128)S(1)}, f32[8,512]{1,0:T(8,128)}, u32[]{:S(2)}) copy-start(f32[8,512]{1,0:T(8,128)} %get-tuple-element.64.chan_ref) | copy-start | bytes 49156
  120.5 5.4 %copy-start.16 = (f32[16,128]{1,0:T(8,128)S(1)}, f32[16,128]{1,0:T(8,128)}, u32[]{:S(2)}) copy-start(f32[16,128]{1,0:T(8,128)} %get-tuple-element.74.part_ref) | copy-start | bytes 24580
  125.9 7.9 %copy-start.19 = (bf16[2,4,128,2048]{3,2,1,0:T(8,128)(2,1)S(1)}, bf16[2,4,128,2048]{3,2,1,0:T(8,128)(2,1)}, u32[]{:S(2)}) copy-start(bf16[2,4,128,2048]{3,2,1,0:T(8,128)(2,1)} %get-tuple-element.62) | copy-start | bytes 12582916
  133.7 2.5 copy-start.20
  136.2 4.6 %copy-start = (f32[1024,512]{1,0:T(8,128)S(1)}, f32[1024,512]{1,0:T(8,128)}, u32[]{:S(2)}) copy-start(f32[1024,512]{1,0:T(8,128)} %get-tuple-element.68.vsum_ref) | copy-start | bytes 6291460
  136.2 4.6 %copy-start.1 = (f32[1024,512]{1,0:T(8,128)S(1)}, f32[1024,512]{1,0:T(8,128)}, u32[]{:S(2)}) copy-start(f32[1024,512]{1,0:T(8,128)} %get-tuple-element.72.y_ref) | copy-start | bytes 6291460
  136.2 4.6 %copy-start.5 = (bf16[1024,512]{1,0:T(8,128)(2,1)S(1)}, bf16[1024,512]{1,0:T(8,128)(2,1)}, u32[]{:S(2)}) copy-start(bf16[1024,512]{1,0:T(8,128)(2,1)} %get-tuple-element.66.val_ref) | copy-start | bytes 3145732
  136.2 4.6 %copy-start.6 = (f32[1024,256]{1,0:T(8,128)S(1)}, f32[1024,256]{1,0:T(8,128)}, u32[]{:S(2)}) copy-start(f32[1024,256]{1,0:T(8,128)} %get-tuple-element.69.ksum_ref) | copy-start | bytes 3145732
  136.3 4.6 %copy-start.7 = (bf16[8,128,512]{2,1,0:T(8,128)(2,1)S(1)}, bf16[8,128,512]{2,1,0:T(8,128)(2,1)}, u32[]{:S(2)}) copy-start(bf16[8,128,512]{2,1,0:T(8,128)(2,1)} %get-tuple-element.73.state_ref) | copy-start | bytes 3145732
  136.3 4.6 %copy-start.8 = (bf16[1024,256]{1,0:T(8,128)(2,1)S(1)}, bf16[1024,256]{1,0:T(8,128)(2,1)}, u32[]{:S(2)}) copy-start(bf16[1024,256]{1,0:T(8,128)(2,1)} %get-tuple-element.67.key_ref) | copy-start | bytes 1572868
  136.3 4.6 %copy-start.9 = (f32[1024,128]{1,0:T(8,128)S(1)}, f32[1024,128]{1,0:T(8,128)}, u32[]{:S(2)}) copy-start(f32[1024,128]{1,0:T(8,128)} %get-tuple-element.70.raw_ref) | copy-start | bytes 1572868
  136.3 4.6 %copy-start.10 = (f32[1024,128]{1,0:T(8,128)S(1)}, f32[1024,128]{1,0:T(8,128)}, u32[]{:S(2)}) copy-start(f32[1024,128]{1,0:T(8,128)} %get-tuple-element.71.cum_ref) | copy-start | bytes 1572868
  136.3 4.6 %copy-start.11 = (f32[4,4352]{1,0:T(4,128)S(1)}, f32[4,4352]{1,0:T(4,128)}, u32[]{:S(2)}) copy-start(f32[4,4352]{1,0:T(4,128)} %conv_ref.3) | copy-start | bytes 208900
  136.3 4.6 %copy-start.15 = (s32[2,1,8]{2,1,0:T(1,128)S(1)}, s32[2,1,8]{2,1,0:T(1,128)}, u32[]{:S(2)}) copy-start(s32[2,1,8]{2,1,0:T(1,128)} %slice.3) | copy-start | bytes 196
  136.3 4.6 %copy-start.17 = (f32[8,128]{1,0:T(8,128)S(1)}, f32[8,128]{1,0:T(8,128)}, u32[]{:S(2)}) copy-start(f32[8,128]{1,0:T(8,128)} %get-tuple-element.65.head_ref) | copy-start | bytes 12292
  136.3 36.3 %slice-start = ((s8[5767168]{0:T(1024)(128)(4,1)}), s8[4194304]{0:T(1024)(128)(4,1)S(1)}, s32[]{:S(2)}) async-start(s8[5767168]{0:T(1024)(128)(4,1)} %bitcast.40), calls=%async_computation | async-start | bytes 8388608
  140.9 31.7 %slice-start.1 = ((s8[5767168]{0:T(1024)(128)(4,1)}), s8[1572864]{0:T(1024)(128)(4,1)S(1)}, s32[]{:S(2)}) async-start(s8[5767168]{0:T(1024)(128)(4,1)} %bitcast.40), calls=%async_computation.1 | async-start | bytes 3145728
  140.9 31.7 %copy-start.18 = (bf16[2,4,128,2048]{3,2,1,0:T(8,128)(2,1)S(1)}, bf16[2,4,128,2048]{3,2,1,0:T(8,128)(2,1)}, u32[]{:S(2)}) copy-start(bf16[2,4,128,2048]{3,2,1,0:T(8,128)(2,1)} %get-tuple-element.57) | copy-start | bytes 12582916
  179.9 8.7 %copy-start.12 = (f32[2048]{0:T(1024)S(1)}, f32[2048]{0:T(1024)}, u32[]{:S(2)}) copy-start(f32[2048]{0:T(1024)} %param.18) | copy-start | bytes 24580
  188.6 85.7 %copy-start.2 = (bf16[1,128,2048]{2,1,0:T(8,128)(2,1)S(1)}, bf16[1,128,2048]{2,1,0:T(8,128)(2,1)}, u32[]{:S(2)}) copy-start(bf16[1,128,2048]{2,1,0:T(8,128)(2,1)} %x_ref.1) | copy-start | bytes 1572868
  188.6 85.7 %copy-start.3 = (bf16[1,128,2048]{2,1,0:T(8,128)(2,1)S(1)}, bf16[1,128,2048]{2,1,0:T(8,128)(2,1)}, u32[]{:S(2)}) copy-start(bf16[1,128,2048]{2,1,0:T(8,128)(2,1)} %cot_ref.3) | copy-start | bytes 1572868
  188.6 85.7 %copy-start.13 = (f32[128,128]{1,0:T(8,128)S(1)}, f32[128,128]{1,0:T(8,128)}, u32[]{:S(2)}) copy-start(f32[128,128]{1,0:T(8,128)} %get-tuple-element.55.inv_ref) | copy-start | bytes 196612

commit v9 on v8

--- a/solution.py
+++ b/solution.py
@@ -48,9 +48,9 @@
         self.ends = []
         total = 0
         for i in range(DOCS - 1):
-            total = total + meta_ref[seq, i]
+            total = total + meta_ref[seq, 0, i]
             self.ends.append(total)
-        self.count = meta_ref[seq, DOCS]
+        self.count = meta_ref[seq, 0, DOCS]
         self.pos = self.start + iota((CHUNK, 1), 0)
         self.doc = self.index(self.pos)
 
@@ -152,8 +152,8 @@
 
     @pl.when(i % 2 == 0)
     def _():
-        for lane in range(0, w_ref.shape[1], 256):
-            lanes = slice(lane, min(lane + 256, w_ref.shape[1]))
+        for lane in range(0, w_ref.shape[1], 512):
+            lanes = slice(lane, min(lane + 512, w_ref.shape[1]))
             proj_v[:, lanes] = mm(rows_ref[...], w_ref[:, lanes], NN)
 
     proj_ref = proj_v.at[pl.ds(pl.multiple_of(i % 2 * CHUNK, CHUNK), CHUNK)]
@@ -242,6 +242,12 @@
         late.end()
 
 
+def head_sums_of(prod, chosen):
+    high = prod.astype(bf16)
+    low = (prod - high.astype(f32)).astype(bf16)
+    return mm(jnp.concatenate([high, low], axis=1), chosen, NN)
+
+
 def backward_kernel(
     meta_ref, proj_ref, grad_ref, chan_ref, conv_ref, head_ref,
     val_ref, key_ref, vsum_ref, ksum_ref, raw_ref, cum_ref, y_ref, state_ref, sums_ref, branch_ref, go_ref,
@@ -290,8 +296,10 @@
     dwrite = jnp.zeros((CHUNK, N), f32)
     dread = jnp.zeros((CHUNK, N), f32)
     end_row = iota((CHUNK, 1), 0) == CHUNK - 1
-    dcum = jnp.zeros((CHUNK, LANES), f32)
-    ddt = jnp.zeros((CHUNK, LANES), f32)
+    carry_all = jnp.zeros((CHUNK, LANES), f32)
+    final_all = jnp.zeros((CHUNK, LANES), f32)
+    direct_all = jnp.zeros((CHUNK, LANES), f32)
+    gain_rows = []
     dcum_rows = []
     for pair in range(heads // 2):
         first = 2 * pair
@@ -324,9 +332,11 @@
         pushed = mm(write, gradb, NN)
         carry_p = pair_cols(low, carry_w, first)
         final_p = pair_cols(low, final_w, first)
-        carry_prod = dy * carried
-        final_prod = xf * pushed
-        gain_prod = jnp.sum(grad * old.astype(f32), axis=0, keepdims=True)
+        chosen = (cols == first + rows // P_SIZE).astype(bf16)
+        chosen = jnp.concatenate([chosen, chosen], axis=0)
+        carry_all = carry_all + head_sums_of(dy * carried, chosen)
+        final_all = final_all + head_sums_of(xf * pushed, chosen)
+        gain_rows.append(jnp.sum(grad * old.astype(f32), axis=0, keepdims=True))
         weights = []
         for which, h in enumerate((first, first + 1)):
             col = dt[:, h : h + 1]
@@ -338,21 +348,7 @@
             direct = dw * decay * scores_t
             ddt_in = jnp.sum(direct, axis=1, keepdims=True)
             dcum_rows.append(jnp.sum(direct * col, axis=0, keepdims=True))
-            half = low if which == 0 else ~low
-            half_row = low_row if which == 0 else ~low_row
-            carry_sum = jnp.sum(jnp.where(half, carry_prod, 0.0), axis=1, keepdims=True)
-            final_sum = jnp.sum(jnp.where(half, final_prod, 0.0), axis=1, keepdims=True)
-            push = final_w[:, h : h + 1] * final_sum
-            at_end = jnp.sum(push, axis=0, keepdims=True) + gain[:, h : h + 1] * jnp.sum(
-                jnp.where(half_row, gain_prod, 0.0), axis=1, keepdims=True
-            )
-            here = cols == h
-            ddt = jnp.where(here, ddt_in + final_d[:, h : h + 1] * final_sum, ddt)
-            dcum = jnp.where(
-                here,
-                carry_w[:, h : h + 1] * carry_sum - push - col * ddt_in + jnp.where(end_row, at_end, 0.0),
-                dcum,
-            )
+            direct_all = jnp.where(cols == h, ddt_in, direct_all)
         dx = mm(jnp.concatenate(weights, axis=1), dy_stack, NN)
         dv[:, lanes] = dx + final_p * pushed + chan_ref[6:7, lanes] * dy
         chan_sums[6:7, lanes] += jnp.sum(dy * xf, axis=0, keepdims=True)
@@ -363,6 +359,12 @@
     dsb = dscores_t.astype(bf16)
     dkeys = jnp.concatenate([dwrite + mm(dsb, read, NN), dread + mm(dsb, write, TN)], axis=1)
 
+    chosen = (iota((inner, LANES), 1) == iota((inner, LANES), 0) // P_SIZE).astype(f32)
+    gain_all = mm(jnp.broadcast_to(jnp.concatenate(gain_rows, axis=1), (8, inner)), chosen, NN, exact)[:1]
+    push = final_w * final_all
+    at_end = jnp.sum(push, axis=0, keepdims=True) + gain * gain_all
+    ddt = direct_all + final_d * final_all
+    dcum = carry_w * carry_all - push - dt * direct_all + jnp.where(end_row, at_end, 0.0)
     extra = jnp.concatenate(dcum_rows + [jnp.zeros((LANES - heads, CHUNK), f32)], axis=0)
     dlog = mm((cols >= rows).astype(f32), dcum + extra.T, NN, exact)
     rate = head_ref[1:2, :]
@@ -1235,7 +1237,6 @@
     )
     in_w = in_w.reshape(width, -1)
     normed = normed.reshape(length, width)
-    meta = meta[:, 0, :8]
 
     params = (conv_weight, row(conv_bias), row(norm_gain), row(step_bias), row(decay_log), row(skip_gain))
     *kept, gated, states, part, chan, head_vec, cot_all, out_w, projected = mixer_forward(

time: 279 us -> 278 us (level)
  no operation moved by 1% of the time
where the time goes in v9:
time: 278 us; the launch traced here: 277 us
  Pallas kernels  244 us (88%)
  matrix products  28.3 us (10%)
    pallas_call x1, Pallas kernels, scatter(): pl.pallas_call(scatter_kernel, out_shape=[jax.ShapeDtypeStruct((tokens, w...  85.8 us
    pallas_call x1, Pallas kernels, gather(): pl.pallas_call(gather_kernel, out_shape=[shape((peers, far, near, 2), (in...  84.3 us
    pallas_call x1, Pallas kernels, mixer_forward(): pl.pallas_call(partial(forward_kernel, span=span, heads=heads), grid=(chu...  32.3 us
    pallas_call x1, Pallas kernels, mixer_backward(): pl.pallas_call(partial(backward_kernel, span=span, heads=heads), grid=(ch...  31.6 us
    dot_general x5, matrix products, mm(): lax.dot_general(a, b, (dims, ((), ())), precision=precision, preferred_el...  28.3 us
    pallas_call x1, Pallas kernels, cube_total(): pl.pallas_call(total_kernel, out_shape=[jax.ShapeDtypeStruct(part.shape,...  7.85 us

profile of v9, /device:TPU:0, one launch (start us, length us, event | category | flops | bytes accessed | tf_op | source)
XLA Modules:
  0.0 277.2 jit_solution(17435566010554633330)
XLA Ops:
  1.3 1.3 broadcast_in_dim.24.bias_ref
  2.6 84.3 %gather_all.1 = (bf16[4,2,2,2,64,1408]{5,4,3,2,1,0:T(8,128)(2,1)}, bf16[2,2,128,2048]{3,2,1,0:T(8,128)(2,1)}, bf16[2,4,128,2048]{3,2,1,0:T(8,128)(2,1)}, bf16[2,...) custom-call(bf16[64,8448]{1,0:T(8,128)(2,1)} %in_ref.1, bf16[128,2048]{1,0:T(8,128)(2,1)} %out_ref.1, ...), custom_call_target="tpu_custom_call" | custom-call | tf_op jit(solution)/shard_map/gather_all/pallas_call | solution.py:844
  86.9 32.3 %mixer_forward.1 = (bf16[1024,512]{1,0:T(8,128)(2,1)}, bf16[1024,256]{1,0:T(8,128)(2,1)}, f32[1024,512]{1,0:T(8,128)}, f32[1024,256]{1,0:T(8,128)}, f32[1024,128...) custom-call(s32[2,8,128]{2,1,0:T(8,128)} %get-tuple-element.56.meta_, ...), custom_call_target="tpu_custom_call", output_to_operand_aliasing={{12}: (9, {}), {13}: (10, {})} | custom-call | flops 536870912 | bytes 12582912 | tf_op jit(solution)/shard_map/mixer_forward/pallas_call | solution.py:420
  119.2 0.0 copy-start.2
  119.2 0.0 copy-start.14
  119.2 0.0 copy-start.16
  119.2 5.4 %fusion.grad_ref = f32[1024,512]{1,0:T(8,128)S(1)} fusion(bf16[1024,2048]{1,0:T(8,128)(2,1)} %bitcast.43, bf16[512,2048]{1,0:T(8,128)(2,1)} %bitcast.46), kind=kOutput, calls=%fused_computation.4 | convolution fusion | flops 2147483648 | bytes 8388608 | tf_op jit(solution)/shard_map/dot_general | solution.py:26
  124.6 0.0 copy-done.2
  124.6 0.0 copy-done.14
  124.6 0.0 copy-done.16
  124.6 0.0 copy-start.19
  124.7 7.9 %cube_total.1 = (f32[16,128]{1,0:T(8,128)S(1)}, bf16[1024,512]{1,0:T(8,128)(2,1)S(1)}) custom-call(f32[16,128]{1,0:T(8,128)S(1)} %copy-done.16, f32[1024,512]{1,0:T(8,128)S(1)} %copy-done.2, f32[8,512]{1,0:T(8,128)S(1)} %copy-done.14, f32[1024,512]{1,0:T(8,128)S(1)} %fusion.grad_ref), custom_call_target="tpu_custom_call" | custom-call | tf_op jit(solution)/shard_map/cube_total/pallas_call | solution.py:905
  132.5 0.0 copy-done.19
  132.5 0.0 copy-start.20
  132.5 2.5 convolution_convert_fusion.2
  135.0 0.0 copy-done.20
  135.0 0.0 copy-start.3
  135.0 0.0 copy-start.4
  135.0 0.0 copy-start.5
  135.0 0.0 copy-start.6
  135.0 0.0 copy-start.7
  135.1 0.0 copy-start.8
  135.1 0.0 copy-start.9
  135.1 0.0 copy-start.10
  135.1 0.0 copy-start.11
  135.1 0.0 copy-start.15
  135.1 0.0 copy-start.17
  135.1 0.0 slice-start
  135.1 4.5 %convolution_convert_fusion.1 = bf16[1024,2048]{1,0:T(8,128)(2,1)} fusion(bf16[1024,512]{1,0:T(8,128)(2,1)S(1)} %get-tuple-element.77, bf16[512,2048]{1,0:T(8,128)(2,1)S(1)} %bitcast.47), kind=kOutput, calls=%fused_computation.2 | convolution fusion | flops 2149580800 | bytes 7340032 | tf_op jit(solution)/shard_map/dot_general | solution.py:26
  139.6 0.0 copy-done.3
  139.6 0.0 copy-done.4
  139.6 0.0 copy-done.5
  139.6 0.0 copy-done.6
  139.7 0.0 copy-done.7
  139.7 0.0 copy-done.8
  139.7 0.0 copy-done.9
  139.7 0.0 slice-start.1
  139.7 31.6 %mixer_backward.1 = (bf16[1024,1408]{1,0:T(8,128)(2,1)S(1)}, f32[8,4352]{1,0:T(8,128)S(1)}, bf16[2,2,128,2048]{3,2,1,0:T(8,128)(2,1)S(1)}, f32[128,2048]{1,0:T(8,128)S(1)}) custom-call(s32[2,8,128]{2,1,0:T(8,128)S(1)} %copy-done.15, f32[1024,1408]{1,0:T(8,128)} %get-tuple-element.61.proj_ref, f32[1024,512]{1,0:T(8,128)S(1)} %fusion.grad_ref, ...), custom_call_target="tpu_custom_call" | custom-call | flops 1610612736 | bytes 15728640 | tf_op jit(solution)/shard_map/mixer_backward/pallas_call | solution.py:466
  171.4 0.0 slice-done
  171.4 0.0 slice-done.1
  171.4 0.0 copy-done.18
  171.4 7.3 %multiply_reduce_fusion = (f32[2048]{0:T(1024)S(1)}, bf16[1024,2048]{1,0:T(8,128)(2,1)S(1)}) fusion(bf16[2,4,128,2048]{3,2,1,0:T(8,128)(2,1)S(1)} %copy-done.18, bf16[1024,1408]{1,0:T(8,128)(2,1)S(1)} %get-tuple-element.78, bf16[2048,1408]{1,0:T(8,128)(2,1)S(1)} %bitcast.39), kind=kOutput, calls=%fused_computation | convolution fusion | flops 5913966592 | bytes 17047552 | tf_op jit(solution)/shard_map/dot_general | solution.py:26
  178.7 0.0 copy-start.12
  178.7 8.7 %convolution_convert_fusion = bf16[2048,1408]{1,0:T(8,128)(2,1)} fusion(bf16[1024,2048]{1,0:T(8,128)(2,1)S(1)} %bitcast.42, bf16[1024,1408]{1,0:T(8,128)(2,1)S(1)} %get-tuple-element.78), kind=kOutput, calls=%fused_computation.1 | convolution fusion | flops 5908463616 | bytes 12845056 | tf_op jit(solution)/shard_map/dot_general | solution.py:26
  187.4 85.8 %scatter_all.1 = (f32[128,2048]{1,0:T(8,128)S(1)}, bf16[64,8192]{1,0:T(8,128)(2,1)S(1)}, f32[128,2048]{1,0:T(8,128)S(1)}, f32[64,384]{1,0:T(8,128)S(1)}, f32[8,4352]{1,0:T(8,128)S(1)}) custom-call(bf16[2,4,128,2048]{3,2,1,0:T(8,128)(2,1)S(1)} %bitcast.30, bf16[4,2,2,2,64,1408]{5,4,3,2,1,0:T(8,128)(2,1)} %bitcast.40, ...), custom_call_target="tpu_custom_call" | custom-call | bytes 250000000 | tf_op jit(solution)/shard_map/scatter_all/pallas_call | solution.py:1108
  273.2 2.3 finish.1
  275.5 0.7 reduce
  276.2 1.0 copy.32
  (13 shorter events, 0.0 us)
Async XLA Ops:
  119.2 5.4 %copy-start.2 = (f32[1024,512]{1,0:T(8,128)S(1)}, f32[1024,512]{1,0:T(8,128)}, u32[]{:S(2)}) copy-start(f32[1024,512]{1,0:T(8,128)} %get-tuple-element.75.gated_ref) | copy-start | bytes 6291460
  119.2 5.4 %copy-start.14 = (f32[8,512]{1,0:T(8,128)S(1)}, f32[8,512]{1,0:T(8,128)}, u32[]{:S(2)}) copy-start(f32[8,512]{1,0:T(8,128)} %get-tuple-element.64.chan_ref) | copy-start | bytes 49156
  119.2 5.4 %copy-start.16 = (f32[16,128]{1,0:T(8,128)S(1)}, f32[16,128]{1,0:T(8,128)}, u32[]{:S(2)}) copy-start(f32[16,128]{1,0:T(8,128)} %get-tuple-element.74.part_ref) | copy-start | bytes 24580
  124.6 7.9 %copy-start.19 = (bf16[2,4,128,2048]{3,2,1,0:T(8,128)(2,1)S(1)}, bf16[2,4,128,2048]{3,2,1,0:T(8,128)(2,1)}, u32[]{:S(2)}) copy-start(bf16[2,4,128,2048]{3,2,1,0:T(8,128)(2,1)} %get-tuple-element.62) | copy-start | bytes 12582916
  132.5 2.5 copy-start.20
  135.0 4.6 %copy-start.3 = (f32[1024,512]{1,0:T(8,128)S(1)}, f32[1024,512]{1,0:T(8,128)}, u32[]{:S(2)}) copy-start(f32[1024,512]{1,0:T(8,128)} %get-tuple-element.68.vsum_ref) | copy-start | bytes 6291460
  135.0 4.6 %copy-start.4 = (f32[1024,512]{1,0:T(8,128)S(1)}, f32[1024,512]{1,0:T(8,128)}, u32[]{:S(2)}) copy-start(f32[1024,512]{1,0:T(8,128)} %get-tuple-element.72.y_ref) | copy-start | bytes 6291460
  135.0 4.6 %copy-start.5 = (bf16[1024,512]{1,0:T(8,128)(2,1)S(1)}, bf16[1024,512]{1,0:T(8,128)(2,1)}, u32[]{:S(2)}) copy-start(bf16[1024,512]{1,0:T(8,128)(2,1)} %get-tuple-element.66.val_ref) | copy-start | bytes 3145732
  135.0 4.6 %copy-start.6 = (f32[1024,256]{1,0:T(8,128)S(1)}, f32[1024,256]{1,0:T(8,128)}, u32[]{:S(2)}) copy-start(f32[1024,256]{1,0:T(8,128)} %get-tuple-element.69.ksum_ref) | copy-start | bytes 3145732
  135.0 4.6 %copy-start.7 = (bf16[8,128,512]{2,1,0:T(8,128)(2,1)S(1)}, bf16[8,128,512]{2,1,0:T(8,128)(2,1)}, u32[]{:S(2)}) copy-start(bf16[8,128,512]{2,1,0:T(8,128)(2,1)} %get-tuple-element.73.state_ref) | copy-start | bytes 3145732
  135.1 4.6 %copy-start.8 = (bf16[1024,256]{1,0:T(8,128)(2,1)S(1)}, bf16[1024,256]{1,0:T(8,128)(2,1)}, u32[]{:S(2)}) copy-start(bf16[1024,256]{1,0:T(8,128)(2,1)} %get-tuple-element.67.key_ref) | copy-start | bytes 1572868
  135.1 4.6 %copy-start.9 = (f32[1024,128]{1,0:T(8,128)S(1)}, f32[1024,128]{1,0:T(8,128)}, u32[]{:S(2)}) copy-start(f32[1024,128]{1,0:T(8,128)} %get-tuple-element.70.raw_ref) | copy-start | bytes 1572868
  135.1 4.6 %copy-start.10 = (f32[1024,128]{1,0:T(8,128)S(1)}, f32[1024,128]{1,0:T(8,128)}, u32[]{:S(2)}) copy-start(f32[1024,128]{1,0:T(8,128)} %get-tuple-element.71.cum_ref) | copy-start | bytes 1572868
  135.1 4.6 %copy-start.11 = (f32[4,4352]{1,0:T(4,128)S(1)}, f32[4,4352]{1,0:T(4,128)}, u32[]{:S(2)}) copy-start(f32[4,4352]{1,0:T(4,128)} %conv_ref.3) | copy-start | bytes 208900
  135.1 4.6 %copy-start.15 = (s32[2,8,128]{2,1,0:T(8,128)S(1)}, s32[2,8,128]{2,1,0:T(8,128)}, u32[]{:S(2)}) copy-start(s32[2,8,128]{2,1,0:T(8,128)} %get-tuple-element.56.meta_ref) | copy-start | bytes 24580
  135.1 4.6 %copy-start.17 = (f32[8,128]{1,0:T(8,128)S(1)}, f32[8,128]{1,0:T(8,128)}, u32[]{:S(2)}) copy-start(f32[8,128]{1,0:T(8,128)} %get-tuple-element.65.head_ref) | copy-start | bytes 12292
  135.1 36.3 %slice-start = ((s8[5767168]{0:T(1024)(128)(4,1)}), s8[4194304]{0:T(1024)(128)(4,1)S(1)}, s32[]{:S(2)}) async-start(s8[5767168]{0:T(1024)(128)(4,1)} %bitcast.37), calls=%async_computation | async-start | bytes 8388608
  139.7 31.7 %slice-start.1 = ((s8[5767168]{0:T(1024)(128)(4,1)}), s8[1572864]{0:T(1024)(128)(4,1)S(1)}, s32[]{:S(2)}) async-start(s8[5767168]{0:T(1024)(128)(4,1)} %bitcast.37), calls=%async_computation.1 | async-start | bytes 3145728
  139.7 31.7 %copy-start.18 = (bf16[2,4,128,2048]{3,2,1,0:T(8,128)(2,1)S(1)}, bf16[2,4,128,2048]{3,2,1,0:T(8,128)(2,1)}, u32[]{:S(2)}) copy-start(bf16[2,4,128,2048]{3,2,1,0:T(8,128)(2,1)} %get-tuple-element.57) | copy-start | bytes 12582916
  178.7 8.7 %copy-start.12 = (f32[2048]{0:T(1024)S(1)}, f32[2048]{0:T(1024)}, u32[]{:S(2)}) copy-start(f32[2048]{0:T(1024)} %param.18) | copy-start | bytes 24580
  187.4 85.8 %copy-start = (bf16[1,128,2048]{2,1,0:T(8,128)(2,1)S(1)}, bf16[1,128,2048]{2,1,0:T(8,128)(2,1)}, u32[]{:S(2)}) copy-start(bf16[1,128,2048]{2,1,0:T(8,128)(2,1)} %x_ref.1) | copy-start | bytes 1572868
  187.4 85.8 %copy-start.1 = (bf16[1,128,2048]{2,1,0:T(8,128)(2,1)S(1)}, bf16[1,128,2048]{2,1,0:T(8,128)(2,1)}, u32[]{:S(2)}) copy-start(bf16[1,128,2048]{2,1,0:T(8,128)(2,1)} %cot_ref.3) | copy-start | bytes 1572868
  187.4 85.8 %copy-start.13 = (f32[128,128]{1,0:T(8,128)S(1)}, f32[128,128]{1,0:T(8,128)}, u32[]{:S(2)}) copy-start(f32[128,128]{1,0:T(8,128)} %get-tuple-element.55.inv_ref) | copy-start | bytes 196612

commit v10 on v9

--- a/solution.py
+++ b/solution.py
@@ -1180,8 +1180,8 @@
 
 
 def finish_kernel(
-    x_ref, cot_ref, gain_ref, inv_ref, og_ref, ob_ref, ow_ref, ok_ref, u_ref,
-    out_ref, gx_ref, gw_ref, gs_ref, gc_ref, gb_ref, gp_ref, gn_ref, g0_ref, g1_ref, g2_ref,
+    x_ref, cot_ref, gain_ref, inv_ref, go_ref, og_ref, ob_ref, ow_ref, ok_ref, u_ref,
+    out_ref, gx_ref, gw_ref, gs_ref, oo_ref, gc_ref, gb_ref, gp_ref, gn_ref, g0_ref, g1_ref, g2_ref,
 ):
     x = x_ref[0].astype(f32)
     out_ref[0] = (x + ob_ref[...]).astype(bf16)
@@ -1192,6 +1192,7 @@
     gw_ref[:, : 2 * E] = ow_ref[...].astype(f32)
     gw_ref[:, 2 * E :] = ok_ref[:, :KEYS]
     gs_ref[...] = ok_ref[:, KEYS : KEYS + H]
+    oo_ref[...] = go_ref[...]
     gc_ref[...] = u_ref[:CONV, :]
     gb_ref[...] = u_ref[CONV : CONV + 1, :]
     gn_ref[...] = u_ref[5:6, :E]
@@ -1200,7 +1201,7 @@
         ref[...] = u_ref[7:8, i * LANES : i * LANES + H]
 
 
-def finish(inputs, cotangent, gain, inv, sums):
+def finish(inputs, cotangent, gain, inv, grad_out, sums):
     tokens, width = inputs.shape[1:]
     og, ow, ob, ok, u = sums
     shape = lambda *dims: jax.ShapeDtypeStruct(dims, f32)
@@ -1209,13 +1210,13 @@
         finish_kernel,
         out_shape=[
             jax.ShapeDtypeStruct(inputs.shape, bf16), shape(*inputs.shape), shape(rows, 2 * E + KEYS), shape(rows, H),
-            shape(CONV, E + KEYS), shape(1, E + KEYS), shape(1, width), shape(1, E), shape(1, H), shape(1, H), shape(1, H),
+            shape(*grad_out.shape), shape(CONV, E + KEYS), shape(1, E + KEYS), shape(1, width), shape(1, E), shape(1, H), shape(1, H), shape(1, H),
         ],
-        in_specs=[VMEM] * 9,
-        out_specs=[VMEM] * 11,
+        in_specs=[VMEM] * 10,
+        out_specs=[VMEM] * 12,
         compiler_params=pltpu.CompilerParams(vmem_limit_bytes=32 * 2**20),
         name="finish",
-    )(inputs, cotangent, gain, inv, og, ob, ow, ok, u)
+    )(inputs, cotangent, gain, inv, grad_out, og, ob, ow, ok, u)
 
 
 def body(
@@ -1263,9 +1264,9 @@
         row(products),
         row(pre_gain),
     )
-    outs = finish(inputs, cotangent, row(pre_gain), inv, summed)
-    output, grad_inputs, grad_in_weight, grad_step_weight, grad_conv_weight = outs[:5]
-    grad_conv_bias, grad_pre_gain, grad_norm_gain, grad_step_bias, grad_decay_log, grad_skip = [o[0] for o in outs[5:]]
+    outs = finish(inputs, cotangent, row(pre_gain), inv, grad_out_weight, summed)
+    output, grad_inputs, grad_in_weight, grad_step_weight, grad_out_weight, grad_conv_weight = outs[:6]
+    grad_conv_bias, grad_pre_gain, grad_norm_gain, grad_step_bias, grad_decay_log, grad_skip = [o[0] for o in outs[6:]]
     return (
         output, grad_inputs, grad_pre_gain, grad_in_weight, grad_step_weight, grad_conv_weight, grad_conv_bias,
         grad_step_bias, grad_decay_log, grad_skip, grad_norm_gain, grad_out_weight,

time: 278 us -> 277 us (level)
  no operation moved by 1% of the time
where the time goes in v10:
time: 277 us
  Pallas kernels  245 us (88%)
  matrix products  28.3 us (10%)
    pallas_call x1, Pallas kernels, scatter(): pl.pallas_call(scatter_kernel, out_shape=[jax.ShapeDtypeStruct((tokens, w...  85.8 us
    pallas_call x1, Pallas kernels, gather(): pl.pallas_call(gather_kernel, out_shape=[shape((peers, far, near, 2), (in...  84.3 us
    pallas_call x1, Pallas kernels, mixer_forward(): pl.pallas_call(partial(forward_kernel, span=span, heads=heads), grid=(chu...  32.3 us
    pallas_call x1, Pallas kernels, mixer_backward(): pl.pallas_call(partial(backward_kernel, span=span, heads=heads), grid=(ch...  31.7 us
    dot_general x5, matrix products, mm(): lax.dot_general(a, b, (dims, ((), ())), precision=precision, preferred_el...  28.3 us
    pallas_call x1, Pallas kernels, cube_total(): pl.pallas_call(total_kernel, out_shape=[jax.ShapeDtypeStruct(part.shape,...  7.85 us

profile of v10, /device:TPU:0, one launch (start us, length us, event | category | flops | bytes accessed | tf_op | source)
XLA Modules:
  0.0 276.6 jit_solution(16262096274332513504)
XLA Ops:
  1.3 1.3 broadcast_in_dim.24.bias_ref
  2.6 84.3 %gather_all.1 = (bf16[4,2,2,2,64,1408]{5,4,3,2,1,0:T(8,128)(2,1)}, bf16[2,2,128,2048]{3,2,1,0:T(8,128)(2,1)}, bf16[2,4,128,2048]{3,2,1,0:T(8,128)(2,1)}, bf16[2,...) custom-call(bf16[64,8448]{1,0:T(8,128)(2,1)} %in_ref.1, bf16[128,2048]{1,0:T(8,128)(2,1)} %out_ref.1, ...), custom_call_target="tpu_custom_call" | custom-call | tf_op jit(solution)/shard_map/gather_all/pallas_call | solution.py:844
  86.9 32.3 %mixer_forward.1 = (bf16[1024,512]{1,0:T(8,128)(2,1)}, bf16[1024,256]{1,0:T(8,128)(2,1)}, f32[1024,512]{1,0:T(8,128)}, f32[1024,256]{1,0:T(8,128)}, f32[1024,128...) custom-call(s32[2,8,128]{2,1,0:T(8,128)} %get-tuple-element.57.meta_, ...), custom_call_target="tpu_custom_call", output_to_operand_aliasing={{12}: (9, {}), {13}: (10, {})} | custom-call | flops 536870912 | bytes 12582912 | tf_op jit(solution)/shard_map/mixer_forward/pallas_call | solution.py:420
  119.2 0.0 copy-start
  119.2 0.0 copy-start.14
  119.2 0.0 copy-start.16
  119.2 5.4 %fusion.grad_ref = f32[1024,512]{1,0:T(8,128)S(1)} fusion(bf16[1024,2048]{1,0:T(8,128)(2,1)} %bitcast.43, bf16[512,2048]{1,0:T(8,128)(2,1)} %bitcast.46), kind=kOutput, calls=%fused_computation.4 | convolution fusion | flops 2147483648 | bytes 8388608 | tf_op jit(solution)/shard_map/dot_general | solution.py:26
  124.6 0.0 copy-done
  124.6 0.0 copy-done.14
  124.6 0.0 copy-done.16
  124.6 0.0 copy-start.19
  124.7 7.9 %cube_total.1 = (f32[16,128]{1,0:T(8,128)S(1)}, bf16[1024,512]{1,0:T(8,128)(2,1)S(1)}) custom-call(f32[16,128]{1,0:T(8,128)S(1)} %copy-done.16, f32[1024,512]{1,0:T(8,128)S(1)} %copy-done, f32[8,512]{1,0:T(8,128)S(1)} %copy-done.14, f32[1024,512]{1,0:T(8,128)S(1)} %fusion.grad_ref), custom_call_target="tpu_custom_call" | custom-call | tf_op jit(solution)/shard_map/cube_total/pallas_call | solution.py:905
  132.5 0.0 copy-done.19
  132.5 0.0 copy-start.20
  132.5 2.5 convolution_convert_fusion.2
  135.0 0.0 copy-done.20
  135.0 0.0 copy-start.3
  135.0 0.0 copy-start.4
  135.0 0.0 copy-start.5
  135.0 0.0 copy-start.6
  135.0 0.0 copy-start.7
  135.1 0.0 copy-start.8
  135.1 0.0 copy-start.9
  135.1 0.0 copy-start.10
  135.1 0.0 copy-start.11
  135.1 0.0 copy-start.15
  135.1 0.0 copy-start.17
  135.1 0.0 slice-start
  135.1 4.5 %convolution_convert_fusion.1 = bf16[1024,2048]{1,0:T(8,128)(2,1)} fusion(bf16[1024,512]{1,0:T(8,128)(2,1)S(1)} %get-tuple-element.78, bf16[512,2048]{1,0:T(8,128)(2,1)S(1)} %bitcast.47), kind=kOutput, calls=%fused_computation.2 | convolution fusion | flops 2149580800 | bytes 7340032 | tf_op jit(solution)/shard_map/dot_general | solution.py:26
  139.6 0.0 copy-done.3
  139.6 0.0 copy-done.7
  139.6 0.0 copy-done.8
  139.6 0.0 copy-done.9
  139.6 0.0 copy-done.10
  139.7 0.0 copy-done.11
  139.7 0.0 copy-done.15
  139.7 0.0 copy-done.17
  139.7 0.0 slice-start.1
  139.7 31.7 %mixer_backward.1 = (bf16[1024,1408]{1,0:T(8,128)(2,1)S(1)}, f32[8,4352]{1,0:T(8,128)S(1)}, bf16[2,2,128,2048]{3,2,1,0:T(8,128)(2,1)S(1)}, f32[128,2048]{1,0:T(8,128)S(1)}) custom-call(s32[2,8,128]{2,1,0:T(8,128)S(1)} %copy-done.15, f32[1024,1408]{1,0:T(8,128)} %get-tuple-element.62.proj_ref, f32[1024,512]{1,0:T(8,128)S(1)} %fusion.grad_ref, ...), custom_call_target="tpu_custom_call" | custom-call | flops 1610612736 | bytes 15728640 | tf_op jit(solution)/shard_map/mixer_backward/pallas_call | solution.py:466
  171.4 0.0 slice-done
  171.4 0.0 slice-done.1
  171.4 0.0 copy-done.18
  171.4 7.3 %multiply_reduce_fusion = (f32[2048]{0:T(1024)S(1)}, bf16[1024,2048]{1,0:T(8,128)(2,1)S(1)}) fusion(bf16[2,4,128,2048]{3,2,1,0:T(8,128)(2,1)S(1)} %copy-done.18, bf16[1024,1408]{1,0:T(8,128)(2,1)S(1)} %get-tuple-element.80, bf16[2048,1408]{1,0:T(8,128)(2,1)S(1)} %bitcast.39), kind=kOutput, calls=%fused_computation | convolution fusion | flops 5913966592 | bytes 17047552 | tf_op jit(solution)/shard_map/dot_general | solution.py:26
  178.7 0.0 copy-start.12
  178.7 8.7 %convolution_convert_fusion = bf16[2048,1408]{1,0:T(8,128)(2,1)} fusion(bf16[1024,2048]{1,0:T(8,128)(2,1)S(1)} %bitcast.42, bf16[1024,1408]{1,0:T(8,128)(2,1)S(1)} %get-tuple-element.80), kind=kOutput, calls=%fused_computation.1 | convolution fusion | flops 5908463616 | bytes 12845056 | tf_op jit(solution)/shard_map/dot_general | solution.py:26
  187.4 85.8 %scatter_all.1 = (f32[128,2048]{1,0:T(8,128)S(1)}, bf16[64,8192]{1,0:T(8,128)(2,1)S(1)}, f32[128,2048]{1,0:T(8,128)S(1)}, f32[64,384]{1,0:T(8,128)S(1)}, f32[8,4352]{1,0:T(8,128)S(1)}) custom-call(bf16[2,4,128,2048]{3,2,1,0:T(8,128)(2,1)S(1)} %bitcast.30, bf16[4,2,2,2,64,1408]{5,4,3,2,1,0:T(8,128)(2,1)} %bitcast.40, ...), custom_call_target="tpu_custom_call" | custom-call | bytes 250000000 | tf_op jit(solution)/shard_map/scatter_all/pallas_call | solution.py:1108
  273.2 2.7 finish.1
  276.0 0.7 reduce
  (12 shorter events, 0.0 us)
Async XLA Ops:
  119.2 5.4 %copy-start = (f32[1024,512]{1,0:T(8,128)S(1)}, f32[1024,512]{1,0:T(8,128)}, u32[]{:S(2)}) copy-start(f32[1024,512]{1,0:T(8,128)} %get-tuple-element.76.gated_ref) | copy-start | bytes 6291460
  119.2 5.4 %copy-start.14 = (f32[8,512]{1,0:T(8,128)S(1)}, f32[8,512]{1,0:T(8,128)}, u32[]{:S(2)}) copy-start(f32[8,512]{1,0:T(8,128)} %get-tuple-element.65.chan_ref) | copy-start | bytes 49156
  119.2 5.4 %copy-start.16 = (f32[16,128]{1,0:T(8,128)S(1)}, f32[16,128]{1,0:T(8,128)}, u32[]{:S(2)}) copy-start(f32[16,128]{1,0:T(8,128)} %get-tuple-element.75.part_ref) | copy-start | bytes 24580
  124.6 7.9 %copy-start.19 = (bf16[2,4,128,2048]{3,2,1,0:T(8,128)(2,1)S(1)}, bf16[2,4,128,2048]{3,2,1,0:T(8,128)(2,1)}, u32[]{:S(2)}) copy-start(bf16[2,4,128,2048]{3,2,1,0:T(8,128)(2,1)} %get-tuple-element.63) | copy-start | bytes 12582916
  132.5 2.5 copy-start.20
  135.0 4.6 %copy-start.3 = (f32[1024,512]{1,0:T(8,128)S(1)}, f32[1024,512]{1,0:T(8,128)}, u32[]{:S(2)}) copy-start(f32[1024,512]{1,0:T(8,128)} %get-tuple-element.69.vsum_ref) | copy-start | bytes 6291460
  135.0 4.6 %copy-start.4 = (f32[1024,512]{1,0:T(8,128)S(1)}, f32[1024,512]{1,0:T(8,128)}, u32[]{:S(2)}) copy-start(f32[1024,512]{1,0:T(8,128)} %get-tuple-element.73.y_ref) | copy-start | bytes 6291460
  135.0 4.6 %copy-start.5 = (bf16[1024,512]{1,0:T(8,128)(2,1)S(1)}, bf16[1024,512]{1,0:T(8,128)(2,1)}, u32[]{:S(2)}) copy-start(bf16[1024,512]{1,0:T(8,128)(2,1)} %get-tuple-element.67.val_ref) | copy-start | bytes 3145732
  135.0 4.6 %copy-start.6 = (f32[1024,256]{1,0:T(8,128)S(1)}, f32[1024,256]{1,0:T(8,128)}, u32[]{:S(2)}) copy-start(f32[1024,256]{1,0:T(8,128)} %get-tuple-element.70.ksum_ref) | copy-start | bytes 3145732
  135.0 4.6 %copy-start.7 = (bf16[8,128,512]{2,1,0:T(8,128)(2,1)S(1)}, bf16[8,128,512]{2,1,0:T(8,128)(2,1)}, u32[]{:S(2)}) copy-start(bf16[8,128,512]{2,1,0:T(8,128)(2,1)} %get-tuple-element.74.state_ref) | copy-start | bytes 3145732
  135.1 4.6 %copy-start.8 = (bf16[1024,256]{1,0:T(8,128)(2,1)S(1)}, bf16[1024,256]{1,0:T(8,128)(2,1)}, u32[]{:S(2)}) copy-start(bf16[1024,256]{1,0:T(8,128)(2,1)} %get-tuple-element.68.key_ref) | copy-start | bytes 1572868
  135.1 4.6 %copy-start.9 = (f32[1024,128]{1,0:T(8,128)S(1)}, f32[1024,128]{1,0:T(8,128)}, u32[]{:S(2)}) copy-start(f32[1024,128]{1,0:T(8,128)} %get-tuple-element.71.raw_ref) | copy-start | bytes 1572868
  135.1 4.6 %copy-start.10 = (f32[1024,128]{1,0:T(8,128)S(1)}, f32[1024,128]{1,0:T(8,128)}, u32[]{:S(2)}) copy-start(f32[1024,128]{1,0:T(8,128)} %get-tuple-element.72.cum_ref) | copy-start | bytes 1572868
  135.1 4.6 %copy-start.11 = (f32[4,4352]{1,0:T(4,128)S(1)}, f32[4,4352]{1,0:T(4,128)}, u32[]{:S(2)}) copy-start(f32[4,4352]{1,0:T(4,128)} %conv_ref.3) | copy-start | bytes 208900
  135.1 4.6 %copy-start.15 = (s32[2,8,128]{2,1,0:T(8,128)S(1)}, s32[2,8,128]{2,1,0:T(8,128)}, u32[]{:S(2)}) copy-start(s32[2,8,128]{2,1,0:T(8,128)} %get-tuple-element.57.meta_ref) | copy-start | bytes 24580
  135.1 4.6 %copy-start.17 = (f32[8,128]{1,0:T(8,128)S(1)}, f32[8,128]{1,0:T(8,128)}, u32[]{:S(2)}) copy-start(f32[8,128]{1,0:T(8,128)} %get-tuple-element.66.head_ref) | copy-start | bytes 12292
  135.1 36.3 %slice-start = ((s8[5767168]{0:T(1024)(128)(4,1)}), s8[4194304]{0:T(1024)(128)(4,1)S(1)}, s32[]{:S(2)}) async-start(s8[5767168]{0:T(1024)(128)(4,1)} %bitcast.37), calls=%async_computation | async-start | bytes 8388608
  139.7 31.7 %slice-start.1 = ((s8[5767168]{0:T(1024)(128)(4,1)}), s8[1572864]{0:T(1024)(128)(4,1)S(1)}, s32[]{:S(2)}) async-start(s8[5767168]{0:T(1024)(128)(4,1)} %bitcast.37), calls=%async_computation.1 | async-start | bytes 3145728
  139.7 31.7 %copy-start.18 = (bf16[2,4,128,2048]{3,2,1,0:T(8,128)(2,1)S(1)}, bf16[2,4,128,2048]{3,2,1,0:T(8,128)(2,1)}, u32[]{:S(2)}) copy-start(bf16[2,4,128,2048]{3,2,1,0:T(8,128)(2,1)} %get-tuple-element.58) | copy-start | bytes 12582916
  178.7 8.7 %copy-start.12 = (f32[2048]{0:T(1024)S(1)}, f32[2048]{0:T(1024)}, u32[]{:S(2)}) copy-start(f32[2048]{0:T(1024)} %param.18) | copy-start | bytes 24580
  187.4 85.8 %copy-start.1 = (bf16[1,128,2048]{2,1,0:T(8,128)(2,1)S(1)}, bf16[1,128,2048]{2,1,0:T(8,128)(2,1)}, u32[]{:S(2)}) copy-start(bf16[1,128,2048]{2,1,0:T(8,128)(2,1)} %x_ref.1) | copy-start | bytes 1572868
  187.4 85.8 %copy-start.2 = (bf16[1,128,2048]{2,1,0:T(8,128)(2,1)S(1)}, bf16[1,128,2048]{2,1,0:T(8,128)(2,1)}, u32[]{:S(2)}) copy-start(bf16[1,128,2048]{2,1,0:T(8,128)(2,1)} %cot_ref.3) | copy-start | bytes 1572868
  187.4 85.8 %copy-start.13 = (f32[128,128]{1,0:T(8,128)S(1)}, f32[128,128]{1,0:T(8,128)}, u32[]{:S(2)}) copy-start(f32[128,128]{1,0:T(8,128)} %get-tuple-element.56.inv_ref) | copy-start | bytes 196612
